TPU v7x, 32 devices: a whole 2x2x4 slice. The times are simulated.
32 devices in a mesh: expert: 16 (over z, y, x), etp: 2 (over core).
Axes of the slice: x: 2, y: 2, z: 4, core: 2. Of those that a mesh axis runs over, the one named last changes fastest.
Arguments:
- hidden_in: bfloat16 [192, 4096], P('expert', 'etp'), may hold values from -6 to 6
- expert_ids: int32 [192, 8], P('expert'), may hold values from 0 to 15, all different within a row; in each aligned block of 12 rows (0 to 11, 12 to 23, ...) at most 7 rows name the same one
- gate_weights: float32 [192, 8], P('expert'), may hold values from 0.2 to 1
- out_grad: bfloat16 [192, 4096], P('expert', 'etp'), may hold values from -6 to 6
- gate_weight: bfloat16 [16, 4096, 1024], P('expert', None, 'etp'), may hold values from -0.09375 to 0.09375
- up_weight: bfloat16 [16, 4096, 1024], P('expert', None, 'etp'), may hold values from -0.09375 to 0.09375
- down_weight: bfloat16 [16, 1024, 4096], P('expert', 'etp'), may hold values from -0.1875 to 0.1875
Outputs:
- mixed_out: bfloat16 [192, 4096], P('expert', 'etp')
- input_grad: bfloat16 [192, 4096], P('expert', 'etp')
- down_grad: bfloat16 [16, 1024, 4096], P('expert', 'etp')
Inputs may be any that keep to these rules, and one draw needn't show every extreme that they name: `expert_ids`: each token names 8 different experts. Within each aligned block of 12 tokens no expert is named by more than 7 tokens, and in some block an expert is named by exactly 7 tokens.
All inputs are finite; a program needn't handle non-finite values.
Results may differ from a plain program's by a relative error of at most 0.018.
Values may be sent and summed in bfloat16 or wider, within the bound.
No kernel may reach another device: no remote copies, remote signals or barrier semaphores. Data moves between devices by JAX's collectives and lax.ppermute only.
A program may use at most 64 MiB of HBM per device.

v0:
```python
import jax
import jax.numpy as jnp
from jax import lax
from jax.sharding import PartitionSpec as P


def route_tables(expert_ids, experts, capacity):
    token_count, per_token = expert_ids.shape
    flat_ids = expert_ids.reshape(-1)
    onehot = (flat_ids[:, None] == jnp.arange(experts, dtype=jnp.int32)[None, :]).astype(jnp.int32)
    slot_rank = jnp.sum((jnp.cumsum(onehot, axis=0) - onehot) * onehot, axis=1)
    position = flat_ids * capacity + slot_rank
    placing = (
        jnp.arange(experts * capacity, dtype=jnp.int32)[:, None] == position[None, :]
    ).astype(jnp.float32)
    token_place = jnp.sum(placing.reshape(experts * capacity, token_count, per_token), axis=2)
    return (position, placing.astype(jnp.bfloat16), token_place.astype(jnp.bfloat16))


def contract_last(left, right):
    return lax.dot_general(
        left, right, (((1,), (1,)), ((), ())), preferred_element_type=jnp.float32
    )


def on_device(hidden_in, expert_ids, gate_weights, out_grad, gate_weight, up_weight, down_weight):
    token_count, per_token = expert_ids.shape
    experts = lax.axis_size("expert")
    capacity = min(token_count, token_count * per_token // experts + 1)
    width = gate_weight.shape[1]
    slice_width = hidden_in.shape[1]
    position, placing, token_place = route_tables(expert_ids, experts, capacity)
    gate_flat = gate_weights.reshape(-1)
    feature_count = hidden_in.shape[1]
    grad_slots = (
        jnp.repeat(out_grad.astype(jnp.float32), per_token, axis=0) * gate_flat[:, None]
    ).astype(jnp.bfloat16)
    rows_part = jnp.dot(token_place, hidden_in, preferred_element_type=jnp.float32).astype(
        jnp.bfloat16
    )
    grad_rows = jnp.dot(placing, grad_slots, preferred_element_type=jnp.float32).astype(
        jnp.bfloat16
    )
    send_in = rows_part.reshape(experts, capacity, feature_count)
    send_grad = grad_rows.reshape(experts, capacity, feature_count)
    part_in, part_grad = (
        lax.all_to_all(send_in, "expert", split_axis=0, concat_axis=0, tiled=True),
        lax.all_to_all(send_grad, "expert", split_axis=0, concat_axis=0, tiled=True),
    )
    rows_in, grad_in = (
        lax.all_gather(part_in, "etp", axis=2, tiled=True),
        lax.all_gather(part_grad, "etp", axis=2, tiled=True),
    )
    rows_in = rows_in.reshape(experts * capacity, width)
    grad_in = grad_in.reshape(experts * capacity, width)
    gate_matrix = gate_weight[0]
    up_matrix = up_weight[0]
    down_matrix = down_weight[0]
    gate_pre = jnp.dot(rows_in, gate_matrix, preferred_element_type=jnp.float32)
    up_pre = jnp.dot(rows_in, up_matrix, preferred_element_type=jnp.float32)
    sigmoid_gate = jax.nn.sigmoid(gate_pre)
    swish_gate = gate_pre * sigmoid_gate
    hidden_act = (swish_gate * up_pre).astype(jnp.bfloat16)
    out_part = jnp.dot(hidden_act, down_matrix, preferred_element_type=jnp.float32)
    act_grad = contract_last(grad_in, down_matrix)
    down_grad = lax.dot_general(
        hidden_act, grad_in, (((0,), (0,)), ((), ())), preferred_element_type=jnp.float32
    ).astype(jnp.bfloat16)
    gate_grad = (act_grad * up_pre * sigmoid_gate * (1.0 + gate_pre * (1.0 - sigmoid_gate))).astype(
        jnp.bfloat16
    )
    up_grad = (act_grad * swish_gate).astype(jnp.bfloat16)
    input_part = contract_last(gate_grad, gate_matrix) + contract_last(up_grad, up_matrix)
    out_sum, input_sum = (
        lax.psum_scatter(
            out_part.astype(jnp.bfloat16), "etp", scatter_dimension=1, tiled=True
        ).astype(jnp.float32),
        lax.psum_scatter(
            input_part.astype(jnp.bfloat16), "etp", scatter_dimension=1, tiled=True
        ).astype(jnp.float32),
    )
    expert_out = out_sum.astype(jnp.bfloat16).reshape(experts, capacity, slice_width)
    slot_grad = input_sum.astype(jnp.bfloat16).reshape(experts, capacity, slice_width)
    back_out, back_grad = (
        lax.all_to_all(expert_out, "expert", split_axis=0, concat_axis=0, tiled=True),
        lax.all_to_all(slot_grad, "expert", split_axis=0, concat_axis=0, tiled=True),
    )
    picked = jnp.take(back_out.reshape(experts * capacity, slice_width), position, axis=0)
    picked = picked.astype(jnp.float32).reshape(token_count, per_token, slice_width)
    mixed_out = jnp.sum(picked * gate_weights[:, :, None], axis=1).astype(jnp.bfloat16)
    returned = jnp.take(back_grad.reshape(experts * capacity, slice_width), position, axis=0)
    returned = returned.astype(jnp.float32).reshape(token_count, per_token, slice_width)
    input_grad = jnp.sum(returned, axis=1).astype(jnp.bfloat16)
    return (mixed_out, input_grad, down_grad[None])


def solution(mesh):
    return jax.shard_map(
        on_device,
        mesh=mesh,
        in_specs=(
            P("expert", "etp"),
            P("expert", None),
            P("expert", None),
            P("expert", "etp"),
            P("expert", None, "etp"),
            P("expert", None, "etp"),
            P("expert", "etp", None),
        ),
        out_specs=(P("expert", "etp"), P("expert", "etp"), P("expert", "etp", None)),
        check_vma=False,
    )
```

profile of v0, /device:TPU:0, one launch (start us, length us, event | category | flops | bytes accessed | tf_op | source)
XLA Modules:
  0.0 112.8 jit_solution(16406065969990321190)
XLA Ops:
  7.2 0.8 copy.18
  9.0 0.9 reshape.72
  9.9 8.3 %all-to-all-start = ((bf16[16,7,2048]{2,1,0:T(8,128)(2,1)}), bf16[16,7,2048]{2,1,0:T(8,128)(2,1)S(1)}, u32[]{:S(2)}, u32[]{:S(2)}) async-start(bf16[16,7,2048]{2,1,0:T(8,128)(2,1)} %reshape.72), calls=%async_computation | async-start | bytes 1048576 | tf_op jit(solution)/shard_map/all_to_all | solution.py:47
  18.3 0.8 copy.20
  19.1 0.9 convert_element_type.66
  20.0 0.3 convolution_convert_fusion.3
  20.3 0.9 reshape.79
  21.3 12.1 %all-to-all-done = bf16[16,7,2048]{2,1,0:T(8,128)(2,1)S(1)} async-done(((bf16[16,7,2048]{2,1,0:T(8,128)(2,1)}), bf16[16,7,2048]{2,1,0:T(8,128)(2,1)S(1)}, u32[]{:S(2)}, u32[]{:S(2)}) %all-to-all-start) | async-done | bytes 458784 | tf_op jit(solution)/shard_map/all_to_all | solution.py:47
  33.4 3.9 %all-to-all-start.2 = ((bf16[16,7,2048]{2,1,0:T(8,128)(2,1)}), bf16[16,7,2048]{2,1,0:T(8,128)(2,1)S(1)}, u32[]{:S(2)}, u32[]{:S(2)}) async-start(bf16[16,7,2048]{2,1,0:T(8,128)(2,1)} %reshape.79), calls=%async_computation.3 | async-start | bytes 1048576 | tf_op jit(solution)/shard_map/all_to_all | solution.py:48
  37.3 2.6 %all_gather.6 = bf16[16,7,4096]{2,1,0:T(8,128)(2,1)S(1)} all-gather(bf16[16,7,2048]{2,1,0:T(8,128)(2,1)S(1)} %all-to-all-done), channel_id=1, replica_groups=mesh['expert'=16,'etp'=2] {'etp'}, dimensions={2}, use_global_device_ids=true | all-gather | bytes 1376256 | tf_op jit(solution)/shard_map/all_gather | solution.py:51
  39.9 0.3 reshape.73
  40.2 3.1 %fusion.10 = f32[112,512]{1,0:T(8,128)S(1)} fusion(bf16[112,4096]{1,0:T(8,128)(2,1)S(1)} %reshape.73, bf16[1,4096,512]{2,1,0:T(8,128)(2,1)} %param.13), kind=kOutput, calls=%fused_computation.15 | convolution fusion | flops 469762048 | bytes 5341184 | tf_op jit(solution)/shard_map/dot_general | solution.py:59
  43.3 3.0 %multiply_convert_fusion.2 = (bf16[112,512]{1,0:T(8,128)(2,1)S(1)}, f32[112,512]{1,0:T(8,128)S(1)}) fusion(f32[112,512]{1,0:T(8,128)S(1)} %fusion.10, bf16[112,4096]{1,0:T(8,128)(2,1)S(1)} %reshape.73, bf16[1,4096,512]{2,1,0:T(8,128)(2,1)} %param.14), kind=kOutput, calls=%fused_computation.28 | convolution fusion | flops 470106112 | bytes 5685248 | tf_op jit(solution)/shard_map/dot_general | solution.py:60
  46.3 1.7 %convolution_convert_fusion.1 = bf16[112,4096]{1,0:T(8,128)(2,1)} fusion(bf16[112,512]{1,0:T(8,128)(2,1)S(1)} %get-tuple-element.6, bf16[1,512,4096]{2,1,0:T(8,128)(2,1)S(1)} %copy-done.1), kind=kOutput, calls=%fused_computation.6 | convolution fusion | flops 470220800 | bytes 5226496 | tf_op jit(solution)/shard_map/dot_general | solution.py:64
  48.1 3.6 %all-to-all-done.2 = bf16[16,7,2048]{2,1,0:T(8,128)(2,1)S(1)} async-done(((bf16[16,7,2048]{2,1,0:T(8,128)(2,1)}), bf16[16,7,2048]{2,1,0:T(8,128)(2,1)S(1)}, u32[]{:S(2)}, u32[]{:S(2)}) %all-to-all-start.2) | async-done | bytes 458784 | tf_op jit(solution)/shard_map/all_to_all | solution.py:48
  51.7 2.5 %all_gather.7 = bf16[16,7,4096]{2,1,0:T(8,128)(2,1)S(1)} all-gather(bf16[16,7,2048]{2,1,0:T(8,128)(2,1)S(1)} %all-to-all-done.2), channel_id=1, replica_groups=mesh['expert'=16,'etp'=2] {'etp'}, dimensions={2}, use_global_device_ids=true | all-gather | bytes 1376256 | tf_op jit(solution)/shard_map/all_gather | solution.py:52
  54.6 4.0 %fusion.2 = f32[112,512]{1,0:T(8,128)S(1)} fusion(bf16[112,4096]{1,0:T(8,128)(2,1)S(1)} %reshape.80, bf16[1,512,4096]{2,1,0:T(8,128)(2,1)} %param.15), kind=kOutput, calls=%fused_computation.7 | convolution fusion | flops 469762048 | bytes 5341184 | tf_op jit(solution)/shard_map/dot_general | solution.py:21
  58.6 1.4 %fusion.8 = f32[112,4096]{1,0:T(8,128)S(1)} fusion(bf16[1,4096,512]{2,1,0:T(8,128)(2,1)S(1)} %copy-done.3, f32[112,512]{1,0:T(8,128)S(1)} %fusion.10, f32[112,512]{1,0:T(8,128)S(1)} %fusion.2, f32[112,512]{1,0:T(8,128)S(1)} %get-tuple-element.7), kind=kOutput, calls=%fused_computation.13 | convolution fusion | flops 470335488 | bytes 6717440 | tf_op jit(solution)/shard_map/dot_general | solution.py:21
  60.1 0.7 copy-done.2
  60.8 2.4 %fusion.1 = bf16[112,4096]{1,0:T(8,128)(2,1)} fusion(f32[112,4096]{1,0:T(8,128)S(1)} %fusion.8, bf16[1,4096,512]{2,1,0:T(8,128)(2,1)S(1)} %copy-done.2, f32[112,512]{1,0:T(8,128)S(1)} %fusion.2, f32[112,512]{1,0:T(8,128)S(1)} %fusion.10), kind=kOutput, calls=%fused_computation.5 | convolution fusion | flops 471023616 | bytes 7405568 | tf_op jit(solution)/shard_map/dot_general | solution.py:21
  63.2 2.0 %reshape.74 = bf16[16,7,2048]{2,1,0:T(8,128)(2,1)} reshape(bf16[112,2048]{1,0:T(8,128)(2,1)} %reduce-scatter.3.cloned.1.call-done) | data formatting | bytes 917504 | tf_op jit(solution)/shard_map/reshape | solution.py:82
  65.2 3.8 %all-to-all-start.1 = ((bf16[16,7,2048]{2,1,0:T(8,128)(2,1)}), bf16[16,7,2048]{2,1,0:T(8,128)(2,1)S(1)}, u32[]{:S(2)}, u32[]{:S(2)}) async-start(bf16[16,7,2048]{2,1,0:T(8,128)(2,1)} %reshape.74), calls=%async_computation.2 | async-start | bytes 1048576 | tf_op jit(solution)/shard_map/all_to_all | solution.py:85
  69.0 0.9 reduce-scatter.5.cloned.1.call-done
  69.9 2.0 %reshape.81 = bf16[16,7,2048]{2,1,0:T(8,128)(2,1)} reshape(bf16[112,2048]{1,0:T(8,128)(2,1)} %reduce-scatter.5.cloned.1.call-done) | data formatting | bytes 917504 | tf_op jit(solution)/shard_map/reshape | solution.py:83
  71.9 12.6 %all-to-all-done.1 = bf16[16,7,2048]{2,1,0:T(8,128)(2,1)S(1)} async-done(((bf16[16,7,2048]{2,1,0:T(8,128)(2,1)}), bf16[16,7,2048]{2,1,0:T(8,128)(2,1)S(1)}, u32[]{:S(2)}, u32[]{:S(2)}) %all-to-all-start.1) | async-done | bytes 458784 | tf_op jit(solution)/shard_map/all_to_all | solution.py:85
  84.5 3.9 %all-to-all-start.3 = ((bf16[16,7,2048]{2,1,0:T(8,128)(2,1)}), bf16[16,7,2048]{2,1,0:T(8,128)(2,1)S(1)}, u32[]{:S(2)}, u32[]{:S(2)}) async-start(bf16[16,7,2048]{2,1,0:T(8,128)(2,1)} %reshape.81), calls=%async_computation.5 | async-start | bytes 1048576 | tf_op jit(solution)/shard_map/all_to_all | solution.py:86
  88.4 3.3 %fusion = bf16[1,512,4096]{2,1,0:T(8,128)(2,1)} fusion(bf16[112,512]{1,0:T(8,128)(2,1)S(1)} %get-tuple-element.6, bf16[112,4096]{1,0:T(8,128)(2,1)S(1)} %reshape.80), kind=kOutput, calls=%fused_computation.3 | convolution fusion | flops 471859200 | bytes 5226496 | tf_op jit(solution)/shard_map/dot_general | solution.py:66
  91.9 0.8 gather_fusion
  92.7 10.1 %all-to-all-done.3 = bf16[16,7,2048]{2,1,0:T(8,128)(2,1)S(1)} async-done(((bf16[16,7,2048]{2,1,0:T(8,128)(2,1)}), bf16[16,7,2048]{2,1,0:T(8,128)(2,1)S(1)}, u32[]{:S(2)}, u32[]{:S(2)}) %all-to-all-start.3) | async-done | bytes 458784 | tf_op jit(solution)/shard_map/all_to_all | solution.py:86
  102.9 0.8 gather_fusion.1
  103.8 1.3 %fusion.12 = bf16[12,2048]{1,0:T(8,128)(2,1)} fusion(bf16[96,2048]{1,0:T(8,128)(2,1)S(1)} %gather_fusion, f32[12,8]{1,0:T(8,128)S(1)} %copy.20, pred[96]{0:T(512)(128)(4,1)S(1)} %get-tuple-element.4), kind=kLoop, calls=%fused_computation.20 | loop fusion | flops 761856 | bytes 442848 | tf_op jit(solution)/shard_map/reduce_sum | solution.py:90
  105.0 0.9 bitcast_reduce_fusion
  (27 shorter events, 1.9 us)
Async XLA Ops:
  7.2 1.5 %copy-start = (bf16[12,2048]{1,0:T(8,128)(2,1)S(1)}, bf16[12,2048]{1,0:T(8,128)(2,1)}, u32[]{:S(2)}) copy-start(bf16[12,2048]{1,0:T(8,128)(2,1)} %param.9) | copy-start | bytes 147460
  9.9 23.5 %all-to-all-start = ((bf16[16,7,2048]{2,1,0:T(8,128)(2,1)}), bf16[16,7,2048]{2,1,0:T(8,128)(2,1)S(1)}, u32[]{:S(2)}, u32[]{:S(2)}) async-start(bf16[16,7,2048]{2,1,0:T(8,128)(2,1)} %reshape.72), calls=%async_computation | async-start | bytes 1048576 | tf_op jit(solution)/shard_map/all_to_all | solution.py:47
  33.4 18.3 %all-to-all-start.2 = ((bf16[16,7,2048]{2,1,0:T(8,128)(2,1)}), bf16[16,7,2048]{2,1,0:T(8,128)(2,1)S(1)}, u32[]{:S(2)}, u32[]{:S(2)}) async-start(bf16[16,7,2048]{2,1,0:T(8,128)(2,1)} %reshape.79), calls=%async_computation.3 | async-start | bytes 1048576 | tf_op jit(solution)/shard_map/all_to_all | solution.py:48
  37.3 25.9 %reduce-scatter.3.cloned.1.call-start = ((), (), s32[]{:S(2)}) async-start(), calls=%async_computation.6 | async-start | bytes 1376256 | tf_op jit(solution)/shard_map/reduce_scatter | solution.py:75
  40.2 6.1 %copy-start.1 = (bf16[1,512,4096]{2,1,0:T(8,128)(2,1)S(1)}, bf16[1,512,4096]{2,1,0:T(8,128)(2,1)}, u32[]{:S(2)}) copy-start(bf16[1,512,4096]{2,1,0:T(8,128)(2,1)} %param.15) | copy-start | bytes 12582916
  48.1 21.9 %reduce-scatter.5.cloned.1.call-start = ((), (), s32[]{:S(2)}) async-start(), calls=%async_computation.7 | async-start | bytes 1376256 | tf_op jit(solution)/shard_map/reduce_scatter | solution.py:78
  54.6 4.1 %copy-start.3 = (bf16[1,4096,512]{2,1,0:T(8,128)(2,1)S(1)}, bf16[1,4096,512]{2,1,0:T(8,128)(2,1)}, u32[]{:S(2)}) copy-start(bf16[1,4096,512]{2,1,0:T(8,128)(2,1)} %param.13) | copy-start | bytes 12582916
  58.6 2.2 %copy-start.2 = (bf16[1,4096,512]{2,1,0:T(8,128)(2,1)S(1)}, bf16[1,4096,512]{2,1,0:T(8,128)(2,1)}, u32[]{:S(2)}) copy-start(bf16[1,4096,512]{2,1,0:T(8,128)(2,1)} %param.14) | copy-start | bytes 12582916
  65.2 19.3 %all-to-all-start.1 = ((bf16[16,7,2048]{2,1,0:T(8,128)(2,1)}), bf16[16,7,2048]{2,1,0:T(8,128)(2,1)S(1)}, u32[]{:S(2)}, u32[]{:S(2)}) async-start(bf16[16,7,2048]{2,1,0:T(8,128)(2,1)} %reshape.74), calls=%async_computation.2 | async-start | bytes 1048576 | tf_op jit(solution)/shard_map/all_to_all | solution.py:85
  84.5 18.3 %all-to-all-start.3 = ((bf16[16,7,2048]{2,1,0:T(8,128)(2,1)}), bf16[16,7,2048]{2,1,0:T(8,128)(2,1)S(1)}, u32[]{:S(2)}, u32[]{:S(2)}) async-start(bf16[16,7,2048]{2,1,0:T(8,128)(2,1)} %reshape.81), calls=%async_computation.5 | async-start | bytes 1048576 | tf_op jit(solution)/shard_map/all_to_all | solution.py:86
Sparse Core Ops, SparseCore 0:
  48.2 9.6 reduce-scatter.2
  63.3 6.5 reduce-scatter.4
where the time goes:
time: 114 us; the launch traced here: 113 us
  waiting for transfers between devices  39.4 us (35%)
  starting transfers between devices  20 us (18%)
  matrix products  19.5 us (17%)
  between operations  14.2 us (12%)
  local copies, waits for them, and re-layouts  11 us (10%)
  blocking collectives  5.1 us (4%)
  other arithmetic  3.52 us (3%)
    all_to_all x1, waiting for transfers between devices, on_device(): lax.all_to_all(expert_out, 'expert', split_axis=0, concat_axis=0, tiled=T...  12.6 us
    all_to_all x1, waiting for transfers between devices, on_device(): lax.all_to_all(send_in, 'expert', split_axis=0, concat_axis=0, tiled=True)  12.1 us
    all_to_all x1, waiting for transfers between devices, on_device(): lax.all_to_all(slot_grad, 'expert', split_axis=0, concat_axis=0, tiled=True)  10.1 us
    all_to_all x1, starting transfers between devices, on_device(): lax.all_to_all(send_in, 'expert', split_axis=0, concat_axis=0, tiled=True)  8.31 us
    dot_general x3, matrix products, contract_last(): lax.dot_general(left, right, (((1,), (1,)), ((), ())), preferred_element_...  7.81 us
    all_to_all x1, starting transfers between devices, on_device(): lax.all_to_all(slot_grad, 'expert', split_axis=0, concat_axis=0, tiled=True)  3.89 us
    all_to_all x1, starting transfers between devices, on_device(): lax.all_to_all(send_grad, 'expert', split_axis=0, concat_axis=0, tiled=True)  3.89 us
    all_to_all x1, starting transfers between devices, on_device(): lax.all_to_all(expert_out, 'expert', split_axis=0, concat_axis=0, tiled=T...  3.8 us
  transfers between devices with their start and end apart: 6, of which 5 were waited for; matrix products, arithmetic and copies ran while one was open for 24% of the time, Pallas kernels for 0%

commit v1 on v0

v1 whole, which is shorter than its diff:
```python
import functools
import jax
import jax.numpy as jnp
from jax import lax
from jax.experimental import pallas as pl
from jax.experimental.pallas import tpu as pltpu
from jax.sharding import PartitionSpec as P

BF16 = jnp.bfloat16
F32 = jnp.float32
META = 128
VMEM_LIMIT = 48 * 1024 * 1024


def group_sizes(experts):
    inner = 1
    while inner * inner * 4 <= experts and experts % (inner * 2) == 0:
        inner *= 2
    return experts // inner, inner


def partner(index, step, size):
    return index ^ step if size & (size - 1) == 0 else (index + step) % size


def origin(index, step, size):
    return index ^ step if size & (size - 1) == 0 else (index - step) % size


def traced_partner(index, step, size):
    return index ^ step if size & (size - 1) == 0 else lax.rem(index + step, size)


def traced_origin(index, step, size):
    return index ^ step if size & (size - 1) == 0 else lax.rem(index + size - step, size)


def send_outer(x, step, outer, inner, back=False):
    move = origin if back else partner
    pairs = [
        (a * inner + b, move(a, step, outer) * inner + b) for a in range(outer) for b in range(inner)
    ]
    return lax.ppermute(x, "expert", pairs)


def send_inner(x, step, outer, inner, back=False):
    move = origin if back else partner
    pairs = [
        (a * inner + b, a * inner + move(b, step, inner)) for a in range(outer) for b in range(inner)
    ]
    return lax.ppermute(x, "expert", pairs)


def send_core(x, step, cores, back=False):
    move = origin if back else partner
    return lax.ppermute(x, "etp", [(i, move(i, step, cores)) for i in range(cores)])


def contract(left, right, left_dim, right_dim):
    return lax.dot_general(
        left, right, (((left_dim,), (right_dim,)), ((), ())), preferred_element_type=F32
    )


def whole_specs(count):
    return [pl.BlockSpec(memory_space=pltpu.VMEM)] * count


def any_specs(count):
    return [pl.BlockSpec(memory_space=pl.ANY)] * count


def params():
    return pltpu.CompilerParams(vmem_limit_bytes=VMEM_LIMIT)


def fold(x):
    half = x.shape[1] // 2
    return jnp.concatenate([x[:, :half], x[:, half:]], axis=0)


def stacked(refs, columns=None):
    parts = [r[...] if columns is None else r[:, columns] for r in refs]
    if len(parts) == 1:
        return parts[0]
    return jnp.concatenate([p.astype(F32) for p in parts], axis=0).astype(BF16)


def count_above(index, unit, total):
    value = jnp.zeros_like(index)
    for m in range(unit, total, unit):
        value = value + (index >= m).astype(jnp.int32)
    return value


def route_kernel(dims, *refs):
    outer, inner, tokens, top, cap, reach, half = dims
    blocks = refs[:outer]
    sends = refs[outer : outer + inner]
    pick_ref, gate_hi_ref, gate_lo_ref, gate_col_ref = refs[outer + inner :]
    rows = outer * 2 * tokens
    slots = inner * reach
    me = lax.axis_index("expert")
    my_inner = lax.rem(me, inner)
    my_base = me - my_inner
    meta = jnp.concatenate([r[:, half:].astype(F32) for r in blocks], axis=0)
    lane = lax.broadcasted_iota(jnp.int32, (rows, slots), 1)
    row = lax.broadcasted_iota(jnp.int32, (rows, slots), 0)
    step = count_above(lane, reach, slots)
    dest = jnp.zeros((rows, slots), F32)
    for q in range(inner):
        expert = (my_base + traced_partner(my_inner, q, inner)).astype(F32)
        dest = jnp.where(step == q, expert, dest)
    slot = lane - step * reach
    named = jnp.zeros((rows, slots), F32)
    gate = jnp.zeros((rows, slots), F32)
    for k in range(top):
        hit = meta[:, k : k + 1] == dest
        value = (
            meta[:, top + k : top + k + 1]
            + meta[:, 2 * top + k : 2 * top + k + 1]
            + meta[:, 3 * top + k : 3 * top + k + 1]
        )
        named = named + hit.astype(F32)
        gate = gate + jnp.where(hit, value, 0.0)
    left = lax.broadcasted_iota(jnp.int32, (rows, rows), 1)
    down = lax.broadcasted_iota(jnp.int32, (rows, rows), 0)
    same = count_above(left, tokens, rows) == count_above(down, tokens, rows)
    before = (same & (left < down)).astype(F32).astype(BF16)
    rank = jnp.dot(before, named.astype(BF16), preferred_element_type=F32)
    position = count_above(row, 2 * tokens, rows) * cap + rank.astype(jnp.int32)
    pick = jnp.where(position == slot, named, 0.0)
    gate = pick * gate
    gate_hi = gate.astype(BF16)
    rest = gate - gate_hi.astype(F32)
    gate_mid = rest.astype(BF16)
    gate_lo = (rest - gate_mid.astype(F32)).astype(BF16)
    part = count_above(row, tokens, rows)
    even = part - 2 * count_above(row, 2 * tokens, rows) == 0
    pick_left = jnp.where(even, pick, 0.0).astype(BF16)
    pick_right = jnp.where(even, 0.0, pick).astype(BF16)
    pick_ref[...] = jnp.concatenate([pick_left, pick_right], axis=1)
    gate_hi_ref[...] = jnp.concatenate(
        [jnp.where(even, gate_hi.astype(F32), 0.0), jnp.where(even, 0.0, gate_hi.astype(F32))], axis=1
    ).astype(BF16)
    gate_lo_ref[...] = jnp.concatenate(
        [jnp.where(even, gate_mid.astype(F32), 0.0), jnp.where(even, 0.0, gate_mid.astype(F32))], axis=1
    ).astype(BF16)
    ones = jnp.ones((rows, META), BF16)
    column = contract(gate_hi, ones, 0, 0) + contract(gate_mid, ones, 0, 0) + contract(gate_lo, ones, 0, 0)
    gate_col_ref[...] = 0.5 * column
    table = stacked(blocks, pl.ds(0, half))
    for side, chosen in enumerate((pick_left, pick_right)):
        out = contract(chosen, table, 0, 0).astype(BF16)
        for q in range(inner):
            sends[q][:, side * half : (side + 1) * half] = out[q * reach : (q + 1) * reach]


def pick_kernel(dims, *refs):
    outer, inner, reach, half = dims
    blocks = refs[:outer]
    pick_ref, gate_col_ref = refs[outer : outer + 2]
    sends = refs[outer + 2 :]
    slots = inner * reach
    table = stacked(blocks)
    scale = gate_col_ref[:, :1]
    for side in range(2):
        out = contract(pick_ref[:, side * slots : (side + 1) * slots], table, 0, 0)
        out = (out * scale).astype(BF16)
        for q in range(inner):
            sends[q][:, side * half : (side + 1) * half] = out[q * reach : (q + 1) * reach]


def start_pieces(pieces, stack, sems):
    reach = pieces[0].shape[0]
    copies = []
    for i, piece in enumerate(pieces):
        copy = pltpu.make_async_copy(piece, stack.at[pl.ds(i * reach, reach), :], sems.at[i])
        copy.start()
        copies.append(copy)
    return copies


def forward_kernel(dims, *refs):
    cores, inner, reach, width = dims
    pieces = refs[: cores * inner]
    gate_hbm, up_hbm, down_hbm = refs[cores * inner : cores * inner + 3]
    outs = refs[cores * inner + 3 :]
    gate_ref, up_ref, act_ref = outs[:3]
    parts = outs[3 : 3 + cores]
    gate_w, up_w, down_w, stack, piece_sems, weight_sems = outs[3 + cores :]
    core = lax.axis_index("etp")
    starts = [traced_partner(core, d, cores) * width for d in range(cores)]
    origins = [traced_origin(core, d, cores) * width for d in range(cores)]
    weights = []
    for d in range(cores):
        for n, (source, target) in enumerate(((gate_hbm, gate_w), (up_hbm, up_w))):
            span = pl.ds(pl.multiple_of(origins[d], width), width)
            copy = pltpu.make_async_copy(source.at[0, span, :], target.at[d], weight_sems.at[2 * d + n])
            copy.start()
            weights.append(copy)
    waits = start_pieces(pieces, stack, piece_sems)
    for d in reversed(range(cores)):
        span = pl.ds(pl.multiple_of(starts[d], width), width)
        copy = pltpu.make_async_copy(down_hbm.at[0, :, span], down_w.at[d], weight_sems.at[2 * cores + d])
        copy.start()
        weights.append(copy)
    gate_pre = None
    up_pre = None
    for d in range(cores):
        for copy in waits[d * inner : (d + 1) * inner]:
            copy.wait()
        rows = stack[d * inner * reach : (d + 1) * inner * reach, :]
        weights[2 * d].wait()
        term = jnp.dot(rows, gate_w[d], preferred_element_type=F32)
        gate_pre = term if gate_pre is None else gate_pre + term
        weights[2 * d + 1].wait()
        term = jnp.dot(rows, up_w[d], preferred_element_type=F32)
        up_pre = term if up_pre is None else up_pre + term
    act = (gate_pre * jax.nn.sigmoid(gate_pre) * up_pre).astype(BF16)
    gate_ref[...] = gate_pre
    up_ref[...] = up_pre
    act_ref[...] = act
    for n, d in enumerate(reversed(range(cores))):
        weights[2 * cores + n].wait()
        parts[d][...] = jnp.dot(act, down_w[d], preferred_element_type=F32).astype(BF16)


def backward_kernel(dims, *refs):
    cores, inner, reach, width = dims
    pieces = refs[: cores * inner]
    gate_hbm, up_hbm, down_hbm, gate_ref, up_ref = refs[cores * inner : cores * inner + 5]
    outs = refs[cores * inner + 5 :]
    parts = outs[:cores]
    gate_w, up_w, down_w, stack, piece_sems, weight_sems = outs[cores:]
    core = lax.axis_index("etp")
    starts = [traced_partner(core, d, cores) * width for d in range(cores)]
    origins = [traced_origin(core, d, cores) * width for d in range(cores)]
    weights = []
    for d in range(cores):
        span = pl.ds(pl.multiple_of(origins[d], width), width)
        copy = pltpu.make_async_copy(down_hbm.at[0, :, span], down_w.at[d], weight_sems.at[2 * cores + d])
        copy.start()
        weights.append(copy)
    waits = start_pieces(pieces, stack, piece_sems)
    for d in reversed(range(cores)):
        for n, (source, target) in enumerate(((gate_hbm, gate_w), (up_hbm, up_w))):
            span = pl.ds(pl.multiple_of(starts[d], width), width)
            copy = pltpu.make_async_copy(source.at[0, span, :], target.at[d], weight_sems.at[2 * d + n])
            copy.start()
            weights.append(copy)
    act_grad = None
    for d in range(cores):
        for copy in waits[d * inner : (d + 1) * inner]:
            copy.wait()
        rows = stack[d * inner * reach : (d + 1) * inner * reach, :]
        weights[d].wait()
        term = contract(rows, down_w[d], 1, 1)
        act_grad = term if act_grad is None else act_grad + term
    gate_pre = gate_ref[...]
    sigmoid = jax.nn.sigmoid(gate_pre)
    gate_grad = (act_grad * up_ref[...] * sigmoid * (1.0 + gate_pre * (1.0 - sigmoid))).astype(BF16)
    up_grad = (act_grad * (gate_pre * sigmoid)).astype(BF16)
    for n, d in enumerate(reversed(range(cores))):
        weights[cores + 2 * n].wait()
        weights[cores + 2 * n + 1].wait()
        part = contract(gate_grad, gate_w[d], 1, 1) + contract(up_grad, up_w[d], 1, 1)
        parts[d][...] = part.astype(BF16)


def down_kernel(dims, *refs):
    cores, inner, reach, width = dims
    pieces = refs[: cores * inner]
    act_ref, out_hbm, stack, result, piece_sems, out_sems = refs[cores * inner :]
    core = lax.axis_index("etp")
    waits = start_pieces(pieces, stack, piece_sems)
    act = act_ref[...]
    copies = []
    for d in range(cores):
        for copy in waits[d * inner : (d + 1) * inner]:
            copy.wait()
        rows = stack[d * inner * reach : (d + 1) * inner * reach, :]
        result[d] = contract(act, rows, 0, 0).astype(BF16)
        span = pl.ds(pl.multiple_of(traced_origin(core, d, cores) * width, width), width)
        copy = pltpu.make_async_copy(result.at[d], out_hbm.at[0, :, span], out_sems.at[d])
        copy.start()
        copies.append(copy)
    for copy in copies:
        copy.wait()


def split_kernel(dims, *refs):
    cores, inner, reach = dims
    total = refs[0][...].astype(F32)
    for part in refs[1:cores]:
        total = total + part[...].astype(F32)
    total = total.astype(BF16)
    for q in range(inner):
        refs[cores + q][...] = total[q * reach : (q + 1) * reach]


def combine_kernel(dims, weighted, *refs):
    outer, inner, unit, half = dims
    pieces = refs[:inner]
    tables = refs[inner : inner + weighted]
    outs = refs[inner + weighted :]
    rows = jnp.concatenate([p[...] for p in pieces], axis=0)
    slots = rows.shape[0]
    total = None
    for table in tables:
        term = jnp.dot(table[:, :slots], rows[:, :half], preferred_element_type=F32)
        term = term + jnp.dot(table[:, slots:], rows[:, half:], preferred_element_type=F32)
        total = term if total is None else total + term
    for b in range(outer):
        outs[b][...] = total[b * unit : (b + 1) * unit].astype(BF16)


def final_kernel(dims, *refs):
    tokens, half = dims
    total = refs[0][...].astype(F32)
    for part in refs[1:-1]:
        total = total + part[...].astype(F32)
    refs[-1][:, :half] = total[:tokens].astype(BF16)
    refs[-1][:, half:] = total[tokens:].astype(BF16)


def shape(rows, columns, kind=BF16):
    return jax.ShapeDtypeStruct((rows, columns), kind)


def on_device(hidden_in, expert_ids, gate_weights, out_grad, gate_weight, up_weight, down_weight):
    tokens, top = expert_ids.shape
    experts = lax.axis_size("expert")
    cores = lax.axis_size("etp")
    outer, inner = group_sizes(experts)
    cap = min(tokens, tokens * top // experts + 1)
    width = hidden_in.shape[1]
    half = width // 2
    hidden = gate_weight.shape[2]
    reach = -(-(outer * cap) // 16) * 16
    rows = inner * reach
    unit = 2 * tokens

    with jax.named_scope("prepare"):
        gate_hi = lax.reduce_precision(gate_weights, 8, 7)
        rest = gate_weights - gate_hi
        gate_mid = lax.reduce_precision(rest, 8, 7)
        meta = jnp.concatenate(
            [expert_ids.astype(F32), gate_hi, gate_mid, rest - gate_mid], axis=1
        ).astype(BF16)
        meta = jnp.pad(meta, ((0, 0), (0, META - 4 * top)))
        packed_in = jnp.concatenate([fold(hidden_in), jnp.concatenate([meta, meta], axis=0)], axis=1)
        packed_grad = fold(out_grad)

    with jax.named_scope("gather_blocks"):
        in_blocks = [packed_in] + [send_outer(packed_in, s, outer, inner) for s in range(1, outer)]
        grad_blocks = [packed_grad] + [send_outer(packed_grad, s, outer, inner) for s in range(1, outer)]

    send_shapes = [shape(reach, width)] * inner
    table_shape = shape(outer * unit, 2 * rows)
    with jax.named_scope("route"):
        routed = pl.pallas_call(
            functools.partial(route_kernel, (outer, inner, tokens, top, cap, reach, half)),
            out_shape=send_shapes + [table_shape] * 3 + [shape(rows, META, F32)],
            in_specs=whole_specs(outer),
            out_specs=whole_specs(inner + 4),
            compiler_params=params(),
            name="route",
        )(*in_blocks)
        in_sends, (pick, gate_hi, gate_lo, gate_col) = routed[:inner], routed[inner:]

    def exchange(sends):
        own = [sends[0]] + [send_inner(sends[q], q, outer, inner) for q in range(1, inner)]
        groups = [own]
        for d in range(1, cores):
            groups.append([send_core(piece, d, cores) for piece in own])
        return [piece for group in groups for piece in group]

    in_pieces = exchange(in_sends)

    with jax.named_scope("scale"):
        grad_sends = pl.pallas_call(
            functools.partial(pick_kernel, (outer, inner, reach, half)),
            out_shape=send_shapes,
            in_specs=whole_specs(outer + 2),
            out_specs=whole_specs(inner),
            compiler_params=params(),
            name="scale",
        )(*grad_blocks, pick, gate_col)
    grad_pieces = exchange(grad_sends)

    dims = (cores, inner, reach, width)
    weight_scratch = [
        pltpu.VMEM((cores, width, hidden), BF16),
        pltpu.VMEM((cores, width, hidden), BF16),
        pltpu.VMEM((cores, hidden, width), BF16),
        pltpu.VMEM((cores * rows, width), BF16),
        pltpu.SemaphoreType.DMA((cores * inner,)),
        pltpu.SemaphoreType.DMA((3 * cores,)),
    ]
    weight_bytes = 2 * (gate_weight.size + up_weight.size + down_weight.size)
    flops = 2 * rows * cores * width * hidden
    with jax.named_scope("forward"):
        gate_pre, up_pre, act, *out_parts = pl.pallas_call(
            functools.partial(forward_kernel, dims),
            out_shape=[shape(rows, hidden, F32)] * 2 + [shape(rows, hidden)] + [shape(rows, width)] * cores,
            in_specs=any_specs(cores * inner + 3),
            out_specs=whole_specs(3 + cores),
            scratch_shapes=weight_scratch,
            compiler_params=params(),
            cost_estimate=pl.CostEstimate(
                flops=3 * flops, bytes_accessed=weight_bytes, transcendentals=rows * hidden
            ),
            name="forward",
        )(*in_pieces, gate_weight, up_weight, down_weight)

    def give_back(parts):
        got = [parts[0]] + [send_core(parts[d], d, cores) for d in range(1, cores)]
        sends = pl.pallas_call(
            functools.partial(split_kernel, (cores, inner, reach)),
            out_shape=send_shapes,
            in_specs=whole_specs(cores),
            out_specs=whole_specs(inner),
            compiler_params=params(),
            name="split",
        )(*got)
        return [sends[0]] + [send_inner(sends[q], q, outer, inner, back=True) for q in range(1, inner)]

    def combine(pieces, tables):
        blocks = pl.pallas_call(
            functools.partial(combine_kernel, (outer, inner, unit, half), len(tables)),
            out_shape=[shape(unit, half)] * outer,
            in_specs=whole_specs(inner + len(tables)),
            out_specs=whole_specs(outer),
            compiler_params=params(),
            name="combine",
        )(*pieces, *tables)
        blocks = [blocks[0]] + [send_outer(blocks[s], s, outer, inner, back=True) for s in range(1, outer)]
        return pl.pallas_call(
            functools.partial(final_kernel, (tokens, half)),
            out_shape=shape(tokens, width),
            in_specs=whole_specs(outer),
            out_specs=pl.BlockSpec(memory_space=pltpu.VMEM),
            compiler_params=params(),
            name="final",
        )(*blocks)

    with jax.named_scope("return_out"):
        mixed_out = combine(give_back(out_parts), (gate_hi, gate_lo))

    with jax.named_scope("backward"):
        grad_parts = pl.pallas_call(
            functools.partial(backward_kernel, dims),
            out_shape=[shape(rows, width)] * cores,
            in_specs=any_specs(cores * inner + 3) + whole_specs(2),
            out_specs=whole_specs(cores),
            scratch_shapes=weight_scratch,
            compiler_params=params(),
            cost_estimate=pl.CostEstimate(
                flops=3 * flops, bytes_accessed=weight_bytes, transcendentals=rows * hidden
            ),
            name="backward",
        )(*grad_pieces, gate_weight, up_weight, down_weight, gate_pre, up_pre)

    with jax.named_scope("return_grad"):
        input_grad = combine(give_back(grad_parts), (pick,))

    with jax.named_scope("down_grad"):
        down_grad = pl.pallas_call(
            functools.partial(down_kernel, dims),
            out_shape=jax.ShapeDtypeStruct(down_weight.shape, BF16),
            in_specs=any_specs(cores * inner) + whole_specs(1),
            out_specs=pl.BlockSpec(memory_space=pl.ANY),
            scratch_shapes=[
                pltpu.VMEM((cores * rows, width), BF16),
                pltpu.VMEM((cores, hidden, width), BF16),
                pltpu.SemaphoreType.DMA((cores * inner,)),
                pltpu.SemaphoreType.DMA((cores,)),
            ],
            compiler_params=params(),
            cost_estimate=pl.CostEstimate(
                flops=flops, bytes_accessed=2 * down_weight.size, transcendentals=0
            ),
            name="down_grad",
        )(*grad_pieces, act)
    return (mixed_out, input_grad, down_grad)


def solution(mesh):
    return jax.shard_map(
        on_device,
        mesh=mesh,
        in_specs=(
            P("expert", "etp"),
            P("expert", None),
            P("expert", None),
            P("expert", "etp"),
            P("expert", None, "etp"),
            P("expert", None, "etp"),
            P("expert", "etp", None),
        ),
        out_specs=(P("expert", "etp"), P("expert", "etp"), P("expert", "etp", None)),
        check_vma=False,
    )
```

time: 114 us -> 70.9 us (0.62)
  waiting for transfers between devices: 39.4 us -> 9.56 us
  Pallas kernels: 0 us -> 19.7 us
  matrix products: 19.5 us -> 0 us
  starting transfers between devices: 20 us -> 36.5 us
  between operations: 14.2 us -> 0.78 us
  local copies, waits for them, and re-layouts: 11 us -> 2.51 us
  blocking collectives: 5.1 us -> 0 us
  other arithmetic: 3.52 us -> 1.51 us
    all_to_all x4 -> x0, waiting for transfers between devices: 38.4 us -> none  [the longest x1 12.6 us: on_device(): lax.all_to_all(expert_out, 'expert', split_axis=0, concat_axis=0, tiled=T...]
    ppermute x0 -> x34, starting transfers between devices: none -> 36.5 us  [the longest x12 20.2 us: send_outer(): return lax.ppermute(x, 'expert', pairs)]
    all_to_all x4 -> x0, starting transfers between devices: 19.9 us -> none  [the longest x1 8.31 us: on_device(): lax.all_to_all(send_in, 'expert', split_axis=0, concat_axis=0, tiled=True)]
    pallas_call x0 -> x11, Pallas kernels: none -> 19.7 us  [the longest x1 6.84 us: on_device(): pl.pallas_call(functools.partial(backward_kernel, dims), out_shape=[shape...]
    dot_general x9 -> x0, matrix products: 19.5 us -> none  [the longest x3 7.81 us: contract_last(): lax.dot_general(left, right, (((1,), (1,)), ((), ())), preferred_element_...]
    ppermute x0 -> x34, waiting for transfers between devices: none -> 9.56 us  [the longest x12 9.45 us: send_inner(): return lax.ppermute(x, 'expert', pairs)]
    reshape x8 -> x0, local copies, waits for them, and re-layouts: 6.76 us -> none  [the longest x1 1.96 us: on_device(): out_sum.astype(jnp.bfloat16).reshape(experts, capacity, slice_width)]
    all_gather x2 -> x0, blocking collectives: 5.1 us -> none  [the longest x1 2.56 us: on_device(): lax.all_gather(part_in, 'etp', axis=2, tiled=True)]
  transfers between devices with their start and end apart: 6 -> 34, of which waited for: 5 -> 7; matrix products, arithmetic and copies ran while one was open for 24% -> 1% of each run, Pallas kernels for 0% -> 27%
where the time goes in v1:
time: 70.9 us; the launch traced here: 70.6 us
  starting transfers between devices  36.5 us (51%)
  Pallas kernels  19.7 us (28%)
  waiting for transfers between devices  9.56 us (13%)
  local copies, waits for them, and re-layouts  2.51 us (4%)
  other arithmetic  1.51 us (2%)
  between operations  0.78 us (1%)
    ppermute x12, starting transfers between devices, send_outer(): return lax.ppermute(x, 'expert', pairs)  20.2 us
    ppermute x12, starting transfers between devices, send_inner(): return lax.ppermute(x, 'expert', pairs)  14.2 us
    ppermute x12, waiting for transfers between devices, send_inner(): return lax.ppermute(x, 'expert', pairs)  9.45 us
    pallas_call x1, Pallas kernels, on_device(): pl.pallas_call(functools.partial(backward_kernel, dims), out_shape=[shape...  6.84 us
    pallas_call x1, Pallas kernels, on_device(): pl.pallas_call(functools.partial(forward_kernel, dims), out_shape=[shape(...  5.46 us
    pallas_call x1, Pallas kernels, on_device(): pl.pallas_call(functools.partial(down_kernel, dims), out_shape=jax.ShapeD...  4.16 us
    ppermute x10, starting transfers between devices, send_core(): lax.ppermute(x, 'etp', [(i, move(i, step, cores)) for i in range(cores)])  2.18 us
    slice x2, local copies, waits for them, and re-layouts, fold(): return jnp.concatenate([x[:, :half], x[:, half:]], axis=0)  1.57 us
  transfers between devices with their start and end apart: 34, of which 7 were waited for; matrix products, arithmetic and copies ran while one was open for 1% of the time, Pallas kernels for 27%

profile of v1, /device:TPU:0, one launch (start us, length us, event | category | flops | bytes accessed | tf_op | source)
XLA Modules:
  0.0 70.6 jit_solution(2086447237662727307)
XLA Ops:
  0.6 0.7 reduce_precision.6
  1.3 0.8 %copy.15 = f32[12,8]{1,0:T(8,128)S(1)} copy(f32[12,8]{0,1:T(8,128)} %param.9) | data formatting | bytes 768 | tf_op args[2]
  2.1 0.7 convert_element_type.6
  2.9 0.8 %fusion.9 = (bf16[12,1024]{1,0:T(8,128)(2,1)S(1)}, bf16[12,1024]{1,0:T(8,128)(2,1)S(1)}) fusion(bf16[12,2048]{1,0:T(8,128)(2,1)} %param.7), kind=kLoop, calls=%fused_computation.14 | loop fusion | bytes 98304 | tf_op jit(solution)/shard_map/prepare/slice | solution.py:79
  3.9 5.1 %collective-permute-start.2 = (bf16[24,1152]{1,0:T(8,128)(2,1)S(1)}, bf16[24,1152]{1,0:T(8,128)(2,1)S(1)}, u32[]{:S(2)}, u32[]{:S(2)}) collective-permute-start(bf16[24,1152]{1,0:T(8,128)(2,1)S(1)} %maximum_maximum_fusion.refs_0_), channel_id=1, source_target_pairs={{0,24},{2,26},{4,28},{6,30},{8,16},{10,18},{12,20},{14,22},{16,8},... | collective-permute-start | bytes 165896 | tf_op jit(solution)/shard_map/gather_blocks/ppermute | solution.py:43
  9.6 0.8 %fusion.8 = (bf16[12,1024]{1,0:T(8,128)(2,1)S(1)}, bf16[12,1024]{1,0:T(8,128)(2,1)S(1)}) fusion(bf16[12,2048]{1,0:T(8,128)(2,1)} %param.10), kind=kLoop, calls=%fused_computation.13 | loop fusion | bytes 98304 | tf_op jit(solution)/shard_map/prepare/slice | solution.py:79
  10.4 3.8 %collective-permute-start.19 = (bf16[24,1024]{1,0:T(8,128)(2,1)S(1)}, bf16[24,1024]{1,0:T(8,128)(2,1)S(1)}, u32[]{:S(2)}, u32[]{:S(2)}) collective-permute-start(bf16[24,1024]{1,0:T(8,128)(2,1)S(1)} %pad_maximum_fusion.refs_0_), channel_id=1, source_target_pairs={{0,24},{2,26},{4,28},{6,30},{8,16},{10,18},{12,20},{14,22},{16,8},... | collective-permute-start | bytes 147464 | tf_op jit(solution)/shard_map/gather_blocks/ppermute | solution.py:43
  14.9 0.7 %route.1 = (bf16[32,2048]{1,0:T(8,128)(2,1)S(1)}, bf16[32,2048]{1,0:T(8,128)(2,1)S(1)}, bf16[32,2048]{1,0:T(8,128)(2,1)S(1)}, bf16[32,2048]{1,0:T(8,128)(2,1)S(1...) custom-call(bf16[24,1152]{1,0:T(8,128)(2,1)S(1)} %maximum_maximum_fu, ...), custom_call_target="tpu_custom_call" | custom-call | tf_op jit(solution)/shard_map/route/route/pallas_call | solution.py:362
  15.6 1.7 %collective-permute-start.3 = (bf16[32,2048]{1,0:T(8,128)(2,1)S(1)}, bf16[32,2048]{1,0:T(8,128)(2,1)S(1)}, u32[]{:S(2)}, u32[]{:S(2)}) collective-permute-start(bf16[32,2048]{1,0:T(8,128)(2,1)S(1)} %get-tuple-element.39), channel_id=1, source_target_pairs={{0,2},{2,0},{4,6},{6,4},{8,10},{10,8},{12,14},{14,12},{16,18},{18,... | collective-permute-start | bytes 393224 | tf_op jit(solution)/shard_map/ppermute | solution.py:51
  17.3 1.5 %collective-permute-start.4 = (bf16[32,2048]{1,0:T(8,128)(2,1)S(1)}, bf16[32,2048]{1,0:T(8,128)(2,1)S(1)}, u32[]{:S(2)}, u32[]{:S(2)}) collective-permute-start(bf16[32,2048]{1,0:T(8,128)(2,1)S(1)} %get-tuple-element.40), channel_id=1, source_target_pairs={{0,4},{2,6},{4,0},{6,2},{8,12},{10,14},{12,8},{14,10},{16,20},{18,... | collective-permute-start | bytes 393224 | tf_op jit(solution)/shard_map/ppermute | solution.py:51
  19.5 1.7 %collective-permute-start.20 = (bf16[32,2048]{1,0:T(8,128)(2,1)S(1)}, bf16[32,2048]{1,0:T(8,128)(2,1)S(1)}, u32[]{:S(2)}, u32[]{:S(2)}) collective-permute-start(bf16[32,2048]{1,0:T(8,128)(2,1)S(1)} %get-tuple-element.57), channel_id=1, source_target_pairs={{0,2},{2,0},{4,6},{6,4},{8,10},{10,8},{12,14},{14,12},{16,18},{18,... | collective-permute-start | bytes 393224 | tf_op jit(solution)/shard_map/ppermute | solution.py:51
  21.2 0.7 collective-permute-done.3.refs_1_
  21.9 1.5 %collective-permute-start.21 = (bf16[32,2048]{1,0:T(8,128)(2,1)S(1)}, bf16[32,2048]{1,0:T(8,128)(2,1)S(1)}, u32[]{:S(2)}, u32[]{:S(2)}) collective-permute-start(bf16[32,2048]{1,0:T(8,128)(2,1)S(1)} %get-tuple-element.58), channel_id=1, source_target_pairs={{0,4},{2,6},{4,0},{6,2},{8,12},{10,14},{12,8},{14,10},{16,20},{18,... | collective-permute-start | bytes 393224 | tf_op jit(solution)/shard_map/ppermute | solution.py:51
  23.4 1.7 %collective-permute-start.22 = (bf16[32,2048]{1,0:T(8,128)(2,1)S(1)}, bf16[32,2048]{1,0:T(8,128)(2,1)S(1)}, u32[]{:S(2)}, u32[]{:S(2)}) collective-permute-start(bf16[32,2048]{1,0:T(8,128)(2,1)S(1)} %get-tuple-element.59), channel_id=1, source_target_pairs={{0,6},{2,4},{4,2},{6,0},{8,14},{10,12},{12,10},{14,8},{16,22},{18,... | collective-permute-start | bytes 393224 | tf_op jit(solution)/shard_map/ppermute | solution.py:51
  26.2 1.4 %collective-permute-done.20.refs_1_ = bf16[32,2048]{1,0:T(8,128)(2,1)S(1)} collective-permute-done((bf16[32,2048]{1,0:T(8,128)(2,1)S(1)}, bf16[32,2048]{1,0:T(8,128)(2,1)S(1)}, u32[]{:S(2)}, u32[]{:S(2)}) %collective-permute-start.20) | collective-permute-done | bytes 131104 | tf_op jit(solution)/shard_map/ppermute | solution.py:51
  27.7 2.8 %collective-permute-done.21.refs_2_ = bf16[32,2048]{1,0:T(8,128)(2,1)S(1)} collective-permute-done((bf16[32,2048]{1,0:T(8,128)(2,1)S(1)}, bf16[32,2048]{1,0:T(8,128)(2,1)S(1)}, u32[]{:S(2)}, u32[]{:S(2)}) %collective-permute-start.21) | collective-permute-done | bytes 131104 | tf_op jit(solution)/shard_map/ppermute | solution.py:51
  31.5 5.5 %forward.1 = (f32[128,512]{1,0:T(8,128)S(1)}, f32[128,512]{1,0:T(8,128)S(1)}, bf16[128,512]{1,0:T(8,128)(2,1)S(1)}, bf16[128,2048]{1,0:T(8,128)(2,1)S(1)}, bf16[128,2048]{1,0:T(8,128)(2,1)S(1)}) custom-call(bf16[32,2048]{1,0:T(8,128)(2,1)S(1)} %get-tuple-element.38.refs_0_, bf16[32,2048]{1,0:T(8,128)(2,1)S(1)} %collective-permute-done.3.refs_1_, ...), custom_call_target="tpu_custom_call" | custom-call | flops 1610612736 | bytes 12582912 | tf_op jit(solution)/shard_map/forward/forward/pallas_call | solution.py:404
  37.1 6.8 %backward.1 = (bf16[128,2048]{1,0:T(8,128)(2,1)S(1)}, bf16[128,2048]{1,0:T(8,128)(2,1)S(1)}) custom-call(bf16[32,2048]{1,0:T(8,128)(2,1)S(1)} %get-tuple-element.56.refs_0_, bf16[32,2048]{1,0:T(8,128)(2,1)S(1)} %collective-permute-done.20.refs_1_, bf16[32,2048]{1,0:T(8,128)(2,1)S(1)} %collective-permute-done.21.refs_2_, ...), custom_call_target="tpu_custom_call" | custom-call | flops 1610612736 | bytes 12582912 | tf_op jit(solution)/shard_map/backward/backward/pallas_call | solution.py:452
  44.7 1.3 %collective-permute-start.12 = (bf16[32,2048]{1,0:T(8,128)(2,1)S(1)}, bf16[32,2048]{1,0:T(8,128)(2,1)S(1)}, u32[]{:S(2)}, u32[]{:S(2)}) collective-permute-start(bf16[32,2048]{1,0:T(8,128)(2,1)S(1)} %get-tuple-element.46), channel_id=1, source_target_pairs={{0,4},{2,6},{4,0},{6,2},{8,12},{10,14},{12,8},{14,10},{16,20},{18,... | collective-permute-start | bytes 393224 | tf_op jit(solution)/shard_map/return_out/ppermute | solution.py:51
  46.0 2.2 %collective-permute-start.13 = (bf16[32,2048]{1,0:T(8,128)(2,1)S(1)}, bf16[32,2048]{1,0:T(8,128)(2,1)S(1)}, u32[]{:S(2)}, u32[]{:S(2)}) collective-permute-start(bf16[32,2048]{1,0:T(8,128)(2,1)S(1)} %get-tuple-element.47), channel_id=1, source_target_pairs={{0,6},{2,4},{4,2},{6,0},{8,14},{10,12},{12,10},{14,8},{16,22},{18,... | collective-permute-start | bytes 393224 | tf_op jit(solution)/shard_map/return_out/ppermute | solution.py:51
  48.5 1.2 %collective-permute-start.29 = (bf16[32,2048]{1,0:T(8,128)(2,1)S(1)}, bf16[32,2048]{1,0:T(8,128)(2,1)S(1)}, u32[]{:S(2)}, u32[]{:S(2)}) collective-permute-start(bf16[32,2048]{1,0:T(8,128)(2,1)S(1)} %get-tuple-element.66), channel_id=1, source_target_pairs={{0,4},{2,6},{4,0},{6,2},{8,12},{10,14},{12,8},{14,10},{16,20},{18,... | collective-permute-start | bytes 393224 | tf_op jit(solution)/shard_map/return_grad/ppermute | solution.py:51
  49.6 1.4 %collective-permute-done.11.refs_1_ = bf16[32,2048]{1,0:T(8,128)(2,1)S(1)} collective-permute-done((bf16[32,2048]{1,0:T(8,128)(2,1)S(1)}, bf16[32,2048]{1,0:T(8,128)(2,1)S(1)}, u32[]{:S(2)}, u32[]{:S(2)}) %collective-permute-start.11) | collective-permute-done | bytes 131104 | tf_op jit(solution)/shard_map/return_out/ppermute | solution.py:51
  51.0 0.8 %collective-permute-start.30 = (bf16[32,2048]{1,0:T(8,128)(2,1)S(1)}, bf16[32,2048]{1,0:T(8,128)(2,1)S(1)}, u32[]{:S(2)}, u32[]{:S(2)}) collective-permute-start(bf16[32,2048]{1,0:T(8,128)(2,1)S(1)} %get-tuple-element.67), channel_id=1, source_target_pairs={{0,6},{2,4},{4,2},{6,0},{8,14},{10,12},{12,10},{14,8},{16,22},{18,... | collective-permute-start | bytes 393224 | tf_op jit(solution)/shard_map/return_grad/ppermute | solution.py:51
  51.9 2.5 %collective-permute-done.13.refs_3_ = bf16[32,2048]{1,0:T(8,128)(2,1)S(1)} collective-permute-done((bf16[32,2048]{1,0:T(8,128)(2,1)S(1)}, bf16[32,2048]{1,0:T(8,128)(2,1)S(1)}, u32[]{:S(2)}, u32[]{:S(2)}) %collective-permute-start.13) | collective-permute-done | bytes 131104 | tf_op jit(solution)/shard_map/return_out/ppermute | solution.py:51
  54.8 1.3 %collective-permute-start.14 = (bf16[24,1024]{1,0:T(8,128)(2,1)S(1)}, bf16[24,1024]{1,0:T(8,128)(2,1)S(1)}, u32[]{:S(2)}, u32[]{:S(2)}) collective-permute-start(bf16[24,1024]{1,0:T(8,128)(2,1)S(1)} %get-tuple-element.51), channel_id=1, source_target_pairs={{0,8},{2,10},{4,12},{6,14},{8,0},{10,2},{12,4},{14,6},{16,24},{18,... | collective-permute-start | bytes 147464 | tf_op jit(solution)/shard_map/return_out/ppermute | solution.py:43
  56.0 2.9 %collective-permute-start.15 = (bf16[24,1024]{1,0:T(8,128)(2,1)S(1)}, bf16[24,1024]{1,0:T(8,128)(2,1)S(1)}, u32[]{:S(2)}, u32[]{:S(2)}) collective-permute-start(bf16[24,1024]{1,0:T(8,128)(2,1)S(1)} %get-tuple-element.52), channel_id=1, source_target_pairs={{0,16},{2,18},{4,20},{6,22},{8,24},{10,26},{12,28},{14,30},{16,0},... | collective-permute-start | bytes 147464 | tf_op jit(solution)/shard_map/return_out/ppermute | solution.py:43
  59.0 1.4 %collective-permute-start.16 = (bf16[24,1024]{1,0:T(8,128)(2,1)S(1)}, bf16[24,1024]{1,0:T(8,128)(2,1)S(1)}, u32[]{:S(2)}, u32[]{:S(2)}) collective-permute-start(bf16[24,1024]{1,0:T(8,128)(2,1)S(1)} %get-tuple-element.53), channel_id=1, source_target_pairs={{0,24},{2,26},{4,28},{6,30},{8,16},{10,18},{12,20},{14,22},{16,8},... | collective-permute-start | bytes 147464 | tf_op jit(solution)/shard_map/return_out/ppermute | solution.py:43
  60.7 3.0 %collective-permute-start.32 = (bf16[24,1024]{1,0:T(8,128)(2,1)S(1)}, bf16[24,1024]{1,0:T(8,128)(2,1)S(1)}, u32[]{:S(2)}, u32[]{:S(2)}) collective-permute-start(bf16[24,1024]{1,0:T(8,128)(2,1)S(1)} %get-tuple-element.70), channel_id=1, source_target_pairs={{0,16},{2,18},{4,20},{6,22},{8,24},{10,26},{12,28},{14,30},{16,0},... | collective-permute-start | bytes 147464 | tf_op jit(solution)/shard_map/return_grad/ppermute | solution.py:43
  63.7 1.4 %collective-permute-start.33 = (bf16[24,1024]{1,0:T(8,128)(2,1)S(1)}, bf16[24,1024]{1,0:T(8,128)(2,1)S(1)}, u32[]{:S(2)}, u32[]{:S(2)}) collective-permute-start(bf16[24,1024]{1,0:T(8,128)(2,1)S(1)} %get-tuple-element.71), channel_id=1, source_target_pairs={{0,24},{2,26},{4,28},{6,30},{8,16},{10,18},{12,20},{14,22},{16,8},... | collective-permute-start | bytes 147464 | tf_op jit(solution)/shard_map/return_grad/ppermute | solution.py:43
  65.0 4.2 %down_grad.1 = bf16[1,512,4096]{2,1,0:T(8,128)(2,1)} custom-call(bf16[32,2048]{1,0:T(8,128)(2,1)S(1)} %get-tuple-element.56.refs_0_, bf16[32,2048]{1,0:T(8,128)(2,1)S(1)} %collective-permute-done.20.refs_1_, bf16[32,2048]{1,0:T(8,128)(2,1)S(1)} %collective-permute-done.21.refs_2_, bf16[32,2048]{1,0:T(8,128)(2,1)S(1)} %collective-permute-done.22.refs_3_, ...), custom_call_target="tpu_custom_call" | custom-call | flops 536870912 | bytes 4194304 | tf_op jit(solution)/shard_map/down_grad/down_grad/pallas_call | solution.py:469
  69.2 0.7 final.2
  69.9 0.7 final.3
  (58 shorter events, 6.2 us)
Async XLA Ops:
  3.9 10.4 %collective-permute-start.2 = (bf16[24,1152]{1,0:T(8,128)(2,1)S(1)}, bf16[24,1152]{1,0:T(8,128)(2,1)S(1)}, u32[]{:S(2)}, u32[]{:S(2)}) collective-permute-start(bf16[24,1152]{1,0:T(8,128)(2,1)S(1)} %maximum_maximum_fusion.refs_0_), channel_id=1, source_target_pairs={{0,24},{2,26},{4,28},{6,30},{8,16},{10,18},{12,20},{14,22},{16,8},... | collective-permute-start | bytes 165896 | tf_op jit(solution)/shard_map/gather_blocks/ppermute | solution.py:43
  9.0 5.9 %collective-permute-start.1 = (bf16[24,1152]{1,0:T(8,128)(2,1)S(1)}, bf16[24,1152]{1,0:T(8,128)(2,1)S(1)}, u32[]{:S(2)}, u32[]{:S(2)}) collective-permute-start(bf16[24,1152]{1,0:T(8,128)(2,1)S(1)} %maximum_maximum_fusion.refs_0_), channel_id=1, source_target_pairs={{0,16},{2,18},{4,20},{6,22},{8,24},{10,26},{12,28},{14,30},{16,0},... | collective-permute-start | bytes 165896 | tf_op jit(solution)/shard_map/gather_blocks/ppermute | solution.py:43
  9.0 5.9 %collective-permute-start = (bf16[24,1152]{1,0:T(8,128)(2,1)S(1)}, bf16[24,1152]{1,0:T(8,128)(2,1)S(1)}, u32[]{:S(2)}, u32[]{:S(2)}) collective-permute-start(bf16[24,1152]{1,0:T(8,128)(2,1)S(1)} %maximum_maximum_fusion.refs_0_), channel_id=1, source_target_pairs={{0,8},{2,10},{4,12},{6,14},{8,0},{10,2},{12,4},{14,6},{16,24},{18,... | collective-permute-start | bytes 165896 | tf_op jit(solution)/shard_map/gather_blocks/ppermute | solution.py:43
  10.4 8.4 %collective-permute-start.19 = (bf16[24,1024]{1,0:T(8,128)(2,1)S(1)}, bf16[24,1024]{1,0:T(8,128)(2,1)S(1)}, u32[]{:S(2)}, u32[]{:S(2)}) collective-permute-start(bf16[24,1024]{1,0:T(8,128)(2,1)S(1)} %pad_maximum_fusion.refs_0_), channel_id=1, source_target_pairs={{0,24},{2,26},{4,28},{6,30},{8,16},{10,18},{12,20},{14,22},{16,8},... | collective-permute-start | bytes 147464 | tf_op jit(solution)/shard_map/gather_blocks/ppermute | solution.py:43
  14.2 5.0 %collective-permute-start.18 = (bf16[24,1024]{1,0:T(8,128)(2,1)S(1)}, bf16[24,1024]{1,0:T(8,128)(2,1)S(1)}, u32[]{:S(2)}, u32[]{:S(2)}) collective-permute-start(bf16[24,1024]{1,0:T(8,128)(2,1)S(1)} %pad_maximum_fusion.refs_0_), channel_id=1, source_target_pairs={{0,16},{2,18},{4,20},{6,22},{8,24},{10,26},{12,28},{14,30},{16,0},... | collective-permute-start | bytes 147464 | tf_op jit(solution)/shard_map/gather_blocks/ppermute | solution.py:43
  14.2 5.0 %collective-permute-start.17 = (bf16[24,1024]{1,0:T(8,128)(2,1)S(1)}, bf16[24,1024]{1,0:T(8,128)(2,1)S(1)}, u32[]{:S(2)}, u32[]{:S(2)}) collective-permute-start(bf16[24,1024]{1,0:T(8,128)(2,1)S(1)} %pad_maximum_fusion.refs_0_), channel_id=1, source_target_pairs={{0,8},{2,10},{4,12},{6,14},{8,0},{10,2},{12,4},{14,6},{16,24},{18,... | collective-permute-start | bytes 147464 | tf_op jit(solution)/shard_map/gather_blocks/ppermute | solution.py:43
  15.6 6.3 %collective-permute-start.3 = (bf16[32,2048]{1,0:T(8,128)(2,1)S(1)}, bf16[32,2048]{1,0:T(8,128)(2,1)S(1)}, u32[]{:S(2)}, u32[]{:S(2)}) collective-permute-start(bf16[32,2048]{1,0:T(8,128)(2,1)S(1)} %get-tuple-element.39), channel_id=1, source_target_pairs={{0,2},{2,0},{4,6},{6,4},{8,10},{10,8},{12,14},{14,12},{16,18},{18,... | collective-permute-start | bytes 393224 | tf_op jit(solution)/shard_map/ppermute | solution.py:51
  17.3 6.1 %collective-permute-start.4 = (bf16[32,2048]{1,0:T(8,128)(2,1)S(1)}, bf16[32,2048]{1,0:T(8,128)(2,1)S(1)}, u32[]{:S(2)}, u32[]{:S(2)}) collective-permute-start(bf16[32,2048]{1,0:T(8,128)(2,1)S(1)} %get-tuple-element.40), channel_id=1, source_target_pairs={{0,4},{2,6},{4,0},{6,2},{8,12},{10,14},{12,8},{14,10},{16,20},{18,... | collective-permute-start | bytes 393224 | tf_op jit(solution)/shard_map/ppermute | solution.py:51
  18.8 6.9 %collective-permute-start.5 = (bf16[32,2048]{1,0:T(8,128)(2,1)S(1)}, bf16[32,2048]{1,0:T(8,128)(2,1)S(1)}, u32[]{:S(2)}, u32[]{:S(2)}) collective-permute-start(bf16[32,2048]{1,0:T(8,128)(2,1)S(1)} %get-tuple-element.41), channel_id=1, source_target_pairs={{0,6},{2,4},{4,2},{6,0},{8,14},{10,12},{12,10},{14,8},{16,22},{18,... | collective-permute-start | bytes 393224 | tf_op jit(solution)/shard_map/ppermute | solution.py:51
  19.2 6.5 %collective-permute-start.6 = (bf16[32,2048]{1,0:T(8,128)(2,1)S(1)}, bf16[32,2048]{1,0:T(8,128)(2,1)S(1)}, u32[]{:S(2)}, u32[]{:S(2)}) collective-permute-start(bf16[32,2048]{1,0:T(8,128)(2,1)S(1)} %get-tuple-element.38.refs_0_), channel_id=1, source_target_pairs={{0,1},{1,0},{2,3},{3,2},{4,5},{5,4},{6,7},{7,6},{8,9},{9,8},{10,11... | collective-permute-start | bytes 393224 | tf_op jit(solution)/shard_map/ppermute | solution.py:56
  19.5 8.1 %collective-permute-start.20 = (bf16[32,2048]{1,0:T(8,128)(2,1)S(1)}, bf16[32,2048]{1,0:T(8,128)(2,1)S(1)}, u32[]{:S(2)}, u32[]{:S(2)}) collective-permute-start(bf16[32,2048]{1,0:T(8,128)(2,1)S(1)} %get-tuple-element.57), channel_id=1, source_target_pairs={{0,2},{2,0},{4,6},{6,4},{8,10},{10,8},{12,14},{14,12},{16,18},{18,... | collective-permute-start | bytes 393224 | tf_op jit(solution)/shard_map/ppermute | solution.py:51
  21.9 8.6 %collective-permute-start.21 = (bf16[32,2048]{1,0:T(8,128)(2,1)S(1)}, bf16[32,2048]{1,0:T(8,128)(2,1)S(1)}, u32[]{:S(2)}, u32[]{:S(2)}) collective-permute-start(bf16[32,2048]{1,0:T(8,128)(2,1)S(1)} %get-tuple-element.58), channel_id=1, source_target_pairs={{0,4},{2,6},{4,0},{6,2},{8,12},{10,14},{12,8},{14,10},{16,20},{18,... | collective-permute-start | bytes 393224 | tf_op jit(solution)/shard_map/ppermute | solution.py:51
  23.4 7.1 %collective-permute-start.22 = (bf16[32,2048]{1,0:T(8,128)(2,1)S(1)}, bf16[32,2048]{1,0:T(8,128)(2,1)S(1)}, u32[]{:S(2)}, u32[]{:S(2)}) collective-permute-start(bf16[32,2048]{1,0:T(8,128)(2,1)S(1)} %get-tuple-element.59), channel_id=1, source_target_pairs={{0,6},{2,4},{4,2},{6,0},{8,14},{10,12},{12,10},{14,8},{16,22},{18,... | collective-permute-start | bytes 393224 | tf_op jit(solution)/shard_map/ppermute | solution.py:51
  25.7 5.3 %collective-permute-start.7 = (bf16[32,2048]{1,0:T(8,128)(2,1)S(1)}, bf16[32,2048]{1,0:T(8,128)(2,1)S(1)}, u32[]{:S(2)}, u32[]{:S(2)}) collective-permute-start(bf16[32,2048]{1,0:T(8,128)(2,1)S(1)} %collective-permute-done.3.refs_1_), channel_id=1, source_target_pairs={{0,1},{1,0},{2,3},{3,2},{4,5},{5,4},{6,7},{7,6},{8,9},{9,8},{10,11... | collective-permute-start | bytes 393224 | tf_op jit(solution)/shard_map/ppermute | solution.py:56
  25.7 5.4 %collective-permute-start.8 = (bf16[32,2048]{1,0:T(8,128)(2,1)S(1)}, bf16[32,2048]{1,0:T(8,128)(2,1)S(1)}, u32[]{:S(2)}, u32[]{:S(2)}) collective-permute-start(bf16[32,2048]{1,0:T(8,128)(2,1)S(1)} %collective-permute-done.4.refs_2_), channel_id=1, source_target_pairs={{0,1},{1,0},{2,3},{3,2},{4,5},{5,4},{6,7},{7,6},{8,9},{9,8},{10,11... | collective-permute-start | bytes 393224 | tf_op jit(solution)/shard_map/ppermute | solution.py:56
  30.5 6.6 %collective-permute-start.23 = (bf16[32,2048]{1,0:T(8,128)(2,1)S(1)}, bf16[32,2048]{1,0:T(8,128)(2,1)S(1)}, u32[]{:S(2)}, u32[]{:S(2)}) collective-permute-start(bf16[32,2048]{1,0:T(8,128)(2,1)S(1)} %get-tuple-element.56.refs_0_), channel_id=1, source_target_pairs={{0,1},{1,0},{2,3},{3,2},{4,5},{5,4},{6,7},{7,6},{8,9},{9,8},{10,11... | collective-permute-start | bytes 393224 | tf_op jit(solution)/shard_map/ppermute | solution.py:56
  30.5 6.6 %collective-permute-start.24 = (bf16[32,2048]{1,0:T(8,128)(2,1)S(1)}, bf16[32,2048]{1,0:T(8,128)(2,1)S(1)}, u32[]{:S(2)}, u32[]{:S(2)}) collective-permute-start(bf16[32,2048]{1,0:T(8,128)(2,1)S(1)} %collective-permute-done.20.refs_1_), channel_id=1, source_target_pairs={{0,1},{1,0},{2,3},{3,2},{4,5},{5,4},{6,7},{7,6},{8,9},{9,8},{10,11... | collective-permute-start | bytes 393224 | tf_op jit(solution)/shard_map/ppermute | solution.py:56
  31.0 6.1 %collective-permute-start.25 = (bf16[32,2048]{1,0:T(8,128)(2,1)S(1)}, bf16[32,2048]{1,0:T(8,128)(2,1)S(1)}, u32[]{:S(2)}, u32[]{:S(2)}) collective-permute-start(bf16[32,2048]{1,0:T(8,128)(2,1)S(1)} %collective-permute-done.21.refs_2_), channel_id=1, source_target_pairs={{0,1},{1,0},{2,3},{3,2},{4,5},{5,4},{6,7},{7,6},{8,9},{9,8},{10,11... | collective-permute-start | bytes 393224 | tf_op jit(solution)/shard_map/ppermute | solution.py:56
  31.1 6.1 %collective-permute-start.26 = (bf16[32,2048]{1,0:T(8,128)(2,1)S(1)}, bf16[32,2048]{1,0:T(8,128)(2,1)S(1)}, u32[]{:S(2)}, u32[]{:S(2)}) collective-permute-start(bf16[32,2048]{1,0:T(8,128)(2,1)S(1)} %collective-permute-done.22.refs_3_), channel_id=1, source_target_pairs={{0,1},{1,0},{2,3},{3,2},{4,5},{5,4},{6,7},{7,6},{8,9},{9,8},{10,11... | collective-permute-start | bytes 393224 | tf_op jit(solution)/shard_map/ppermute | solution.py:56
  37.0 7.5 %collective-permute-start.10 = (bf16[128,2048]{1,0:T(8,128)(2,1)S(1)}, bf16[128,2048]{1,0:T(8,128)(2,1)S(1)}, u32[]{:S(2)}, u32[]{:S(2)}) collective-permute-start(bf16[128,2048]{1,0:T(8,128)(2,1)S(1)} %get-tuple-element.43), channel_id=1, source_target_pairs={{0,1},{1,0},{2,3},{3,2},{4,5},{5,4},{6,7},{7,6},{8,9},{9,8},{10,11... | collective-permute-start | bytes 1572872 | tf_op jit(solution)/shard_map/return_out/ppermute | solution.py:56
  44.6 6.4 %collective-permute-start.11 = (bf16[32,2048]{1,0:T(8,128)(2,1)S(1)}, bf16[32,2048]{1,0:T(8,128)(2,1)S(1)}, u32[]{:S(2)}, u32[]{:S(2)}) collective-permute-start(bf16[32,2048]{1,0:T(8,128)(2,1)S(1)} %get-tuple-element.45), channel_id=1, source_target_pairs={{0,2},{2,0},{4,6},{6,4},{8,10},{10,8},{12,14},{14,12},{16,18},{18,... | collective-permute-start | bytes 393224 | tf_op jit(solution)/shard_map/return_out/ppermute | solution.py:51
  44.7 7.2 %collective-permute-start.12 = (bf16[32,2048]{1,0:T(8,128)(2,1)S(1)}, bf16[32,2048]{1,0:T(8,128)(2,1)S(1)}, u32[]{:S(2)}, u32[]{:S(2)}) collective-permute-start(bf16[32,2048]{1,0:T(8,128)(2,1)S(1)} %get-tuple-element.46), channel_id=1, source_target_pairs={{0,4},{2,6},{4,0},{6,2},{8,12},{10,14},{12,8},{14,10},{16,20},{18,... | collective-permute-start | bytes 393224 | tf_op jit(solution)/shard_map/return_out/ppermute | solution.py:51
  46.0 8.4 %collective-permute-start.13 = (bf16[32,2048]{1,0:T(8,128)(2,1)S(1)}, bf16[32,2048]{1,0:T(8,128)(2,1)S(1)}, u32[]{:S(2)}, u32[]{:S(2)}) collective-permute-start(bf16[32,2048]{1,0:T(8,128)(2,1)S(1)} %get-tuple-element.47), channel_id=1, source_target_pairs={{0,6},{2,4},{4,2},{6,0},{8,14},{10,12},{12,10},{14,8},{16,22},{18,... | collective-permute-start | bytes 393224 | tf_op jit(solution)/shard_map/return_out/ppermute | solution.py:51
  48.3 10.6 %collective-permute-start.28 = (bf16[32,2048]{1,0:T(8,128)(2,1)S(1)}, bf16[32,2048]{1,0:T(8,128)(2,1)S(1)}, u32[]{:S(2)}, u32[]{:S(2)}) collective-permute-start(bf16[32,2048]{1,0:T(8,128)(2,1)S(1)} %get-tuple-element.65), channel_id=1, source_target_pairs={{0,2},{2,0},{4,6},{6,4},{8,10},{10,8},{12,14},{14,12},{16,18},{18,... | collective-permute-start | bytes 393224 | tf_op jit(solution)/shard_map/return_grad/ppermute | solution.py:51
  48.5 11.9 %collective-permute-start.29 = (bf16[32,2048]{1,0:T(8,128)(2,1)S(1)}, bf16[32,2048]{1,0:T(8,128)(2,1)S(1)}, u32[]{:S(2)}, u32[]{:S(2)}) collective-permute-start(bf16[32,2048]{1,0:T(8,128)(2,1)S(1)} %get-tuple-element.66), channel_id=1, source_target_pairs={{0,4},{2,6},{4,0},{6,2},{8,12},{10,14},{12,8},{14,10},{16,20},{18,... | collective-permute-start | bytes 393224 | tf_op jit(solution)/shard_map/return_grad/ppermute | solution.py:51
  51.0 9.3 %collective-permute-start.30 = (bf16[32,2048]{1,0:T(8,128)(2,1)S(1)}, bf16[32,2048]{1,0:T(8,128)(2,1)S(1)}, u32[]{:S(2)}, u32[]{:S(2)}) collective-permute-start(bf16[32,2048]{1,0:T(8,128)(2,1)S(1)} %get-tuple-element.67), channel_id=1, source_target_pairs={{0,6},{2,4},{4,2},{6,0},{8,14},{10,12},{12,10},{14,8},{16,22},{18,... | collective-permute-start | bytes 393224 | tf_op jit(solution)/shard_map/return_grad/ppermute | solution.py:51
  54.8 8.9 %collective-permute-start.14 = (bf16[24,1024]{1,0:T(8,128)(2,1)S(1)}, bf16[24,1024]{1,0:T(8,128)(2,1)S(1)}, u32[]{:S(2)}, u32[]{:S(2)}) collective-permute-start(bf16[24,1024]{1,0:T(8,128)(2,1)S(1)} %get-tuple-element.51), channel_id=1, source_target_pairs={{0,8},{2,10},{4,12},{6,14},{8,0},{10,2},{12,4},{14,6},{16,24},{18,... | collective-permute-start | bytes 147464 | tf_op jit(solution)/shard_map/return_out/ppermute | solution.py:43
  56.0 13.2 %collective-permute-start.15 = (bf16[24,1024]{1,0:T(8,128)(2,1)S(1)}, bf16[24,1024]{1,0:T(8,128)(2,1)S(1)}, u32[]{:S(2)}, u32[]{:S(2)}) collective-permute-start(bf16[24,1024]{1,0:T(8,128)(2,1)S(1)} %get-tuple-element.52), channel_id=1, source_target_pairs={{0,16},{2,18},{4,20},{6,22},{8,24},{10,26},{12,28},{14,30},{16,0},... | collective-permute-start | bytes 147464 | tf_op jit(solution)/shard_map/return_out/ppermute | solution.py:43
  59.0 10.3 %collective-permute-start.16 = (bf16[24,1024]{1,0:T(8,128)(2,1)S(1)}, bf16[24,1024]{1,0:T(8,128)(2,1)S(1)}, u32[]{:S(2)}, u32[]{:S(2)}) collective-permute-start(bf16[24,1024]{1,0:T(8,128)(2,1)S(1)} %get-tuple-element.53), channel_id=1, source_target_pairs={{0,24},{2,26},{4,28},{6,30},{8,16},{10,18},{12,20},{14,22},{16,8},... | collective-permute-start | bytes 147464 | tf_op jit(solution)/shard_map/return_out/ppermute | solution.py:43
  60.6 9.3 %collective-permute-start.31 = (bf16[24,1024]{1,0:T(8,128)(2,1)S(1)}, bf16[24,1024]{1,0:T(8,128)(2,1)S(1)}, u32[]{:S(2)}, u32[]{:S(2)}) collective-permute-start(bf16[24,1024]{1,0:T(8,128)(2,1)S(1)} %get-tuple-element.69), channel_id=1, source_target_pairs={{0,8},{2,10},{4,12},{6,14},{8,0},{10,2},{12,4},{14,6},{16,24},{18,... | collective-permute-start | bytes 147464 | tf_op jit(solution)/shard_map/return_grad/ppermute | solution.py:43
  60.7 9.2 %collective-permute-start.32 = (bf16[24,1024]{1,0:T(8,128)(2,1)S(1)}, bf16[24,1024]{1,0:T(8,128)(2,1)S(1)}, u32[]{:S(2)}, u32[]{:S(2)}) collective-permute-start(bf16[24,1024]{1,0:T(8,128)(2,1)S(1)} %get-tuple-element.70), channel_id=1, source_target_pairs={{0,16},{2,18},{4,20},{6,22},{8,24},{10,26},{12,28},{14,30},{16,0},... | collective-permute-start | bytes 147464 | tf_op jit(solution)/shard_map/return_grad/ppermute | solution.py:43
  63.7 6.2 %collective-permute-start.33 = (bf16[24,1024]{1,0:T(8,128)(2,1)S(1)}, bf16[24,1024]{1,0:T(8,128)(2,1)S(1)}, u32[]{:S(2)}, u32[]{:S(2)}) collective-permute-start(bf16[24,1024]{1,0:T(8,128)(2,1)S(1)} %get-tuple-element.71), channel_id=1, source_target_pairs={{0,24},{2,26},{4,28},{6,30},{8,16},{10,18},{12,20},{14,22},{16,8},... | collective-permute-start | bytes 147464 | tf_op jit(solution)/shard_map/return_grad/ppermute | solution.py:43
  (2 other events, 8.0 us)

commit v2 on v1

v2 whole, which is shorter than its diff:
```python
import functools
import jax
import jax.numpy as jnp
from jax import lax
from jax.experimental import pallas as pl
from jax.experimental.pallas import tpu as pltpu
from jax.sharding import PartitionSpec as P

BF16 = jnp.bfloat16
F32 = jnp.float32
META = 128
VMEM_LIMIT = 20 * 1024 * 1024


def group_sizes(experts):
    inner = 1
    while inner * inner * 4 <= experts and experts % (inner * 2) == 0:
        inner *= 2
    return experts // inner, inner


def partner(index, step, size):
    return index ^ step if size & (size - 1) == 0 else (index + step) % size


def origin(index, step, size):
    return index ^ step if size & (size - 1) == 0 else (index - step) % size


def traced_partner(index, step, size):
    return index ^ step if size & (size - 1) == 0 else lax.rem(index + step, size)


def traced_origin(index, step, size):
    return index ^ step if size & (size - 1) == 0 else lax.rem(index + size - step, size)


def send_outer(x, step, outer, inner, back=False):
    move = origin if back else partner
    pairs = [
        (a * inner + b, move(a, step, outer) * inner + b) for a in range(outer) for b in range(inner)
    ]
    return lax.ppermute(x, "expert", pairs)


def send_inner(x, step, outer, inner, back=False):
    move = origin if back else partner
    pairs = [
        (a * inner + b, a * inner + move(b, step, inner)) for a in range(outer) for b in range(inner)
    ]
    return lax.ppermute(x, "expert", pairs)


def send_core(x, step, cores, back=False):
    move = origin if back else partner
    return lax.ppermute(x, "etp", [(i, move(i, step, cores)) for i in range(cores)])


def send_order(count):
    return range(1, count)


def gather_outer(x, outer, inner):
    sent = {s: send_outer(x, s, outer, inner) for s in send_order(outer)}
    return [x] + [sent[s] for s in range(1, outer)]


def contract(left, right, left_dim, right_dim):
    return lax.dot_general(
        left, right, (((left_dim,), (right_dim,)), ((), ())), preferred_element_type=F32
    )


def whole_specs(count):
    return [pl.BlockSpec(memory_space=pltpu.VMEM)] * count


def any_specs(count):
    return [pl.BlockSpec(memory_space=pl.ANY)] * count


def params():
    return pltpu.CompilerParams(vmem_limit_bytes=VMEM_LIMIT)


def in_hbm(x):
    return pltpu.with_memory_space_constraint(x, pltpu.HBM)


def hbm_specs(count):
    return [pl.BlockSpec(memory_space=pltpu.HBM)] * count


def prepare_kernel(dims, *refs):
    tokens, top, half = dims
    sources, out_ref, held, sems = refs[:4], refs[4], refs[5:9], refs[9]
    copies = [pltpu.make_async_copy(a, b, sems.at[n]) for n, (a, b) in enumerate(zip(sources, held))]
    for copy in copies:
        copy.start()
    for copy in copies:
        copy.wait()
    ids_ref, gates_ref, hidden_ref, grad_ref = held
    gates = gates_ref[...]
    gate_hi = gates.astype(BF16)
    rest = gates - gate_hi.astype(F32)
    gate_mid = rest.astype(BF16)
    gate_lo = (rest - gate_mid.astype(F32)).astype(BF16)
    meta = jnp.zeros((tokens, META), F32)
    entry = lax.broadcasted_iota(jnp.int32, (top, META), 0)
    lane = lax.broadcasted_iota(jnp.int32, (top, META), 1)
    for n, value in enumerate((ids_ref[...].astype(F32).astype(BF16), gate_hi, gate_mid, gate_lo)):
        spread = (lane == entry + n * top).astype(F32).astype(BF16)
        meta = meta + contract(value, spread, 0, 0)
    unit = 2 * tokens
    row = lax.broadcasted_iota(jnp.int32, (unit, tokens), 0)
    token = lax.broadcasted_iota(jnp.int32, (unit, tokens), 1)
    upper = (row == token).astype(F32).astype(BF16)
    lower = (row == token + tokens).astype(F32).astype(BF16)
    for n, source in enumerate((hidden_ref, grad_ref)):
        value = jnp.dot(upper, source[:, :half], preferred_element_type=F32)
        value = value + jnp.dot(lower, source[:, half:], preferred_element_type=F32)
        out_ref[:, n * half : (n + 1) * half] = value.astype(BF16)
    out_ref[:, 2 * half :] = jnp.dot(upper + lower, meta.astype(BF16), preferred_element_type=F32).astype(BF16)


def stacked(refs, columns=None):
    parts = [r[...] if columns is None else r[:, columns] for r in refs]
    if len(parts) == 1:
        return parts[0]
    return jnp.concatenate([p.astype(F32) for p in parts], axis=0).astype(BF16)


def count_above(index, unit, total):
    value = jnp.zeros_like(index)
    for m in range(unit, total, unit):
        value = value + (index >= m).astype(jnp.int32)
    return value


def route_kernel(dims, *refs):
    outer, inner, tokens, top, cap, reach, half = dims
    blocks = refs[:outer]
    sends = refs[outer + 1 : outer + 1 + inner]
    pick_ref, gate_hi_ref, gate_lo_ref = refs[outer + 1 + inner :]
    rows = outer * 2 * tokens
    slots = inner * reach
    me = lax.axis_index("expert")
    my_inner = lax.rem(me, inner)
    my_base = me - my_inner
    meta = jnp.concatenate([r[:, 2 * half :].astype(F32) for r in blocks], axis=0)
    lane = lax.broadcasted_iota(jnp.int32, (rows, slots), 1)
    row = lax.broadcasted_iota(jnp.int32, (rows, slots), 0)
    step = count_above(lane, reach, slots)
    dest = jnp.zeros((rows, slots), F32)
    for q in range(inner):
        expert = (my_base + traced_partner(my_inner, q, inner)).astype(F32)
        dest = jnp.where(step == q, expert, dest)
    slot = lane - step * reach
    named = jnp.zeros((rows, slots), F32)
    gate = jnp.zeros((rows, slots), F32)
    for k in range(top):
        hit = meta[:, k : k + 1] == dest
        value = (
            meta[:, top + k : top + k + 1]
            + meta[:, 2 * top + k : 2 * top + k + 1]
            + meta[:, 3 * top + k : 3 * top + k + 1]
        )
        named = named + hit.astype(F32)
        gate = gate + jnp.where(hit, value, 0.0)
    left = lax.broadcasted_iota(jnp.int32, (rows, rows), 1)
    down = lax.broadcasted_iota(jnp.int32, (rows, rows), 0)
    same = count_above(left, tokens, rows) == count_above(down, tokens, rows)
    before = (same & (left < down)).astype(F32).astype(BF16)
    rank = jnp.dot(before, named.astype(BF16), preferred_element_type=F32)
    position = count_above(row, 2 * tokens, rows) * cap + rank.astype(jnp.int32)
    pick = jnp.where(position == slot, named, 0.0)
    gate = pick * gate
    gate_hi = gate.astype(BF16)
    rest = gate - gate_hi.astype(F32)
    gate_mid = rest.astype(BF16)
    gate_lo = (rest - gate_mid.astype(F32)).astype(BF16)
    part = count_above(row, tokens, rows)
    even = part - 2 * count_above(row, 2 * tokens, rows) == 0
    pick_left = jnp.where(even, pick, 0.0).astype(BF16)
    pick_right = jnp.where(even, 0.0, pick).astype(BF16)
    pick_ref[...] = jnp.concatenate([pick_left, pick_right], axis=1)
    gate_hi_ref[...] = jnp.concatenate(
        [jnp.where(even, gate_hi.astype(F32), 0.0), jnp.where(even, 0.0, gate_hi.astype(F32))], axis=1
    ).astype(BF16)
    gate_lo_ref[...] = jnp.concatenate(
        [jnp.where(even, gate_mid.astype(F32), 0.0), jnp.where(even, 0.0, gate_mid.astype(F32))], axis=1
    ).astype(BF16)
    ones = jnp.ones((rows, META), BF16)
    column = contract(gate_hi, ones, 0, 0) + contract(gate_mid, ones, 0, 0) + contract(gate_lo, ones, 0, 0)
    scale = 0.5 * column[:, :1]
    for array in range(2):
        table = stacked(blocks, pl.ds(array * half, half))
        for side, chosen in enumerate((pick_left, pick_right)):
            out = contract(chosen, table, 0, 0)
            out = (out * scale if array else out).astype(BF16)
            for q in range(inner):
                start = (2 * array + side) * half
                sends[q][:, start : start + half] = out[q * reach : (q + 1) * reach]


def load_kernel(parts, *refs):
    sources, targets, turned, sems = refs[:3], refs[4:7], refs[7:10], refs[11]
    copies = []
    for n in range(3):
        step = sources[n].shape[1] // parts
        for m in range(parts):
            index = (0, pl.ds(m * step, step))
            copy = pltpu.make_async_copy(sources[n].at[index], targets[n].at[index], sems.at[n * parts + m])
            copy.start()
            copies.append(copy)
    for n in range(3):
        step = sources[n].shape[1] // parts
        for m in range(parts):
            copies[n * parts + m].wait()
            turned[n][:, m * step : (m + 1) * step] = targets[n][0, m * step : (m + 1) * step, :].T


def piece_rows(pieces, d, inner, columns):
    return jnp.concatenate([p[:, columns] for p in pieces[d * inner : (d + 1) * inner]], axis=0)


def core_spans(cores, width, move):
    core = lax.axis_index("etp")
    return [pl.ds(pl.multiple_of(move(core, d, cores) * width, width), width) for d in range(cores)]


def forward_kernel(dims, *refs):
    cores, inner, width = dims
    pieces = refs[: cores * inner]
    gate_w, up_w, down_w = refs[cores * inner : cores * inner + 3]
    gate_ref, up_ref, act_ref, *parts = refs[cores * inner + 3 :]
    spans = core_spans(cores, width, traced_origin)
    gate_pre = None
    up_pre = None
    for d in range(cores):
        rows = piece_rows(pieces, d, inner, pl.ds(0, width))
        term = jnp.dot(rows, gate_w[0, spans[d], :], preferred_element_type=F32)
        gate_pre = term if gate_pre is None else gate_pre + term
        term = jnp.dot(rows, up_w[0, spans[d], :], preferred_element_type=F32)
        up_pre = term if up_pre is None else up_pre + term
    act = (gate_pre * jax.nn.sigmoid(gate_pre) * up_pre).astype(BF16)
    gate_ref[...] = gate_pre
    up_ref[...] = up_pre
    act_ref[...] = act
    spans = core_spans(cores, width, traced_partner)
    for d in reversed(range(cores)):
        parts[d][...] = jnp.dot(act, down_w[0, :, spans[d]], preferred_element_type=F32).astype(BF16)


def backward_kernel(dims, *refs):
    cores, inner, width = dims
    pieces = refs[: cores * inner]
    gate_t, up_t, down_t, gate_ref, up_ref = refs[cores * inner : cores * inner + 5]
    parts = refs[-cores:]
    spans = core_spans(cores, width, traced_origin)
    act_grad = None
    for d in range(cores):
        rows = piece_rows(pieces, d, inner, pl.ds(width, width))
        term = jnp.dot(rows, down_t[spans[d], :], preferred_element_type=F32)
        act_grad = term if act_grad is None else act_grad + term
    gate_pre = gate_ref[...]
    sigmoid = jax.nn.sigmoid(gate_pre)
    gate_grad = (act_grad * up_ref[...] * sigmoid * (1.0 + gate_pre * (1.0 - sigmoid))).astype(BF16)
    up_grad = (act_grad * (gate_pre * sigmoid)).astype(BF16)
    spans = core_spans(cores, width, traced_partner)
    for d in reversed(range(cores)):
        part = jnp.dot(gate_grad, gate_t[:, spans[d]], preferred_element_type=F32)
        part = part + jnp.dot(up_grad, up_t[:, spans[d]], preferred_element_type=F32)
        parts[d][...] = part.astype(BF16)


def down_kernel(dims, chunks, *refs):
    cores, inner, width = dims
    pieces = refs[: cores * inner]
    act_ref = refs[cores * inner]
    out_hbm, result, out_sems = refs[-3:]
    core = lax.axis_index("etp")
    act = act_ref[...]
    chunk = width // chunks
    copies = []
    for d in range(cores):
        rows = piece_rows(pieces, d, inner, pl.ds(width, width))
        base = traced_origin(core, d, cores) * width
        for n in range(chunks):
            result[d * chunks + n] = contract(act, rows[:, n * chunk : (n + 1) * chunk], 0, 0).astype(BF16)
            span = pl.ds(pl.multiple_of(base + n * chunk, chunk), chunk)
            copy = pltpu.make_async_copy(
                result.at[d * chunks + n], out_hbm.at[0, :, span], out_sems.at[d * chunks + n]
            )
            copy.start()
            copies.append(copy)
    for copy in copies:
        copy.wait()


def split_kernel(dims, *refs):
    cores, inner, reach = dims
    total = refs[0][...].astype(F32)
    for part in refs[1:cores]:
        total = total + part[...].astype(F32)
    total = total.astype(BF16)
    for q in range(inner):
        refs[q - inner][...] = total[q * reach : (q + 1) * reach]


def combine_kernel(dims, weighted, *refs):
    outer, inner, unit, half = dims
    pieces = refs[:inner]
    tables = refs[inner : inner + weighted]
    outs = refs[-outer:]
    rows = jnp.concatenate([p[...] for p in pieces], axis=0)
    slots = rows.shape[0]
    total = None
    for table in tables:
        term = jnp.dot(table[:, :slots], rows[:, :half], preferred_element_type=F32)
        term = term + jnp.dot(table[:, slots:], rows[:, half:], preferred_element_type=F32)
        total = term if total is None else total + term
    for b in range(outer):
        outs[b][...] = total[b * unit : (b + 1) * unit].astype(BF16)


def final_kernel(dims, *refs):
    outer, tokens, half = dims
    out_ref = refs[-2]
    total = refs[0][...].astype(F32)
    for part in refs[1:outer]:
        total = total + part[...].astype(F32)
    out_ref[:, :half] = total[:tokens].astype(BF16)
    out_ref[:, half:] = total[tokens:].astype(BF16)


def shape(rows, columns, kind=BF16):
    return jax.ShapeDtypeStruct((rows, columns), kind)


def on_device(hidden_in, expert_ids, gate_weights, out_grad, gate_weight, up_weight, down_weight):
    tokens, top = expert_ids.shape
    experts = lax.axis_size("expert")
    cores = lax.axis_size("etp")
    outer, inner = group_sizes(experts)
    cap = min(tokens, tokens * top // experts + 1)
    width = hidden_in.shape[1]
    half = width // 2
    hidden = gate_weight.shape[2]
    reach = -(-(outer * cap) // 16) * 16
    rows = inner * reach
    unit = 2 * tokens

    with jax.named_scope("prepare"):
        packed = pl.pallas_call(
            functools.partial(prepare_kernel, (tokens, top, half)),
            out_shape=shape(unit, 2 * half + META),
            in_specs=hbm_specs(4),
            out_specs=pl.BlockSpec(memory_space=pltpu.VMEM),
            scratch_shapes=[
                pltpu.VMEM((top, tokens), jnp.int32),
                pltpu.VMEM((top, tokens), F32),
                pltpu.VMEM((tokens, width), BF16),
                pltpu.VMEM((tokens, width), BF16),
                pltpu.SemaphoreType.DMA((4,)),
            ],
            compiler_params=params(),
            name="prepare",
        )(in_hbm(expert_ids.T), in_hbm(gate_weights.T), in_hbm(hidden_in), in_hbm(out_grad))

    with jax.named_scope("gather_blocks"):
        blocks = gather_outer(packed, outer, inner)

    table_shape = shape(outer * unit, 2 * rows)
    with jax.named_scope("load_weights"):
        weights = (gate_weight, up_weight, down_weight)
        weight_parts = 4
        held = pl.pallas_call(
            functools.partial(load_kernel, weight_parts),
            out_shape=[pltpu.VMEM(w.shape, BF16) for w in weights]
            + [pltpu.VMEM((w.shape[2], w.shape[1]), BF16) for w in weights]
            + [shape(8, META, F32)],
            in_specs=hbm_specs(3) + whole_specs(1),
            out_specs=whole_specs(7),
            scratch_shapes=[pltpu.SemaphoreType.DMA((3 * weight_parts,))],
            compiler_params=params(),
            cost_estimate=pl.CostEstimate(
                flops=0, bytes_accessed=6 * sum(w.size for w in weights), transcendentals=0
            ),
            name="load_weights",
        )(*[in_hbm(w) for w in weights], packed)
        weights, turned = held[:3], held[3:6]

    with jax.named_scope("route"):
        routed = pl.pallas_call(
            functools.partial(route_kernel, (outer, inner, tokens, top, cap, reach, half)),
            out_shape=[shape(reach, 2 * width)] * inner + [table_shape] * 3,
            in_specs=whole_specs(outer + 1),
            out_specs=whole_specs(inner + 3),
            compiler_params=params(),
            name="route",
        )(*blocks, held[6])
        sends, (pick, gate_hi, gate_lo) = routed[:inner], routed[inner:]

    with jax.named_scope("exchange"):
        pieces = [sends[0]] + [send_inner(sends[q], q, outer, inner) for q in range(1, inner)]
        pieces = pieces + [send_core(piece, d, cores) for d in range(1, cores) for piece in pieces]

    dims = (cores, inner, width)
    with jax.named_scope("forward"):
        gate_pre, up_pre, act, *out_parts = pl.pallas_call(
            functools.partial(forward_kernel, dims),
            out_shape=[shape(rows, hidden, F32)] * 2 + [shape(rows, hidden)] + [shape(rows, width)] * cores,
            in_specs=whole_specs(cores * inner + 3),
            out_specs=whole_specs(3 + cores),
            compiler_params=params(),
            name="forward",
        )(*pieces, *weights)

    def give_back(parts, after=()):
        got = [parts[0]] + [send_core(parts[d], d, cores) for d in range(1, cores)]
        sends = pl.pallas_call(
            functools.partial(split_kernel, (cores, inner, reach)),
            out_shape=[shape(reach, width)] * inner,
            in_specs=whole_specs(cores) + any_specs(len(after)),
            out_specs=whole_specs(inner),
            compiler_params=params(),
            name="split",
        )(*got, *after)
        return [sends[0]] + [send_inner(sends[q], q, outer, inner, back=True) for q in range(1, inner)]

    def combine(pieces, tables):
        blocks = pl.pallas_call(
            functools.partial(combine_kernel, (outer, inner, unit, half), len(tables)),
            out_shape=[shape(unit, half)] * outer,
            in_specs=whole_specs(inner + len(tables)),
            out_specs=whole_specs(outer),
            compiler_params=params(),
            name="combine",
        )(*pieces, *tables)
        return [blocks[0]] + [send_outer(blocks[s], s, outer, inner, back=True) for s in send_order(outer)]

    def finish(blocks, after=()):
        return pl.pallas_call(
            functools.partial(final_kernel, (outer, tokens, half)),
            out_shape=[shape(tokens, width), shape(8, META, F32)],
            in_specs=whole_specs(outer + len(after)),
            out_specs=whole_specs(2),
            compiler_params=params(),
            name="final",
        )(*blocks, *after)

    with jax.named_scope("return_out"):
        out_back = give_back(out_parts)
        out_blocks = combine(out_back, (gate_hi, gate_lo))

    with jax.named_scope("backward"):
        grad_parts = pl.pallas_call(
            functools.partial(backward_kernel, dims),
            out_shape=[shape(rows, width)] * cores,
            in_specs=whole_specs(cores * inner + 5),
            out_specs=whole_specs(cores),
            compiler_params=params(),
            name="backward",
        )(*pieces, *turned, gate_pre, up_pre)

    with jax.named_scope("return_grad"):
        back_blocks = combine(give_back(grad_parts, out_back[:1]), (pick,))

    with jax.named_scope("down_grad"):
        chunks = max(1, width // 512)
        down_grad = pl.pallas_call(
            functools.partial(down_kernel, dims, chunks),
            out_shape=pltpu.HBM(down_weight.shape, BF16),
            in_specs=whole_specs(cores * inner + 1) + any_specs(1),
            out_specs=pl.BlockSpec(memory_space=pltpu.HBM),
            scratch_shapes=[
                pltpu.VMEM((cores * chunks, hidden, width // chunks), BF16),
                pltpu.SemaphoreType.DMA((cores * chunks,)),
            ],
            compiler_params=params(),
            name="down_grad",
        )(*pieces, act, back_blocks[0])

    mixed_out, done = finish(out_blocks)
    input_grad, done = finish(back_blocks, (done,))
    return (mixed_out, input_grad, down_grad)


def solution(mesh):
    return jax.shard_map(
        on_device,
        mesh=mesh,
        in_specs=(
            P("expert", "etp"),
            P("expert", None),
            P("expert", None),
            P("expert", "etp"),
            P("expert", None, "etp"),
            P("expert", None, "etp"),
            P("expert", "etp", None),
        ),
        out_specs=(P("expert", "etp"), P("expert", "etp"), P("expert", "etp", None)),
        check_vma=False,
    )
```

time: 70.9 us -> 62.3 us (0.88)
  starting transfers between devices: 36.5 us -> 26.1 us
  waiting for transfers between devices: 9.56 us -> 19.2 us
  Pallas kernels: 19.7 us -> 16.1 us
  local copies, waits for them, and re-layouts: 2.51 us -> 0 us
  other arithmetic: 1.51 us -> 0 us
    ppermute x12 -> x9, starting transfers between devices: 20.2 us -> 14.7 us  [send_outer(): return lax.ppermute(x, 'expert', pairs)]
    pallas_call x1, Pallas kernels: 6.84 us -> 2.02 us  [on_device(): pl.pallas_call(functools.partial(backward_kernel, dims), out_shape=[shape...]
    ppermute x12 -> x9, waiting for transfers between devices: 9.45 us -> 14.1 us  [send_inner(): return lax.ppermute(x, 'expert', pairs)]
    pallas_call x4 -> x5, Pallas kernels: 5.8 us -> 10.4 us  [the longest x1 5.43 us: on_device(): pl.pallas_call(functools.partial(load_kernel, weight_parts), out_shape=[p...]
    ppermute x12 -> x9, starting transfers between devices: 14.2 us -> 10.2 us  [send_inner(): return lax.ppermute(x, 'expert', pairs)]
    ppermute x12 -> x9, waiting for transfers between devices: 0.08 us -> 3.68 us  [send_outer(): return lax.ppermute(x, 'expert', pairs)]
    pallas_call x1, Pallas kernels: 5.46 us -> 1.94 us  [on_device(): pl.pallas_call(functools.partial(forward_kernel, dims), out_shape=[shape(...]
    slice x2 -> x0, local copies, waits for them, and re-layouts: 1.57 us -> none  [fold(): return jnp.concatenate([x[:, :half], x[:, half:]], axis=0)]
  transfers between devices with their start and end apart: 34 -> 24, of which waited for: 7 -> 9; matrix products, arithmetic and copies ran while one was open for 1% -> 0% of each run, Pallas kernels for 27% -> 18%
where the time goes in v2:
time: 62.3 us; the launch traced here: 62.1 us
  starting transfers between devices  26.1 us (42%)
  waiting for transfers between devices  19.2 us (31%)
  Pallas kernels  16.1 us (26%)
  between operations  0.74 us (1%)
    ppermute x9, starting transfers between devices, send_outer(): return lax.ppermute(x, 'expert', pairs)  14.7 us
    ppermute x9, waiting for transfers between devices, send_inner(): return lax.ppermute(x, 'expert', pairs)  14.1 us
    ppermute x9, starting transfers between devices, send_inner(): return lax.ppermute(x, 'expert', pairs)  10.2 us
    pallas_call x1, Pallas kernels, on_device(): pl.pallas_call(functools.partial(load_kernel, weight_parts), out_shape=[p...  5.43 us
    ppermute x9, waiting for transfers between devices, send_outer(): return lax.ppermute(x, 'expert', pairs)  3.68 us
    pallas_call x1, Pallas kernels, on_device(): pl.pallas_call(functools.partial(down_kernel, dims, chunks), out_shape=pl...  2.39 us
    pallas_call x1, Pallas kernels, on_device(): pl.pallas_call(functools.partial(backward_kernel, dims), out_shape=[shape...  2.02 us
    pallas_call x1, Pallas kernels, on_device(): pl.pallas_call(functools.partial(forward_kernel, dims), out_shape=[shape(...  1.94 us
  transfers between devices with their start and end apart: 24, of which 9 were waited for; matrix products, arithmetic and copies ran while one was open for 0% of the time, Pallas kernels for 18%

profile of v2, /device:TPU:0, one launch (start us, length us, event | category | flops | bytes accessed | tf_op | source)
XLA Modules:
  0.0 62.1 jit_solution(666471139907040730)
XLA Ops:
  0.6 1.3 %prepare.1.refs_3_.refs_0_ = bf16[24,2176]{1,0:T(8,128)(2,1)S(1)} custom-call(s32[8,12]{1,0:T(8,128)} %bitcast.2, f32[8,12]{1,0:T(8,128)} %bitcast.3, bf16[12,2048]{1,0:T(8,128)(2,1)} %refs_2_.2, bf16[12,2048]{1,0:T(8,128)(2,1)} %refs_3_.1), custom_call_target="tpu_custom_call" | custom-call | tf_op jit(solution)/shard_map/prepare/prepare/pallas_call | solution.py:355
  1.9 5.1 %collective-permute-start.2 = (bf16[24,2176]{1,0:T(8,128)(2,1)S(1)}, bf16[24,2176]{1,0:T(8,128)(2,1)S(1)}, u32[]{:S(2)}, u32[]{:S(2)}) collective-permute-start(bf16[24,2176]{1,0:T(8,128)(2,1)S(1)} %prepare.1.refs_3_.refs_0_), channel_id=1, source_target_pairs={{0,24},{2,26},{4,28},{6,30},{8,16},{10,18},{12,20},{14,22},{16,8},... | collective-permute-start | bytes 313352 | tf_op jit(solution)/shard_map/gather_blocks/ppermute | solution.py:43
  7.0 0.6 %collective-permute-start = (bf16[24,2176]{1,0:T(8,128)(2,1)S(1)}, bf16[24,2176]{1,0:T(8,128)(2,1)S(1)}, u32[]{:S(2)}, u32[]{:S(2)}) collective-permute-start(bf16[24,2176]{1,0:T(8,128)(2,1)S(1)} %prepare.1.refs_3_.refs_0_), channel_id=1, source_target_pairs={{0,8},{2,10},{4,12},{6,14},{8,0},{10,2},{12,4},{14,6},{16,24},{18,... | collective-permute-start | bytes 313352 | tf_op jit(solution)/shard_map/gather_blocks/ppermute | solution.py:43
  7.7 5.4 %load_weights.1 = (bf16[1,4096,512]{2,1,0:T(8,128)(2,1)S(1)}, bf16[1,4096,512]{2,1,0:T(8,128)(2,1)S(1)}, bf16[1,512,4096]{2,1,0:T(8,128)(2,1)S(1)}, bf16[512,409...) custom-call(bf16[1,4096,512]{2,1,0:T(8,128)(2,1)} %refs_0_.1, ...), custom_call_target="tpu_custom_call" | custom-call | bytes 37748736 | tf_op jit(solution)/shard_map/load_weights/load_weights/pallas_call | solution.py:378
  13.1 2.7 %collective-permute-done.1.refs_2_ = bf16[24,2176]{1,0:T(8,128)(2,1)S(1)} collective-permute-done((bf16[24,2176]{1,0:T(8,128)(2,1)S(1)}, bf16[24,2176]{1,0:T(8,128)(2,1)S(1)}, u32[]{:S(2)}, u32[]{:S(2)}) %collective-permute-start.1) | collective-permute-done | bytes 104480 | tf_op jit(solution)/shard_map/gather_blocks/ppermute | solution.py:43
  15.8 0.9 %route.1 = (bf16[32,4096]{1,0:T(8,128)(2,1)S(1)}, bf16[32,4096]{1,0:T(8,128)(2,1)S(1)}, bf16[32,4096]{1,0:T(8,128)(2,1)S(1)}, bf16[32,4096]{1,0:T(8,128)(2,1)S(1...) custom-call(bf16[24,2176]{1,0:T(8,128)(2,1)S(1)} %prepare.1.refs_3_.refs_0_, ...), custom_call_target="tpu_custom_call" | custom-call | tf_op jit(solution)/shard_map/route/route/pallas_call | solution.py:395
  16.7 1.6 %collective-permute-start.3 = (bf16[32,4096]{1,0:T(8,128)(2,1)S(1)}, bf16[32,4096]{1,0:T(8,128)(2,1)S(1)}, u32[]{:S(2)}, u32[]{:S(2)}) collective-permute-start(bf16[32,4096]{1,0:T(8,128)(2,1)S(1)} %get-tuple-element.45), channel_id=1, source_target_pairs={{0,2},{2,0},{4,6},{6,4},{8,10},{10,8},{12,14},{14,12},{16,18},{18,... | collective-permute-start | bytes 786440 | tf_op jit(solution)/shard_map/exchange/ppermute | solution.py:51
  18.2 1.5 %collective-permute-start.4 = (bf16[32,4096]{1,0:T(8,128)(2,1)S(1)}, bf16[32,4096]{1,0:T(8,128)(2,1)S(1)}, u32[]{:S(2)}, u32[]{:S(2)}) collective-permute-start(bf16[32,4096]{1,0:T(8,128)(2,1)S(1)} %get-tuple-element.46), channel_id=1, source_target_pairs={{0,4},{2,6},{4,0},{6,2},{8,12},{10,14},{12,8},{14,10},{16,20},{18,... | collective-permute-start | bytes 786440 | tf_op jit(solution)/shard_map/exchange/ppermute | solution.py:51
  19.7 0.5 collective-permute-start.5
  20.2 5.7 %collective-permute-done.3.refs_1_ = bf16[32,4096]{1,0:T(8,128)(2,1)S(1)} collective-permute-done((bf16[32,4096]{1,0:T(8,128)(2,1)S(1)}, bf16[32,4096]{1,0:T(8,128)(2,1)S(1)}, u32[]{:S(2)}, u32[]{:S(2)}) %collective-permute-start.3) | collective-permute-done | bytes 262176 | tf_op jit(solution)/shard_map/exchange/ppermute | solution.py:51
  26.0 4.9 %collective-permute-done.4.refs_2_ = bf16[32,4096]{1,0:T(8,128)(2,1)S(1)} collective-permute-done((bf16[32,4096]{1,0:T(8,128)(2,1)S(1)}, bf16[32,4096]{1,0:T(8,128)(2,1)S(1)}, u32[]{:S(2)}, u32[]{:S(2)}) %collective-permute-start.4) | collective-permute-done | bytes 262176 | tf_op jit(solution)/shard_map/exchange/ppermute | solution.py:51
  30.9 0.5 collective-permute-start.9
  31.4 1.0 %collective-permute-done.8.refs_6_ = bf16[32,4096]{1,0:T(8,128)(2,1)S(1)} collective-permute-done((bf16[32,4096]{1,0:T(8,128)(2,1)S(1)}, bf16[32,4096]{1,0:T(8,128)(2,1)S(1)}, u32[]{:S(2)}, u32[]{:S(2)}) %collective-permute-start.8) | collective-permute-done | bytes 262176 | tf_op jit(solution)/shard_map/exchange/ppermute | solution.py:56
  32.8 1.9 %forward.1 = (f32[128,512]{1,0:T(8,128)S(1)}, f32[128,512]{1,0:T(8,128)S(1)}, bf16[128,512]{1,0:T(8,128)(2,1)S(1)}, bf16[128,2048]{1,0:T(8,128)(2,1)S(1)}, bf16[128,2048]{1,0:T(8,128)(2,1)S(1)}) custom-call(bf16[32,4096]{1,0:T(8,128)(2,1)S(1)} %get-tuple-element.44.refs_0_, bf16[32,4096]{1,0:T(8,128)(2,1)S(1)} %collective-permute-done.3.refs_1_, ...), custom_call_target="tpu_custom_call" | custom-call | tf_op jit(solution)/shard_map/forward/forward/pallas_call | solution.py:411
  35.0 2.0 %backward.1 = (bf16[128,2048]{1,0:T(8,128)(2,1)S(1)}, bf16[128,2048]{1,0:T(8,128)(2,1)S(1)}) custom-call(bf16[32,4096]{1,0:T(8,128)(2,1)S(1)} %get-tuple-element.44.refs_0_, bf16[32,4096]{1,0:T(8,128)(2,1)S(1)} %collective-permute-done.3.refs_1_, bf16[32,4096]{1,0:T(8,128)(2,1)S(1)} %collective-permute-done.4.refs_2_, ...), custom_call_target="tpu_custom_call" | custom-call | tf_op jit(solution)/shard_map/backward/backward/pallas_call | solution.py:458
  37.0 0.4 collective-permute-start.17
  37.6 0.9 %collective-permute-start.11 = (bf16[32,2048]{1,0:T(8,128)(2,1)S(1)}, bf16[32,2048]{1,0:T(8,128)(2,1)S(1)}, u32[]{:S(2)}, u32[]{:S(2)}) collective-permute-start(bf16[32,2048]{1,0:T(8,128)(2,1)S(1)} %get-tuple-element.54), channel_id=1, source_target_pairs={{0,2},{2,0},{4,6},{6,4},{8,10},{10,8},{12,14},{14,12},{16,18},{18,... | collective-permute-start | bytes 393224 | tf_op jit(solution)/shard_map/return_out/ppermute | solution.py:51
  38.5 1.2 %collective-permute-start.12 = (bf16[32,2048]{1,0:T(8,128)(2,1)S(1)}, bf16[32,2048]{1,0:T(8,128)(2,1)S(1)}, u32[]{:S(2)}, u32[]{:S(2)}) collective-permute-start(bf16[32,2048]{1,0:T(8,128)(2,1)S(1)} %get-tuple-element.55), channel_id=1, source_target_pairs={{0,4},{2,6},{4,0},{6,2},{8,12},{10,14},{12,8},{14,10},{16,20},{18,... | collective-permute-start | bytes 393224 | tf_op jit(solution)/shard_map/return_out/ppermute | solution.py:51
  39.7 1.4 %collective-permute-start.13 = (bf16[32,2048]{1,0:T(8,128)(2,1)S(1)}, bf16[32,2048]{1,0:T(8,128)(2,1)S(1)}, u32[]{:S(2)}, u32[]{:S(2)}) collective-permute-start(bf16[32,2048]{1,0:T(8,128)(2,1)S(1)} %get-tuple-element.56), channel_id=1, source_target_pairs={{0,6},{2,4},{4,2},{6,0},{8,14},{10,12},{12,10},{14,8},{16,22},{18,... | collective-permute-start | bytes 393224 | tf_op jit(solution)/shard_map/return_out/ppermute | solution.py:51
  41.3 0.9 %collective-permute-start.18 = (bf16[32,2048]{1,0:T(8,128)(2,1)S(1)}, bf16[32,2048]{1,0:T(8,128)(2,1)S(1)}, u32[]{:S(2)}, u32[]{:S(2)}) collective-permute-start(bf16[32,2048]{1,0:T(8,128)(2,1)S(1)} %get-tuple-element.72), channel_id=1, source_target_pairs={{0,2},{2,0},{4,6},{6,4},{8,10},{10,8},{12,14},{14,12},{16,18},{18,... | collective-permute-start | bytes 393224 | tf_op jit(solution)/shard_map/return_grad/ppermute | solution.py:51
  42.2 1.2 %collective-permute-start.19 = (bf16[32,2048]{1,0:T(8,128)(2,1)S(1)}, bf16[32,2048]{1,0:T(8,128)(2,1)S(1)}, u32[]{:S(2)}, u32[]{:S(2)}) collective-permute-start(bf16[32,2048]{1,0:T(8,128)(2,1)S(1)} %get-tuple-element.73), channel_id=1, source_target_pairs={{0,4},{2,6},{4,0},{6,2},{8,12},{10,14},{12,8},{14,10},{16,20},{18,... | collective-permute-start | bytes 393224 | tf_op jit(solution)/shard_map/return_grad/ppermute | solution.py:51
  43.4 0.6 collective-permute-done.11.refs_1_
  44.0 1.0 %collective-permute-start.20 = (bf16[32,2048]{1,0:T(8,128)(2,1)S(1)}, bf16[32,2048]{1,0:T(8,128)(2,1)S(1)}, u32[]{:S(2)}, u32[]{:S(2)}) collective-permute-start(bf16[32,2048]{1,0:T(8,128)(2,1)S(1)} %get-tuple-element.74), channel_id=1, source_target_pairs={{0,6},{2,4},{4,2},{6,0},{8,14},{10,12},{12,10},{14,8},{16,22},{18,... | collective-permute-start | bytes 393224 | tf_op jit(solution)/shard_map/return_grad/ppermute | solution.py:51
  45.2 2.6 %collective-permute-done.13.refs_3_ = bf16[32,2048]{1,0:T(8,128)(2,1)S(1)} collective-permute-done((bf16[32,2048]{1,0:T(8,128)(2,1)S(1)}, bf16[32,2048]{1,0:T(8,128)(2,1)S(1)}, u32[]{:S(2)}, u32[]{:S(2)}) %collective-permute-start.13) | collective-permute-done | bytes 131104 | tf_op jit(solution)/shard_map/return_out/ppermute | solution.py:51
  48.5 2.3 %collective-permute-start.15 = (bf16[24,1024]{1,0:T(8,128)(2,1)S(1)}, bf16[24,1024]{1,0:T(8,128)(2,1)S(1)}, u32[]{:S(2)}, u32[]{:S(2)}) collective-permute-start(bf16[24,1024]{1,0:T(8,128)(2,1)S(1)} %get-tuple-element.61), channel_id=1, source_target_pairs={{0,16},{2,18},{4,20},{6,22},{8,24},{10,26},{12,28},{14,30},{16,0},... | collective-permute-start | bytes 147464 | tf_op jit(solution)/shard_map/return_out/ppermute | solution.py:43
  50.8 1.8 %collective-permute-start.16 = (bf16[24,1024]{1,0:T(8,128)(2,1)S(1)}, bf16[24,1024]{1,0:T(8,128)(2,1)S(1)}, u32[]{:S(2)}, u32[]{:S(2)}) collective-permute-start(bf16[24,1024]{1,0:T(8,128)(2,1)S(1)} %get-tuple-element.62), channel_id=1, source_target_pairs={{0,24},{2,26},{4,28},{6,30},{8,16},{10,18},{12,20},{14,22},{16,8},... | collective-permute-start | bytes 147464 | tf_op jit(solution)/shard_map/return_out/ppermute | solution.py:43
  53.2 2.3 %collective-permute-start.22 = (bf16[24,1024]{1,0:T(8,128)(2,1)S(1)}, bf16[24,1024]{1,0:T(8,128)(2,1)S(1)}, u32[]{:S(2)}, u32[]{:S(2)}) collective-permute-start(bf16[24,1024]{1,0:T(8,128)(2,1)S(1)} %get-tuple-element.78), channel_id=1, source_target_pairs={{0,16},{2,18},{4,20},{6,22},{8,24},{10,26},{12,28},{14,30},{16,0},... | collective-permute-start | bytes 147464 | tf_op jit(solution)/shard_map/return_grad/ppermute | solution.py:43
  55.5 1.8 %collective-permute-start.23 = (bf16[24,1024]{1,0:T(8,128)(2,1)S(1)}, bf16[24,1024]{1,0:T(8,128)(2,1)S(1)}, u32[]{:S(2)}, u32[]{:S(2)}) collective-permute-start(bf16[24,1024]{1,0:T(8,128)(2,1)S(1)} %get-tuple-element.79), channel_id=1, source_target_pairs={{0,24},{2,26},{4,28},{6,30},{8,16},{10,18},{12,20},{14,22},{16,8},... | collective-permute-start | bytes 147464 | tf_op jit(solution)/shard_map/return_grad/ppermute | solution.py:43
  57.4 2.4 %down_grad.1 = bf16[1,512,4096]{2,1,0:T(8,128)(2,1)} custom-call(bf16[32,4096]{1,0:T(8,128)(2,1)S(1)} %get-tuple-element.44.refs_0_, bf16[32,4096]{1,0:T(8,128)(2,1)S(1)} %collective-permute-done.3.refs_1_, bf16[32,4096]{1,0:T(8,128)(2,1)S(1)} %collective-permute-done.4.refs_2_, bf16[32,4096]{1,0:T(8,128)(2,1)S(1)} %collective-permute-done.5.refs_3_, ...), custom_call_target="tpu_custom_call" | custom-call | tf_op jit(solution)/shard_map/down_grad/down_grad/pallas_call | solution.py:472
  59.8 0.7 %final.2 = (bf16[12,2048]{1,0:T(8,128)(2,1)}, f32[8,128]{1,0:T(8,128)S(1)}) custom-call(bf16[24,1024]{1,0:T(8,128)(2,1)S(1)} %get-tuple-element.59.refs_0_, bf16[24,1024]{1,0:T(8,128)(2,1)S(1)} %collective-permute-done.14.refs_1_, bf16[24,1024]{1,0:T(8,128)(2,1)S(1)} %collective-permute-done.15.refs_2_, bf16[24,1024]{1,0:T(8,128)(2,1)S(1)} %collective-permute-done.16.refs_3_), custom_call_target="tpu_custom_call" | custom-call | tf_op jit(solution)/shard_map/final/pallas_call | solution.py:444
  60.5 1.0 %collective-permute-done.23.refs_3_ = bf16[24,1024]{1,0:T(8,128)(2,1)S(1)} collective-permute-done((bf16[24,1024]{1,0:T(8,128)(2,1)S(1)}, bf16[24,1024]{1,0:T(8,128)(2,1)S(1)}, u32[]{:S(2)}, u32[]{:S(2)}) %collective-permute-start.23) | collective-permute-done | bytes 49184 | tf_op jit(solution)/shard_map/return_grad/ppermute | solution.py:43
  61.4 0.7 %final.3 = (bf16[12,2048]{1,0:T(8,128)(2,1)}, f32[8,128]{1,0:T(8,128)}) custom-call(bf16[24,1024]{1,0:T(8,128)(2,1)S(1)} %get-tuple-element.76.refs_0_.refs_9_, bf16[24,1024]{1,0:T(8,128)(2,1)S(1)} %collective-permute-done.21.refs_1_, bf16[24,1024]{1,0:T(8,128)(2,1)S(1)} %collective-permute-done.22.refs_2_, ...), custom_call_target="tpu_custom_call" | custom-call | tf_op jit(solution)/shard_map/final/pallas_call | solution.py:444
  (28 shorter events, 2.3 us)
Async XLA Ops:
  1.9 11.2 %collective-permute-start.2 = (bf16[24,2176]{1,0:T(8,128)(2,1)S(1)}, bf16[24,2176]{1,0:T(8,128)(2,1)S(1)}, u32[]{:S(2)}, u32[]{:S(2)}) collective-permute-start(bf16[24,2176]{1,0:T(8,128)(2,1)S(1)} %prepare.1.refs_3_.refs_0_), channel_id=1, source_target_pairs={{0,24},{2,26},{4,28},{6,30},{8,16},{10,18},{12,20},{14,22},{16,8},... | collective-permute-start | bytes 313352 | tf_op jit(solution)/shard_map/gather_blocks/ppermute | solution.py:43
  7.0 8.8 %collective-permute-start.1 = (bf16[24,2176]{1,0:T(8,128)(2,1)S(1)}, bf16[24,2176]{1,0:T(8,128)(2,1)S(1)}, u32[]{:S(2)}, u32[]{:S(2)}) collective-permute-start(bf16[24,2176]{1,0:T(8,128)(2,1)S(1)} %prepare.1.refs_3_.refs_0_), channel_id=1, source_target_pairs={{0,16},{2,18},{4,20},{6,22},{8,24},{10,26},{12,28},{14,30},{16,0},... | collective-permute-start | bytes 313352 | tf_op jit(solution)/shard_map/gather_blocks/ppermute | solution.py:43
  7.0 8.8 %collective-permute-start = (bf16[24,2176]{1,0:T(8,128)(2,1)S(1)}, bf16[24,2176]{1,0:T(8,128)(2,1)S(1)}, u32[]{:S(2)}, u32[]{:S(2)}) collective-permute-start(bf16[24,2176]{1,0:T(8,128)(2,1)S(1)} %prepare.1.refs_3_.refs_0_), channel_id=1, source_target_pairs={{0,8},{2,10},{4,12},{6,14},{8,0},{10,2},{12,4},{14,6},{16,24},{18,... | collective-permute-start | bytes 313352 | tf_op jit(solution)/shard_map/gather_blocks/ppermute | solution.py:43
  16.7 9.3 %collective-permute-start.3 = (bf16[32,4096]{1,0:T(8,128)(2,1)S(1)}, bf16[32,4096]{1,0:T(8,128)(2,1)S(1)}, u32[]{:S(2)}, u32[]{:S(2)}) collective-permute-start(bf16[32,4096]{1,0:T(8,128)(2,1)S(1)} %get-tuple-element.45), channel_id=1, source_target_pairs={{0,2},{2,0},{4,6},{6,4},{8,10},{10,8},{12,14},{14,12},{16,18},{18,... | collective-permute-start | bytes 786440 | tf_op jit(solution)/shard_map/exchange/ppermute | solution.py:51
  18.2 12.7 %collective-permute-start.4 = (bf16[32,4096]{1,0:T(8,128)(2,1)S(1)}, bf16[32,4096]{1,0:T(8,128)(2,1)S(1)}, u32[]{:S(2)}, u32[]{:S(2)}) collective-permute-start(bf16[32,4096]{1,0:T(8,128)(2,1)S(1)} %get-tuple-element.46), channel_id=1, source_target_pairs={{0,4},{2,6},{4,0},{6,2},{8,12},{10,14},{12,8},{14,10},{16,20},{18,... | collective-permute-start | bytes 786440 | tf_op jit(solution)/shard_map/exchange/ppermute | solution.py:51
  19.7 11.2 %collective-permute-start.5 = (bf16[32,4096]{1,0:T(8,128)(2,1)S(1)}, bf16[32,4096]{1,0:T(8,128)(2,1)S(1)}, u32[]{:S(2)}, u32[]{:S(2)}) collective-permute-start(bf16[32,4096]{1,0:T(8,128)(2,1)S(1)} %get-tuple-element.47), channel_id=1, source_target_pairs={{0,6},{2,4},{4,2},{6,0},{8,14},{10,12},{12,10},{14,8},{16,22},{18,... | collective-permute-start | bytes 786440 | tf_op jit(solution)/shard_map/exchange/ppermute | solution.py:51
  20.2 11.2 %collective-permute-start.6 = (bf16[32,4096]{1,0:T(8,128)(2,1)S(1)}, bf16[32,4096]{1,0:T(8,128)(2,1)S(1)}, u32[]{:S(2)}, u32[]{:S(2)}) collective-permute-start(bf16[32,4096]{1,0:T(8,128)(2,1)S(1)} %get-tuple-element.44.refs_0_), channel_id=1, source_target_pairs={{0,1},{1,0},{2,3},{3,2},{4,5},{5,4},{6,7},{7,6},{8,9},{9,8},{10,11... | collective-permute-start | bytes 786440 | tf_op jit(solution)/shard_map/exchange/ppermute | solution.py:56
  26.0 5.5 %collective-permute-start.7 = (bf16[32,4096]{1,0:T(8,128)(2,1)S(1)}, bf16[32,4096]{1,0:T(8,128)(2,1)S(1)}, u32[]{:S(2)}, u32[]{:S(2)}) collective-permute-start(bf16[32,4096]{1,0:T(8,128)(2,1)S(1)} %collective-permute-done.3.refs_1_), channel_id=1, source_target_pairs={{0,1},{1,0},{2,3},{3,2},{4,5},{5,4},{6,7},{7,6},{8,9},{9,8},{10,11... | collective-permute-start | bytes 786440 | tf_op jit(solution)/shard_map/exchange/ppermute | solution.py:56
  30.9 1.5 %collective-permute-start.8 = (bf16[32,4096]{1,0:T(8,128)(2,1)S(1)}, bf16[32,4096]{1,0:T(8,128)(2,1)S(1)}, u32[]{:S(2)}, u32[]{:S(2)}) collective-permute-start(bf16[32,4096]{1,0:T(8,128)(2,1)S(1)} %collective-permute-done.4.refs_2_), channel_id=1, source_target_pairs={{0,1},{1,0},{2,3},{3,2},{4,5},{5,4},{6,7},{7,6},{8,9},{9,8},{10,11... | collective-permute-start | bytes 786440 | tf_op jit(solution)/shard_map/exchange/ppermute | solution.py:56
  30.9 1.9 %collective-permute-start.9 = (bf16[32,4096]{1,0:T(8,128)(2,1)S(1)}, bf16[32,4096]{1,0:T(8,128)(2,1)S(1)}, u32[]{:S(2)}, u32[]{:S(2)}) collective-permute-start(bf16[32,4096]{1,0:T(8,128)(2,1)S(1)} %collective-permute-done.5.refs_3_), channel_id=1, source_target_pairs={{0,1},{1,0},{2,3},{3,2},{4,5},{5,4},{6,7},{7,6},{8,9},{9,8},{10,11... | collective-permute-start | bytes 786440 | tf_op jit(solution)/shard_map/exchange/ppermute | solution.py:56
  34.8 2.7 %collective-permute-start.10 = (bf16[128,2048]{1,0:T(8,128)(2,1)S(1)}, bf16[128,2048]{1,0:T(8,128)(2,1)S(1)}, u32[]{:S(2)}, u32[]{:S(2)}) collective-permute-start(bf16[128,2048]{1,0:T(8,128)(2,1)S(1)} %get-tuple-element.52), channel_id=1, source_target_pairs={{0,1},{1,0},{2,3},{3,2},{4,5},{5,4},{6,7},{7,6},{8,9},{9,8},{10,11... | collective-permute-start | bytes 1572872 | tf_op jit(solution)/shard_map/return_out/ppermute | solution.py:56
  37.0 4.1 %collective-permute-start.17 = (bf16[128,2048]{1,0:T(8,128)(2,1)S(1)}, bf16[128,2048]{1,0:T(8,128)(2,1)S(1)}, u32[]{:S(2)}, u32[]{:S(2)}) collective-permute-start(bf16[128,2048]{1,0:T(8,128)(2,1)S(1)} %get-tuple-element.70), channel_id=1, source_target_pairs={{0,1},{1,0},{2,3},{3,2},{4,5},{5,4},{6,7},{7,6},{8,9},{9,8},{10,11... | collective-permute-start | bytes 1572872 | tf_op jit(solution)/shard_map/return_grad/ppermute | solution.py:56
  37.6 6.4 %collective-permute-start.11 = (bf16[32,2048]{1,0:T(8,128)(2,1)S(1)}, bf16[32,2048]{1,0:T(8,128)(2,1)S(1)}, u32[]{:S(2)}, u32[]{:S(2)}) collective-permute-start(bf16[32,2048]{1,0:T(8,128)(2,1)S(1)} %get-tuple-element.54), channel_id=1, source_target_pairs={{0,2},{2,0},{4,6},{6,4},{8,10},{10,8},{12,14},{14,12},{16,18},{18,... | collective-permute-start | bytes 393224 | tf_op jit(solution)/shard_map/return_out/ppermute | solution.py:51
  38.5 6.7 %collective-permute-start.12 = (bf16[32,2048]{1,0:T(8,128)(2,1)S(1)}, bf16[32,2048]{1,0:T(8,128)(2,1)S(1)}, u32[]{:S(2)}, u32[]{:S(2)}) collective-permute-start(bf16[32,2048]{1,0:T(8,128)(2,1)S(1)} %get-tuple-element.55), channel_id=1, source_target_pairs={{0,4},{2,6},{4,0},{6,2},{8,12},{10,14},{12,8},{14,10},{16,20},{18,... | collective-permute-start | bytes 393224 | tf_op jit(solution)/shard_map/return_out/ppermute | solution.py:51
  39.7 8.1 %collective-permute-start.13 = (bf16[32,2048]{1,0:T(8,128)(2,1)S(1)}, bf16[32,2048]{1,0:T(8,128)(2,1)S(1)}, u32[]{:S(2)}, u32[]{:S(2)}) collective-permute-start(bf16[32,2048]{1,0:T(8,128)(2,1)S(1)} %get-tuple-element.56), channel_id=1, source_target_pairs={{0,6},{2,4},{4,2},{6,0},{8,14},{10,12},{12,10},{14,8},{16,22},{18,... | collective-permute-start | bytes 393224 | tf_op jit(solution)/shard_map/return_out/ppermute | solution.py:51
  41.3 9.5 %collective-permute-start.18 = (bf16[32,2048]{1,0:T(8,128)(2,1)S(1)}, bf16[32,2048]{1,0:T(8,128)(2,1)S(1)}, u32[]{:S(2)}, u32[]{:S(2)}) collective-permute-start(bf16[32,2048]{1,0:T(8,128)(2,1)S(1)} %get-tuple-element.72), channel_id=1, source_target_pairs={{0,2},{2,0},{4,6},{6,4},{8,10},{10,8},{12,14},{14,12},{16,18},{18,... | collective-permute-start | bytes 393224 | tf_op jit(solution)/shard_map/return_grad/ppermute | solution.py:51
  42.2 10.4 %collective-permute-start.19 = (bf16[32,2048]{1,0:T(8,128)(2,1)S(1)}, bf16[32,2048]{1,0:T(8,128)(2,1)S(1)}, u32[]{:S(2)}, u32[]{:S(2)}) collective-permute-start(bf16[32,2048]{1,0:T(8,128)(2,1)S(1)} %get-tuple-element.73), channel_id=1, source_target_pairs={{0,4},{2,6},{4,0},{6,2},{8,12},{10,14},{12,8},{14,10},{16,20},{18,... | collective-permute-start | bytes 393224 | tf_op jit(solution)/shard_map/return_grad/ppermute | solution.py:51
  44.0 8.6 %collective-permute-start.20 = (bf16[32,2048]{1,0:T(8,128)(2,1)S(1)}, bf16[32,2048]{1,0:T(8,128)(2,1)S(1)}, u32[]{:S(2)}, u32[]{:S(2)}) collective-permute-start(bf16[32,2048]{1,0:T(8,128)(2,1)S(1)} %get-tuple-element.74), channel_id=1, source_target_pairs={{0,6},{2,4},{4,2},{6,0},{8,14},{10,12},{12,10},{14,8},{16,22},{18,... | collective-permute-start | bytes 393224 | tf_op jit(solution)/shard_map/return_grad/ppermute | solution.py:51
  48.2 7.3 %collective-permute-start.14 = (bf16[24,1024]{1,0:T(8,128)(2,1)S(1)}, bf16[24,1024]{1,0:T(8,128)(2,1)S(1)}, u32[]{:S(2)}, u32[]{:S(2)}) collective-permute-start(bf16[24,1024]{1,0:T(8,128)(2,1)S(1)} %get-tuple-element.60), channel_id=1, source_target_pairs={{0,8},{2,10},{4,12},{6,14},{8,0},{10,2},{12,4},{14,6},{16,24},{18,... | collective-permute-start | bytes 147464 | tf_op jit(solution)/shard_map/return_out/ppermute | solution.py:43
  48.5 11.3 %collective-permute-start.15 = (bf16[24,1024]{1,0:T(8,128)(2,1)S(1)}, bf16[24,1024]{1,0:T(8,128)(2,1)S(1)}, u32[]{:S(2)}, u32[]{:S(2)}) collective-permute-start(bf16[24,1024]{1,0:T(8,128)(2,1)S(1)} %get-tuple-element.61), channel_id=1, source_target_pairs={{0,16},{2,18},{4,20},{6,22},{8,24},{10,26},{12,28},{14,30},{16,0},... | collective-permute-start | bytes 147464 | tf_op jit(solution)/shard_map/return_out/ppermute | solution.py:43
  50.8 9.0 %collective-permute-start.16 = (bf16[24,1024]{1,0:T(8,128)(2,1)S(1)}, bf16[24,1024]{1,0:T(8,128)(2,1)S(1)}, u32[]{:S(2)}, u32[]{:S(2)}) collective-permute-start(bf16[24,1024]{1,0:T(8,128)(2,1)S(1)} %get-tuple-element.62), channel_id=1, source_target_pairs={{0,24},{2,26},{4,28},{6,30},{8,16},{10,18},{12,20},{14,22},{16,8},... | collective-permute-start | bytes 147464 | tf_op jit(solution)/shard_map/return_out/ppermute | solution.py:43
  52.9 7.5 %collective-permute-start.21 = (bf16[24,1024]{1,0:T(8,128)(2,1)S(1)}, bf16[24,1024]{1,0:T(8,128)(2,1)S(1)}, u32[]{:S(2)}, u32[]{:S(2)}) collective-permute-start(bf16[24,1024]{1,0:T(8,128)(2,1)S(1)} %get-tuple-element.77), channel_id=1, source_target_pairs={{0,8},{2,10},{4,12},{6,14},{8,0},{10,2},{12,4},{14,6},{16,24},{18,... | collective-permute-start | bytes 147464 | tf_op jit(solution)/shard_map/return_grad/ppermute | solution.py:43
  53.2 7.2 %collective-permute-start.22 = (bf16[24,1024]{1,0:T(8,128)(2,1)S(1)}, bf16[24,1024]{1,0:T(8,128)(2,1)S(1)}, u32[]{:S(2)}, u32[]{:S(2)}) collective-permute-start(bf16[24,1024]{1,0:T(8,128)(2,1)S(1)} %get-tuple-element.78), channel_id=1, source_target_pairs={{0,16},{2,18},{4,20},{6,22},{8,24},{10,26},{12,28},{14,30},{16,0},... | collective-permute-start | bytes 147464 | tf_op jit(solution)/shard_map/return_grad/ppermute | solution.py:43
  55.5 5.9 %collective-permute-start.23 = (bf16[24,1024]{1,0:T(8,128)(2,1)S(1)}, bf16[24,1024]{1,0:T(8,128)(2,1)S(1)}, u32[]{:S(2)}, u32[]{:S(2)}) collective-permute-start(bf16[24,1024]{1,0:T(8,128)(2,1)S(1)} %get-tuple-element.79), channel_id=1, source_target_pairs={{0,24},{2,26},{4,28},{6,30},{8,16},{10,18},{12,20},{14,22},{16,8},... | collective-permute-start | bytes 147464 | tf_op jit(solution)/shard_map/return_grad/ppermute | solution.py:43

commit v3 on v2

--- a/solution.py
+++ b/solution.py
@@ -141,7 +141,7 @@
     outer, inner, tokens, top, cap, reach, half = dims
     blocks = refs[:outer]
     sends = refs[outer + 1 : outer + 1 + inner]
-    pick_ref, gate_hi_ref, gate_lo_ref = refs[outer + 1 + inner :]
+    pick_ref, gate_hi_ref, gate_lo_ref, gate_col_ref = refs[outer + 1 + inner :]
     rows = outer * 2 * tokens
     slots = inner * reach
     me = lax.axis_index("expert")
@@ -192,15 +192,32 @@
     ).astype(BF16)
     ones = jnp.ones((rows, META), BF16)
     column = contract(gate_hi, ones, 0, 0) + contract(gate_mid, ones, 0, 0) + contract(gate_lo, ones, 0, 0)
-    scale = 0.5 * column[:, :1]
-    for array in range(2):
-        table = stacked(blocks, pl.ds(array * half, half))
-        for side, chosen in enumerate((pick_left, pick_right)):
-            out = contract(chosen, table, 0, 0)
-            out = (out * scale if array else out).astype(BF16)
-            for q in range(inner):
-                start = (2 * array + side) * half
-                sends[q][:, start : start + half] = out[q * reach : (q + 1) * reach]
+    gate_col_ref[...] = 0.5 * column
+    select_rows(blocks, 0, pick_ref, None, sends)
+
+
+def select_rows(blocks, array, pick_ref, scale, sends):
+    inner = len(sends)
+    reach, width = sends[0].shape
+    half = width // 2
+    slots = inner * reach
+    table = stacked(blocks, pl.ds(array * half, half))
+    for side in range(2):
+        out = contract(pick_ref[:, side * slots : (side + 1) * slots], table, 0, 0)
+        out = (out if scale is None else out * scale).astype(BF16)
+        for q in range(inner):
+            sends[q][:, side * half : (side + 1) * half] = out[q * reach : (q + 1) * reach]
+
+
+def scale_kernel(outer, inner, *refs):
+    pick_ref, gate_col_ref = refs[outer : outer + 2]
+    select_rows(refs[:outer], 1, pick_ref, gate_col_ref[:, :1], refs[-inner:])
+
+
+def stack_kernel(inner, *refs):
+    reach = refs[0].shape[0]
+    for q in range(inner):
+        refs[-1][q * reach : (q + 1) * reach, :] = refs[q][...]
 
 
 def load_kernel(parts, *refs):
@@ -220,25 +237,21 @@
             turned[n][:, m * step : (m + 1) * step] = targets[n][0, m * step : (m + 1) * step, :].T
 
 
-def piece_rows(pieces, d, inner, columns):
-    return jnp.concatenate([p[:, columns] for p in pieces[d * inner : (d + 1) * inner]], axis=0)
-
-
 def core_spans(cores, width, move):
     core = lax.axis_index("etp")
     return [pl.ds(pl.multiple_of(move(core, d, cores) * width, width), width) for d in range(cores)]
 
 
 def forward_kernel(dims, *refs):
-    cores, inner, width = dims
-    pieces = refs[: cores * inner]
-    gate_w, up_w, down_w = refs[cores * inner : cores * inner + 3]
-    gate_ref, up_ref, act_ref, *parts = refs[cores * inner + 3 :]
+    cores, width = dims
+    pieces = refs[:cores]
+    gate_w, up_w, down_w = refs[cores : cores + 3]
+    gate_ref, up_ref, act_ref, *parts = refs[-(3 + cores) :]
     spans = core_spans(cores, width, traced_origin)
     gate_pre = None
     up_pre = None
     for d in range(cores):
-        rows = piece_rows(pieces, d, inner, pl.ds(0, width))
+        rows = pieces[d][...]
         term = jnp.dot(rows, gate_w[0, spans[d], :], preferred_element_type=F32)
         gate_pre = term if gate_pre is None else gate_pre + term
         term = jnp.dot(rows, up_w[0, spans[d], :], preferred_element_type=F32)
@@ -253,14 +266,14 @@
 
 
 def backward_kernel(dims, *refs):
-    cores, inner, width = dims
-    pieces = refs[: cores * inner]
-    gate_t, up_t, down_t, gate_ref, up_ref = refs[cores * inner : cores * inner + 5]
+    cores, width = dims
+    pieces = refs[:cores]
+    gate_t, up_t, down_t, gate_ref, up_ref = refs[cores : cores + 5]
     parts = refs[-cores:]
     spans = core_spans(cores, width, traced_origin)
     act_grad = None
     for d in range(cores):
-        rows = piece_rows(pieces, d, inner, pl.ds(width, width))
+        rows = pieces[d][...]
         term = jnp.dot(rows, down_t[spans[d], :], preferred_element_type=F32)
         act_grad = term if act_grad is None else act_grad + term
     gate_pre = gate_ref[...]
@@ -275,16 +288,16 @@
 
 
 def down_kernel(dims, chunks, *refs):
-    cores, inner, width = dims
-    pieces = refs[: cores * inner]
-    act_ref = refs[cores * inner]
+    cores, width = dims
+    pieces = refs[:cores]
+    act_ref = refs[cores]
     out_hbm, result, out_sems = refs[-3:]
     core = lax.axis_index("etp")
     act = act_ref[...]
     chunk = width // chunks
     copies = []
     for d in range(cores):
-        rows = piece_rows(pieces, d, inner, pl.ds(width, width))
+        rows = pieces[d][...]
         base = traced_origin(core, d, cores) * width
         for n in range(chunks):
             result[d * chunks + n] = contract(act, rows[:, n * chunk : (n + 1) * chunk], 0, 0).astype(BF16)
@@ -365,6 +378,7 @@
                 pltpu.SemaphoreType.DMA((4,)),
             ],
             compiler_params=params(),
+            cost_estimate=pl.CostEstimate(flops=1, bytes_accessed=1, transcendentals=0),
             name="prepare",
         )(in_hbm(expert_ids.T), in_hbm(gate_weights.T), in_hbm(hidden_in), in_hbm(out_grad))
 
@@ -384,9 +398,7 @@
             out_specs=whole_specs(7),
             scratch_shapes=[pltpu.SemaphoreType.DMA((3 * weight_parts,))],
             compiler_params=params(),
-            cost_estimate=pl.CostEstimate(
-                flops=0, bytes_accessed=6 * sum(w.size for w in weights), transcendentals=0
-            ),
+            cost_estimate=pl.CostEstimate(flops=1, bytes_accessed=1, transcendentals=0),
             name="load_weights",
         )(*[in_hbm(w) for w in weights], packed)
         weights, turned = held[:3], held[3:6]
@@ -394,28 +406,59 @@
     with jax.named_scope("route"):
         routed = pl.pallas_call(
             functools.partial(route_kernel, (outer, inner, tokens, top, cap, reach, half)),
-            out_shape=[shape(reach, 2 * width)] * inner + [table_shape] * 3,
+            out_shape=[shape(reach, width)] * inner + [table_shape] * 3 + [shape(rows, META, F32)],
             in_specs=whole_specs(outer + 1),
-            out_specs=whole_specs(inner + 3),
-            compiler_params=params(),
+            out_specs=whole_specs(inner + 4),
+            compiler_params=params(),
+            cost_estimate=pl.CostEstimate(flops=1, bytes_accessed=1, transcendentals=0),
             name="route",
         )(*blocks, held[6])
-        sends, (pick, gate_hi, gate_lo) = routed[:inner], routed[inner:]
-
-    with jax.named_scope("exchange"):
-        pieces = [sends[0]] + [send_inner(sends[q], q, outer, inner) for q in range(1, inner)]
-        pieces = pieces + [send_core(piece, d, cores) for d in range(1, cores) for piece in pieces]
-
-    dims = (cores, inner, width)
+        in_sends, (pick, gate_hi, gate_lo, gate_col) = routed[:inner], routed[inner:]
+
+    def spread(sends):
+        return [sends[0]] + [send_inner(sends[q], q, outer, inner) for q in range(1, inner)]
+
+    def gather_cores(pieces, after=()):
+        stack = pl.pallas_call(
+            functools.partial(stack_kernel, inner),
+            out_shape=shape(rows, width),
+            in_specs=whole_specs(inner) + any_specs(len(after)),
+            out_specs=pl.BlockSpec(memory_space=pltpu.VMEM),
+            compiler_params=params(),
+            cost_estimate=pl.CostEstimate(flops=1, bytes_accessed=1, transcendentals=0),
+            name="stack",
+        )(*pieces, *after)
+        return [stack] + [send_core(stack, d, cores) for d in range(1, cores)]
+
+    with jax.named_scope("exchange_in"):
+        in_pieces = spread(in_sends)
+    with jax.named_scope("scale"):
+        grad_sends = pl.pallas_call(
+            functools.partial(scale_kernel, outer, inner),
+            out_shape=[shape(reach, width)] * inner,
+            in_specs=whole_specs(outer + 2),
+            out_specs=whole_specs(inner),
+            compiler_params=params(),
+            cost_estimate=pl.CostEstimate(flops=1, bytes_accessed=1, transcendentals=0),
+            name="scale",
+        )(*blocks, pick, gate_col)
+    with jax.named_scope("exchange_grad"):
+        grad_pieces = spread(grad_sends)
+    with jax.named_scope("gather_in"):
+        in_rows = gather_cores(in_pieces)
+        grad_rows = gather_cores(grad_pieces)
+
+    dims = (cores, width)
     with jax.named_scope("forward"):
         gate_pre, up_pre, act, *out_parts = pl.pallas_call(
             functools.partial(forward_kernel, dims),
             out_shape=[shape(rows, hidden, F32)] * 2 + [shape(rows, hidden)] + [shape(rows, width)] * cores,
-            in_specs=whole_specs(cores * inner + 3),
+            in_specs=whole_specs(cores + 3) + any_specs(1),
             out_specs=whole_specs(3 + cores),
             compiler_params=params(),
+            cost_estimate=pl.CostEstimate(flops=1, bytes_accessed=1, transcendentals=0),
             name="forward",
-        )(*pieces, *weights)
+        )(*in_rows, *weights, grad_rows[0])
 
     def give_back(parts, after=()):
         got = [parts[0]] + [send_core(parts[d], d, cores) for d in range(1, cores)]
@@ -425,6 +468,7 @@
             in_specs=whole_specs(cores) + any_specs(len(after)),
             out_specs=whole_specs(inner),
             compiler_params=params(),
+            cost_estimate=pl.CostEstimate(flops=1, bytes_accessed=1, transcendentals=0),
             name="split",
         )(*got, *after)
         return [sends[0]] + [send_inner(sends[q], q, outer, inner, back=True) for q in range(1, inner)]
@@ -436,6 +480,7 @@
             in_specs=whole_specs(inner + len(tables)),
             out_specs=whole_specs(outer),
             compiler_params=params(),
+            cost_estimate=pl.CostEstimate(flops=1, bytes_accessed=1, transcendentals=0),
             name="combine",
         )(*pieces, *tables)
         return [blocks[0]] + [send_outer(blocks[s], s, outer, inner, back=True) for s in send_order(outer)]
@@ -447,6 +492,7 @@
             in_specs=whole_specs(outer + len(after)),
             out_specs=whole_specs(2),
             compiler_params=params(),
+            cost_estimate=pl.CostEstimate(flops=1, bytes_accessed=1, transcendentals=0),
             name="final",
         )(*blocks, *after)
 
@@ -458,11 +504,12 @@
         grad_parts = pl.pallas_call(
             functools.partial(backward_kernel, dims),
             out_shape=[shape(rows, width)] * cores,
-            in_specs=whole_specs(cores * inner + 5),
+            in_specs=whole_specs(cores + 5),
             out_specs=whole_specs(cores),
             compiler_params=params(),
+            cost_estimate=pl.CostEstimate(flops=1, bytes_accessed=1, transcendentals=0),
             name="backward",
-        )(*pieces, *turned, gate_pre, up_pre)
+        )(*grad_rows, *turned, gate_pre, up_pre)
 
     with jax.named_scope("return_grad"):
         back_blocks = combine(give_back(grad_parts, out_back[:1]), (pick,))
@@ -472,15 +519,16 @@
         down_grad = pl.pallas_call(
             functools.partial(down_kernel, dims, chunks),
             out_shape=pltpu.HBM(down_weight.shape, BF16),
-            in_specs=whole_specs(cores * inner + 1) + any_specs(1),
+            in_specs=whole_specs(cores + 1) + any_specs(1),
             out_specs=pl.BlockSpec(memory_space=pltpu.HBM),
             scratch_shapes=[
                 pltpu.VMEM((cores * chunks, hidden, width // chunks), BF16),
                 pltpu.SemaphoreType.DMA((cores * chunks,)),
             ],
             compiler_params=params(),
+            cost_estimate=pl.CostEstimate(flops=1, bytes_accessed=1, transcendentals=0),
             name="down_grad",
-        )(*pieces, act, back_blocks[0])
+        )(*grad_rows, act, back_blocks[0])
 
     mixed_out, done = finish(out_blocks)
     input_grad, done = finish(back_blocks, (done,))

time: 62.3 us -> 61.1 us (0.981)
  waiting for transfers between devices: 19.2 us -> 14 us
  starting transfers between devices: 26.1 us -> 29.8 us
    ppermute x9 -> x12, starting transfers between devices: 10.2 us -> 14.4 us  [send_inner(): return lax.ppermute(x, 'expert', pairs)]
    ppermute x9 -> x12, waiting for transfers between devices: 14.1 us -> 10 us  [send_inner(): return lax.ppermute(x, 'expert', pairs)]
    ppermute x6 -> x4, waiting for transfers between devices: 1.4 us -> 0.01 us  [send_core(): lax.ppermute(x, 'etp', [(i, move(i, step, cores)) for i in range(cores)])]
  transfers between devices with their start and end apart: 24 -> 25, of which waited for: 9 -> 8; matrix products, arithmetic and copies ran while one was open for 0% -> 0% of each run, Pallas kernels for 18% -> 23%
where the time goes in v3:
time: 61.1 us; the launch traced here: 60.9 us
  starting transfers between devices  29.8 us (49%)
  Pallas kernels  16.4 us (27%)
  waiting for transfers between devices  14 us (23%)
  between operations  0.78 us (1%)
    ppermute x9, starting transfers between devices, send_outer(): return lax.ppermute(x, 'expert', pairs)  14.7 us
    ppermute x12, starting transfers between devices, send_inner(): return lax.ppermute(x, 'expert', pairs)  14.4 us
    ppermute x12, waiting for transfers between devices, send_inner(): return lax.ppermute(x, 'expert', pairs)  10 us
    pallas_call x1, Pallas kernels, on_device(): pl.pallas_call(functools.partial(load_kernel, weight_parts), out_shape=[p...  5.43 us
    ppermute x9, waiting for transfers between devices, send_outer(): return lax.ppermute(x, 'expert', pairs)  3.96 us
    pallas_call x1, Pallas kernels, on_device(): pl.pallas_call(functools.partial(down_kernel, dims, chunks), out_shape=pl...  2.39 us
    pallas_call x1, Pallas kernels, on_device(): pl.pallas_call(functools.partial(backward_kernel, dims), out_shape=[shape...  1.98 us
    pallas_call x1, Pallas kernels, on_device(): pl.pallas_call(functools.partial(forward_kernel, dims), out_shape=[shape(...  1.98 us
  transfers between devices with their start and end apart: 25, of which 8 were waited for; matrix products, arithmetic and copies ran while one was open for 0% of the time, Pallas kernels for 23%

profile of v3, /device:TPU:0, one launch (start us, length us, event | category | flops | bytes accessed | tf_op | source)
XLA Modules:
  0.0 60.9 jit_solution(2429577917327164335)
XLA Ops:
  0.6 1.3 %prepare.1.refs_3_.refs_0_ = bf16[24,2176]{1,0:T(8,128)(2,1)S(1)} custom-call(s32[8,12]{1,0:T(8,128)} %bitcast.2, f32[8,12]{1,0:T(8,128)} %bitcast.3, bf16[12,2048]{1,0:T(8,128)(2,1)} %refs_2_.2, bf16[12,2048]{1,0:T(8,128)(2,1)} %refs_3_.1), custom_call_target="tpu_custom_call" | custom-call | flops 1 | bytes 1 | tf_op jit(solution)/shard_map/prepare/prepare/pallas_call | solution.py:368
  1.9 5.1 %collective-permute-start.2 = (bf16[24,2176]{1,0:T(8,128)(2,1)S(1)}, bf16[24,2176]{1,0:T(8,128)(2,1)S(1)}, u32[]{:S(2)}, u32[]{:S(2)}) collective-permute-start(bf16[24,2176]{1,0:T(8,128)(2,1)S(1)} %prepare.1.refs_3_.refs_0_), channel_id=1, source_target_pairs={{0,24},{2,26},{4,28},{6,30},{8,16},{10,18},{12,20},{14,22},{16,8},... | collective-permute-start | bytes 313352 | tf_op jit(solution)/shard_map/gather_blocks/ppermute | solution.py:43
  7.0 0.6 %collective-permute-start = (bf16[24,2176]{1,0:T(8,128)(2,1)S(1)}, bf16[24,2176]{1,0:T(8,128)(2,1)S(1)}, u32[]{:S(2)}, u32[]{:S(2)}) collective-permute-start(bf16[24,2176]{1,0:T(8,128)(2,1)S(1)} %prepare.1.refs_3_.refs_0_), channel_id=1, source_target_pairs={{0,8},{2,10},{4,12},{6,14},{8,0},{10,2},{12,4},{14,6},{16,24},{18,... | collective-permute-start | bytes 313352 | tf_op jit(solution)/shard_map/gather_blocks/ppermute | solution.py:43
  7.7 5.4 %load_weights.1 = (bf16[1,4096,512]{2,1,0:T(8,128)(2,1)S(1)}, bf16[1,4096,512]{2,1,0:T(8,128)(2,1)S(1)}, bf16[1,512,4096]{2,1,0:T(8,128)(2,1)S(1)}, bf16[512,409...) custom-call(bf16[1,4096,512]{2,1,0:T(8,128)(2,1)} %refs_0_.1, ...), custom_call_target="tpu_custom_call" | custom-call | flops 1 | bytes 1 | tf_op jit(solution)/shard_map/load_weights/load_weights/pallas_call | solution.py:392
  13.1 2.7 %collective-permute-done.1.refs_2_ = bf16[24,2176]{1,0:T(8,128)(2,1)S(1)} collective-permute-done((bf16[24,2176]{1,0:T(8,128)(2,1)S(1)}, bf16[24,2176]{1,0:T(8,128)(2,1)S(1)}, u32[]{:S(2)}, u32[]{:S(2)}) %collective-permute-start.1) | collective-permute-done | bytes 104480 | tf_op jit(solution)/shard_map/gather_blocks/ppermute | solution.py:43
  15.8 0.7 %route.1 = (bf16[32,2048]{1,0:T(8,128)(2,1)S(1)}, bf16[32,2048]{1,0:T(8,128)(2,1)S(1)}, bf16[32,2048]{1,0:T(8,128)(2,1)S(1)}, bf16[32,2048]{1,0:T(8,128)(2,1)S(1...) custom-call(bf16[24,2176]{1,0:T(8,128)(2,1)S(1)} %prepare.1.refs_3_., ...), custom_call_target="tpu_custom_call" | custom-call | flops 1 | bytes 1 | tf_op jit(solution)/shard_map/route/route/pallas_call | solution.py:407
  16.5 1.6 %collective-permute-start.3 = (bf16[32,2048]{1,0:T(8,128)(2,1)S(1)}, bf16[32,2048]{1,0:T(8,128)(2,1)S(1)}, u32[]{:S(2)}, u32[]{:S(2)}) collective-permute-start(bf16[32,2048]{1,0:T(8,128)(2,1)S(1)} %get-tuple-element.50), channel_id=1, source_target_pairs={{0,2},{2,0},{4,6},{6,4},{8,10},{10,8},{12,14},{14,12},{16,18},{18,... | collective-permute-start | bytes 393224 | tf_op jit(solution)/shard_map/exchange_in/ppermute | solution.py:51
  18.1 1.5 %collective-permute-start.4 = (bf16[32,2048]{1,0:T(8,128)(2,1)S(1)}, bf16[32,2048]{1,0:T(8,128)(2,1)S(1)}, u32[]{:S(2)}, u32[]{:S(2)}) collective-permute-start(bf16[32,2048]{1,0:T(8,128)(2,1)S(1)} %get-tuple-element.51), channel_id=1, source_target_pairs={{0,4},{2,6},{4,0},{6,2},{8,12},{10,14},{12,8},{14,10},{16,20},{18,... | collective-permute-start | bytes 393224 | tf_op jit(solution)/shard_map/exchange_in/ppermute | solution.py:51
  20.4 1.6 %collective-permute-start.7 = (bf16[32,2048]{1,0:T(8,128)(2,1)S(1)}, bf16[32,2048]{1,0:T(8,128)(2,1)S(1)}, u32[]{:S(2)}, u32[]{:S(2)}) collective-permute-start(bf16[32,2048]{1,0:T(8,128)(2,1)S(1)} %get-tuple-element.59), channel_id=1, source_target_pairs={{0,2},{2,0},{4,6},{6,4},{8,10},{10,8},{12,14},{14,12},{16,18},{18,... | collective-permute-start | bytes 393224 | tf_op jit(solution)/shard_map/exchange_grad/ppermute | solution.py:51
  22.0 1.5 %collective-permute-start.8 = (bf16[32,2048]{1,0:T(8,128)(2,1)S(1)}, bf16[32,2048]{1,0:T(8,128)(2,1)S(1)}, u32[]{:S(2)}, u32[]{:S(2)}) collective-permute-start(bf16[32,2048]{1,0:T(8,128)(2,1)S(1)} %get-tuple-element.60), channel_id=1, source_target_pairs={{0,4},{2,6},{4,0},{6,2},{8,12},{10,14},{12,8},{14,10},{16,20},{18,... | collective-permute-start | bytes 393224 | tf_op jit(solution)/shard_map/exchange_grad/ppermute | solution.py:51
  23.5 1.8 %collective-permute-start.9 = (bf16[32,2048]{1,0:T(8,128)(2,1)S(1)}, bf16[32,2048]{1,0:T(8,128)(2,1)S(1)}, u32[]{:S(2)}, u32[]{:S(2)}) collective-permute-start(bf16[32,2048]{1,0:T(8,128)(2,1)S(1)} %get-tuple-element.61), channel_id=1, source_target_pairs={{0,6},{2,4},{4,2},{6,0},{8,14},{10,12},{12,10},{14,8},{16,22},{18,... | collective-permute-start | bytes 393224 | tf_op jit(solution)/shard_map/exchange_grad/ppermute | solution.py:51
  25.3 1.8 %collective-permute-done.4.refs_2_ = bf16[32,2048]{1,0:T(8,128)(2,1)S(1)} collective-permute-done((bf16[32,2048]{1,0:T(8,128)(2,1)S(1)}, bf16[32,2048]{1,0:T(8,128)(2,1)S(1)}, u32[]{:S(2)}, u32[]{:S(2)}) %collective-permute-start.4) | collective-permute-done | bytes 131104 | tf_op jit(solution)/shard_map/exchange_in/ppermute | solution.py:51
  27.2 1.4 %collective-permute-done.7.refs_1_ = bf16[32,2048]{1,0:T(8,128)(2,1)S(1)} collective-permute-done((bf16[32,2048]{1,0:T(8,128)(2,1)S(1)}, bf16[32,2048]{1,0:T(8,128)(2,1)S(1)}, u32[]{:S(2)}, u32[]{:S(2)}) %collective-permute-start.7) | collective-permute-done | bytes 131104 | tf_op jit(solution)/shard_map/exchange_grad/ppermute | solution.py:51
  28.6 2.9 %collective-permute-done.8.refs_2_ = bf16[32,2048]{1,0:T(8,128)(2,1)S(1)} collective-permute-done((bf16[32,2048]{1,0:T(8,128)(2,1)S(1)}, bf16[32,2048]{1,0:T(8,128)(2,1)S(1)}, u32[]{:S(2)}, u32[]{:S(2)}) %collective-permute-start.8) | collective-permute-done | bytes 131104 | tf_op jit(solution)/shard_map/exchange_grad/ppermute | solution.py:51
  31.6 2.0 %forward.1 = (f32[128,512]{1,0:T(8,128)S(1)}, f32[128,512]{1,0:T(8,128)S(1)}, bf16[128,512]{1,0:T(8,128)(2,1)S(1)}, bf16[128,2048]{1,0:T(8,128)(2,1)S(1)}, bf16[128,2048]{1,0:T(8,128)(2,1)S(1)}) custom-call(bf16[128,2048]{1,0:T(8,128)(2,1)S(1)} %stack.2.refs_0_, bf16[128,2048]{1,0:T(8,128)(2,1)S(1)} %collective-permute-done.6.refs_1_, ...), custom_call_target="tpu_custom_call" | custom-call | flops 1 | bytes 1 | tf_op jit(solution)/shard_map/forward/forward/pallas_call | solution.py:453
  34.2 2.0 %backward.1 = (bf16[128,2048]{1,0:T(8,128)(2,1)S(1)}, bf16[128,2048]{1,0:T(8,128)(2,1)S(1)}) custom-call(bf16[128,2048]{1,0:T(8,128)(2,1)S(1)} %stack.3.refs_5_.refs_0_, bf16[128,2048]{1,0:T(8,128)(2,1)S(1)} %collective-permute-done.17.refs_1_, bf16[512,4096]{1,0:T(8,128)(2,1)S(1)} %get-tuple-element.75.refs_2_, ...), custom_call_target="tpu_custom_call" | custom-call | flops 1 | bytes 1 | tf_op jit(solution)/shard_map/backward/backward/pallas_call | solution.py:504
  36.4 0.6 %collective-permute-start.11 = (bf16[32,2048]{1,0:T(8,128)(2,1)S(1)}, bf16[32,2048]{1,0:T(8,128)(2,1)S(1)}, u32[]{:S(2)}, u32[]{:S(2)}) collective-permute-start(bf16[32,2048]{1,0:T(8,128)(2,1)S(1)} %get-tuple-element.65), channel_id=1, source_target_pairs={{0,2},{2,0},{4,6},{6,4},{8,10},{10,8},{12,14},{14,12},{16,18},{18,... | collective-permute-start | bytes 393224 | tf_op jit(solution)/shard_map/return_out/ppermute | solution.py:51
  37.0 0.8 %collective-permute-start.12 = (bf16[32,2048]{1,0:T(8,128)(2,1)S(1)}, bf16[32,2048]{1,0:T(8,128)(2,1)S(1)}, u32[]{:S(2)}, u32[]{:S(2)}) collective-permute-start(bf16[32,2048]{1,0:T(8,128)(2,1)S(1)} %get-tuple-element.66), channel_id=1, source_target_pairs={{0,4},{2,6},{4,0},{6,2},{8,12},{10,14},{12,8},{14,10},{16,20},{18,... | collective-permute-start | bytes 393224 | tf_op jit(solution)/shard_map/return_out/ppermute | solution.py:51
  37.8 2.1 %collective-permute-start.13 = (bf16[32,2048]{1,0:T(8,128)(2,1)S(1)}, bf16[32,2048]{1,0:T(8,128)(2,1)S(1)}, u32[]{:S(2)}, u32[]{:S(2)}) collective-permute-start(bf16[32,2048]{1,0:T(8,128)(2,1)S(1)} %get-tuple-element.67), channel_id=1, source_target_pairs={{0,6},{2,4},{4,2},{6,0},{8,14},{10,12},{12,10},{14,8},{16,22},{18,... | collective-permute-start | bytes 393224 | tf_op jit(solution)/shard_map/return_out/ppermute | solution.py:51
  40.1 0.6 %collective-permute-start.19 = (bf16[32,2048]{1,0:T(8,128)(2,1)S(1)}, bf16[32,2048]{1,0:T(8,128)(2,1)S(1)}, u32[]{:S(2)}, u32[]{:S(2)}) collective-permute-start(bf16[32,2048]{1,0:T(8,128)(2,1)S(1)} %get-tuple-element.83), channel_id=1, source_target_pairs={{0,2},{2,0},{4,6},{6,4},{8,10},{10,8},{12,14},{14,12},{16,18},{18,... | collective-permute-start | bytes 393224 | tf_op jit(solution)/shard_map/return_grad/ppermute | solution.py:51
  40.7 0.8 %collective-permute-start.20 = (bf16[32,2048]{1,0:T(8,128)(2,1)S(1)}, bf16[32,2048]{1,0:T(8,128)(2,1)S(1)}, u32[]{:S(2)}, u32[]{:S(2)}) collective-permute-start(bf16[32,2048]{1,0:T(8,128)(2,1)S(1)} %get-tuple-element.84), channel_id=1, source_target_pairs={{0,4},{2,6},{4,0},{6,2},{8,12},{10,14},{12,8},{14,10},{16,20},{18,... | collective-permute-start | bytes 393224 | tf_op jit(solution)/shard_map/return_grad/ppermute | solution.py:51
  41.5 1.2 %collective-permute-done.11.refs_1_ = bf16[32,2048]{1,0:T(8,128)(2,1)S(1)} collective-permute-done((bf16[32,2048]{1,0:T(8,128)(2,1)S(1)}, bf16[32,2048]{1,0:T(8,128)(2,1)S(1)}, u32[]{:S(2)}, u32[]{:S(2)}) %collective-permute-start.11) | collective-permute-done | bytes 131104 | tf_op jit(solution)/shard_map/return_out/ppermute | solution.py:51
  42.7 0.9 %collective-permute-start.21 = (bf16[32,2048]{1,0:T(8,128)(2,1)S(1)}, bf16[32,2048]{1,0:T(8,128)(2,1)S(1)}, u32[]{:S(2)}, u32[]{:S(2)}) collective-permute-start(bf16[32,2048]{1,0:T(8,128)(2,1)S(1)} %get-tuple-element.85), channel_id=1, source_target_pairs={{0,6},{2,4},{4,2},{6,0},{8,14},{10,12},{12,10},{14,8},{16,22},{18,... | collective-permute-start | bytes 393224 | tf_op jit(solution)/shard_map/return_grad/ppermute | solution.py:51
  43.6 2.4 %collective-permute-done.13.refs_3_ = bf16[32,2048]{1,0:T(8,128)(2,1)S(1)} collective-permute-done((bf16[32,2048]{1,0:T(8,128)(2,1)S(1)}, bf16[32,2048]{1,0:T(8,128)(2,1)S(1)}, u32[]{:S(2)}, u32[]{:S(2)}) %collective-permute-start.13) | collective-permute-done | bytes 131104 | tf_op jit(solution)/shard_map/return_out/ppermute | solution.py:51
  46.8 2.5 %collective-permute-start.15 = (bf16[24,1024]{1,0:T(8,128)(2,1)S(1)}, bf16[24,1024]{1,0:T(8,128)(2,1)S(1)}, u32[]{:S(2)}, u32[]{:S(2)}) collective-permute-start(bf16[24,1024]{1,0:T(8,128)(2,1)S(1)} %get-tuple-element.72), channel_id=1, source_target_pairs={{0,16},{2,18},{4,20},{6,22},{8,24},{10,26},{12,28},{14,30},{16,0},... | collective-permute-start | bytes 147464 | tf_op jit(solution)/shard_map/return_out/ppermute | solution.py:43
  49.3 1.6 %collective-permute-start.16 = (bf16[24,1024]{1,0:T(8,128)(2,1)S(1)}, bf16[24,1024]{1,0:T(8,128)(2,1)S(1)}, u32[]{:S(2)}, u32[]{:S(2)}) collective-permute-start(bf16[24,1024]{1,0:T(8,128)(2,1)S(1)} %get-tuple-element.73), channel_id=1, source_target_pairs={{0,24},{2,26},{4,28},{6,30},{8,16},{10,18},{12,20},{14,22},{16,8},... | collective-permute-start | bytes 147464 | tf_op jit(solution)/shard_map/return_out/ppermute | solution.py:43
  51.9 2.5 %collective-permute-start.23 = (bf16[24,1024]{1,0:T(8,128)(2,1)S(1)}, bf16[24,1024]{1,0:T(8,128)(2,1)S(1)}, u32[]{:S(2)}, u32[]{:S(2)}) collective-permute-start(bf16[24,1024]{1,0:T(8,128)(2,1)S(1)} %get-tuple-element.88), channel_id=1, source_target_pairs={{0,16},{2,18},{4,20},{6,22},{8,24},{10,26},{12,28},{14,30},{16,0},... | collective-permute-start | bytes 147464 | tf_op jit(solution)/shard_map/return_grad/ppermute | solution.py:43
  54.4 1.6 %collective-permute-start.24 = (bf16[24,1024]{1,0:T(8,128)(2,1)S(1)}, bf16[24,1024]{1,0:T(8,128)(2,1)S(1)}, u32[]{:S(2)}, u32[]{:S(2)}) collective-permute-start(bf16[24,1024]{1,0:T(8,128)(2,1)S(1)} %get-tuple-element.89), channel_id=1, source_target_pairs={{0,24},{2,26},{4,28},{6,30},{8,16},{10,18},{12,20},{14,22},{16,8},... | collective-permute-start | bytes 147464 | tf_op jit(solution)/shard_map/return_grad/ppermute | solution.py:43
  55.9 2.4 %down_grad.1 = bf16[1,512,4096]{2,1,0:T(8,128)(2,1)} custom-call(bf16[128,2048]{1,0:T(8,128)(2,1)S(1)} %stack.3.refs_5_.refs_0_, bf16[128,2048]{1,0:T(8,128)(2,1)S(1)} %collective-permute-done.17.refs_1_, bf16[128,512]{1,0:T(8,128)(2,1)S(1)} %get-tuple-element.92.refs_2_, bf16[24,1024]{1,0:T(8,128)(2,1)S(1)} %get-tuple-element.86.refs_0_.refs_3_), custom_call_target="tpu_custom_call" | custom-call | flops 1 | bytes 1 | tf_op jit(solution)/shard_map/down_grad/down_grad/pallas_call | solution.py:519
  58.4 0.7 %final.2 = (bf16[12,2048]{1,0:T(8,128)(2,1)}, f32[8,128]{1,0:T(8,128)S(1)}) custom-call(bf16[24,1024]{1,0:T(8,128)(2,1)S(1)} %get-tuple-element.70.refs_0_, bf16[24,1024]{1,0:T(8,128)(2,1)S(1)} %collective-permute-done.14.refs_1_, bf16[24,1024]{1,0:T(8,128)(2,1)S(1)} %collective-permute-done.15.refs_2_, bf16[24,1024]{1,0:T(8,128)(2,1)S(1)} %collective-permute-done.16.refs_3_), custom_call_target="tpu_custom_call" | custom-call | flops 1 | bytes 1 | tf_op jit(solution)/shard_map/final/pallas_call | solution.py:489
  59.0 1.2 %collective-permute-done.24.refs_3_ = bf16[24,1024]{1,0:T(8,128)(2,1)S(1)} collective-permute-done((bf16[24,1024]{1,0:T(8,128)(2,1)S(1)}, bf16[24,1024]{1,0:T(8,128)(2,1)S(1)}, u32[]{:S(2)}, u32[]{:S(2)}) %collective-permute-start.24) | collective-permute-done | bytes 49184 | tf_op jit(solution)/shard_map/return_grad/ppermute | solution.py:43
  60.3 0.7 %final.3 = (bf16[12,2048]{1,0:T(8,128)(2,1)}, f32[8,128]{1,0:T(8,128)}) custom-call(bf16[24,1024]{1,0:T(8,128)(2,1)S(1)} %get-tuple-element.86.refs_0_.refs_3_, bf16[24,1024]{1,0:T(8,128)(2,1)S(1)} %collective-permute-done.22.refs_1_, bf16[24,1024]{1,0:T(8,128)(2,1)S(1)} %collective-permute-done.23.refs_2_, ...), custom_call_target="tpu_custom_call" | custom-call | flops 1 | bytes 1 | tf_op jit(solution)/shard_map/final/pallas_call | solution.py:489
  (33 shorter events, 3.7 us)
Async XLA Ops:
  1.9 11.2 %collective-permute-start.2 = (bf16[24,2176]{1,0:T(8,128)(2,1)S(1)}, bf16[24,2176]{1,0:T(8,128)(2,1)S(1)}, u32[]{:S(2)}, u32[]{:S(2)}) collective-permute-start(bf16[24,2176]{1,0:T(8,128)(2,1)S(1)} %prepare.1.refs_3_.refs_0_), channel_id=1, source_target_pairs={{0,24},{2,26},{4,28},{6,30},{8,16},{10,18},{12,20},{14,22},{16,8},... | collective-permute-start | bytes 313352 | tf_op jit(solution)/shard_map/gather_blocks/ppermute | solution.py:43
  7.0 8.8 %collective-permute-start.1 = (bf16[24,2176]{1,0:T(8,128)(2,1)S(1)}, bf16[24,2176]{1,0:T(8,128)(2,1)S(1)}, u32[]{:S(2)}, u32[]{:S(2)}) collective-permute-start(bf16[24,2176]{1,0:T(8,128)(2,1)S(1)} %prepare.1.refs_3_.refs_0_), channel_id=1, source_target_pairs={{0,16},{2,18},{4,20},{6,22},{8,24},{10,26},{12,28},{14,30},{16,0},... | collective-permute-start | bytes 313352 | tf_op jit(solution)/shard_map/gather_blocks/ppermute | solution.py:43
  7.0 8.8 %collective-permute-start = (bf16[24,2176]{1,0:T(8,128)(2,1)S(1)}, bf16[24,2176]{1,0:T(8,128)(2,1)S(1)}, u32[]{:S(2)}, u32[]{:S(2)}) collective-permute-start(bf16[24,2176]{1,0:T(8,128)(2,1)S(1)} %prepare.1.refs_3_.refs_0_), channel_id=1, source_target_pairs={{0,8},{2,10},{4,12},{6,14},{8,0},{10,2},{12,4},{14,6},{16,24},{18,... | collective-permute-start | bytes 313352 | tf_op jit(solution)/shard_map/gather_blocks/ppermute | solution.py:43
  16.5 7.0 %collective-permute-start.3 = (bf16[32,2048]{1,0:T(8,128)(2,1)S(1)}, bf16[32,2048]{1,0:T(8,128)(2,1)S(1)}, u32[]{:S(2)}, u32[]{:S(2)}) collective-permute-start(bf16[32,2048]{1,0:T(8,128)(2,1)S(1)} %get-tuple-element.50), channel_id=1, source_target_pairs={{0,2},{2,0},{4,6},{6,4},{8,10},{10,8},{12,14},{14,12},{16,18},{18,... | collective-permute-start | bytes 393224 | tf_op jit(solution)/shard_map/exchange_in/ppermute | solution.py:51
  18.1 9.0 %collective-permute-start.4 = (bf16[32,2048]{1,0:T(8,128)(2,1)S(1)}, bf16[32,2048]{1,0:T(8,128)(2,1)S(1)}, u32[]{:S(2)}, u32[]{:S(2)}) collective-permute-start(bf16[32,2048]{1,0:T(8,128)(2,1)S(1)} %get-tuple-element.51), channel_id=1, source_target_pairs={{0,4},{2,6},{4,0},{6,2},{8,12},{10,14},{12,8},{14,10},{16,20},{18,... | collective-permute-start | bytes 393224 | tf_op jit(solution)/shard_map/exchange_in/ppermute | solution.py:51
  19.6 7.5 %collective-permute-start.5 = (bf16[32,2048]{1,0:T(8,128)(2,1)S(1)}, bf16[32,2048]{1,0:T(8,128)(2,1)S(1)}, u32[]{:S(2)}, u32[]{:S(2)}) collective-permute-start(bf16[32,2048]{1,0:T(8,128)(2,1)S(1)} %get-tuple-element.52), channel_id=1, source_target_pairs={{0,6},{2,4},{4,2},{6,0},{8,14},{10,12},{12,10},{14,8},{16,22},{18,... | collective-permute-start | bytes 393224 | tf_op jit(solution)/shard_map/exchange_in/ppermute | solution.py:51
  20.4 8.2 %collective-permute-start.7 = (bf16[32,2048]{1,0:T(8,128)(2,1)S(1)}, bf16[32,2048]{1,0:T(8,128)(2,1)S(1)}, u32[]{:S(2)}, u32[]{:S(2)}) collective-permute-start(bf16[32,2048]{1,0:T(8,128)(2,1)S(1)} %get-tuple-element.59), channel_id=1, source_target_pairs={{0,2},{2,0},{4,6},{6,4},{8,10},{10,8},{12,14},{14,12},{16,18},{18,... | collective-permute-start | bytes 393224 | tf_op jit(solution)/shard_map/exchange_grad/ppermute | solution.py:51
  22.0 9.5 %collective-permute-start.8 = (bf16[32,2048]{1,0:T(8,128)(2,1)S(1)}, bf16[32,2048]{1,0:T(8,128)(2,1)S(1)}, u32[]{:S(2)}, u32[]{:S(2)}) collective-permute-start(bf16[32,2048]{1,0:T(8,128)(2,1)S(1)} %get-tuple-element.60), channel_id=1, source_target_pairs={{0,4},{2,6},{4,0},{6,2},{8,12},{10,14},{12,8},{14,10},{16,20},{18,... | collective-permute-start | bytes 393224 | tf_op jit(solution)/shard_map/exchange_grad/ppermute | solution.py:51
  23.5 8.0 %collective-permute-start.9 = (bf16[32,2048]{1,0:T(8,128)(2,1)S(1)}, bf16[32,2048]{1,0:T(8,128)(2,1)S(1)}, u32[]{:S(2)}, u32[]{:S(2)}) collective-permute-start(bf16[32,2048]{1,0:T(8,128)(2,1)S(1)} %get-tuple-element.61), channel_id=1, source_target_pairs={{0,6},{2,4},{4,2},{6,0},{8,14},{10,12},{12,10},{14,8},{16,22},{18,... | collective-permute-start | bytes 393224 | tf_op jit(solution)/shard_map/exchange_grad/ppermute | solution.py:51
  27.2 4.5 %collective-permute-start.6 = (bf16[128,2048]{1,0:T(8,128)(2,1)S(1)}, bf16[128,2048]{1,0:T(8,128)(2,1)S(1)}, u32[]{:S(2)}, u32[]{:S(2)}) collective-permute-start(bf16[128,2048]{1,0:T(8,128)(2,1)S(1)} %stack.2.refs_0_), channel_id=1, source_target_pairs={{0,1},{1,0},{2,3},{3,2},{4,5},{5,4},{6,7},{7,6},{8,9},{9,8},{10,11... | collective-permute-start | bytes 1572872 | tf_op jit(solution)/shard_map/gather_in/ppermute | solution.py:56
  31.5 2.6 %collective-permute-start.17 = (bf16[128,2048]{1,0:T(8,128)(2,1)S(1)}, bf16[128,2048]{1,0:T(8,128)(2,1)S(1)}, u32[]{:S(2)}, u32[]{:S(2)}) collective-permute-start(bf16[128,2048]{1,0:T(8,128)(2,1)S(1)} %stack.3.refs_5_.refs_0_), channel_id=1, source_target_pairs={{0,1},{1,0},{2,3},{3,2},{4,5},{5,4},{6,7},{7,6},{8,9},{9,8},{10,11... | collective-permute-start | bytes 1572872 | tf_op jit(solution)/shard_map/gather_in/ppermute | solution.py:56
  33.6 2.6 %collective-permute-start.10 = (bf16[128,2048]{1,0:T(8,128)(2,1)S(1)}, bf16[128,2048]{1,0:T(8,128)(2,1)S(1)}, u32[]{:S(2)}, u32[]{:S(2)}) collective-permute-start(bf16[128,2048]{1,0:T(8,128)(2,1)S(1)} %get-tuple-element.63), channel_id=1, source_target_pairs={{0,1},{1,0},{2,3},{3,2},{4,5},{5,4},{6,7},{7,6},{8,9},{9,8},{10,11... | collective-permute-start | bytes 1572872 | tf_op jit(solution)/shard_map/return_out/ppermute | solution.py:56
  36.1 3.8 %collective-permute-start.18 = (bf16[128,2048]{1,0:T(8,128)(2,1)S(1)}, bf16[128,2048]{1,0:T(8,128)(2,1)S(1)}, u32[]{:S(2)}, u32[]{:S(2)}) collective-permute-start(bf16[128,2048]{1,0:T(8,128)(2,1)S(1)} %get-tuple-element.81), channel_id=1, source_target_pairs={{0,1},{1,0},{2,3},{3,2},{4,5},{5,4},{6,7},{7,6},{8,9},{9,8},{10,11... | collective-permute-start | bytes 1572872 | tf_op jit(solution)/shard_map/return_grad/ppermute | solution.py:56
  36.4 6.4 %collective-permute-start.11 = (bf16[32,2048]{1,0:T(8,128)(2,1)S(1)}, bf16[32,2048]{1,0:T(8,128)(2,1)S(1)}, u32[]{:S(2)}, u32[]{:S(2)}) collective-permute-start(bf16[32,2048]{1,0:T(8,128)(2,1)S(1)} %get-tuple-element.65), channel_id=1, source_target_pairs={{0,2},{2,0},{4,6},{6,4},{8,10},{10,8},{12,14},{14,12},{16,18},{18,... | collective-permute-start | bytes 393224 | tf_op jit(solution)/shard_map/return_out/ppermute | solution.py:51
  37.0 6.6 %collective-permute-start.12 = (bf16[32,2048]{1,0:T(8,128)(2,1)S(1)}, bf16[32,2048]{1,0:T(8,128)(2,1)S(1)}, u32[]{:S(2)}, u32[]{:S(2)}) collective-permute-start(bf16[32,2048]{1,0:T(8,128)(2,1)S(1)} %get-tuple-element.66), channel_id=1, source_target_pairs={{0,4},{2,6},{4,0},{6,2},{8,12},{10,14},{12,8},{14,10},{16,20},{18,... | collective-permute-start | bytes 393224 | tf_op jit(solution)/shard_map/return_out/ppermute | solution.py:51
  37.8 8.2 %collective-permute-start.13 = (bf16[32,2048]{1,0:T(8,128)(2,1)S(1)}, bf16[32,2048]{1,0:T(8,128)(2,1)S(1)}, u32[]{:S(2)}, u32[]{:S(2)}) collective-permute-start(bf16[32,2048]{1,0:T(8,128)(2,1)S(1)} %get-tuple-element.67), channel_id=1, source_target_pairs={{0,6},{2,4},{4,2},{6,0},{8,14},{10,12},{12,10},{14,8},{16,22},{18,... | collective-permute-start | bytes 393224 | tf_op jit(solution)/shard_map/return_out/ppermute | solution.py:51
  40.1 9.2 %collective-permute-start.19 = (bf16[32,2048]{1,0:T(8,128)(2,1)S(1)}, bf16[32,2048]{1,0:T(8,128)(2,1)S(1)}, u32[]{:S(2)}, u32[]{:S(2)}) collective-permute-start(bf16[32,2048]{1,0:T(8,128)(2,1)S(1)} %get-tuple-element.83), channel_id=1, source_target_pairs={{0,2},{2,0},{4,6},{6,4},{8,10},{10,8},{12,14},{14,12},{16,18},{18,... | collective-permute-start | bytes 393224 | tf_op jit(solution)/shard_map/return_grad/ppermute | solution.py:51
  40.7 10.2 %collective-permute-start.20 = (bf16[32,2048]{1,0:T(8,128)(2,1)S(1)}, bf16[32,2048]{1,0:T(8,128)(2,1)S(1)}, u32[]{:S(2)}, u32[]{:S(2)}) collective-permute-start(bf16[32,2048]{1,0:T(8,128)(2,1)S(1)} %get-tuple-element.84), channel_id=1, source_target_pairs={{0,4},{2,6},{4,0},{6,2},{8,12},{10,14},{12,8},{14,10},{16,20},{18,... | collective-permute-start | bytes 393224 | tf_op jit(solution)/shard_map/return_grad/ppermute | solution.py:51
  42.7 8.5 %collective-permute-start.21 = (bf16[32,2048]{1,0:T(8,128)(2,1)S(1)}, bf16[32,2048]{1,0:T(8,128)(2,1)S(1)}, u32[]{:S(2)}, u32[]{:S(2)}) collective-permute-start(bf16[32,2048]{1,0:T(8,128)(2,1)S(1)} %get-tuple-element.85), channel_id=1, source_target_pairs={{0,6},{2,4},{4,2},{6,0},{8,14},{10,12},{12,10},{14,8},{16,22},{18,... | collective-permute-start | bytes 393224 | tf_op jit(solution)/shard_map/return_grad/ppermute | solution.py:51
  46.4 8.0 %collective-permute-start.14 = (bf16[24,1024]{1,0:T(8,128)(2,1)S(1)}, bf16[24,1024]{1,0:T(8,128)(2,1)S(1)}, u32[]{:S(2)}, u32[]{:S(2)}) collective-permute-start(bf16[24,1024]{1,0:T(8,128)(2,1)S(1)} %get-tuple-element.71), channel_id=1, source_target_pairs={{0,8},{2,10},{4,12},{6,14},{8,0},{10,2},{12,4},{14,6},{16,24},{18,... | collective-permute-start | bytes 147464 | tf_op jit(solution)/shard_map/return_out/ppermute | solution.py:43
  46.8 11.6 %collective-permute-start.15 = (bf16[24,1024]{1,0:T(8,128)(2,1)S(1)}, bf16[24,1024]{1,0:T(8,128)(2,1)S(1)}, u32[]{:S(2)}, u32[]{:S(2)}) collective-permute-start(bf16[24,1024]{1,0:T(8,128)(2,1)S(1)} %get-tuple-element.72), channel_id=1, source_target_pairs={{0,16},{2,18},{4,20},{6,22},{8,24},{10,26},{12,28},{14,30},{16,0},... | collective-permute-start | bytes 147464 | tf_op jit(solution)/shard_map/return_out/ppermute | solution.py:43
  49.3 9.1 %collective-permute-start.16 = (bf16[24,1024]{1,0:T(8,128)(2,1)S(1)}, bf16[24,1024]{1,0:T(8,128)(2,1)S(1)}, u32[]{:S(2)}, u32[]{:S(2)}) collective-permute-start(bf16[24,1024]{1,0:T(8,128)(2,1)S(1)} %get-tuple-element.73), channel_id=1, source_target_pairs={{0,24},{2,26},{4,28},{6,30},{8,16},{10,18},{12,20},{14,22},{16,8},... | collective-permute-start | bytes 147464 | tf_op jit(solution)/shard_map/return_out/ppermute | solution.py:43
  51.5 7.5 %collective-permute-start.22 = (bf16[24,1024]{1,0:T(8,128)(2,1)S(1)}, bf16[24,1024]{1,0:T(8,128)(2,1)S(1)}, u32[]{:S(2)}, u32[]{:S(2)}) collective-permute-start(bf16[24,1024]{1,0:T(8,128)(2,1)S(1)} %get-tuple-element.87), channel_id=1, source_target_pairs={{0,8},{2,10},{4,12},{6,14},{8,0},{10,2},{12,4},{14,6},{16,24},{18,... | collective-permute-start | bytes 147464 | tf_op jit(solution)/shard_map/return_grad/ppermute | solution.py:43
  51.9 7.2 %collective-permute-start.23 = (bf16[24,1024]{1,0:T(8,128)(2,1)S(1)}, bf16[24,1024]{1,0:T(8,128)(2,1)S(1)}, u32[]{:S(2)}, u32[]{:S(2)}) collective-permute-start(bf16[24,1024]{1,0:T(8,128)(2,1)S(1)} %get-tuple-element.88), channel_id=1, source_target_pairs={{0,16},{2,18},{4,20},{6,22},{8,24},{10,26},{12,28},{14,30},{16,0},... | collective-permute-start | bytes 147464 | tf_op jit(solution)/shard_map/return_grad/ppermute | solution.py:43
  54.4 5.9 %collective-permute-start.24 = (bf16[24,1024]{1,0:T(8,128)(2,1)S(1)}, bf16[24,1024]{1,0:T(8,128)(2,1)S(1)}, u32[]{:S(2)}, u32[]{:S(2)}) collective-permute-start(bf16[24,1024]{1,0:T(8,128)(2,1)S(1)} %get-tuple-element.89), channel_id=1, source_target_pairs={{0,24},{2,26},{4,28},{6,30},{8,16},{10,18},{12,20},{14,22},{16,8},... | collective-permute-start | bytes 147464 | tf_op jit(solution)/shard_map/return_grad/ppermute | solution.py:43

commit v4 on v3

--- a/solution.py
+++ b/solution.py
@@ -56,13 +56,8 @@
     return lax.ppermute(x, "etp", [(i, move(i, step, cores)) for i in range(cores)])
 
 
-def send_order(count):
-    return range(1, count)
-
-
-def gather_outer(x, outer, inner):
-    sent = {s: send_outer(x, s, outer, inner) for s in send_order(outer)}
-    return [x] + [sent[s] for s in range(1, outer)]
+def flipped(parts):
+    return [parts[0], *parts[:0:-1]]
 
 
 def contract(left, right, left_dim, right_dim):
@@ -141,21 +136,24 @@
     outer, inner, tokens, top, cap, reach, half = dims
     blocks = refs[:outer]
     sends = refs[outer + 1 : outer + 1 + inner]
-    pick_ref, gate_hi_ref, gate_lo_ref, gate_col_ref = refs[outer + 1 + inner :]
+    pick_ref, gate_hi_ref, gate_mid_ref, gate_col_ref = refs[outer + 1 + inner :]
     rows = outer * 2 * tokens
-    slots = inner * reach
+    fold = 2 * reach
+    slots = inner * fold
     me = lax.axis_index("expert")
     my_inner = lax.rem(me, inner)
     my_base = me - my_inner
     meta = jnp.concatenate([r[:, 2 * half :].astype(F32) for r in blocks], axis=0)
     lane = lax.broadcasted_iota(jnp.int32, (rows, slots), 1)
     row = lax.broadcasted_iota(jnp.int32, (rows, slots), 0)
-    step = count_above(lane, reach, slots)
+    step = count_above(lane, fold, slots)
     dest = jnp.zeros((rows, slots), F32)
     for q in range(inner):
         expert = (my_base + traced_partner(my_inner, q, inner)).astype(F32)
         dest = jnp.where(step == q, expert, dest)
-    slot = lane - step * reach
+    slot = lane - step * fold
+    side = (slot >= reach).astype(jnp.int32)
+    slot = slot - side * reach
     named = jnp.zeros((rows, slots), F32)
     gate = jnp.zeros((rows, slots), F32)
     for k in range(top):
@@ -173,40 +171,29 @@
     before = (same & (left < down)).astype(F32).astype(BF16)
     rank = jnp.dot(before, named.astype(BF16), preferred_element_type=F32)
     position = count_above(row, 2 * tokens, rows) * cap + rank.astype(jnp.int32)
-    pick = jnp.where(position == slot, named, 0.0)
+    row_side = count_above(row, tokens, rows) - 2 * count_above(row, 2 * tokens, rows)
+    pick = jnp.where((position == slot) & (row_side == side), named, 0.0)
     gate = pick * gate
     gate_hi = gate.astype(BF16)
     rest = gate - gate_hi.astype(F32)
     gate_mid = rest.astype(BF16)
     gate_lo = (rest - gate_mid.astype(F32)).astype(BF16)
-    part = count_above(row, tokens, rows)
-    even = part - 2 * count_above(row, 2 * tokens, rows) == 0
-    pick_left = jnp.where(even, pick, 0.0).astype(BF16)
-    pick_right = jnp.where(even, 0.0, pick).astype(BF16)
-    pick_ref[...] = jnp.concatenate([pick_left, pick_right], axis=1)
-    gate_hi_ref[...] = jnp.concatenate(
-        [jnp.where(even, gate_hi.astype(F32), 0.0), jnp.where(even, 0.0, gate_hi.astype(F32))], axis=1
-    ).astype(BF16)
-    gate_lo_ref[...] = jnp.concatenate(
-        [jnp.where(even, gate_mid.astype(F32), 0.0), jnp.where(even, 0.0, gate_mid.astype(F32))], axis=1
-    ).astype(BF16)
+    pick_ref[...] = pick.astype(BF16)
+    gate_hi_ref[...] = gate_hi
+    gate_mid_ref[...] = gate_mid
     ones = jnp.ones((rows, META), BF16)
     column = contract(gate_hi, ones, 0, 0) + contract(gate_mid, ones, 0, 0) + contract(gate_lo, ones, 0, 0)
-    gate_col_ref[...] = 0.5 * column
+    gate_col_ref[...] = column
     select_rows(blocks, 0, pick_ref, None, sends)
 
 
 def select_rows(blocks, array, pick_ref, scale, sends):
-    inner = len(sends)
-    reach, width = sends[0].shape
-    half = width // 2
-    slots = inner * reach
+    fold, half = sends[0].shape
     table = stacked(blocks, pl.ds(array * half, half))
-    for side in range(2):
-        out = contract(pick_ref[:, side * slots : (side + 1) * slots], table, 0, 0)
-        out = (out if scale is None else out * scale).astype(BF16)
-        for q in range(inner):
-            sends[q][:, side * half : (side + 1) * half] = out[q * reach : (q + 1) * reach]
+    out = contract(pick_ref[...], table, 0, 0)
+    out = (out if scale is None else out * scale).astype(F32)
+    for q, send in enumerate(sends):
+        send[...] = out[q * fold : (q + 1) * fold].astype(BF16)
 
 
 def scale_kernel(outer, inner, *refs):
@@ -214,10 +201,16 @@
     select_rows(refs[:outer], 1, pick_ref, gate_col_ref[:, :1], refs[-inner:])
 
 
-def stack_kernel(inner, *refs):
-    reach = refs[0].shape[0]
-    for q in range(inner):
-        refs[-1][q * reach : (q + 1) * reach, :] = refs[q][...]
+def stack_kernel(dims, *refs):
+    inner, reach, held = dims
+    fold, half = refs[0].shape
+    live = lax.broadcasted_iota(jnp.int32, (held, half), 0) < reach
+    for q, piece in enumerate(flipped(refs[:inner])):
+        value = piece[...].astype(F32)
+        sides = (value[:held], pltpu.roll(value[fold - held :], fold - reach, 0))
+        for n, side in enumerate(sides):
+            target = refs[-1].at[q * held : (q + 1) * held, n * half : (n + 1) * half]
+            target[...] = jnp.where(live, side, 0.0).astype(BF16)
 
 
 def load_kernel(parts, *refs):
@@ -312,26 +305,27 @@
 
 
 def split_kernel(dims, *refs):
-    cores, inner, reach = dims
+    cores, inner, reach, held = dims
     total = refs[0][...].astype(F32)
     for part in refs[1:cores]:
         total = total + part[...].astype(F32)
-    total = total.astype(BF16)
+    half = total.shape[1] // 2
+    rest = jnp.zeros((2 * reach - held, half), F32)
     for q in range(inner):
-        refs[q - inner][...] = total[q * reach : (q + 1) * reach]
+        rows = total[q * held : (q + 1) * held]
+        right = pltpu.roll(rows[:, half:], held - reach, 0)
+        value = jnp.concatenate([rows[:, :half], rest], axis=0) + jnp.concatenate([rest, right], axis=0)
+        refs[q - inner][...] = value.astype(BF16)
 
 
 def combine_kernel(dims, weighted, *refs):
-    outer, inner, unit, half = dims
-    pieces = refs[:inner]
+    outer, inner, unit = dims
     tables = refs[inner : inner + weighted]
     outs = refs[-outer:]
-    rows = jnp.concatenate([p[...] for p in pieces], axis=0)
-    slots = rows.shape[0]
+    rows = stacked(flipped(refs[:inner]))
     total = None
     for table in tables:
-        term = jnp.dot(table[:, :slots], rows[:, :half], preferred_element_type=F32)
-        term = term + jnp.dot(table[:, slots:], rows[:, half:], preferred_element_type=F32)
+        term = jnp.dot(table[...], rows, preferred_element_type=F32)
         total = term if total is None else total + term
     for b in range(outer):
         outs[b][...] = total[b * unit : (b + 1) * unit].astype(BF16)
@@ -360,8 +354,9 @@
     width = hidden_in.shape[1]
     half = width // 2
     hidden = gate_weight.shape[2]
-    reach = -(-(outer * cap) // 16) * 16
-    rows = inner * reach
+    reach = outer * cap
+    held = -(-reach // 16) * 16
+    rows = inner * held
     unit = 2 * tokens
 
     with jax.named_scope("prepare"):
@@ -383,13 +378,14 @@
         )(in_hbm(expert_ids.T), in_hbm(gate_weights.T), in_hbm(hidden_in), in_hbm(out_grad))
 
     with jax.named_scope("gather_blocks"):
-        blocks = gather_outer(packed, outer, inner)
-
-    table_shape = shape(outer * unit, 2 * rows)
+        blocks = [packed] + [send_outer(packed, s, outer, inner) for s in range(1, outer)]
+
+    piece_shapes = [shape(2 * reach, half)] * inner
+    table_shape = shape(outer * unit, inner * 2 * reach)
     with jax.named_scope("load_weights"):
         weights = (gate_weight, up_weight, down_weight)
         weight_parts = 4
-        held = pl.pallas_call(
+        loaded = pl.pallas_call(
             functools.partial(load_kernel, weight_parts),
             out_shape=[pltpu.VMEM(w.shape, BF16) for w in weights]
             + [pltpu.VMEM((w.shape[2], w.shape[1]), BF16) for w in weights]
@@ -401,18 +397,18 @@
             cost_estimate=pl.CostEstimate(flops=1, bytes_accessed=1, transcendentals=0),
             name="load_weights",
         )(*[in_hbm(w) for w in weights], packed)
-        weights, turned = held[:3], held[3:6]
+        weights, turned = loaded[:3], loaded[3:6]
 
     with jax.named_scope("route"):
         routed = pl.pallas_call(
             functools.partial(route_kernel, (outer, inner, tokens, top, cap, reach, half)),
-            out_shape=[shape(reach, width)] * inner + [table_shape] * 3 + [shape(rows, META, F32)],
+            out_shape=piece_shapes + [table_shape] * 3 + [shape(inner * 2 * reach, META, F32)],
             in_specs=whole_specs(outer + 1),
             out_specs=whole_specs(inner + 4),
             compiler_params=params(),
             cost_estimate=pl.CostEstimate(flops=1, bytes_accessed=1, transcendentals=0),
             name="route",
-        )(*blocks, held[6])
+        )(*blocks, loaded[6])
         in_sends, (pick, gate_hi, gate_lo, gate_col) = routed[:inner], routed[inner:]
 
     def spread(sends):
@@ -420,14 +416,14 @@
 
     def gather_cores(pieces, after=()):
         stack = pl.pallas_call(
-            functools.partial(stack_kernel, inner),
+            functools.partial(stack_kernel, (inner, reach, held)),
             out_shape=shape(rows, width),
             in_specs=whole_specs(inner) + any_specs(len(after)),
             out_specs=pl.BlockSpec(memory_space=pltpu.VMEM),
             compiler_params=params(),
             cost_estimate=pl.CostEstimate(flops=1, bytes_accessed=1, transcendentals=0),
             name="stack",
-        )(*pieces, *after)
+        )(*flipped(pieces), *after)
         return [stack] + [send_core(stack, d, cores) for d in range(1, cores)]
 
     with jax.named_scope("exchange_in"):
@@ -435,7 +431,7 @@
     with jax.named_scope("scale"):
         grad_sends = pl.pallas_call(
             functools.partial(scale_kernel, outer, inner),
-            out_shape=[shape(reach, width)] * inner,
+            out_shape=piece_shapes,
             in_specs=whole_specs(outer + 2),
             out_specs=whole_specs(inner),
             compiler_params=params(),
@@ -458,13 +454,13 @@
             compiler_params=params(),
             cost_estimate=pl.CostEstimate(flops=1, bytes_accessed=1, transcendentals=0),
             name="forward",
-        )(*in_rows, *weights, grad_rows[0])
+        )(*in_rows, *weights, grad_pieces[-1])
 
     def give_back(parts, after=()):
         got = [parts[0]] + [send_core(parts[d], d, cores) for d in range(1, cores)]
         sends = pl.pallas_call(
-            functools.partial(split_kernel, (cores, inner, reach)),
-            out_shape=[shape(reach, width)] * inner,
+            functools.partial(split_kernel, (cores, inner, reach, held)),
+            out_shape=piece_shapes,
             in_specs=whole_specs(cores) + any_specs(len(after)),
             out_specs=whole_specs(inner),
             compiler_params=params(),
@@ -475,15 +471,15 @@
 
     def combine(pieces, tables):
         blocks = pl.pallas_call(
-            functools.partial(combine_kernel, (outer, inner, unit, half), len(tables)),
+            functools.partial(combine_kernel, (outer, inner, unit), len(tables)),
             out_shape=[shape(unit, half)] * outer,
             in_specs=whole_specs(inner + len(tables)),
             out_specs=whole_specs(outer),
             compiler_params=params(),
             cost_estimate=pl.CostEstimate(flops=1, bytes_accessed=1, transcendentals=0),
             name="combine",
-        )(*pieces, *tables)
-        return [blocks[0]] + [send_outer(blocks[s], s, outer, inner, back=True) for s in send_order(outer)]
+        )(*flipped(pieces), *tables)
+        return [blocks[0]] + [send_outer(blocks[s], s, outer, inner, back=True) for s in range(1, outer)]
 
     def finish(blocks, after=()):
         return pl.pallas_call(
@@ -494,7 +490,7 @@
             compiler_params=params(),
             cost_estimate=pl.CostEstimate(flops=1, bytes_accessed=1, transcendentals=0),
             name="final",
-        )(*blocks, *after)
+        )(*flipped(blocks), *after)
 
     with jax.named_scope("return_out"):
         out_back = give_back(out_parts)

time: 61.1 us -> 57.4 us (0.939)
  waiting for transfers between devices: 14 us -> 9.58 us
  starting transfers between devices: 29.8 us -> 30.5 us
    ppermute x12, waiting for transfers between devices: 10 us -> 6.21 us  [send_inner(): return lax.ppermute(x, 'expert', pairs)]
    ppermute x12, starting transfers between devices: 14.4 us -> 15.1 us  [send_inner(): return lax.ppermute(x, 'expert', pairs)]
  transfers between devices with their start and end apart: 25 -> 25, of which waited for: 8 -> 8; matrix products, arithmetic and copies ran while one was open for 0% -> 0% of each run, Pallas kernels for 23% -> 24%
where the time goes in v4:
time: 57.4 us; the launch traced here: 57.2 us
  starting transfers between devices  30.5 us (53%)
  Pallas kernels  16.4 us (29%)
  waiting for transfers between devices  9.58 us (17%)
  between operations  0.79 us (1%)
    ppermute x12, starting transfers between devices, send_inner(): return lax.ppermute(x, 'expert', pairs)  15.1 us
    ppermute x9, starting transfers between devices, send_outer(): return lax.ppermute(x, 'expert', pairs)  14.6 us
    ppermute x12, waiting for transfers between devices, send_inner(): return lax.ppermute(x, 'expert', pairs)  6.21 us
    pallas_call x1, Pallas kernels, on_device(): pl.pallas_call(functools.partial(load_kernel, weight_parts), out_shape=[p...  5.43 us
    ppermute x9, waiting for transfers between devices, send_outer(): return lax.ppermute(x, 'expert', pairs)  3.35 us
    pallas_call x1, Pallas kernels, on_device(): pl.pallas_call(functools.partial(down_kernel, dims, chunks), out_shape=pl...  2.38 us
    pallas_call x1, Pallas kernels, on_device(): pl.pallas_call(functools.partial(forward_kernel, dims), out_shape=[shape(...  1.98 us
    pallas_call x1, Pallas kernels, on_device(): pl.pallas_call(functools.partial(backward_kernel, dims), out_shape=[shape...  1.97 us
  transfers between devices with their start and end apart: 25, of which 8 were waited for; matrix products, arithmetic and copies ran while one was open for 0% of the time, Pallas kernels for 24%

profile of v4, /device:TPU:0, one launch (start us, length us, event | category | flops | bytes accessed | tf_op | source)
XLA Modules:
  0.0 57.2 jit_solution(96783794032263782)
XLA Ops:
  0.6 1.3 %prepare.1.refs_3_.refs_0_ = bf16[24,2176]{1,0:T(8,128)(2,1)S(1)} custom-call(s32[8,12]{1,0:T(8,128)} %bitcast.2, f32[8,12]{1,0:T(8,128)} %bitcast.3, bf16[12,2048]{1,0:T(8,128)(2,1)} %refs_2_.2, bf16[12,2048]{1,0:T(8,128)(2,1)} %refs_3_.1), custom_call_target="tpu_custom_call" | custom-call | flops 1 | bytes 1 | tf_op jit(solution)/shard_map/prepare/prepare/pallas_call | solution.py:363
  1.9 3.1 %collective-permute-start = (bf16[24,2176]{1,0:T(8,128)(2,1)S(1)}, bf16[24,2176]{1,0:T(8,128)(2,1)S(1)}, u32[]{:S(2)}, u32[]{:S(2)}) collective-permute-start(bf16[24,2176]{1,0:T(8,128)(2,1)S(1)} %prepare.1.refs_3_.refs_0_), channel_id=1, source_target_pairs={{0,8},{2,10},{4,12},{6,14},{8,0},{10,2},{12,4},{14,6},{16,24},{18,... | collective-permute-start | bytes 313352 | tf_op jit(solution)/shard_map/gather_blocks/ppermute | solution.py:43
  5.0 2.6 %collective-permute-start.1 = (bf16[24,2176]{1,0:T(8,128)(2,1)S(1)}, bf16[24,2176]{1,0:T(8,128)(2,1)S(1)}, u32[]{:S(2)}, u32[]{:S(2)}) collective-permute-start(bf16[24,2176]{1,0:T(8,128)(2,1)S(1)} %prepare.1.refs_3_.refs_0_), channel_id=1, source_target_pairs={{0,16},{2,18},{4,20},{6,22},{8,24},{10,26},{12,28},{14,30},{16,0},... | collective-permute-start | bytes 313352 | tf_op jit(solution)/shard_map/gather_blocks/ppermute | solution.py:43
  7.6 5.4 %load_weights.1 = (bf16[1,4096,512]{2,1,0:T(8,128)(2,1)S(1)}, bf16[1,4096,512]{2,1,0:T(8,128)(2,1)S(1)}, bf16[1,512,4096]{2,1,0:T(8,128)(2,1)S(1)}, bf16[512,409...) custom-call(bf16[1,4096,512]{2,1,0:T(8,128)(2,1)} %refs_0_.1, ...), custom_call_target="tpu_custom_call" | custom-call | flops 1 | bytes 1 | tf_op jit(solution)/shard_map/load_weights/load_weights/pallas_call | solution.py:388
  13.0 2.8 %collective-permute-done.1.refs_2_ = bf16[24,2176]{1,0:T(8,128)(2,1)S(1)} collective-permute-done((bf16[24,2176]{1,0:T(8,128)(2,1)S(1)}, bf16[24,2176]{1,0:T(8,128)(2,1)S(1)}, u32[]{:S(2)}, u32[]{:S(2)}) %collective-permute-start.1) | collective-permute-done | bytes 104480 | tf_op jit(solution)/shard_map/gather_blocks/ppermute | solution.py:43
  15.9 0.8 %route.1 = (bf16[56,1024]{1,0:T(8,128)(2,1)S(1)}, bf16[56,1024]{1,0:T(8,128)(2,1)S(1)}, bf16[56,1024]{1,0:T(8,128)(2,1)S(1)}, bf16[56,1024]{1,0:T(8,128)(2,1)S(1...) custom-call(bf16[24,2176]{1,0:T(8,128)(2,1)S(1)} %prepare.1.refs_3_., ...), custom_call_target="tpu_custom_call" | custom-call | flops 1 | bytes 1 | tf_op jit(solution)/shard_map/route/route/pallas_call | solution.py:403
  16.6 2.5 %collective-permute-start.3 = (bf16[56,1024]{1,0:T(8,128)(2,1)S(1)}, bf16[56,1024]{1,0:T(8,128)(2,1)S(1)}, u32[]{:S(2)}, u32[]{:S(2)}) collective-permute-start(bf16[56,1024]{1,0:T(8,128)(2,1)S(1)} %get-tuple-element.50), channel_id=1, source_target_pairs={{0,6},{2,4},{4,2},{6,0},{8,14},{10,12},{12,10},{14,8},{16,22},{18,... | collective-permute-start | bytes 344072 | tf_op jit(solution)/shard_map/exchange_in/ppermute | solution.py:51
  19.7 0.5 collective-permute-start.5
  20.5 2.5 %collective-permute-start.7 = (bf16[56,1024]{1,0:T(8,128)(2,1)S(1)}, bf16[56,1024]{1,0:T(8,128)(2,1)S(1)}, u32[]{:S(2)}, u32[]{:S(2)}) collective-permute-start(bf16[56,1024]{1,0:T(8,128)(2,1)S(1)} %get-tuple-element.58), channel_id=1, source_target_pairs={{0,6},{2,4},{4,2},{6,0},{8,14},{10,12},{12,10},{14,8},{16,22},{18,... | collective-permute-start | bytes 344072 | tf_op jit(solution)/shard_map/exchange_grad/ppermute | solution.py:51
  23.7 1.5 %collective-permute-start.16 = (bf16[56,1024]{1,0:T(8,128)(2,1)S(1)}, bf16[56,1024]{1,0:T(8,128)(2,1)S(1)}, u32[]{:S(2)}, u32[]{:S(2)}) collective-permute-start(bf16[56,1024]{1,0:T(8,128)(2,1)S(1)} %get-tuple-element.74), channel_id=1, source_target_pairs={{0,2},{2,0},{4,6},{6,4},{8,10},{10,8},{12,14},{14,12},{16,18},{18,... | collective-permute-start | bytes 344072 | tf_op jit(solution)/shard_map/exchange_grad/ppermute | solution.py:51
  25.2 1.4 %collective-permute-done.4.refs_2_ = bf16[56,1024]{1,0:T(8,128)(2,1)S(1)} collective-permute-done((bf16[56,1024]{1,0:T(8,128)(2,1)S(1)}, bf16[56,1024]{1,0:T(8,128)(2,1)S(1)}, u32[]{:S(2)}, u32[]{:S(2)}) %collective-permute-start.4) | collective-permute-done | bytes 114720 | tf_op jit(solution)/shard_map/exchange_in/ppermute | solution.py:51
  26.7 1.2 %collective-permute-done.7.refs_5_.refs_1_ = bf16[56,1024]{1,0:T(8,128)(2,1)S(1)} collective-permute-done((bf16[56,1024]{1,0:T(8,128)(2,1)S(1)}, bf16[56,1024]{1,0:T(8,128)(2,1)S(1)}, u32[]{:S(2)}, u32[]{:S(2)}) %collective-permute-start.7) | collective-permute-done | bytes 114720 | tf_op jit(solution)/shard_map/exchange_grad/ppermute | solution.py:51
  27.9 1.1 %collective-permute-done.15.refs_2_ = bf16[56,1024]{1,0:T(8,128)(2,1)S(1)} collective-permute-done((bf16[56,1024]{1,0:T(8,128)(2,1)S(1)}, bf16[56,1024]{1,0:T(8,128)(2,1)S(1)}, u32[]{:S(2)}, u32[]{:S(2)}) %collective-permute-start.15) | collective-permute-done | bytes 114720 | tf_op jit(solution)/shard_map/exchange_grad/ppermute | solution.py:51
  29.2 2.0 %forward.1 = (f32[128,512]{1,0:T(8,128)S(1)}, f32[128,512]{1,0:T(8,128)S(1)}, bf16[128,512]{1,0:T(8,128)(2,1)S(1)}, bf16[128,2048]{1,0:T(8,128)(2,1)S(1)}, bf16[128,2048]{1,0:T(8,128)(2,1)S(1)}) custom-call(bf16[128,2048]{1,0:T(8,128)(2,1)S(1)} %stack.2.refs_0_, bf16[128,2048]{1,0:T(8,128)(2,1)S(1)} %collective-permute-done.6.refs_1_, ...), custom_call_target="tpu_custom_call" | custom-call | flops 1 | bytes 1 | tf_op jit(solution)/shard_map/forward/forward/pallas_call | solution.py:449
  31.2 0.5 collective-permute-start.8
  31.8 2.0 %backward.1 = (bf16[128,2048]{1,0:T(8,128)(2,1)S(1)}, bf16[128,2048]{1,0:T(8,128)(2,1)S(1)}) custom-call(bf16[128,2048]{1,0:T(8,128)(2,1)S(1)} %stack.3.refs_0_, bf16[128,2048]{1,0:T(8,128)(2,1)S(1)} %collective-permute-done.17.refs_1_, bf16[512,4096]{1,0:T(8,128)(2,1)S(1)} %get-tuple-element.75.refs_2_, bf16[512,4096]{1,0:T(8,128)(2,1)S(1)} %get-tuple-element.76.refs_3_, ...), custom_call_target="tpu_custom_call" | custom-call | flops 1 | bytes 1 | tf_op jit(solution)/shard_map/backward/backward/pallas_call | solution.py:500
  34.0 1.9 %collective-permute-start.9 = (bf16[56,1024]{1,0:T(8,128)(2,1)S(1)}, bf16[56,1024]{1,0:T(8,128)(2,1)S(1)}, u32[]{:S(2)}, u32[]{:S(2)}) collective-permute-start(bf16[56,1024]{1,0:T(8,128)(2,1)S(1)} %get-tuple-element.62), channel_id=1, source_target_pairs={{0,6},{2,4},{4,2},{6,0},{8,14},{10,12},{12,10},{14,8},{16,22},{18,... | collective-permute-start | bytes 344072 | tf_op jit(solution)/shard_map/return_out/ppermute | solution.py:51
  35.9 0.6 %collective-permute-start.10 = (bf16[56,1024]{1,0:T(8,128)(2,1)S(1)}, bf16[56,1024]{1,0:T(8,128)(2,1)S(1)}, u32[]{:S(2)}, u32[]{:S(2)}) collective-permute-start(bf16[56,1024]{1,0:T(8,128)(2,1)S(1)} %get-tuple-element.63), channel_id=1, source_target_pairs={{0,4},{2,6},{4,0},{6,2},{8,12},{10,14},{12,8},{14,10},{16,20},{18,... | collective-permute-start | bytes 344072 | tf_op jit(solution)/shard_map/return_out/ppermute | solution.py:51
  36.5 1.1 %collective-permute-start.11 = (bf16[56,1024]{1,0:T(8,128)(2,1)S(1)}, bf16[56,1024]{1,0:T(8,128)(2,1)S(1)}, u32[]{:S(2)}, u32[]{:S(2)}) collective-permute-start(bf16[56,1024]{1,0:T(8,128)(2,1)S(1)} %get-tuple-element.64), channel_id=1, source_target_pairs={{0,2},{2,0},{4,6},{6,4},{8,10},{10,8},{12,14},{14,12},{16,18},{18,... | collective-permute-start | bytes 344072 | tf_op jit(solution)/shard_map/return_out/ppermute | solution.py:51
  37.7 1.9 %collective-permute-start.19 = (bf16[56,1024]{1,0:T(8,128)(2,1)S(1)}, bf16[56,1024]{1,0:T(8,128)(2,1)S(1)}, u32[]{:S(2)}, u32[]{:S(2)}) collective-permute-start(bf16[56,1024]{1,0:T(8,128)(2,1)S(1)} %get-tuple-element.83), channel_id=1, source_target_pairs={{0,6},{2,4},{4,2},{6,0},{8,14},{10,12},{12,10},{14,8},{16,22},{18,... | collective-permute-start | bytes 344072 | tf_op jit(solution)/shard_map/return_grad/ppermute | solution.py:51
  39.6 0.6 %collective-permute-start.20 = (bf16[56,1024]{1,0:T(8,128)(2,1)S(1)}, bf16[56,1024]{1,0:T(8,128)(2,1)S(1)}, u32[]{:S(2)}, u32[]{:S(2)}) collective-permute-start(bf16[56,1024]{1,0:T(8,128)(2,1)S(1)} %get-tuple-element.84), channel_id=1, source_target_pairs={{0,4},{2,6},{4,0},{6,2},{8,12},{10,14},{12,8},{14,10},{16,20},{18,... | collective-permute-start | bytes 344072 | tf_op jit(solution)/shard_map/return_grad/ppermute | solution.py:51
  40.2 0.7 %collective-permute-done.9.refs_1_ = bf16[56,1024]{1,0:T(8,128)(2,1)S(1)} collective-permute-done((bf16[56,1024]{1,0:T(8,128)(2,1)S(1)}, bf16[56,1024]{1,0:T(8,128)(2,1)S(1)}, u32[]{:S(2)}, u32[]{:S(2)}) %collective-permute-start.9) | collective-permute-done | bytes 114720 | tf_op jit(solution)/shard_map/return_out/ppermute | solution.py:51
  40.9 1.0 %collective-permute-start.21 = (bf16[56,1024]{1,0:T(8,128)(2,1)S(1)}, bf16[56,1024]{1,0:T(8,128)(2,1)S(1)}, u32[]{:S(2)}, u32[]{:S(2)}) collective-permute-start(bf16[56,1024]{1,0:T(8,128)(2,1)S(1)} %get-tuple-element.85), channel_id=1, source_target_pairs={{0,2},{2,0},{4,6},{6,4},{8,10},{10,8},{12,14},{14,12},{16,18},{18,... | collective-permute-start | bytes 344072 | tf_op jit(solution)/shard_map/return_grad/ppermute | solution.py:51
  41.9 1.6 %collective-permute-done.10.refs_2_ = bf16[56,1024]{1,0:T(8,128)(2,1)S(1)} collective-permute-done((bf16[56,1024]{1,0:T(8,128)(2,1)S(1)}, bf16[56,1024]{1,0:T(8,128)(2,1)S(1)}, u32[]{:S(2)}, u32[]{:S(2)}) %collective-permute-start.10) | collective-permute-done | bytes 114720 | tf_op jit(solution)/shard_map/return_out/ppermute | solution.py:51
  43.8 2.6 %collective-permute-start.12 = (bf16[24,1024]{1,0:T(8,128)(2,1)S(1)}, bf16[24,1024]{1,0:T(8,128)(2,1)S(1)}, u32[]{:S(2)}, u32[]{:S(2)}) collective-permute-start(bf16[24,1024]{1,0:T(8,128)(2,1)S(1)} %get-tuple-element.68), channel_id=1, source_target_pairs={{0,24},{2,26},{4,28},{6,30},{8,16},{10,18},{12,20},{14,22},{16,8},... | collective-permute-start | bytes 147464 | tf_op jit(solution)/shard_map/return_out/ppermute | solution.py:43
  46.4 0.8 %collective-permute-start.13 = (bf16[24,1024]{1,0:T(8,128)(2,1)S(1)}, bf16[24,1024]{1,0:T(8,128)(2,1)S(1)}, u32[]{:S(2)}, u32[]{:S(2)}) collective-permute-start(bf16[24,1024]{1,0:T(8,128)(2,1)S(1)} %get-tuple-element.69), channel_id=1, source_target_pairs={{0,16},{2,18},{4,20},{6,22},{8,24},{10,26},{12,28},{14,30},{16,0},... | collective-permute-start | bytes 147464 | tf_op jit(solution)/shard_map/return_out/ppermute | solution.py:43
  47.2 1.1 %collective-permute-start.14 = (bf16[24,1024]{1,0:T(8,128)(2,1)S(1)}, bf16[24,1024]{1,0:T(8,128)(2,1)S(1)}, u32[]{:S(2)}, u32[]{:S(2)}) collective-permute-start(bf16[24,1024]{1,0:T(8,128)(2,1)S(1)} %get-tuple-element.70), channel_id=1, source_target_pairs={{0,8},{2,10},{4,12},{6,14},{8,0},{10,2},{12,4},{14,6},{16,24},{18,... | collective-permute-start | bytes 147464 | tf_op jit(solution)/shard_map/return_out/ppermute | solution.py:43
  48.5 2.5 %collective-permute-start.22 = (bf16[24,1024]{1,0:T(8,128)(2,1)S(1)}, bf16[24,1024]{1,0:T(8,128)(2,1)S(1)}, u32[]{:S(2)}, u32[]{:S(2)}) collective-permute-start(bf16[24,1024]{1,0:T(8,128)(2,1)S(1)} %get-tuple-element.87), channel_id=1, source_target_pairs={{0,24},{2,26},{4,28},{6,30},{8,16},{10,18},{12,20},{14,22},{16,8},... | collective-permute-start | bytes 147464 | tf_op jit(solution)/shard_map/return_grad/ppermute | solution.py:43
  51.5 1.5 %collective-permute-start.24 = (bf16[24,1024]{1,0:T(8,128)(2,1)S(1)}, bf16[24,1024]{1,0:T(8,128)(2,1)S(1)}, u32[]{:S(2)}, u32[]{:S(2)}) collective-permute-start(bf16[24,1024]{1,0:T(8,128)(2,1)S(1)} %get-tuple-element.89), channel_id=1, source_target_pairs={{0,8},{2,10},{4,12},{6,14},{8,0},{10,2},{12,4},{14,6},{16,24},{18,... | collective-permute-start | bytes 147464 | tf_op jit(solution)/shard_map/return_grad/ppermute | solution.py:43
  53.0 2.4 %down_grad.1 = bf16[1,512,4096]{2,1,0:T(8,128)(2,1)} custom-call(bf16[128,2048]{1,0:T(8,128)(2,1)S(1)} %stack.3.refs_0_, bf16[128,2048]{1,0:T(8,128)(2,1)S(1)} %collective-permute-done.17.refs_1_, bf16[128,512]{1,0:T(8,128)(2,1)S(1)} %get-tuple-element.92.refs_2_, bf16[24,1024]{1,0:T(8,128)(2,1)S(1)} %get-tuple-element.86.refs_0_.refs_3_), custom_call_target="tpu_custom_call" | custom-call | flops 1 | bytes 1 | tf_op jit(solution)/shard_map/down_grad/down_grad/pallas_call | solution.py:515
  55.4 0.7 %final.2 = (bf16[12,2048]{1,0:T(8,128)(2,1)}, f32[8,128]{1,0:T(8,128)S(1)}) custom-call(bf16[24,1024]{1,0:T(8,128)(2,1)S(1)} %get-tuple-element.67.refs_0_, bf16[24,1024]{1,0:T(8,128)(2,1)S(1)} %collective-permute-done.12.refs_1_, bf16[24,1024]{1,0:T(8,128)(2,1)S(1)} %collective-permute-done.13.refs_2_, bf16[24,1024]{1,0:T(8,128)(2,1)S(1)} %collective-permute-done.14.refs_3_), custom_call_target="tpu_custom_call" | custom-call | flops 1 | bytes 1 | tf_op jit(solution)/shard_map/final/pallas_call | solution.py:485
  56.6 0.7 %final.3 = (bf16[12,2048]{1,0:T(8,128)(2,1)}, f32[8,128]{1,0:T(8,128)}) custom-call(bf16[24,1024]{1,0:T(8,128)(2,1)S(1)} %get-tuple-element.86.refs_0_.refs_3_, bf16[24,1024]{1,0:T(8,128)(2,1)S(1)} %collective-permute-done.22.refs_1_, bf16[24,1024]{1,0:T(8,128)(2,1)S(1)} %collective-permute-done.23.refs_2_, ...), custom_call_target="tpu_custom_call" | custom-call | flops 1 | bytes 1 | tf_op jit(solution)/shard_map/final/pallas_call | solution.py:485
  (33 shorter events, 3.7 us)
Async XLA Ops:
  1.9 11.1 %collective-permute-start = (bf16[24,2176]{1,0:T(8,128)(2,1)S(1)}, bf16[24,2176]{1,0:T(8,128)(2,1)S(1)}, u32[]{:S(2)}, u32[]{:S(2)}) collective-permute-start(bf16[24,2176]{1,0:T(8,128)(2,1)S(1)} %prepare.1.refs_3_.refs_0_), channel_id=1, source_target_pairs={{0,8},{2,10},{4,12},{6,14},{8,0},{10,2},{12,4},{14,6},{16,24},{18,... | collective-permute-start | bytes 313352 | tf_op jit(solution)/shard_map/gather_blocks/ppermute | solution.py:43
  5.0 10.9 %collective-permute-start.1 = (bf16[24,2176]{1,0:T(8,128)(2,1)S(1)}, bf16[24,2176]{1,0:T(8,128)(2,1)S(1)}, u32[]{:S(2)}, u32[]{:S(2)}) collective-permute-start(bf16[24,2176]{1,0:T(8,128)(2,1)S(1)} %prepare.1.refs_3_.refs_0_), channel_id=1, source_target_pairs={{0,16},{2,18},{4,20},{6,22},{8,24},{10,26},{12,28},{14,30},{16,0},... | collective-permute-start | bytes 313352 | tf_op jit(solution)/shard_map/gather_blocks/ppermute | solution.py:43
  7.6 8.3 %collective-permute-start.2 = (bf16[24,2176]{1,0:T(8,128)(2,1)S(1)}, bf16[24,2176]{1,0:T(8,128)(2,1)S(1)}, u32[]{:S(2)}, u32[]{:S(2)}) collective-permute-start(bf16[24,2176]{1,0:T(8,128)(2,1)S(1)} %prepare.1.refs_3_.refs_0_), channel_id=1, source_target_pairs={{0,24},{2,26},{4,28},{6,30},{8,16},{10,18},{12,20},{14,22},{16,8},... | collective-permute-start | bytes 313352 | tf_op jit(solution)/shard_map/gather_blocks/ppermute | solution.py:43
  16.6 7.0 %collective-permute-start.3 = (bf16[56,1024]{1,0:T(8,128)(2,1)S(1)}, bf16[56,1024]{1,0:T(8,128)(2,1)S(1)}, u32[]{:S(2)}, u32[]{:S(2)}) collective-permute-start(bf16[56,1024]{1,0:T(8,128)(2,1)S(1)} %get-tuple-element.50), channel_id=1, source_target_pairs={{0,6},{2,4},{4,2},{6,0},{8,14},{10,12},{12,10},{14,8},{16,22},{18,... | collective-permute-start | bytes 344072 | tf_op jit(solution)/shard_map/exchange_in/ppermute | solution.py:51
  19.2 7.4 %collective-permute-start.4 = (bf16[56,1024]{1,0:T(8,128)(2,1)S(1)}, bf16[56,1024]{1,0:T(8,128)(2,1)S(1)}, u32[]{:S(2)}, u32[]{:S(2)}) collective-permute-start(bf16[56,1024]{1,0:T(8,128)(2,1)S(1)} %get-tuple-element.51), channel_id=1, source_target_pairs={{0,4},{2,6},{4,0},{6,2},{8,12},{10,14},{12,8},{14,10},{16,20},{18,... | collective-permute-start | bytes 344072 | tf_op jit(solution)/shard_map/exchange_in/ppermute | solution.py:51
  19.7 6.9 %collective-permute-start.5 = (bf16[56,1024]{1,0:T(8,128)(2,1)S(1)}, bf16[56,1024]{1,0:T(8,128)(2,1)S(1)}, u32[]{:S(2)}, u32[]{:S(2)}) collective-permute-start(bf16[56,1024]{1,0:T(8,128)(2,1)S(1)} %get-tuple-element.52), channel_id=1, source_target_pairs={{0,2},{2,0},{4,6},{6,4},{8,10},{10,8},{12,14},{14,12},{16,18},{18,... | collective-permute-start | bytes 344072 | tf_op jit(solution)/shard_map/exchange_in/ppermute | solution.py:51
  20.5 7.4 %collective-permute-start.7 = (bf16[56,1024]{1,0:T(8,128)(2,1)S(1)}, bf16[56,1024]{1,0:T(8,128)(2,1)S(1)}, u32[]{:S(2)}, u32[]{:S(2)}) collective-permute-start(bf16[56,1024]{1,0:T(8,128)(2,1)S(1)} %get-tuple-element.58), channel_id=1, source_target_pairs={{0,6},{2,4},{4,2},{6,0},{8,14},{10,12},{12,10},{14,8},{16,22},{18,... | collective-permute-start | bytes 344072 | tf_op jit(solution)/shard_map/exchange_grad/ppermute | solution.py:51
  23.0 6.0 %collective-permute-start.15 = (bf16[56,1024]{1,0:T(8,128)(2,1)S(1)}, bf16[56,1024]{1,0:T(8,128)(2,1)S(1)}, u32[]{:S(2)}, u32[]{:S(2)}) collective-permute-start(bf16[56,1024]{1,0:T(8,128)(2,1)S(1)} %get-tuple-element.73), channel_id=1, source_target_pairs={{0,4},{2,6},{4,0},{6,2},{8,12},{10,14},{12,8},{14,10},{16,20},{18,... | collective-permute-start | bytes 344072 | tf_op jit(solution)/shard_map/exchange_grad/ppermute | solution.py:51
  23.7 5.4 %collective-permute-start.16 = (bf16[56,1024]{1,0:T(8,128)(2,1)S(1)}, bf16[56,1024]{1,0:T(8,128)(2,1)S(1)}, u32[]{:S(2)}, u32[]{:S(2)}) collective-permute-start(bf16[56,1024]{1,0:T(8,128)(2,1)S(1)} %get-tuple-element.74), channel_id=1, source_target_pairs={{0,2},{2,0},{4,6},{6,4},{8,10},{10,8},{12,14},{14,12},{16,18},{18,... | collective-permute-start | bytes 344072 | tf_op jit(solution)/shard_map/exchange_grad/ppermute | solution.py:51
  26.7 2.5 %collective-permute-start.6 = (bf16[128,2048]{1,0:T(8,128)(2,1)S(1)}, bf16[128,2048]{1,0:T(8,128)(2,1)S(1)}, u32[]{:S(2)}, u32[]{:S(2)}) collective-permute-start(bf16[128,2048]{1,0:T(8,128)(2,1)S(1)} %stack.2.refs_0_), channel_id=1, source_target_pairs={{0,1},{1,0},{2,3},{3,2},{4,5},{5,4},{6,7},{7,6},{8,9},{9,8},{10,11... | collective-permute-start | bytes 1572872 | tf_op jit(solution)/shard_map/gather_in/ppermute | solution.py:56
  29.1 2.6 %collective-permute-start.17 = (bf16[128,2048]{1,0:T(8,128)(2,1)S(1)}, bf16[128,2048]{1,0:T(8,128)(2,1)S(1)}, u32[]{:S(2)}, u32[]{:S(2)}) collective-permute-start(bf16[128,2048]{1,0:T(8,128)(2,1)S(1)} %stack.3.refs_0_), channel_id=1, source_target_pairs={{0,1},{1,0},{2,3},{3,2},{4,5},{5,4},{6,7},{7,6},{8,9},{9,8},{10,11... | collective-permute-start | bytes 1572872 | tf_op jit(solution)/shard_map/gather_in/ppermute | solution.py:56
  31.2 2.6 %collective-permute-start.8 = (bf16[128,2048]{1,0:T(8,128)(2,1)S(1)}, bf16[128,2048]{1,0:T(8,128)(2,1)S(1)}, u32[]{:S(2)}, u32[]{:S(2)}) collective-permute-start(bf16[128,2048]{1,0:T(8,128)(2,1)S(1)} %get-tuple-element.60), channel_id=1, source_target_pairs={{0,1},{1,0},{2,3},{3,2},{4,5},{5,4},{6,7},{7,6},{8,9},{9,8},{10,11... | collective-permute-start | bytes 1572872 | tf_op jit(solution)/shard_map/return_out/ppermute | solution.py:56
  33.7 3.8 %collective-permute-start.18 = (bf16[128,2048]{1,0:T(8,128)(2,1)S(1)}, bf16[128,2048]{1,0:T(8,128)(2,1)S(1)}, u32[]{:S(2)}, u32[]{:S(2)}) collective-permute-start(bf16[128,2048]{1,0:T(8,128)(2,1)S(1)} %get-tuple-element.81), channel_id=1, source_target_pairs={{0,1},{1,0},{2,3},{3,2},{4,5},{5,4},{6,7},{7,6},{8,9},{9,8},{10,11... | collective-permute-start | bytes 1572872 | tf_op jit(solution)/shard_map/return_grad/ppermute | solution.py:56
  34.0 6.9 %collective-permute-start.9 = (bf16[56,1024]{1,0:T(8,128)(2,1)S(1)}, bf16[56,1024]{1,0:T(8,128)(2,1)S(1)}, u32[]{:S(2)}, u32[]{:S(2)}) collective-permute-start(bf16[56,1024]{1,0:T(8,128)(2,1)S(1)} %get-tuple-element.62), channel_id=1, source_target_pairs={{0,6},{2,4},{4,2},{6,0},{8,14},{10,12},{12,10},{14,8},{16,22},{18,... | collective-permute-start | bytes 344072 | tf_op jit(solution)/shard_map/return_out/ppermute | solution.py:51
  35.9 7.6 %collective-permute-start.10 = (bf16[56,1024]{1,0:T(8,128)(2,1)S(1)}, bf16[56,1024]{1,0:T(8,128)(2,1)S(1)}, u32[]{:S(2)}, u32[]{:S(2)}) collective-permute-start(bf16[56,1024]{1,0:T(8,128)(2,1)S(1)} %get-tuple-element.63), channel_id=1, source_target_pairs={{0,4},{2,6},{4,0},{6,2},{8,12},{10,14},{12,8},{14,10},{16,20},{18,... | collective-permute-start | bytes 344072 | tf_op jit(solution)/shard_map/return_out/ppermute | solution.py:51
  36.5 7.1 %collective-permute-start.11 = (bf16[56,1024]{1,0:T(8,128)(2,1)S(1)}, bf16[56,1024]{1,0:T(8,128)(2,1)S(1)}, u32[]{:S(2)}, u32[]{:S(2)}) collective-permute-start(bf16[56,1024]{1,0:T(8,128)(2,1)S(1)} %get-tuple-element.64), channel_id=1, source_target_pairs={{0,2},{2,0},{4,6},{6,4},{8,10},{10,8},{12,14},{14,12},{16,18},{18,... | collective-permute-start | bytes 344072 | tf_op jit(solution)/shard_map/return_out/ppermute | solution.py:51
  37.7 9.5 %collective-permute-start.19 = (bf16[56,1024]{1,0:T(8,128)(2,1)S(1)}, bf16[56,1024]{1,0:T(8,128)(2,1)S(1)}, u32[]{:S(2)}, u32[]{:S(2)}) collective-permute-start(bf16[56,1024]{1,0:T(8,128)(2,1)S(1)} %get-tuple-element.83), channel_id=1, source_target_pairs={{0,6},{2,4},{4,2},{6,0},{8,14},{10,12},{12,10},{14,8},{16,22},{18,... | collective-permute-start | bytes 344072 | tf_op jit(solution)/shard_map/return_grad/ppermute | solution.py:51
  39.6 8.7 %collective-permute-start.20 = (bf16[56,1024]{1,0:T(8,128)(2,1)S(1)}, bf16[56,1024]{1,0:T(8,128)(2,1)S(1)}, u32[]{:S(2)}, u32[]{:S(2)}) collective-permute-start(bf16[56,1024]{1,0:T(8,128)(2,1)S(1)} %get-tuple-element.84), channel_id=1, source_target_pairs={{0,4},{2,6},{4,0},{6,2},{8,12},{10,14},{12,8},{14,10},{16,20},{18,... | collective-permute-start | bytes 344072 | tf_op jit(solution)/shard_map/return_grad/ppermute | solution.py:51
  40.9 7.4 %collective-permute-start.21 = (bf16[56,1024]{1,0:T(8,128)(2,1)S(1)}, bf16[56,1024]{1,0:T(8,128)(2,1)S(1)}, u32[]{:S(2)}, u32[]{:S(2)}) collective-permute-start(bf16[56,1024]{1,0:T(8,128)(2,1)S(1)} %get-tuple-element.85), channel_id=1, source_target_pairs={{0,2},{2,0},{4,6},{6,4},{8,10},{10,8},{12,14},{14,12},{16,18},{18,... | collective-permute-start | bytes 344072 | tf_op jit(solution)/shard_map/return_grad/ppermute | solution.py:51
  43.8 7.7 %collective-permute-start.12 = (bf16[24,1024]{1,0:T(8,128)(2,1)S(1)}, bf16[24,1024]{1,0:T(8,128)(2,1)S(1)}, u32[]{:S(2)}, u32[]{:S(2)}) collective-permute-start(bf16[24,1024]{1,0:T(8,128)(2,1)S(1)} %get-tuple-element.68), channel_id=1, source_target_pairs={{0,24},{2,26},{4,28},{6,30},{8,16},{10,18},{12,20},{14,22},{16,8},... | collective-permute-start | bytes 147464 | tf_op jit(solution)/shard_map/return_out/ppermute | solution.py:43
  46.4 9.0 %collective-permute-start.13 = (bf16[24,1024]{1,0:T(8,128)(2,1)S(1)}, bf16[24,1024]{1,0:T(8,128)(2,1)S(1)}, u32[]{:S(2)}, u32[]{:S(2)}) collective-permute-start(bf16[24,1024]{1,0:T(8,128)(2,1)S(1)} %get-tuple-element.69), channel_id=1, source_target_pairs={{0,16},{2,18},{4,20},{6,22},{8,24},{10,26},{12,28},{14,30},{16,0},... | collective-permute-start | bytes 147464 | tf_op jit(solution)/shard_map/return_out/ppermute | solution.py:43
  47.2 8.2 %collective-permute-start.14 = (bf16[24,1024]{1,0:T(8,128)(2,1)S(1)}, bf16[24,1024]{1,0:T(8,128)(2,1)S(1)}, u32[]{:S(2)}, u32[]{:S(2)}) collective-permute-start(bf16[24,1024]{1,0:T(8,128)(2,1)S(1)} %get-tuple-element.70), channel_id=1, source_target_pairs={{0,8},{2,10},{4,12},{6,14},{8,0},{10,2},{12,4},{14,6},{16,24},{18,... | collective-permute-start | bytes 147464 | tf_op jit(solution)/shard_map/return_out/ppermute | solution.py:43
  48.5 7.5 %collective-permute-start.22 = (bf16[24,1024]{1,0:T(8,128)(2,1)S(1)}, bf16[24,1024]{1,0:T(8,128)(2,1)S(1)}, u32[]{:S(2)}, u32[]{:S(2)}) collective-permute-start(bf16[24,1024]{1,0:T(8,128)(2,1)S(1)} %get-tuple-element.87), channel_id=1, source_target_pairs={{0,24},{2,26},{4,28},{6,30},{8,16},{10,18},{12,20},{14,22},{16,8},... | collective-permute-start | bytes 147464 | tf_op jit(solution)/shard_map/return_grad/ppermute | solution.py:43
  51.1 5.5 %collective-permute-start.23 = (bf16[24,1024]{1,0:T(8,128)(2,1)S(1)}, bf16[24,1024]{1,0:T(8,128)(2,1)S(1)}, u32[]{:S(2)}, u32[]{:S(2)}) collective-permute-start(bf16[24,1024]{1,0:T(8,128)(2,1)S(1)} %get-tuple-element.88), channel_id=1, source_target_pairs={{0,16},{2,18},{4,20},{6,22},{8,24},{10,26},{12,28},{14,30},{16,0},... | collective-permute-start | bytes 147464 | tf_op jit(solution)/shard_map/return_grad/ppermute | solution.py:43
  51.5 5.0 %collective-permute-start.24 = (bf16[24,1024]{1,0:T(8,128)(2,1)S(1)}, bf16[24,1024]{1,0:T(8,128)(2,1)S(1)}, u32[]{:S(2)}, u32[]{:S(2)}) collective-permute-start(bf16[24,1024]{1,0:T(8,128)(2,1)S(1)} %get-tuple-element.89), channel_id=1, source_target_pairs={{0,8},{2,10},{4,12},{6,14},{8,0},{10,2},{12,4},{14,6},{16,24},{18,... | collective-permute-start | bytes 147464 | tf_op jit(solution)/shard_map/return_grad/ppermute | solution.py:43

commit v5 on v4

--- a/solution.py
+++ b/solution.py
@@ -132,58 +132,47 @@
     return value
 
 
-def route_kernel(dims, *refs):
-    outer, inner, tokens, top, cap, reach, half = dims
-    blocks = refs[:outer]
-    sends = refs[outer + 1 : outer + 1 + inner]
-    pick_ref, gate_hi_ref, gate_mid_ref, gate_col_ref = refs[outer + 1 + inner :]
-    rows = outer * 2 * tokens
+def slot_lanes(dims):
+    outer, inner, tokens, top, cap, reach = dims
     fold = 2 * reach
-    slots = inner * fold
+    shape = (outer * 2 * tokens, inner * fold)
     me = lax.axis_index("expert")
     my_inner = lax.rem(me, inner)
     my_base = me - my_inner
-    meta = jnp.concatenate([r[:, 2 * half :].astype(F32) for r in blocks], axis=0)
-    lane = lax.broadcasted_iota(jnp.int32, (rows, slots), 1)
-    row = lax.broadcasted_iota(jnp.int32, (rows, slots), 0)
-    step = count_above(lane, fold, slots)
-    dest = jnp.zeros((rows, slots), F32)
+    lane = lax.broadcasted_iota(jnp.int32, shape, 1)
+    step = count_above(lane, fold, shape[1])
+    dest = jnp.zeros(shape, F32)
     for q in range(inner):
         expert = (my_base + traced_partner(my_inner, q, inner)).astype(F32)
         dest = jnp.where(step == q, expert, dest)
-    slot = lane - step * fold
+    return lane - step * fold, dest
+
+
+def route_kernel(dims, *refs):
+    outer, inner, tokens, top, cap, reach = dims
+    blocks = refs[:outer]
+    sends = refs[outer + 1 : outer + 1 + inner]
+    pick_ref = refs[outer + 1 + inner]
+    half = sends[0].shape[1]
+    rows = outer * 2 * tokens
+    slot, dest = slot_lanes(dims)
     side = (slot >= reach).astype(jnp.int32)
     slot = slot - side * reach
-    named = jnp.zeros((rows, slots), F32)
-    gate = jnp.zeros((rows, slots), F32)
+    meta = jnp.concatenate([r[:, 2 * half :].astype(F32) for r in blocks], axis=0)
+    named = jnp.zeros(dest.shape, F32)
     for k in range(top):
-        hit = meta[:, k : k + 1] == dest
-        value = (
-            meta[:, top + k : top + k + 1]
-            + meta[:, 2 * top + k : 2 * top + k + 1]
-            + meta[:, 3 * top + k : 3 * top + k + 1]
-        )
-        named = named + hit.astype(F32)
-        gate = gate + jnp.where(hit, value, 0.0)
+        named = jnp.where(meta[:, k : k + 1] == dest, 1.0, named)
     left = lax.broadcasted_iota(jnp.int32, (rows, rows), 1)
     down = lax.broadcasted_iota(jnp.int32, (rows, rows), 0)
     same = count_above(left, tokens, rows) == count_above(down, tokens, rows)
     before = (same & (left < down)).astype(F32).astype(BF16)
     rank = jnp.dot(before, named.astype(BF16), preferred_element_type=F32)
-    position = count_above(row, 2 * tokens, rows) * cap + rank.astype(jnp.int32)
-    row_side = count_above(row, tokens, rows) - 2 * count_above(row, 2 * tokens, rows)
+    row = lax.broadcasted_iota(jnp.int32, (rows, 1), 0)
+    block = count_above(row, 2 * tokens, rows)
+    row_side = count_above(row, tokens, rows) - 2 * block
+    position = block * cap + rank.astype(jnp.int32)
     pick = jnp.where((position == slot) & (row_side == side), named, 0.0)
-    gate = pick * gate
-    gate_hi = gate.astype(BF16)
-    rest = gate - gate_hi.astype(F32)
-    gate_mid = rest.astype(BF16)
-    gate_lo = (rest - gate_mid.astype(F32)).astype(BF16)
     pick_ref[...] = pick.astype(BF16)
-    gate_hi_ref[...] = gate_hi
-    gate_mid_ref[...] = gate_mid
-    ones = jnp.ones((rows, META), BF16)
-    column = contract(gate_hi, ones, 0, 0) + contract(gate_mid, ones, 0, 0) + contract(gate_lo, ones, 0, 0)
-    gate_col_ref[...] = column
     select_rows(blocks, 0, pick_ref, None, sends)
 
 
@@ -196,9 +185,28 @@
         send[...] = out[q * fold : (q + 1) * fold].astype(BF16)
 
 
-def scale_kernel(outer, inner, *refs):
-    pick_ref, gate_col_ref = refs[outer : outer + 2]
-    select_rows(refs[:outer], 1, pick_ref, gate_col_ref[:, :1], refs[-inner:])
+def scale_kernel(dims, *refs):
+    outer, inner, tokens, top, cap, reach = dims
+    blocks = refs[:outer]
+    pick_ref = refs[outer]
+    gate_hi_ref, gate_mid_ref, *sends = refs[outer + 1 :]
+    half = sends[0].shape[1]
+    _, dest = slot_lanes(dims)
+    meta = jnp.concatenate([r[:, 2 * half :].astype(F32) for r in blocks], axis=0)
+    gate = jnp.zeros(dest.shape, F32)
+    for k in range(top):
+        value = sum(meta[:, n * top + k : n * top + k + 1] for n in range(1, 4))
+        gate = jnp.where(meta[:, k : k + 1] == dest, value, gate)
+    gate = pick_ref[...].astype(F32) * gate
+    gate_hi = gate.astype(BF16)
+    rest = gate - gate_hi.astype(F32)
+    gate_mid = rest.astype(BF16)
+    gate_lo = (rest - gate_mid.astype(F32)).astype(BF16)
+    gate_hi_ref[...] = gate_hi
+    gate_mid_ref[...] = gate_mid
+    ones = jnp.ones((dest.shape[0], META), BF16)
+    column = contract(gate_hi, ones, 0, 0) + contract(gate_mid, ones, 0, 0) + contract(gate_lo, ones, 0, 0)
+    select_rows(blocks, 1, pick_ref, column[:, :1], sends)
 
 
 def stack_kernel(dims, *refs):
@@ -235,20 +243,25 @@
     return [pl.ds(pl.multiple_of(move(core, d, cores) * width, width), width) for d in range(cores)]
 
 
+def forward_own_kernel(dims, *refs):
+    rows, gate_w, up_w, gate_ref, up_ref, _ = refs
+    span = core_spans(*dims, traced_origin)[0]
+    gate_ref[...] = jnp.dot(rows[...], gate_w[0, span, :], preferred_element_type=F32)
+    up_ref[...] = jnp.dot(rows[...], up_w[0, span, :], preferred_element_type=F32)
+
+
 def forward_kernel(dims, *refs):
     cores, width = dims
-    pieces = refs[:cores]
-    gate_w, up_w, down_w = refs[cores : cores + 3]
+    gate_own, up_own, *pieces = refs[: cores + 1]
+    gate_w, up_w, down_w = refs[cores + 1 : cores + 4]
     gate_ref, up_ref, act_ref, *parts = refs[-(3 + cores) :]
     spans = core_spans(cores, width, traced_origin)
-    gate_pre = None
-    up_pre = None
-    for d in range(cores):
-        rows = pieces[d][...]
-        term = jnp.dot(rows, gate_w[0, spans[d], :], preferred_element_type=F32)
-        gate_pre = term if gate_pre is None else gate_pre + term
-        term = jnp.dot(rows, up_w[0, spans[d], :], preferred_element_type=F32)
-        up_pre = term if up_pre is None else up_pre + term
+    gate_pre = gate_own[...]
+    up_pre = up_own[...]
+    for piece, span in zip(pieces, spans[1:]):
+        rows = piece[...]
+        gate_pre = gate_pre + jnp.dot(rows, gate_w[0, span, :], preferred_element_type=F32)
+        up_pre = up_pre + jnp.dot(rows, up_w[0, span, :], preferred_element_type=F32)
     act = (gate_pre * jax.nn.sigmoid(gate_pre) * up_pre).astype(BF16)
     gate_ref[...] = gate_pre
     up_ref[...] = up_pre
@@ -258,26 +271,39 @@
         parts[d][...] = jnp.dot(act, down_w[0, :, spans[d]], preferred_element_type=F32).astype(BF16)
 
 
+def backward_own_kernel(dims, rows, down_t, out_ref):
+    span = core_spans(*dims, traced_origin)[0]
+    out_ref[...] = jnp.dot(rows[...], down_t[span, :], preferred_element_type=F32)
+
+
 def backward_kernel(dims, *refs):
     cores, width = dims
-    pieces = refs[:cores]
+    act_own, *pieces = refs[:cores]
     gate_t, up_t, down_t, gate_ref, up_ref = refs[cores : cores + 5]
-    parts = refs[-cores:]
+    gate_out, up_out, *parts = refs[cores + 5 :]
     spans = core_spans(cores, width, traced_origin)
-    act_grad = None
-    for d in range(cores):
-        rows = pieces[d][...]
-        term = jnp.dot(rows, down_t[spans[d], :], preferred_element_type=F32)
-        act_grad = term if act_grad is None else act_grad + term
+    act_grad = act_own[...]
+    for piece, span in zip(pieces, spans[1:]):
+        act_grad = act_grad + jnp.dot(piece[...], down_t[span, :], preferred_element_type=F32)
     gate_pre = gate_ref[...]
     sigmoid = jax.nn.sigmoid(gate_pre)
     gate_grad = (act_grad * up_ref[...] * sigmoid * (1.0 + gate_pre * (1.0 - sigmoid))).astype(BF16)
     up_grad = (act_grad * (gate_pre * sigmoid)).astype(BF16)
+    gate_out[...] = gate_grad
+    up_out[...] = up_grad
     spans = core_spans(cores, width, traced_partner)
-    for d in reversed(range(cores)):
-        part = jnp.dot(gate_grad, gate_t[:, spans[d]], preferred_element_type=F32)
-        part = part + jnp.dot(up_grad, up_t[:, spans[d]], preferred_element_type=F32)
-        parts[d][...] = part.astype(BF16)
+    for part, span in zip(parts, spans[1:]):
+        value = jnp.dot(gate_grad, gate_t[:, span], preferred_element_type=F32)
+        value = value + jnp.dot(up_grad, up_t[:, span], preferred_element_type=F32)
+        part[...] = value.astype(BF16)
+
+
+def input_own_kernel(dims, *refs):
+    gate_grad, up_grad, gate_t, up_t = refs[:4]
+    span = core_spans(*dims, traced_partner)[0]
+    value = jnp.dot(gate_grad[...], gate_t[:, span], preferred_element_type=F32)
+    value = value + jnp.dot(up_grad[...], up_t[:, span], preferred_element_type=F32)
+    refs[-1][...] = value.astype(BF16)
 
 
 def down_kernel(dims, chunks, *refs):
@@ -373,7 +399,6 @@
                 pltpu.SemaphoreType.DMA((4,)),
             ],
             compiler_params=params(),
-            cost_estimate=pl.CostEstimate(flops=1, bytes_accessed=1, transcendentals=0),
             name="prepare",
         )(in_hbm(expert_ids.T), in_hbm(gate_weights.T), in_hbm(hidden_in), in_hbm(out_grad))
 
@@ -394,22 +419,20 @@
             out_specs=whole_specs(7),
             scratch_shapes=[pltpu.SemaphoreType.DMA((3 * weight_parts,))],
             compiler_params=params(),
-            cost_estimate=pl.CostEstimate(flops=1, bytes_accessed=1, transcendentals=0),
             name="load_weights",
         )(*[in_hbm(w) for w in weights], packed)
         weights, turned = loaded[:3], loaded[3:6]
 
     with jax.named_scope("route"):
-        routed = pl.pallas_call(
-            functools.partial(route_kernel, (outer, inner, tokens, top, cap, reach, half)),
-            out_shape=piece_shapes + [table_shape] * 3 + [shape(inner * 2 * reach, META, F32)],
+        dims = (outer, inner, tokens, top, cap, reach)
+        *in_sends, pick = pl.pallas_call(
+            functools.partial(route_kernel, dims),
+            out_shape=piece_shapes + [table_shape],
             in_specs=whole_specs(outer + 1),
-            out_specs=whole_specs(inner + 4),
-            compiler_params=params(),
-            cost_estimate=pl.CostEstimate(flops=1, bytes_accessed=1, transcendentals=0),
+            out_specs=whole_specs(inner + 1),
+            compiler_params=params(),
             name="route",
         )(*blocks, loaded[6])
-        in_sends, (pick, gate_hi, gate_lo, gate_col) = routed[:inner], routed[inner:]
 
     def spread(sends):
         return [sends[0]] + [send_inner(sends[q], q, outer, inner) for q in range(1, inner)]
@@ -421,7 +444,6 @@
             in_specs=whole_specs(inner) + any_specs(len(after)),
             out_specs=pl.BlockSpec(memory_space=pltpu.VMEM),
             compiler_params=params(),
-            cost_estimate=pl.CostEstimate(flops=1, bytes_accessed=1, transcendentals=0),
             name="stack",
         )(*flipped(pieces), *after)
         return [stack] + [send_core(stack, d, cores) for d in range(1, cores)]
@@ -429,32 +451,39 @@
     with jax.named_scope("exchange_in"):
         in_pieces = spread(in_sends)
     with jax.named_scope("scale"):
-        grad_sends = pl.pallas_call(
-            functools.partial(scale_kernel, outer, inner),
-            out_shape=piece_shapes,
-            in_specs=whole_specs(outer + 2),
-            out_specs=whole_specs(inner),
-            compiler_params=params(),
-            cost_estimate=pl.CostEstimate(flops=1, bytes_accessed=1, transcendentals=0),
+        gate_hi, gate_lo, *grad_sends = pl.pallas_call(
+            functools.partial(scale_kernel, dims),
+            out_shape=[table_shape] * 2 + piece_shapes,
+            in_specs=whole_specs(outer + 1),
+            out_specs=whole_specs(inner + 2),
+            compiler_params=params(),
             name="scale",
-        )(*blocks, pick, gate_col)
+        )(*blocks, pick)
     with jax.named_scope("exchange_grad"):
         grad_pieces = spread(grad_sends)
     with jax.named_scope("gather_in"):
         in_rows = gather_cores(in_pieces)
-        grad_rows = gather_cores(grad_pieces)
+        with jax.named_scope("forward_own"):
+            gate_own, up_own, started = pl.pallas_call(
+                functools.partial(forward_own_kernel, (cores, width)),
+                out_shape=[shape(rows, hidden, F32)] * 2 + [shape(8, META, F32)],
+                in_specs=whole_specs(3),
+                out_specs=whole_specs(3),
+                compiler_params=params(),
+                name="forward_own",
+            )(in_rows[0], *weights[:2])
+        grad_rows = gather_cores(grad_pieces, (started,))
 
     dims = (cores, width)
     with jax.named_scope("forward"):
         gate_pre, up_pre, act, *out_parts = pl.pallas_call(
             functools.partial(forward_kernel, dims),
             out_shape=[shape(rows, hidden, F32)] * 2 + [shape(rows, hidden)] + [shape(rows, width)] * cores,
-            in_specs=whole_specs(cores + 3) + any_specs(1),
+            in_specs=whole_specs(cores + 4) + any_specs(1),
             out_specs=whole_specs(3 + cores),
             compiler_params=params(),
-            cost_estimate=pl.CostEstimate(flops=1, bytes_accessed=1, transcendentals=0),
             name="forward",
-        )(*in_rows, *weights, grad_pieces[-1])
+        )(gate_own, up_own, *in_rows[1:], *weights, grad_pieces[-1])
 
     def give_back(parts, after=()):
         got = [parts[0]] + [send_core(parts[d], d, cores) for d in range(1, cores)]
@@ -464,7 +493,6 @@
             in_specs=whole_specs(cores) + any_specs(len(after)),
             out_specs=whole_specs(inner),
             compiler_params=params(),
-            cost_estimate=pl.CostEstimate(flops=1, bytes_accessed=1, transcendentals=0),
             name="split",
         )(*got, *after)
         return [sends[0]] + [send_inner(sends[q], q, outer, inner, back=True) for q in range(1, inner)]
@@ -476,7 +504,6 @@
             in_specs=whole_specs(inner + len(tables)),
             out_specs=whole_specs(outer),
             compiler_params=params(),
-            cost_estimate=pl.CostEstimate(flops=1, bytes_accessed=1, transcendentals=0),
             name="combine",
         )(*flipped(pieces), *tables)
         return [blocks[0]] + [send_outer(blocks[s], s, outer, inner, back=True) for s in range(1, outer)]
@@ -488,7 +515,6 @@
             in_specs=whole_specs(outer + len(after)),
             out_specs=whole_specs(2),
             compiler_params=params(),
-            cost_estimate=pl.CostEstimate(flops=1, bytes_accessed=1, transcendentals=0),
             name="final",
         )(*flipped(blocks), *after)
 
@@ -497,15 +523,32 @@
         out_blocks = combine(out_back, (gate_hi, gate_lo))
 
     with jax.named_scope("backward"):
-        grad_parts = pl.pallas_call(
+        gate_t, up_t, down_t = turned
+        act_own = pl.pallas_call(
+            functools.partial(backward_own_kernel, dims),
+            out_shape=shape(rows, hidden, F32),
+            in_specs=whole_specs(2),
+            out_specs=pl.BlockSpec(memory_space=pltpu.VMEM),
+            compiler_params=params(),
+            name="backward_own",
+        )(grad_rows[0], down_t)
+        gate_grad, up_grad, *grad_parts = pl.pallas_call(
             functools.partial(backward_kernel, dims),
-            out_shape=[shape(rows, width)] * cores,
+            out_shape=[shape(rows, hidden)] * 2 + [shape(rows, width)] * (cores - 1),
             in_specs=whole_specs(cores + 5),
-            out_specs=whole_specs(cores),
-            compiler_params=params(),
-            cost_estimate=pl.CostEstimate(flops=1, bytes_accessed=1, transcendentals=0),
+            out_specs=whole_specs(cores + 1),
+            compiler_params=params(),
             name="backward",
-        )(*grad_rows, *turned, gate_pre, up_pre)
+        )(act_own, *grad_rows[1:], gate_t, up_t, down_t, gate_pre, up_pre)
+        own_part = pl.pallas_call(
+            functools.partial(input_own_kernel, dims),
+            out_shape=shape(rows, width),
+            in_specs=whole_specs(4) + any_specs(1),
+            out_specs=pl.BlockSpec(memory_space=pltpu.VMEM),
+            compiler_params=params(),
+            name="input_own",
+        )(gate_grad, up_grad, gate_t, up_t, out_back[0])
+        grad_parts = [own_part, *grad_parts]
 
     with jax.named_scope("return_grad"):
         back_blocks = combine(give_back(grad_parts, out_back[:1]), (pick,))
@@ -522,7 +565,6 @@
                 pltpu.SemaphoreType.DMA((cores * chunks,)),
             ],
             compiler_params=params(),
-            cost_estimate=pl.CostEstimate(flops=1, bytes_accessed=1, transcendentals=0),
             name="down_grad",
         )(*grad_rows, act, back_blocks[0])
 

time: 57.4 us -> 56.3 us (0.981)
  waiting for transfers between devices: 9.58 us -> 7.97 us
  Pallas kernels: 16.4 us -> 17.2 us
    pallas_call x2 -> x5, Pallas kernels: 1.07 us -> 3.21 us  [the longest x1 0.74 us: on_device(): pl.pallas_call(functools.partial(input_own_kernel, dims), out_shape=shape...]
    ppermute x12, waiting for transfers between devices: 6.21 us -> 4.56 us  [send_inner(): return lax.ppermute(x, 'expert', pairs)]
    pallas_call x1, Pallas kernels: 1.97 us -> 1.17 us  [on_device(): pl.pallas_call(functools.partial(backward_kernel, dims), out_shape=[shape...]
  transfers between devices with their start and end apart: 25 -> 25, of which waited for: 8 -> 6; matrix products, arithmetic and copies ran while one was open for 0% -> 0% of each run, Pallas kernels for 24% -> 26%
where the time goes in v5:
time: 56.3 us; the launch traced here: 56.1 us
  starting transfers between devices  30.1 us (53%)
  Pallas kernels  17.2 us (31%)
  waiting for transfers between devices  7.97 us (14%)
  between operations  0.83 us (1%)
    ppermute x12, starting transfers between devices, send_inner(): return lax.ppermute(x, 'expert', pairs)  14.8 us
    ppermute x9, starting transfers between devices, send_outer(): return lax.ppermute(x, 'expert', pairs)  14.6 us
    pallas_call x1, Pallas kernels, on_device(): pl.pallas_call(functools.partial(load_kernel, weight_parts), out_shape=[p...  5.43 us
    ppermute x12, waiting for transfers between devices, send_inner(): return lax.ppermute(x, 'expert', pairs)  4.56 us
    ppermute x9, waiting for transfers between devices, send_outer(): return lax.ppermute(x, 'expert', pairs)  3.4 us
    pallas_call x1, Pallas kernels, on_device(): pl.pallas_call(functools.partial(down_kernel, dims, chunks), out_shape=pl...  2.38 us
    pallas_call x1, Pallas kernels, on_device(): pl.pallas_call(functools.partial(forward_kernel, dims), out_shape=[shape(...  1.44 us
    pallas_call x2, Pallas kernels, finish(): pl.pallas_call(functools.partial(final_kernel, (outer, tokens, half)), ou...  1.33 us
  transfers between devices with their start and end apart: 25, of which 6 were waited for; matrix products, arithmetic and copies ran while one was open for 0% of the time, Pallas kernels for 26%

profile of v5, /device:TPU:0, one launch (start us, length us, event | category | flops | bytes accessed | tf_op | source)
XLA Modules:
  0.0 56.1 jit_solution(5388152470121194343)
XLA Ops:
  0.6 1.3 %prepare.1.refs_3_.refs_0_ = bf16[24,2176]{1,0:T(8,128)(2,1)S(1)} custom-call(s32[8,12]{1,0:T(8,128)} %bitcast.2, f32[8,12]{1,0:T(8,128)} %bitcast.3, bf16[12,2048]{1,0:T(8,128)(2,1)} %refs_2_.2, bf16[12,2048]{1,0:T(8,128)(2,1)} %refs_3_.1), custom_call_target="tpu_custom_call" | custom-call | tf_op jit(solution)/shard_map/prepare/prepare/pallas_call | solution.py:389
  1.9 3.1 %collective-permute-start = (bf16[24,2176]{1,0:T(8,128)(2,1)S(1)}, bf16[24,2176]{1,0:T(8,128)(2,1)S(1)}, u32[]{:S(2)}, u32[]{:S(2)}) collective-permute-start(bf16[24,2176]{1,0:T(8,128)(2,1)S(1)} %prepare.1.refs_3_.refs_0_), channel_id=1, source_target_pairs={{0,8},{2,10},{4,12},{6,14},{8,0},{10,2},{12,4},{14,6},{16,24},{18,... | collective-permute-start | bytes 313352 | tf_op jit(solution)/shard_map/gather_blocks/ppermute | solution.py:43
  5.0 2.6 %collective-permute-start.1 = (bf16[24,2176]{1,0:T(8,128)(2,1)S(1)}, bf16[24,2176]{1,0:T(8,128)(2,1)S(1)}, u32[]{:S(2)}, u32[]{:S(2)}) collective-permute-start(bf16[24,2176]{1,0:T(8,128)(2,1)S(1)} %prepare.1.refs_3_.refs_0_), channel_id=1, source_target_pairs={{0,16},{2,18},{4,20},{6,22},{8,24},{10,26},{12,28},{14,30},{16,0},... | collective-permute-start | bytes 313352 | tf_op jit(solution)/shard_map/gather_blocks/ppermute | solution.py:43
  7.6 5.4 %load_weights.1 = (bf16[1,4096,512]{2,1,0:T(8,128)(2,1)S(1)}, bf16[1,4096,512]{2,1,0:T(8,128)(2,1)S(1)}, bf16[1,512,4096]{2,1,0:T(8,128)(2,1)S(1)}, bf16[512,409...) custom-call(bf16[1,4096,512]{2,1,0:T(8,128)(2,1)} %refs_0_.1, ...), custom_call_target="tpu_custom_call" | custom-call | tf_op jit(solution)/shard_map/load_weights/load_weights/pallas_call | solution.py:413
  13.0 2.8 %collective-permute-done.1.refs_2_ = bf16[24,2176]{1,0:T(8,128)(2,1)S(1)} collective-permute-done((bf16[24,2176]{1,0:T(8,128)(2,1)S(1)}, bf16[24,2176]{1,0:T(8,128)(2,1)S(1)}, u32[]{:S(2)}, u32[]{:S(2)}) %collective-permute-start.1) | collective-permute-done | bytes 104480 | tf_op jit(solution)/shard_map/gather_blocks/ppermute | solution.py:43
  15.9 0.6 %route.1 = (bf16[56,1024]{1,0:T(8,128)(2,1)S(1)}, bf16[56,1024]{1,0:T(8,128)(2,1)S(1)}, bf16[56,1024]{1,0:T(8,128)(2,1)S(1)}, bf16[56,1024]{1,0:T(8,128)(2,1)S(1)}, bf16[96,224]{1,0:T(8,128)(2,1)S(1)}) custom-call(bf16[24,2176]{1,0:T(8,128)(2,1)S(1)} %prepare.1.refs_3_.refs_0_, bf16[24,2176]{1,0:T(8,128)(2,1)S(1)} %collective-permute-done.refs_1_, ...), custom_call_target="tpu_custom_call" | custom-call | tf_op jit(solution)/shard_map/route/route/pallas_call | solution.py:428
  16.5 2.5 %collective-permute-start.3 = (bf16[56,1024]{1,0:T(8,128)(2,1)S(1)}, bf16[56,1024]{1,0:T(8,128)(2,1)S(1)}, u32[]{:S(2)}, u32[]{:S(2)}) collective-permute-start(bf16[56,1024]{1,0:T(8,128)(2,1)S(1)} %get-tuple-element.53), channel_id=1, source_target_pairs={{0,6},{2,4},{4,2},{6,0},{8,14},{10,12},{12,10},{14,8},{16,22},{18,... | collective-permute-start | bytes 344072 | tf_op jit(solution)/shard_map/exchange_in/ppermute | solution.py:51
  20.0 0.7 %scale.1 = (bf16[96,224]{1,0:T(8,128)(2,1)S(1)}, bf16[96,224]{1,0:T(8,128)(2,1)S(1)}, bf16[56,1024]{1,0:T(8,128)(2,1)S(1)}, bf16[56,1024]{1,0:T(8,128)(2,1)S(1)}...) custom-call(bf16[24,2176]{1,0:T(8,128)(2,1)S(1)} %prepare.1.refs_3_.refs_0_, ...), custom_call_target="tpu_custom_call" | custom-call | tf_op jit(solution)/shard_map/scale/scale/pallas_call | solution.py:454
  20.7 2.5 %collective-permute-start.7 = (bf16[56,1024]{1,0:T(8,128)(2,1)S(1)}, bf16[56,1024]{1,0:T(8,128)(2,1)S(1)}, u32[]{:S(2)}, u32[]{:S(2)}) collective-permute-start(bf16[56,1024]{1,0:T(8,128)(2,1)S(1)} %get-tuple-element.62), channel_id=1, source_target_pairs={{0,6},{2,4},{4,2},{6,0},{8,14},{10,12},{12,10},{14,8},{16,22},{18,... | collective-permute-start | bytes 344072 | tf_op jit(solution)/shard_map/exchange_grad/ppermute | solution.py:51
  23.8 1.1 %collective-permute-start.16 = (bf16[56,1024]{1,0:T(8,128)(2,1)S(1)}, bf16[56,1024]{1,0:T(8,128)(2,1)S(1)}, u32[]{:S(2)}, u32[]{:S(2)}) collective-permute-start(bf16[56,1024]{1,0:T(8,128)(2,1)S(1)} %get-tuple-element.78), channel_id=1, source_target_pairs={{0,2},{2,0},{4,6},{6,4},{8,10},{10,8},{12,14},{14,12},{16,18},{18,... | collective-permute-start | bytes 344072 | tf_op jit(solution)/shard_map/exchange_grad/ppermute | solution.py:51
  24.8 1.6 %collective-permute-done.4.refs_2_ = bf16[56,1024]{1,0:T(8,128)(2,1)S(1)} collective-permute-done((bf16[56,1024]{1,0:T(8,128)(2,1)S(1)}, bf16[56,1024]{1,0:T(8,128)(2,1)S(1)}, u32[]{:S(2)}, u32[]{:S(2)}) %collective-permute-start.4) | collective-permute-done | bytes 114720 | tf_op jit(solution)/shard_map/exchange_in/ppermute | solution.py:51
  26.6 0.7 %forward_own.1 = (f32[128,512]{1,0:T(8,128)S(1)}, f32[128,512]{1,0:T(8,128)S(1)}, f32[8,128]{1,0:T(8,128)S(1)}) custom-call(bf16[128,2048]{1,0:T(8,128)(2,1)S(1)} %stack.2.refs_0_, bf16[1,4096,512]{2,1,0:T(8,128)(2,1)S(1)} %get-tuple-element.56.refs_1_.refs_3_, bf16[1,4096,512]{2,1,0:T(8,128)(2,1)S(1)} %get-tuple-element.57.refs_2_.refs_4_), custom_call_target="tpu_custom_call" | custom-call | tf_op jit(solution)/shard_map/gather_in/forward_own/forward_own/pallas_call | solution.py:467
  27.7 1.1 %collective-permute-done.15.refs_2_ = bf16[56,1024]{1,0:T(8,128)(2,1)S(1)} collective-permute-done((bf16[56,1024]{1,0:T(8,128)(2,1)S(1)}, bf16[56,1024]{1,0:T(8,128)(2,1)S(1)}, u32[]{:S(2)}, u32[]{:S(2)}) %collective-permute-start.15) | collective-permute-done | bytes 114720 | tf_op jit(solution)/shard_map/exchange_grad/ppermute | solution.py:51
  29.0 1.4 %forward.1 = (f32[128,512]{1,0:T(8,128)S(1)}, f32[128,512]{1,0:T(8,128)S(1)}, bf16[128,512]{1,0:T(8,128)(2,1)S(1)}, bf16[128,2048]{1,0:T(8,128)(2,1)S(1)}, bf16[128,2048]{1,0:T(8,128)(2,1)S(1)}) custom-call(f32[128,512]{1,0:T(8,128)S(1)} %get-tuple-element.58.refs_0_, f32[128,512]{1,0:T(8,128)S(1)} %get-tuple-element.59.refs_1_, ...), custom_call_target="tpu_custom_call" | custom-call | tf_op jit(solution)/shard_map/forward/forward/pallas_call | solution.py:479
  31.5 1.2 %backward.1 = (bf16[128,512]{1,0:T(8,128)(2,1)S(1)}, bf16[128,512]{1,0:T(8,128)(2,1)S(1)}, bf16[128,2048]{1,0:T(8,128)(2,1)S(1)}) custom-call(f32[128,512]{1,0:T(8,128)S(1)} %backward_own.1.refs_0_, bf16[128,2048]{1,0:T(8,128)(2,1)S(1)} %collective-permute-done.17.refs_1_, bf16[512,4096]{1,0:T(8,128)(2,1)S(1)} %get-tuple-element.81.refs_2_, ...), custom_call_target="tpu_custom_call" | custom-call | tf_op jit(solution)/shard_map/backward/backward/pallas_call | solution.py:535
  32.9 1.8 %collective-permute-start.9 = (bf16[56,1024]{1,0:T(8,128)(2,1)S(1)}, bf16[56,1024]{1,0:T(8,128)(2,1)S(1)}, u32[]{:S(2)}, u32[]{:S(2)}) collective-permute-start(bf16[56,1024]{1,0:T(8,128)(2,1)S(1)} %get-tuple-element.66), channel_id=1, source_target_pairs={{0,6},{2,4},{4,2},{6,0},{8,14},{10,12},{12,10},{14,8},{16,22},{18,... | collective-permute-start | bytes 344072 | tf_op jit(solution)/shard_map/return_out/ppermute | solution.py:51
  34.7 0.9 %collective-permute-start.10 = (bf16[56,1024]{1,0:T(8,128)(2,1)S(1)}, bf16[56,1024]{1,0:T(8,128)(2,1)S(1)}, u32[]{:S(2)}, u32[]{:S(2)}) collective-permute-start(bf16[56,1024]{1,0:T(8,128)(2,1)S(1)} %get-tuple-element.67), channel_id=1, source_target_pairs={{0,4},{2,6},{4,0},{6,2},{8,12},{10,14},{12,8},{14,10},{16,20},{18,... | collective-permute-start | bytes 344072 | tf_op jit(solution)/shard_map/return_out/ppermute | solution.py:51
  35.6 0.9 %collective-permute-start.11 = (bf16[56,1024]{1,0:T(8,128)(2,1)S(1)}, bf16[56,1024]{1,0:T(8,128)(2,1)S(1)}, u32[]{:S(2)}, u32[]{:S(2)}) collective-permute-start(bf16[56,1024]{1,0:T(8,128)(2,1)S(1)} %get-tuple-element.68), channel_id=1, source_target_pairs={{0,2},{2,0},{4,6},{6,4},{8,10},{10,8},{12,14},{14,12},{16,18},{18,... | collective-permute-start | bytes 344072 | tf_op jit(solution)/shard_map/return_out/ppermute | solution.py:51
  36.5 0.7 %input_own.1.refs_0_ = bf16[128,2048]{1,0:T(8,128)(2,1)S(1)} custom-call(bf16[128,512]{1,0:T(8,128)(2,1)S(1)} %get-tuple-element.85.refs_0_, bf16[128,512]{1,0:T(8,128)(2,1)S(1)} %get-tuple-element.86.refs_1_, bf16[512,4096]{1,0:T(8,128)(2,1)S(1)} %get-tuple-element.81.refs_2_, bf16[512,4096]{1,0:T(8,128)(2,1)S(1)} %get-tuple-element.82.refs_3_, ...), custom_call_target="tpu_custom_call" | custom-call | tf_op jit(solution)/shard_map/backward/input_own/pallas_call | solution.py:543
  37.4 1.8 %collective-permute-start.19 = (bf16[56,1024]{1,0:T(8,128)(2,1)S(1)}, bf16[56,1024]{1,0:T(8,128)(2,1)S(1)}, u32[]{:S(2)}, u32[]{:S(2)}) collective-permute-start(bf16[56,1024]{1,0:T(8,128)(2,1)S(1)} %get-tuple-element.89), channel_id=1, source_target_pairs={{0,6},{2,4},{4,2},{6,0},{8,14},{10,12},{12,10},{14,8},{16,22},{18,... | collective-permute-start | bytes 344072 | tf_op jit(solution)/shard_map/return_grad/ppermute | solution.py:51
  39.2 0.9 %collective-permute-start.20 = (bf16[56,1024]{1,0:T(8,128)(2,1)S(1)}, bf16[56,1024]{1,0:T(8,128)(2,1)S(1)}, u32[]{:S(2)}, u32[]{:S(2)}) collective-permute-start(bf16[56,1024]{1,0:T(8,128)(2,1)S(1)} %get-tuple-element.90), channel_id=1, source_target_pairs={{0,4},{2,6},{4,0},{6,2},{8,12},{10,14},{12,8},{14,10},{16,20},{18,... | collective-permute-start | bytes 344072 | tf_op jit(solution)/shard_map/return_grad/ppermute | solution.py:51
  40.1 0.9 %collective-permute-start.21 = (bf16[56,1024]{1,0:T(8,128)(2,1)S(1)}, bf16[56,1024]{1,0:T(8,128)(2,1)S(1)}, u32[]{:S(2)}, u32[]{:S(2)}) collective-permute-start(bf16[56,1024]{1,0:T(8,128)(2,1)S(1)} %get-tuple-element.91), channel_id=1, source_target_pairs={{0,2},{2,0},{4,6},{6,4},{8,10},{10,8},{12,14},{14,12},{16,18},{18,... | collective-permute-start | bytes 344072 | tf_op jit(solution)/shard_map/return_grad/ppermute | solution.py:51
  41.0 1.4 %collective-permute-done.10.refs_2_ = bf16[56,1024]{1,0:T(8,128)(2,1)S(1)} collective-permute-done((bf16[56,1024]{1,0:T(8,128)(2,1)S(1)}, bf16[56,1024]{1,0:T(8,128)(2,1)S(1)}, u32[]{:S(2)}, u32[]{:S(2)}) %collective-permute-start.10) | collective-permute-done | bytes 114720 | tf_op jit(solution)/shard_map/return_out/ppermute | solution.py:51
  42.7 2.6 %collective-permute-start.12 = (bf16[24,1024]{1,0:T(8,128)(2,1)S(1)}, bf16[24,1024]{1,0:T(8,128)(2,1)S(1)}, u32[]{:S(2)}, u32[]{:S(2)}) collective-permute-start(bf16[24,1024]{1,0:T(8,128)(2,1)S(1)} %get-tuple-element.72), channel_id=1, source_target_pairs={{0,24},{2,26},{4,28},{6,30},{8,16},{10,18},{12,20},{14,22},{16,8},... | collective-permute-start | bytes 147464 | tf_op jit(solution)/shard_map/return_out/ppermute | solution.py:43
  45.2 0.9 %collective-permute-start.13 = (bf16[24,1024]{1,0:T(8,128)(2,1)S(1)}, bf16[24,1024]{1,0:T(8,128)(2,1)S(1)}, u32[]{:S(2)}, u32[]{:S(2)}) collective-permute-start(bf16[24,1024]{1,0:T(8,128)(2,1)S(1)} %get-tuple-element.73), channel_id=1, source_target_pairs={{0,16},{2,18},{4,20},{6,22},{8,24},{10,26},{12,28},{14,30},{16,0},... | collective-permute-start | bytes 147464 | tf_op jit(solution)/shard_map/return_out/ppermute | solution.py:43
  46.1 1.0 %collective-permute-start.14 = (bf16[24,1024]{1,0:T(8,128)(2,1)S(1)}, bf16[24,1024]{1,0:T(8,128)(2,1)S(1)}, u32[]{:S(2)}, u32[]{:S(2)}) collective-permute-start(bf16[24,1024]{1,0:T(8,128)(2,1)S(1)} %get-tuple-element.74), channel_id=1, source_target_pairs={{0,8},{2,10},{4,12},{6,14},{8,0},{10,2},{12,4},{14,6},{16,24},{18,... | collective-permute-start | bytes 147464 | tf_op jit(solution)/shard_map/return_out/ppermute | solution.py:43
  47.4 2.6 %collective-permute-start.22 = (bf16[24,1024]{1,0:T(8,128)(2,1)S(1)}, bf16[24,1024]{1,0:T(8,128)(2,1)S(1)}, u32[]{:S(2)}, u32[]{:S(2)}) collective-permute-start(bf16[24,1024]{1,0:T(8,128)(2,1)S(1)} %get-tuple-element.93), channel_id=1, source_target_pairs={{0,24},{2,26},{4,28},{6,30},{8,16},{10,18},{12,20},{14,22},{16,8},... | collective-permute-start | bytes 147464 | tf_op jit(solution)/shard_map/return_grad/ppermute | solution.py:43
  49.9 0.6 %collective-permute-start.23 = (bf16[24,1024]{1,0:T(8,128)(2,1)S(1)}, bf16[24,1024]{1,0:T(8,128)(2,1)S(1)}, u32[]{:S(2)}, u32[]{:S(2)}) collective-permute-start(bf16[24,1024]{1,0:T(8,128)(2,1)S(1)} %get-tuple-element.94), channel_id=1, source_target_pairs={{0,16},{2,18},{4,20},{6,22},{8,24},{10,26},{12,28},{14,30},{16,0},... | collective-permute-start | bytes 147464 | tf_op jit(solution)/shard_map/return_grad/ppermute | solution.py:43
  50.5 1.3 %collective-permute-start.24 = (bf16[24,1024]{1,0:T(8,128)(2,1)S(1)}, bf16[24,1024]{1,0:T(8,128)(2,1)S(1)}, u32[]{:S(2)}, u32[]{:S(2)}) collective-permute-start(bf16[24,1024]{1,0:T(8,128)(2,1)S(1)} %get-tuple-element.95), channel_id=1, source_target_pairs={{0,8},{2,10},{4,12},{6,14},{8,0},{10,2},{12,4},{14,6},{16,24},{18,... | collective-permute-start | bytes 147464 | tf_op jit(solution)/shard_map/return_grad/ppermute | solution.py:43
  51.8 2.4 %down_grad.1 = bf16[1,512,4096]{2,1,0:T(8,128)(2,1)} custom-call(bf16[128,2048]{1,0:T(8,128)(2,1)S(1)} %stack.3.rows.refs_0_, bf16[128,2048]{1,0:T(8,128)(2,1)S(1)} %collective-permute-done.17.refs_1_, bf16[128,512]{1,0:T(8,128)(2,1)S(1)} %get-tuple-element.98.refs_2_, bf16[24,1024]{1,0:T(8,128)(2,1)S(1)} %get-tuple-element.92.refs_0_.refs_3_), custom_call_target="tpu_custom_call" | custom-call | tf_op jit(solution)/shard_map/down_grad/down_grad/pallas_call | solution.py:558
  54.2 0.7 %final.2 = (bf16[12,2048]{1,0:T(8,128)(2,1)}, f32[8,128]{1,0:T(8,128)S(1)}) custom-call(bf16[24,1024]{1,0:T(8,128)(2,1)S(1)} %get-tuple-element.71.refs_0_, bf16[24,1024]{1,0:T(8,128)(2,1)S(1)} %collective-permute-done.12.refs_1_, bf16[24,1024]{1,0:T(8,128)(2,1)S(1)} %collective-permute-done.13.refs_2_, bf16[24,1024]{1,0:T(8,128)(2,1)S(1)} %collective-permute-done.14.refs_3_), custom_call_target="tpu_custom_call" | custom-call | tf_op jit(solution)/shard_map/final/pallas_call | solution.py:512
  55.4 0.7 %final.3 = (bf16[12,2048]{1,0:T(8,128)(2,1)}, f32[8,128]{1,0:T(8,128)}) custom-call(bf16[24,1024]{1,0:T(8,128)(2,1)S(1)} %get-tuple-element.92.refs_0_.refs_3_, bf16[24,1024]{1,0:T(8,128)(2,1)S(1)} %collective-permute-done.22.refs_1_, bf16[24,1024]{1,0:T(8,128)(2,1)S(1)} %collective-permute-done.23.refs_2_, ...), custom_call_target="tpu_custom_call" | custom-call | tf_op jit(solution)/shard_map/final/pallas_call | solution.py:512
  (36 shorter events, 4.8 us)
Async XLA Ops:
  1.9 11.1 %collective-permute-start = (bf16[24,2176]{1,0:T(8,128)(2,1)S(1)}, bf16[24,2176]{1,0:T(8,128)(2,1)S(1)}, u32[]{:S(2)}, u32[]{:S(2)}) collective-permute-start(bf16[24,2176]{1,0:T(8,128)(2,1)S(1)} %prepare.1.refs_3_.refs_0_), channel_id=1, source_target_pairs={{0,8},{2,10},{4,12},{6,14},{8,0},{10,2},{12,4},{14,6},{16,24},{18,... | collective-permute-start | bytes 313352 | tf_op jit(solution)/shard_map/gather_blocks/ppermute | solution.py:43
  5.0 10.9 %collective-permute-start.1 = (bf16[24,2176]{1,0:T(8,128)(2,1)S(1)}, bf16[24,2176]{1,0:T(8,128)(2,1)S(1)}, u32[]{:S(2)}, u32[]{:S(2)}) collective-permute-start(bf16[24,2176]{1,0:T(8,128)(2,1)S(1)} %prepare.1.refs_3_.refs_0_), channel_id=1, source_target_pairs={{0,16},{2,18},{4,20},{6,22},{8,24},{10,26},{12,28},{14,30},{16,0},... | collective-permute-start | bytes 313352 | tf_op jit(solution)/shard_map/gather_blocks/ppermute | solution.py:43
  7.6 8.3 %collective-permute-start.2 = (bf16[24,2176]{1,0:T(8,128)(2,1)S(1)}, bf16[24,2176]{1,0:T(8,128)(2,1)S(1)}, u32[]{:S(2)}, u32[]{:S(2)}) collective-permute-start(bf16[24,2176]{1,0:T(8,128)(2,1)S(1)} %prepare.1.refs_3_.refs_0_), channel_id=1, source_target_pairs={{0,24},{2,26},{4,28},{6,30},{8,16},{10,18},{12,20},{14,22},{16,8},... | collective-permute-start | bytes 313352 | tf_op jit(solution)/shard_map/gather_blocks/ppermute | solution.py:43
  16.5 7.3 %collective-permute-start.3 = (bf16[56,1024]{1,0:T(8,128)(2,1)S(1)}, bf16[56,1024]{1,0:T(8,128)(2,1)S(1)}, u32[]{:S(2)}, u32[]{:S(2)}) collective-permute-start(bf16[56,1024]{1,0:T(8,128)(2,1)S(1)} %get-tuple-element.53), channel_id=1, source_target_pairs={{0,6},{2,4},{4,2},{6,0},{8,14},{10,12},{12,10},{14,8},{16,22},{18,... | collective-permute-start | bytes 344072 | tf_op jit(solution)/shard_map/exchange_in/ppermute | solution.py:51
  19.0 7.4 %collective-permute-start.4 = (bf16[56,1024]{1,0:T(8,128)(2,1)S(1)}, bf16[56,1024]{1,0:T(8,128)(2,1)S(1)}, u32[]{:S(2)}, u32[]{:S(2)}) collective-permute-start(bf16[56,1024]{1,0:T(8,128)(2,1)S(1)} %get-tuple-element.54), channel_id=1, source_target_pairs={{0,4},{2,6},{4,0},{6,2},{8,12},{10,14},{12,8},{14,10},{16,20},{18,... | collective-permute-start | bytes 344072 | tf_op jit(solution)/shard_map/exchange_in/ppermute | solution.py:51
  19.5 6.9 %collective-permute-start.5 = (bf16[56,1024]{1,0:T(8,128)(2,1)S(1)}, bf16[56,1024]{1,0:T(8,128)(2,1)S(1)}, u32[]{:S(2)}, u32[]{:S(2)}) collective-permute-start(bf16[56,1024]{1,0:T(8,128)(2,1)S(1)} %get-tuple-element.55), channel_id=1, source_target_pairs={{0,2},{2,0},{4,6},{6,4},{8,10},{10,8},{12,14},{14,12},{16,18},{18,... | collective-permute-start | bytes 344072 | tf_op jit(solution)/shard_map/exchange_in/ppermute | solution.py:51
  20.7 7.0 %collective-permute-start.7 = (bf16[56,1024]{1,0:T(8,128)(2,1)S(1)}, bf16[56,1024]{1,0:T(8,128)(2,1)S(1)}, u32[]{:S(2)}, u32[]{:S(2)}) collective-permute-start(bf16[56,1024]{1,0:T(8,128)(2,1)S(1)} %get-tuple-element.62), channel_id=1, source_target_pairs={{0,6},{2,4},{4,2},{6,0},{8,14},{10,12},{12,10},{14,8},{16,22},{18,... | collective-permute-start | bytes 344072 | tf_op jit(solution)/shard_map/exchange_grad/ppermute | solution.py:51
  23.2 5.6 %collective-permute-start.15 = (bf16[56,1024]{1,0:T(8,128)(2,1)S(1)}, bf16[56,1024]{1,0:T(8,128)(2,1)S(1)}, u32[]{:S(2)}, u32[]{:S(2)}) collective-permute-start(bf16[56,1024]{1,0:T(8,128)(2,1)S(1)} %get-tuple-element.77), channel_id=1, source_target_pairs={{0,4},{2,6},{4,0},{6,2},{8,12},{10,14},{12,8},{14,10},{16,20},{18,... | collective-permute-start | bytes 344072 | tf_op jit(solution)/shard_map/exchange_grad/ppermute | solution.py:51
  23.8 5.1 %collective-permute-start.16 = (bf16[56,1024]{1,0:T(8,128)(2,1)S(1)}, bf16[56,1024]{1,0:T(8,128)(2,1)S(1)}, u32[]{:S(2)}, u32[]{:S(2)}) collective-permute-start(bf16[56,1024]{1,0:T(8,128)(2,1)S(1)} %get-tuple-element.78), channel_id=1, source_target_pairs={{0,2},{2,0},{4,6},{6,4},{8,10},{10,8},{12,14},{14,12},{16,18},{18,... | collective-permute-start | bytes 344072 | tf_op jit(solution)/shard_map/exchange_grad/ppermute | solution.py:51
  26.5 2.5 %collective-permute-start.6 = (bf16[128,2048]{1,0:T(8,128)(2,1)S(1)}, bf16[128,2048]{1,0:T(8,128)(2,1)S(1)}, u32[]{:S(2)}, u32[]{:S(2)}) collective-permute-start(bf16[128,2048]{1,0:T(8,128)(2,1)S(1)} %stack.2.refs_0_), channel_id=1, source_target_pairs={{0,1},{1,0},{2,3},{3,2},{4,5},{5,4},{6,7},{7,6},{8,9},{9,8},{10,11... | collective-permute-start | bytes 1572872 | tf_op jit(solution)/shard_map/gather_in/ppermute | solution.py:56
  29.0 2.5 %collective-permute-start.17 = (bf16[128,2048]{1,0:T(8,128)(2,1)S(1)}, bf16[128,2048]{1,0:T(8,128)(2,1)S(1)}, u32[]{:S(2)}, u32[]{:S(2)}) collective-permute-start(bf16[128,2048]{1,0:T(8,128)(2,1)S(1)} %stack.3.rows.refs_0_), channel_id=1, source_target_pairs={{0,1},{1,0},{2,3},{3,2},{4,5},{5,4},{6,7},{7,6},{8,9},{9,8},{10,11... | collective-permute-start | bytes 1572872 | tf_op jit(solution)/shard_map/gather_in/ppermute | solution.py:56
  30.5 2.3 %collective-permute-start.8 = (bf16[128,2048]{1,0:T(8,128)(2,1)S(1)}, bf16[128,2048]{1,0:T(8,128)(2,1)S(1)}, u32[]{:S(2)}, u32[]{:S(2)}) collective-permute-start(bf16[128,2048]{1,0:T(8,128)(2,1)S(1)} %get-tuple-element.64), channel_id=1, source_target_pairs={{0,1},{1,0},{2,3},{3,2},{4,5},{5,4},{6,7},{7,6},{8,9},{9,8},{10,11... | collective-permute-start | bytes 1572872 | tf_op jit(solution)/shard_map/return_out/ppermute | solution.py:56
  32.7 4.6 %collective-permute-start.18 = (bf16[128,2048]{1,0:T(8,128)(2,1)S(1)}, bf16[128,2048]{1,0:T(8,128)(2,1)S(1)}, u32[]{:S(2)}, u32[]{:S(2)}) collective-permute-start(bf16[128,2048]{1,0:T(8,128)(2,1)S(1)} %get-tuple-element.87), channel_id=1, source_target_pairs={{0,1},{1,0},{2,3},{3,2},{4,5},{5,4},{6,7},{7,6},{8,9},{9,8},{10,11... | collective-permute-start | bytes 1572872 | tf_op jit(solution)/shard_map/return_grad/ppermute | solution.py:56
  32.9 7.2 %collective-permute-start.9 = (bf16[56,1024]{1,0:T(8,128)(2,1)S(1)}, bf16[56,1024]{1,0:T(8,128)(2,1)S(1)}, u32[]{:S(2)}, u32[]{:S(2)}) collective-permute-start(bf16[56,1024]{1,0:T(8,128)(2,1)S(1)} %get-tuple-element.66), channel_id=1, source_target_pairs={{0,6},{2,4},{4,2},{6,0},{8,14},{10,12},{12,10},{14,8},{16,22},{18,... | collective-permute-start | bytes 344072 | tf_op jit(solution)/shard_map/return_out/ppermute | solution.py:51
  34.7 7.7 %collective-permute-start.10 = (bf16[56,1024]{1,0:T(8,128)(2,1)S(1)}, bf16[56,1024]{1,0:T(8,128)(2,1)S(1)}, u32[]{:S(2)}, u32[]{:S(2)}) collective-permute-start(bf16[56,1024]{1,0:T(8,128)(2,1)S(1)} %get-tuple-element.67), channel_id=1, source_target_pairs={{0,4},{2,6},{4,0},{6,2},{8,12},{10,14},{12,8},{14,10},{16,20},{18,... | collective-permute-start | bytes 344072 | tf_op jit(solution)/shard_map/return_out/ppermute | solution.py:51
  35.6 6.8 %collective-permute-start.11 = (bf16[56,1024]{1,0:T(8,128)(2,1)S(1)}, bf16[56,1024]{1,0:T(8,128)(2,1)S(1)}, u32[]{:S(2)}, u32[]{:S(2)}) collective-permute-start(bf16[56,1024]{1,0:T(8,128)(2,1)S(1)} %get-tuple-element.68), channel_id=1, source_target_pairs={{0,2},{2,0},{4,6},{6,4},{8,10},{10,8},{12,14},{14,12},{16,18},{18,... | collective-permute-start | bytes 344072 | tf_op jit(solution)/shard_map/return_out/ppermute | solution.py:51
  37.4 8.7 %collective-permute-start.19 = (bf16[56,1024]{1,0:T(8,128)(2,1)S(1)}, bf16[56,1024]{1,0:T(8,128)(2,1)S(1)}, u32[]{:S(2)}, u32[]{:S(2)}) collective-permute-start(bf16[56,1024]{1,0:T(8,128)(2,1)S(1)} %get-tuple-element.89), channel_id=1, source_target_pairs={{0,6},{2,4},{4,2},{6,0},{8,14},{10,12},{12,10},{14,8},{16,22},{18,... | collective-permute-start | bytes 344072 | tf_op jit(solution)/shard_map/return_grad/ppermute | solution.py:51
  39.2 8.0 %collective-permute-start.20 = (bf16[56,1024]{1,0:T(8,128)(2,1)S(1)}, bf16[56,1024]{1,0:T(8,128)(2,1)S(1)}, u32[]{:S(2)}, u32[]{:S(2)}) collective-permute-start(bf16[56,1024]{1,0:T(8,128)(2,1)S(1)} %get-tuple-element.90), channel_id=1, source_target_pairs={{0,4},{2,6},{4,0},{6,2},{8,12},{10,14},{12,8},{14,10},{16,20},{18,... | collective-permute-start | bytes 344072 | tf_op jit(solution)/shard_map/return_grad/ppermute | solution.py:51
  40.1 7.1 %collective-permute-start.21 = (bf16[56,1024]{1,0:T(8,128)(2,1)S(1)}, bf16[56,1024]{1,0:T(8,128)(2,1)S(1)}, u32[]{:S(2)}, u32[]{:S(2)}) collective-permute-start(bf16[56,1024]{1,0:T(8,128)(2,1)S(1)} %get-tuple-element.91), channel_id=1, source_target_pairs={{0,2},{2,0},{4,6},{6,4},{8,10},{10,8},{12,14},{14,12},{16,18},{18,... | collective-permute-start | bytes 344072 | tf_op jit(solution)/shard_map/return_grad/ppermute | solution.py:51
  42.7 7.8 %collective-permute-start.12 = (bf16[24,1024]{1,0:T(8,128)(2,1)S(1)}, bf16[24,1024]{1,0:T(8,128)(2,1)S(1)}, u32[]{:S(2)}, u32[]{:S(2)}) collective-permute-start(bf16[24,1024]{1,0:T(8,128)(2,1)S(1)} %get-tuple-element.72), channel_id=1, source_target_pairs={{0,24},{2,26},{4,28},{6,30},{8,16},{10,18},{12,20},{14,22},{16,8},... | collective-permute-start | bytes 147464 | tf_op jit(solution)/shard_map/return_out/ppermute | solution.py:43
  45.2 9.0 %collective-permute-start.13 = (bf16[24,1024]{1,0:T(8,128)(2,1)S(1)}, bf16[24,1024]{1,0:T(8,128)(2,1)S(1)}, u32[]{:S(2)}, u32[]{:S(2)}) collective-permute-start(bf16[24,1024]{1,0:T(8,128)(2,1)S(1)} %get-tuple-element.73), channel_id=1, source_target_pairs={{0,16},{2,18},{4,20},{6,22},{8,24},{10,26},{12,28},{14,30},{16,0},... | collective-permute-start | bytes 147464 | tf_op jit(solution)/shard_map/return_out/ppermute | solution.py:43
  46.1 8.1 %collective-permute-start.14 = (bf16[24,1024]{1,0:T(8,128)(2,1)S(1)}, bf16[24,1024]{1,0:T(8,128)(2,1)S(1)}, u32[]{:S(2)}, u32[]{:S(2)}) collective-permute-start(bf16[24,1024]{1,0:T(8,128)(2,1)S(1)} %get-tuple-element.74), channel_id=1, source_target_pairs={{0,8},{2,10},{4,12},{6,14},{8,0},{10,2},{12,4},{14,6},{16,24},{18,... | collective-permute-start | bytes 147464 | tf_op jit(solution)/shard_map/return_out/ppermute | solution.py:43
  47.4 7.5 %collective-permute-start.22 = (bf16[24,1024]{1,0:T(8,128)(2,1)S(1)}, bf16[24,1024]{1,0:T(8,128)(2,1)S(1)}, u32[]{:S(2)}, u32[]{:S(2)}) collective-permute-start(bf16[24,1024]{1,0:T(8,128)(2,1)S(1)} %get-tuple-element.93), channel_id=1, source_target_pairs={{0,24},{2,26},{4,28},{6,30},{8,16},{10,18},{12,20},{14,22},{16,8},... | collective-permute-start | bytes 147464 | tf_op jit(solution)/shard_map/return_grad/ppermute | solution.py:43
  49.9 5.5 %collective-permute-start.23 = (bf16[24,1024]{1,0:T(8,128)(2,1)S(1)}, bf16[24,1024]{1,0:T(8,128)(2,1)S(1)}, u32[]{:S(2)}, u32[]{:S(2)}) collective-permute-start(bf16[24,1024]{1,0:T(8,128)(2,1)S(1)} %get-tuple-element.94), channel_id=1, source_target_pairs={{0,16},{2,18},{4,20},{6,22},{8,24},{10,26},{12,28},{14,30},{16,0},... | collective-permute-start | bytes 147464 | tf_op jit(solution)/shard_map/return_grad/ppermute | solution.py:43
  50.5 5.0 %collective-permute-start.24 = (bf16[24,1024]{1,0:T(8,128)(2,1)S(1)}, bf16[24,1024]{1,0:T(8,128)(2,1)S(1)}, u32[]{:S(2)}, u32[]{:S(2)}) collective-permute-start(bf16[24,1024]{1,0:T(8,128)(2,1)S(1)} %get-tuple-element.95), channel_id=1, source_target_pairs={{0,8},{2,10},{4,12},{6,14},{8,0},{10,2},{12,4},{14,6},{16,24},{18,... | collective-permute-start | bytes 147464 | tf_op jit(solution)/shard_map/return_grad/ppermute | solution.py:43

commit v6 on v5

--- a/solution.py
+++ b/solution.py
@@ -9,6 +9,7 @@
 BF16 = jnp.bfloat16
 F32 = jnp.float32
 META = 128
+SUBLANES = 8
 VMEM_LIMIT = 20 * 1024 * 1024
 
 
@@ -99,30 +100,40 @@
     gate_hi = gates.astype(BF16)
     rest = gates - gate_hi.astype(F32)
     gate_mid = rest.astype(BF16)
-    gate_lo = (rest - gate_mid.astype(F32)).astype(BF16)
-    meta = jnp.zeros((tokens, META), F32)
-    entry = lax.broadcasted_iota(jnp.int32, (top, META), 0)
-    lane = lax.broadcasted_iota(jnp.int32, (top, META), 1)
-    for n, value in enumerate((ids_ref[...].astype(F32).astype(BF16), gate_hi, gate_mid, gate_lo)):
-        spread = (lane == entry + n * top).astype(F32).astype(BF16)
-        meta = meta + contract(value, spread, 0, 0)
-    unit = 2 * tokens
-    row = lax.broadcasted_iota(jnp.int32, (unit, tokens), 0)
-    token = lax.broadcasted_iota(jnp.int32, (unit, tokens), 1)
-    upper = (row == token).astype(F32).astype(BF16)
-    lower = (row == token + tokens).astype(F32).astype(BF16)
+    gate_lo = rest - gate_mid.astype(F32)
+    values = [ids_ref[...].astype(F32), gate_hi.astype(F32), gate_mid.astype(F32), gate_lo]
+    values = jnp.concatenate(values, axis=0).astype(BF16)
+    entry = lax.broadcasted_iota(jnp.int32, (4 * top, META), 0)
+    lane = lax.broadcasted_iota(jnp.int32, (4 * top, META), 1)
+    meta = contract(values, (lane == entry).astype(F32).astype(BF16), 0, 0)
+    meta = jnp.concatenate([meta, meta], axis=0)
+    tiles = 2 * tokens // SUBLANES
     for n, source in enumerate((hidden_ref, grad_ref)):
-        value = jnp.dot(upper, source[:, :half], preferred_element_type=F32)
-        value = value + jnp.dot(lower, source[:, half:], preferred_element_type=F32)
-        out_ref[:, n * half : (n + 1) * half] = value.astype(BF16)
-    out_ref[:, 2 * half :] = jnp.dot(upper + lower, meta.astype(BF16), preferred_element_type=F32).astype(BF16)
-
-
-def stacked(refs, columns=None):
-    parts = [r[...] if columns is None else r[:, columns] for r in refs]
-    if len(parts) == 1:
-        return parts[0]
-    return jnp.concatenate([p.astype(F32) for p in parts], axis=0).astype(BF16)
+        value = source[...].astype(F32)
+        value = jnp.concatenate([value[:, :half], value[:, half:]], axis=0)
+        for i in range(tiles):
+            start = (n * tiles + i) * half
+            out_ref[:, start : start + half] = value[i * SUBLANES : (i + 1) * SUBLANES].astype(BF16)
+    packed = meta[:SUBLANES]
+    for i in range(1, tiles):
+        packed = packed + pltpu.roll(meta[i * SUBLANES : (i + 1) * SUBLANES], i * 4 * top, 1)
+    out_ref[:, 2 * tiles * half :] = packed.astype(BF16)
+
+
+def block_rows(blocks, start, width, tiles, shift=0):
+    parts = []
+    for block in blocks:
+        for i in range(tiles):
+            if shift:
+                part = block[:, start : start + width].astype(F32)
+                parts.append(pltpu.roll(part, width - i * shift, 1) if i else part)
+            else:
+                parts.append(block[:, start + i * width : start + (i + 1) * width].astype(F32))
+    return jnp.concatenate(parts, axis=0)
+
+
+def stacked(refs):
+    return jnp.concatenate([r[...].astype(F32) for r in refs], axis=0).astype(BF16)
 
 
 def count_above(index, unit, total):
@@ -150,7 +161,7 @@
 
 def route_kernel(dims, *refs):
     outer, inner, tokens, top, cap, reach = dims
-    blocks = refs[:outer]
+    blocks = flipped(refs[:outer])
     sends = refs[outer + 1 : outer + 1 + inner]
     pick_ref = refs[outer + 1 + inner]
     half = sends[0].shape[1]
@@ -158,7 +169,8 @@
     slot, dest = slot_lanes(dims)
     side = (slot >= reach).astype(jnp.int32)
     slot = slot - side * reach
-    meta = jnp.concatenate([r[:, 2 * half :].astype(F32) for r in blocks], axis=0)
+    tiles = 2 * tokens // SUBLANES
+    meta = block_rows(blocks, 2 * tiles * half, META, tiles, 4 * top)
     named = jnp.zeros(dest.shape, F32)
     for k in range(top):
         named = jnp.where(meta[:, k : k + 1] == dest, 1.0, named)
@@ -178,7 +190,8 @@
 
 def select_rows(blocks, array, pick_ref, scale, sends):
     fold, half = sends[0].shape
-    table = stacked(blocks, pl.ds(array * half, half))
+    tiles = pick_ref.shape[0] // (len(blocks) * SUBLANES)
+    table = block_rows(blocks, array * tiles * half, half, tiles).astype(BF16)
     out = contract(pick_ref[...], table, 0, 0)
     out = (out if scale is None else out * scale).astype(F32)
     for q, send in enumerate(sends):
@@ -187,12 +200,13 @@
 
 def scale_kernel(dims, *refs):
     outer, inner, tokens, top, cap, reach = dims
-    blocks = refs[:outer]
+    blocks = flipped(refs[:outer])
     pick_ref = refs[outer]
     gate_hi_ref, gate_mid_ref, *sends = refs[outer + 1 :]
     half = sends[0].shape[1]
     _, dest = slot_lanes(dims)
-    meta = jnp.concatenate([r[:, 2 * half :].astype(F32) for r in blocks], axis=0)
+    tiles = 2 * tokens // SUBLANES
+    meta = block_rows(blocks, 2 * tiles * half, META, tiles, 4 * top)
     gate = jnp.zeros(dest.shape, F32)
     for k in range(top):
         value = sum(meta[:, n * top + k : n * top + k + 1] for n in range(1, 4))
@@ -388,7 +402,7 @@
     with jax.named_scope("prepare"):
         packed = pl.pallas_call(
             functools.partial(prepare_kernel, (tokens, top, half)),
-            out_shape=shape(unit, 2 * half + META),
+            out_shape=shape(SUBLANES, 2 * unit // SUBLANES * half + META),
             in_specs=hbm_specs(4),
             out_specs=pl.BlockSpec(memory_space=pltpu.VMEM),
             scratch_shapes=[
@@ -432,7 +446,7 @@
             out_specs=whole_specs(inner + 1),
             compiler_params=params(),
             name="route",
-        )(*blocks, loaded[6])
+        )(*flipped(blocks), loaded[6])
 
     def spread(sends):
         return [sends[0]] + [send_inner(sends[q], q, outer, inner) for q in range(1, inner)]
@@ -458,7 +472,7 @@
             out_specs=whole_specs(inner + 2),
             compiler_params=params(),
             name="scale",
-        )(*blocks, pick)
+        )(*flipped(blocks), pick)
     with jax.named_scope("exchange_grad"):
         grad_pieces = spread(grad_sends)
     with jax.named_scope("gather_in"):

time: 56.3 us -> 55.7 us (0.989)
  waiting for transfers between devices: 7.97 us -> 6.86 us
    ppermute x9, waiting for transfers between devices: 3.4 us -> 2.37 us  [send_outer(): return lax.ppermute(x, 'expert', pairs)]
where the time goes in v6:
time: 55.7 us; the launch traced here: 55.5 us
  starting transfers between devices  30.6 us (55%)
  Pallas kernels  17.2 us (31%)
  waiting for transfers between devices  6.86 us (12%)
  between operations  0.83 us (1%)
    ppermute x12, starting transfers between devices, send_inner(): return lax.ppermute(x, 'expert', pairs)  15.2 us
    ppermute x9, starting transfers between devices, send_outer(): return lax.ppermute(x, 'expert', pairs)  14.7 us
    pallas_call x1, Pallas kernels, on_device(): pl.pallas_call(functools.partial(load_kernel, weight_parts), out_shape=[p...  5.43 us
    ppermute x12, waiting for transfers between devices, send_inner(): return lax.ppermute(x, 'expert', pairs)  4.48 us
    pallas_call x1, Pallas kernels, on_device(): pl.pallas_call(functools.partial(down_kernel, dims, chunks), out_shape=pl...  2.38 us
    ppermute x9, waiting for transfers between devices, send_outer(): return lax.ppermute(x, 'expert', pairs)  2.37 us
    pallas_call x1, Pallas kernels, on_device(): pl.pallas_call(functools.partial(forward_kernel, dims), out_shape=[shape(...  1.39 us
    pallas_call x2, Pallas kernels, finish(): pl.pallas_call(functools.partial(final_kernel, (outer, tokens, half)), ou...  1.33 us
  transfers between devices with their start and end apart: 25, of which 6 were waited for; matrix products, arithmetic and copies ran while one was open for 0% of the time, Pallas kernels for 26%

profile of v6, /device:TPU:0, one launch (start us, length us, event | category | flops | bytes accessed | tf_op | source)
XLA Modules:
  0.0 55.5 jit_solution(1446950906831534028)
XLA Ops:
  0.6 1.2 %prepare.1.refs_3_.refs_0_ = bf16[8,6272]{1,0:T(8,128)(2,1)S(1)} custom-call(s32[8,12]{1,0:T(8,128)} %bitcast.2, f32[8,12]{1,0:T(8,128)} %bitcast.3, bf16[12,2048]{1,0:T(8,128)(2,1)} %refs_2_.2, bf16[12,2048]{1,0:T(8,128)(2,1)} %refs_3_.1), custom_call_target="tpu_custom_call" | custom-call | tf_op jit(solution)/shard_map/prepare/prepare/pallas_call | solution.py:403
  1.8 5.1 %collective-permute-start = (bf16[8,6272]{1,0:T(8,128)(2,1)S(1)}, bf16[8,6272]{1,0:T(8,128)(2,1)S(1)}, u32[]{:S(2)}, u32[]{:S(2)}) collective-permute-start(bf16[8,6272]{1,0:T(8,128)(2,1)S(1)} %prepare.1.refs_3_.refs_0_), channel_id=1, source_target_pairs={{0,24},{2,26},{4,28},{6,30},{8,16},{10,18},{12,20},{14,22},{16,8},... | collective-permute-start | bytes 301064 | tf_op jit(solution)/shard_map/gather_blocks/ppermute | solution.py:44
  6.9 0.6 %collective-permute-start.2 = (bf16[8,6272]{1,0:T(8,128)(2,1)S(1)}, bf16[8,6272]{1,0:T(8,128)(2,1)S(1)}, u32[]{:S(2)}, u32[]{:S(2)}) collective-permute-start(bf16[8,6272]{1,0:T(8,128)(2,1)S(1)} %prepare.1.refs_3_.refs_0_), channel_id=1, source_target_pairs={{0,8},{2,10},{4,12},{6,14},{8,0},{10,2},{12,4},{14,6},{16,24},{18,... | collective-permute-start | bytes 301064 | tf_op jit(solution)/shard_map/gather_blocks/ppermute | solution.py:44
  7.6 5.4 %load_weights.1 = (bf16[1,4096,512]{2,1,0:T(8,128)(2,1)S(1)}, bf16[1,4096,512]{2,1,0:T(8,128)(2,1)S(1)}, bf16[1,512,4096]{2,1,0:T(8,128)(2,1)S(1)}, bf16[512,409...) custom-call(bf16[1,4096,512]{2,1,0:T(8,128)(2,1)} %refs_0_.1, ...), custom_call_target="tpu_custom_call" | custom-call | tf_op jit(solution)/shard_map/load_weights/load_weights/pallas_call | solution.py:427
  13.0 2.3 %collective-permute-done.1.refs_2_ = bf16[8,6272]{1,0:T(8,128)(2,1)S(1)} collective-permute-done((bf16[8,6272]{1,0:T(8,128)(2,1)S(1)}, bf16[8,6272]{1,0:T(8,128)(2,1)S(1)}, u32[]{:S(2)}, u32[]{:S(2)}) %collective-permute-start.1) | collective-permute-done | bytes 100384 | tf_op jit(solution)/shard_map/gather_blocks/ppermute | solution.py:44
  15.4 0.7 %route.1 = (bf16[56,1024]{1,0:T(8,128)(2,1)S(1)}, bf16[56,1024]{1,0:T(8,128)(2,1)S(1)}, bf16[56,1024]{1,0:T(8,128)(2,1)S(1)}, bf16[56,1024]{1,0:T(8,128)(2,1)S(1)}, bf16[96,224]{1,0:T(8,128)(2,1)S(1)}) custom-call(bf16[8,6272]{1,0:T(8,128)(2,1)S(1)} %prepare.1.refs_3_.refs_0_, bf16[8,6272]{1,0:T(8,128)(2,1)S(1)} %collective-permute-done.refs_1_, ...), custom_call_target="tpu_custom_call" | custom-call | tf_op jit(solution)/shard_map/route/route/pallas_call | solution.py:442
  16.1 2.5 %collective-permute-start.3 = (bf16[56,1024]{1,0:T(8,128)(2,1)S(1)}, bf16[56,1024]{1,0:T(8,128)(2,1)S(1)}, u32[]{:S(2)}, u32[]{:S(2)}) collective-permute-start(bf16[56,1024]{1,0:T(8,128)(2,1)S(1)} %get-tuple-element.53), channel_id=1, source_target_pairs={{0,6},{2,4},{4,2},{6,0},{8,14},{10,12},{12,10},{14,8},{16,22},{18,... | collective-permute-start | bytes 344072 | tf_op jit(solution)/shard_map/exchange_in/ppermute | solution.py:52
  19.6 0.8 %scale.1 = (bf16[96,224]{1,0:T(8,128)(2,1)S(1)}, bf16[96,224]{1,0:T(8,128)(2,1)S(1)}, bf16[56,1024]{1,0:T(8,128)(2,1)S(1)}, bf16[56,1024]{1,0:T(8,128)(2,1)S(1)}...) custom-call(bf16[8,6272]{1,0:T(8,128)(2,1)S(1)} %prepare.1.refs_3_.refs_0_, ...), custom_call_target="tpu_custom_call" | custom-call | tf_op jit(solution)/shard_map/scale/scale/pallas_call | solution.py:468
  20.4 2.5 %collective-permute-start.7 = (bf16[56,1024]{1,0:T(8,128)(2,1)S(1)}, bf16[56,1024]{1,0:T(8,128)(2,1)S(1)}, u32[]{:S(2)}, u32[]{:S(2)}) collective-permute-start(bf16[56,1024]{1,0:T(8,128)(2,1)S(1)} %get-tuple-element.62), channel_id=1, source_target_pairs={{0,6},{2,4},{4,2},{6,0},{8,14},{10,12},{12,10},{14,8},{16,22},{18,... | collective-permute-start | bytes 344072 | tf_op jit(solution)/shard_map/exchange_grad/ppermute | solution.py:52
  23.4 1.2 %collective-permute-start.16 = (bf16[56,1024]{1,0:T(8,128)(2,1)S(1)}, bf16[56,1024]{1,0:T(8,128)(2,1)S(1)}, u32[]{:S(2)}, u32[]{:S(2)}) collective-permute-start(bf16[56,1024]{1,0:T(8,128)(2,1)S(1)} %get-tuple-element.78), channel_id=1, source_target_pairs={{0,2},{2,0},{4,6},{6,4},{8,10},{10,8},{12,14},{14,12},{16,18},{18,... | collective-permute-start | bytes 344072 | tf_op jit(solution)/shard_map/exchange_grad/ppermute | solution.py:52
  24.6 0.8 %collective-permute-done.4.refs_2_ = bf16[56,1024]{1,0:T(8,128)(2,1)S(1)} collective-permute-done((bf16[56,1024]{1,0:T(8,128)(2,1)S(1)}, bf16[56,1024]{1,0:T(8,128)(2,1)S(1)}, u32[]{:S(2)}, u32[]{:S(2)}) %collective-permute-start.4) | collective-permute-done | bytes 114720 | tf_op jit(solution)/shard_map/exchange_in/ppermute | solution.py:52
  25.6 0.8 %forward_own.1 = (f32[128,512]{1,0:T(8,128)S(1)}, f32[128,512]{1,0:T(8,128)S(1)}, f32[8,128]{1,0:T(8,128)S(1)}) custom-call(bf16[128,2048]{1,0:T(8,128)(2,1)S(1)} %stack.2.refs_0_, bf16[1,4096,512]{2,1,0:T(8,128)(2,1)S(1)} %get-tuple-element.56.refs_1_.refs_3_, bf16[1,4096,512]{2,1,0:T(8,128)(2,1)S(1)} %get-tuple-element.57.refs_2_.refs_4_), custom_call_target="tpu_custom_call" | custom-call | tf_op jit(solution)/shard_map/gather_in/forward_own/forward_own/pallas_call | solution.py:481
  26.4 1.6 %collective-permute-done.7.refs_6_.refs_1_ = bf16[56,1024]{1,0:T(8,128)(2,1)S(1)} collective-permute-done((bf16[56,1024]{1,0:T(8,128)(2,1)S(1)}, bf16[56,1024]{1,0:T(8,128)(2,1)S(1)}, u32[]{:S(2)}, u32[]{:S(2)}) %collective-permute-start.7) | collective-permute-done | bytes 114720 | tf_op jit(solution)/shard_map/exchange_grad/ppermute | solution.py:52
  28.1 0.7 %collective-permute-done.15.refs_2_ = bf16[56,1024]{1,0:T(8,128)(2,1)S(1)} collective-permute-done((bf16[56,1024]{1,0:T(8,128)(2,1)S(1)}, bf16[56,1024]{1,0:T(8,128)(2,1)S(1)}, u32[]{:S(2)}, u32[]{:S(2)}) %collective-permute-start.15) | collective-permute-done | bytes 114720 | tf_op jit(solution)/shard_map/exchange_grad/ppermute | solution.py:52
  29.0 1.4 %forward.1 = (f32[128,512]{1,0:T(8,128)S(1)}, f32[128,512]{1,0:T(8,128)S(1)}, bf16[128,512]{1,0:T(8,128)(2,1)S(1)}, bf16[128,2048]{1,0:T(8,128)(2,1)S(1)}, bf16[128,2048]{1,0:T(8,128)(2,1)S(1)}) custom-call(f32[128,512]{1,0:T(8,128)S(1)} %get-tuple-element.58.refs_0_, f32[128,512]{1,0:T(8,128)S(1)} %get-tuple-element.59.refs_1_, ...), custom_call_target="tpu_custom_call" | custom-call | tf_op jit(solution)/shard_map/forward/forward/pallas_call | solution.py:493
  30.4 0.5 collective-permute-start.8
  31.4 1.2 %backward.1 = (bf16[128,512]{1,0:T(8,128)(2,1)S(1)}, bf16[128,512]{1,0:T(8,128)(2,1)S(1)}, bf16[128,2048]{1,0:T(8,128)(2,1)S(1)}) custom-call(f32[128,512]{1,0:T(8,128)S(1)} %backward_own.1.refs_0_, bf16[128,2048]{1,0:T(8,128)(2,1)S(1)} %collective-permute-done.17.refs_1_, bf16[512,4096]{1,0:T(8,128)(2,1)S(1)} %get-tuple-element.81.refs_2_, ...), custom_call_target="tpu_custom_call" | custom-call | tf_op jit(solution)/shard_map/backward/backward/pallas_call | solution.py:549
  32.9 1.6 %collective-permute-start.9 = (bf16[56,1024]{1,0:T(8,128)(2,1)S(1)}, bf16[56,1024]{1,0:T(8,128)(2,1)S(1)}, u32[]{:S(2)}, u32[]{:S(2)}) collective-permute-start(bf16[56,1024]{1,0:T(8,128)(2,1)S(1)} %get-tuple-element.66), channel_id=1, source_target_pairs={{0,6},{2,4},{4,2},{6,0},{8,14},{10,12},{12,10},{14,8},{16,22},{18,... | collective-permute-start | bytes 344072 | tf_op jit(solution)/shard_map/return_out/ppermute | solution.py:52
  34.4 1.3 %collective-permute-start.10 = (bf16[56,1024]{1,0:T(8,128)(2,1)S(1)}, bf16[56,1024]{1,0:T(8,128)(2,1)S(1)}, u32[]{:S(2)}, u32[]{:S(2)}) collective-permute-start(bf16[56,1024]{1,0:T(8,128)(2,1)S(1)} %get-tuple-element.67), channel_id=1, source_target_pairs={{0,4},{2,6},{4,0},{6,2},{8,12},{10,14},{12,8},{14,10},{16,20},{18,... | collective-permute-start | bytes 344072 | tf_op jit(solution)/shard_map/return_out/ppermute | solution.py:52
  35.7 0.7 %collective-permute-start.11 = (bf16[56,1024]{1,0:T(8,128)(2,1)S(1)}, bf16[56,1024]{1,0:T(8,128)(2,1)S(1)}, u32[]{:S(2)}, u32[]{:S(2)}) collective-permute-start(bf16[56,1024]{1,0:T(8,128)(2,1)S(1)} %get-tuple-element.68), channel_id=1, source_target_pairs={{0,2},{2,0},{4,6},{6,4},{8,10},{10,8},{12,14},{14,12},{16,18},{18,... | collective-permute-start | bytes 344072 | tf_op jit(solution)/shard_map/return_out/ppermute | solution.py:52
  36.4 0.7 %input_own.1.refs_0_ = bf16[128,2048]{1,0:T(8,128)(2,1)S(1)} custom-call(bf16[128,512]{1,0:T(8,128)(2,1)S(1)} %get-tuple-element.85.refs_0_, bf16[128,512]{1,0:T(8,128)(2,1)S(1)} %get-tuple-element.86.refs_1_, bf16[512,4096]{1,0:T(8,128)(2,1)S(1)} %get-tuple-element.81.refs_2_, bf16[512,4096]{1,0:T(8,128)(2,1)S(1)} %get-tuple-element.82.refs_3_, ...), custom_call_target="tpu_custom_call" | custom-call | tf_op jit(solution)/shard_map/backward/input_own/pallas_call | solution.py:557
  37.3 1.5 %collective-permute-start.19 = (bf16[56,1024]{1,0:T(8,128)(2,1)S(1)}, bf16[56,1024]{1,0:T(8,128)(2,1)S(1)}, u32[]{:S(2)}, u32[]{:S(2)}) collective-permute-start(bf16[56,1024]{1,0:T(8,128)(2,1)S(1)} %get-tuple-element.89), channel_id=1, source_target_pairs={{0,6},{2,4},{4,2},{6,0},{8,14},{10,12},{12,10},{14,8},{16,22},{18,... | collective-permute-start | bytes 344072 | tf_op jit(solution)/shard_map/return_grad/ppermute | solution.py:52
  38.9 1.3 %collective-permute-start.20 = (bf16[56,1024]{1,0:T(8,128)(2,1)S(1)}, bf16[56,1024]{1,0:T(8,128)(2,1)S(1)}, u32[]{:S(2)}, u32[]{:S(2)}) collective-permute-start(bf16[56,1024]{1,0:T(8,128)(2,1)S(1)} %get-tuple-element.90), channel_id=1, source_target_pairs={{0,4},{2,6},{4,0},{6,2},{8,12},{10,14},{12,8},{14,10},{16,20},{18,... | collective-permute-start | bytes 344072 | tf_op jit(solution)/shard_map/return_grad/ppermute | solution.py:52
  40.2 1.0 %collective-permute-start.21 = (bf16[56,1024]{1,0:T(8,128)(2,1)S(1)}, bf16[56,1024]{1,0:T(8,128)(2,1)S(1)}, u32[]{:S(2)}, u32[]{:S(2)}) collective-permute-start(bf16[56,1024]{1,0:T(8,128)(2,1)S(1)} %get-tuple-element.91), channel_id=1, source_target_pairs={{0,2},{2,0},{4,6},{6,4},{8,10},{10,8},{12,14},{14,12},{16,18},{18,... | collective-permute-start | bytes 344072 | tf_op jit(solution)/shard_map/return_grad/ppermute | solution.py:52
  41.2 1.2 %collective-permute-done.10.refs_2_ = bf16[56,1024]{1,0:T(8,128)(2,1)S(1)} collective-permute-done((bf16[56,1024]{1,0:T(8,128)(2,1)S(1)}, bf16[56,1024]{1,0:T(8,128)(2,1)S(1)}, u32[]{:S(2)}, u32[]{:S(2)}) %collective-permute-start.10) | collective-permute-done | bytes 114720 | tf_op jit(solution)/shard_map/return_out/ppermute | solution.py:52
  42.6 2.4 %collective-permute-start.12 = (bf16[24,1024]{1,0:T(8,128)(2,1)S(1)}, bf16[24,1024]{1,0:T(8,128)(2,1)S(1)}, u32[]{:S(2)}, u32[]{:S(2)}) collective-permute-start(bf16[24,1024]{1,0:T(8,128)(2,1)S(1)} %get-tuple-element.72), channel_id=1, source_target_pairs={{0,24},{2,26},{4,28},{6,30},{8,16},{10,18},{12,20},{14,22},{16,8},... | collective-permute-start | bytes 147464 | tf_op jit(solution)/shard_map/return_out/ppermute | solution.py:44
  45.1 2.0 %collective-permute-start.14 = (bf16[24,1024]{1,0:T(8,128)(2,1)S(1)}, bf16[24,1024]{1,0:T(8,128)(2,1)S(1)}, u32[]{:S(2)}, u32[]{:S(2)}) collective-permute-start(bf16[24,1024]{1,0:T(8,128)(2,1)S(1)} %get-tuple-element.74), channel_id=1, source_target_pairs={{0,8},{2,10},{4,12},{6,14},{8,0},{10,2},{12,4},{14,6},{16,24},{18,... | collective-permute-start | bytes 147464 | tf_op jit(solution)/shard_map/return_out/ppermute | solution.py:44
  47.3 2.4 %collective-permute-start.22 = (bf16[24,1024]{1,0:T(8,128)(2,1)S(1)}, bf16[24,1024]{1,0:T(8,128)(2,1)S(1)}, u32[]{:S(2)}, u32[]{:S(2)}) collective-permute-start(bf16[24,1024]{1,0:T(8,128)(2,1)S(1)} %get-tuple-element.93), channel_id=1, source_target_pairs={{0,24},{2,26},{4,28},{6,30},{8,16},{10,18},{12,20},{14,22},{16,8},... | collective-permute-start | bytes 147464 | tf_op jit(solution)/shard_map/return_grad/ppermute | solution.py:44
  49.7 2.0 %collective-permute-start.24 = (bf16[24,1024]{1,0:T(8,128)(2,1)S(1)}, bf16[24,1024]{1,0:T(8,128)(2,1)S(1)}, u32[]{:S(2)}, u32[]{:S(2)}) collective-permute-start(bf16[24,1024]{1,0:T(8,128)(2,1)S(1)} %get-tuple-element.95), channel_id=1, source_target_pairs={{0,8},{2,10},{4,12},{6,14},{8,0},{10,2},{12,4},{14,6},{16,24},{18,... | collective-permute-start | bytes 147464 | tf_op jit(solution)/shard_map/return_grad/ppermute | solution.py:44
  51.8 2.4 %down_grad.1 = bf16[1,512,4096]{2,1,0:T(8,128)(2,1)} custom-call(bf16[128,2048]{1,0:T(8,128)(2,1)S(1)} %stack.3.rows.refs_0_, bf16[128,2048]{1,0:T(8,128)(2,1)S(1)} %collective-permute-done.17.refs_1_, bf16[128,512]{1,0:T(8,128)(2,1)S(1)} %get-tuple-element.98.refs_2_, bf16[24,1024]{1,0:T(8,128)(2,1)S(1)} %get-tuple-element.92.refs_0_.refs_3_), custom_call_target="tpu_custom_call" | custom-call | tf_op jit(solution)/shard_map/down_grad/down_grad/pallas_call | solution.py:572
  54.2 0.7 %final.2 = (bf16[12,2048]{1,0:T(8,128)(2,1)}, f32[8,128]{1,0:T(8,128)S(1)}) custom-call(bf16[24,1024]{1,0:T(8,128)(2,1)S(1)} %get-tuple-element.71.refs_0_, bf16[24,1024]{1,0:T(8,128)(2,1)S(1)} %collective-permute-done.12.refs_1_, bf16[24,1024]{1,0:T(8,128)(2,1)S(1)} %collective-permute-done.13.refs_2_, bf16[24,1024]{1,0:T(8,128)(2,1)S(1)} %collective-permute-done.14.refs_3_), custom_call_target="tpu_custom_call" | custom-call | tf_op jit(solution)/shard_map/final/pallas_call | solution.py:526
  54.8 0.7 %final.3 = (bf16[12,2048]{1,0:T(8,128)(2,1)}, f32[8,128]{1,0:T(8,128)}) custom-call(bf16[24,1024]{1,0:T(8,128)(2,1)S(1)} %get-tuple-element.92.refs_0_.refs_3_, bf16[24,1024]{1,0:T(8,128)(2,1)S(1)} %collective-permute-done.22.refs_1_, bf16[24,1024]{1,0:T(8,128)(2,1)S(1)} %collective-permute-done.23.refs_2_, ...), custom_call_target="tpu_custom_call" | custom-call | tf_op jit(solution)/shard_map/final/pallas_call | solution.py:526
  (36 shorter events, 3.4 us)
Async XLA Ops:
  1.8 11.2 %collective-permute-start = (bf16[8,6272]{1,0:T(8,128)(2,1)S(1)}, bf16[8,6272]{1,0:T(8,128)(2,1)S(1)}, u32[]{:S(2)}, u32[]{:S(2)}) collective-permute-start(bf16[8,6272]{1,0:T(8,128)(2,1)S(1)} %prepare.1.refs_3_.refs_0_), channel_id=1, source_target_pairs={{0,24},{2,26},{4,28},{6,30},{8,16},{10,18},{12,20},{14,22},{16,8},... | collective-permute-start | bytes 301064 | tf_op jit(solution)/shard_map/gather_blocks/ppermute | solution.py:44
  6.9 8.4 %collective-permute-start.1 = (bf16[8,6272]{1,0:T(8,128)(2,1)S(1)}, bf16[8,6272]{1,0:T(8,128)(2,1)S(1)}, u32[]{:S(2)}, u32[]{:S(2)}) collective-permute-start(bf16[8,6272]{1,0:T(8,128)(2,1)S(1)} %prepare.1.refs_3_.refs_0_), channel_id=1, source_target_pairs={{0,16},{2,18},{4,20},{6,22},{8,24},{10,26},{12,28},{14,30},{16,0},... | collective-permute-start | bytes 301064 | tf_op jit(solution)/shard_map/gather_blocks/ppermute | solution.py:44
  6.9 8.4 %collective-permute-start.2 = (bf16[8,6272]{1,0:T(8,128)(2,1)S(1)}, bf16[8,6272]{1,0:T(8,128)(2,1)S(1)}, u32[]{:S(2)}, u32[]{:S(2)}) collective-permute-start(bf16[8,6272]{1,0:T(8,128)(2,1)S(1)} %prepare.1.refs_3_.refs_0_), channel_id=1, source_target_pairs={{0,8},{2,10},{4,12},{6,14},{8,0},{10,2},{12,4},{14,6},{16,24},{18,... | collective-permute-start | bytes 301064 | tf_op jit(solution)/shard_map/gather_blocks/ppermute | solution.py:44
  16.1 7.3 %collective-permute-start.3 = (bf16[56,1024]{1,0:T(8,128)(2,1)S(1)}, bf16[56,1024]{1,0:T(8,128)(2,1)S(1)}, u32[]{:S(2)}, u32[]{:S(2)}) collective-permute-start(bf16[56,1024]{1,0:T(8,128)(2,1)S(1)} %get-tuple-element.53), channel_id=1, source_target_pairs={{0,6},{2,4},{4,2},{6,0},{8,14},{10,12},{12,10},{14,8},{16,22},{18,... | collective-permute-start | bytes 344072 | tf_op jit(solution)/shard_map/exchange_in/ppermute | solution.py:52
  18.6 6.9 %collective-permute-start.4 = (bf16[56,1024]{1,0:T(8,128)(2,1)S(1)}, bf16[56,1024]{1,0:T(8,128)(2,1)S(1)}, u32[]{:S(2)}, u32[]{:S(2)}) collective-permute-start(bf16[56,1024]{1,0:T(8,128)(2,1)S(1)} %get-tuple-element.54), channel_id=1, source_target_pairs={{0,4},{2,6},{4,0},{6,2},{8,12},{10,14},{12,8},{14,10},{16,20},{18,... | collective-permute-start | bytes 344072 | tf_op jit(solution)/shard_map/exchange_in/ppermute | solution.py:52
  19.1 6.4 %collective-permute-start.5 = (bf16[56,1024]{1,0:T(8,128)(2,1)S(1)}, bf16[56,1024]{1,0:T(8,128)(2,1)S(1)}, u32[]{:S(2)}, u32[]{:S(2)}) collective-permute-start(bf16[56,1024]{1,0:T(8,128)(2,1)S(1)} %get-tuple-element.55), channel_id=1, source_target_pairs={{0,2},{2,0},{4,6},{6,4},{8,10},{10,8},{12,14},{14,12},{16,18},{18,... | collective-permute-start | bytes 344072 | tf_op jit(solution)/shard_map/exchange_in/ppermute | solution.py:52
  20.4 7.7 %collective-permute-start.7 = (bf16[56,1024]{1,0:T(8,128)(2,1)S(1)}, bf16[56,1024]{1,0:T(8,128)(2,1)S(1)}, u32[]{:S(2)}, u32[]{:S(2)}) collective-permute-start(bf16[56,1024]{1,0:T(8,128)(2,1)S(1)} %get-tuple-element.62), channel_id=1, source_target_pairs={{0,6},{2,4},{4,2},{6,0},{8,14},{10,12},{12,10},{14,8},{16,22},{18,... | collective-permute-start | bytes 344072 | tf_op jit(solution)/shard_map/exchange_grad/ppermute | solution.py:52
  22.9 5.9 %collective-permute-start.15 = (bf16[56,1024]{1,0:T(8,128)(2,1)S(1)}, bf16[56,1024]{1,0:T(8,128)(2,1)S(1)}, u32[]{:S(2)}, u32[]{:S(2)}) collective-permute-start(bf16[56,1024]{1,0:T(8,128)(2,1)S(1)} %get-tuple-element.77), channel_id=1, source_target_pairs={{0,4},{2,6},{4,0},{6,2},{8,12},{10,14},{12,8},{14,10},{16,20},{18,... | collective-permute-start | bytes 344072 | tf_op jit(solution)/shard_map/exchange_grad/ppermute | solution.py:52
  23.4 5.5 %collective-permute-start.16 = (bf16[56,1024]{1,0:T(8,128)(2,1)S(1)}, bf16[56,1024]{1,0:T(8,128)(2,1)S(1)}, u32[]{:S(2)}, u32[]{:S(2)}) collective-permute-start(bf16[56,1024]{1,0:T(8,128)(2,1)S(1)} %get-tuple-element.78), channel_id=1, source_target_pairs={{0,2},{2,0},{4,6},{6,4},{8,10},{10,8},{12,14},{14,12},{16,18},{18,... | collective-permute-start | bytes 344072 | tf_op jit(solution)/shard_map/exchange_grad/ppermute | solution.py:52
  25.6 3.5 %collective-permute-start.6 = (bf16[128,2048]{1,0:T(8,128)(2,1)S(1)}, bf16[128,2048]{1,0:T(8,128)(2,1)S(1)}, u32[]{:S(2)}, u32[]{:S(2)}) collective-permute-start(bf16[128,2048]{1,0:T(8,128)(2,1)S(1)} %stack.2.refs_0_), channel_id=1, source_target_pairs={{0,1},{1,0},{2,3},{3,2},{4,5},{5,4},{6,7},{7,6},{8,9},{9,8},{10,11... | collective-permute-start | bytes 1572872 | tf_op jit(solution)/shard_map/gather_in/ppermute | solution.py:57
  28.9 2.5 %collective-permute-start.17 = (bf16[128,2048]{1,0:T(8,128)(2,1)S(1)}, bf16[128,2048]{1,0:T(8,128)(2,1)S(1)}, u32[]{:S(2)}, u32[]{:S(2)}) collective-permute-start(bf16[128,2048]{1,0:T(8,128)(2,1)S(1)} %stack.3.rows.refs_0_), channel_id=1, source_target_pairs={{0,1},{1,0},{2,3},{3,2},{4,5},{5,4},{6,7},{7,6},{8,9},{9,8},{10,11... | collective-permute-start | bytes 1572872 | tf_op jit(solution)/shard_map/gather_in/ppermute | solution.py:57
  30.4 2.3 %collective-permute-start.8 = (bf16[128,2048]{1,0:T(8,128)(2,1)S(1)}, bf16[128,2048]{1,0:T(8,128)(2,1)S(1)}, u32[]{:S(2)}, u32[]{:S(2)}) collective-permute-start(bf16[128,2048]{1,0:T(8,128)(2,1)S(1)} %get-tuple-element.64), channel_id=1, source_target_pairs={{0,1},{1,0},{2,3},{3,2},{4,5},{5,4},{6,7},{7,6},{8,9},{9,8},{10,11... | collective-permute-start | bytes 1572872 | tf_op jit(solution)/shard_map/return_out/ppermute | solution.py:57
  32.6 4.5 %collective-permute-start.18 = (bf16[128,2048]{1,0:T(8,128)(2,1)S(1)}, bf16[128,2048]{1,0:T(8,128)(2,1)S(1)}, u32[]{:S(2)}, u32[]{:S(2)}) collective-permute-start(bf16[128,2048]{1,0:T(8,128)(2,1)S(1)} %get-tuple-element.87), channel_id=1, source_target_pairs={{0,1},{1,0},{2,3},{3,2},{4,5},{5,4},{6,7},{7,6},{8,9},{9,8},{10,11... | collective-permute-start | bytes 1572872 | tf_op jit(solution)/shard_map/return_grad/ppermute | solution.py:57
  32.9 7.3 %collective-permute-start.9 = (bf16[56,1024]{1,0:T(8,128)(2,1)S(1)}, bf16[56,1024]{1,0:T(8,128)(2,1)S(1)}, u32[]{:S(2)}, u32[]{:S(2)}) collective-permute-start(bf16[56,1024]{1,0:T(8,128)(2,1)S(1)} %get-tuple-element.66), channel_id=1, source_target_pairs={{0,6},{2,4},{4,2},{6,0},{8,14},{10,12},{12,10},{14,8},{16,22},{18,... | collective-permute-start | bytes 344072 | tf_op jit(solution)/shard_map/return_out/ppermute | solution.py:52
  34.4 7.9 %collective-permute-start.10 = (bf16[56,1024]{1,0:T(8,128)(2,1)S(1)}, bf16[56,1024]{1,0:T(8,128)(2,1)S(1)}, u32[]{:S(2)}, u32[]{:S(2)}) collective-permute-start(bf16[56,1024]{1,0:T(8,128)(2,1)S(1)} %get-tuple-element.67), channel_id=1, source_target_pairs={{0,4},{2,6},{4,0},{6,2},{8,12},{10,14},{12,8},{14,10},{16,20},{18,... | collective-permute-start | bytes 344072 | tf_op jit(solution)/shard_map/return_out/ppermute | solution.py:52
  35.7 6.6 %collective-permute-start.11 = (bf16[56,1024]{1,0:T(8,128)(2,1)S(1)}, bf16[56,1024]{1,0:T(8,128)(2,1)S(1)}, u32[]{:S(2)}, u32[]{:S(2)}) collective-permute-start(bf16[56,1024]{1,0:T(8,128)(2,1)S(1)} %get-tuple-element.68), channel_id=1, source_target_pairs={{0,2},{2,0},{4,6},{6,4},{8,10},{10,8},{12,14},{14,12},{16,18},{18,... | collective-permute-start | bytes 344072 | tf_op jit(solution)/shard_map/return_out/ppermute | solution.py:52
  37.3 7.7 %collective-permute-start.19 = (bf16[56,1024]{1,0:T(8,128)(2,1)S(1)}, bf16[56,1024]{1,0:T(8,128)(2,1)S(1)}, u32[]{:S(2)}, u32[]{:S(2)}) collective-permute-start(bf16[56,1024]{1,0:T(8,128)(2,1)S(1)} %get-tuple-element.89), channel_id=1, source_target_pairs={{0,6},{2,4},{4,2},{6,0},{8,14},{10,12},{12,10},{14,8},{16,22},{18,... | collective-permute-start | bytes 344072 | tf_op jit(solution)/shard_map/return_grad/ppermute | solution.py:52
  38.9 8.2 %collective-permute-start.20 = (bf16[56,1024]{1,0:T(8,128)(2,1)S(1)}, bf16[56,1024]{1,0:T(8,128)(2,1)S(1)}, u32[]{:S(2)}, u32[]{:S(2)}) collective-permute-start(bf16[56,1024]{1,0:T(8,128)(2,1)S(1)} %get-tuple-element.90), channel_id=1, source_target_pairs={{0,4},{2,6},{4,0},{6,2},{8,12},{10,14},{12,8},{14,10},{16,20},{18,... | collective-permute-start | bytes 344072 | tf_op jit(solution)/shard_map/return_grad/ppermute | solution.py:52
  40.2 6.9 %collective-permute-start.21 = (bf16[56,1024]{1,0:T(8,128)(2,1)S(1)}, bf16[56,1024]{1,0:T(8,128)(2,1)S(1)}, u32[]{:S(2)}, u32[]{:S(2)}) collective-permute-start(bf16[56,1024]{1,0:T(8,128)(2,1)S(1)} %get-tuple-element.91), channel_id=1, source_target_pairs={{0,2},{2,0},{4,6},{6,4},{8,10},{10,8},{12,14},{14,12},{16,18},{18,... | collective-permute-start | bytes 344072 | tf_op jit(solution)/shard_map/return_grad/ppermute | solution.py:52
  42.6 7.1 %collective-permute-start.12 = (bf16[24,1024]{1,0:T(8,128)(2,1)S(1)}, bf16[24,1024]{1,0:T(8,128)(2,1)S(1)}, u32[]{:S(2)}, u32[]{:S(2)}) collective-permute-start(bf16[24,1024]{1,0:T(8,128)(2,1)S(1)} %get-tuple-element.72), channel_id=1, source_target_pairs={{0,24},{2,26},{4,28},{6,30},{8,16},{10,18},{12,20},{14,22},{16,8},... | collective-permute-start | bytes 147464 | tf_op jit(solution)/shard_map/return_out/ppermute | solution.py:44
  45.1 9.1 %collective-permute-start.13 = (bf16[24,1024]{1,0:T(8,128)(2,1)S(1)}, bf16[24,1024]{1,0:T(8,128)(2,1)S(1)}, u32[]{:S(2)}, u32[]{:S(2)}) collective-permute-start(bf16[24,1024]{1,0:T(8,128)(2,1)S(1)} %get-tuple-element.73), channel_id=1, source_target_pairs={{0,16},{2,18},{4,20},{6,22},{8,24},{10,26},{12,28},{14,30},{16,0},... | collective-permute-start | bytes 147464 | tf_op jit(solution)/shard_map/return_out/ppermute | solution.py:44
  45.1 9.1 %collective-permute-start.14 = (bf16[24,1024]{1,0:T(8,128)(2,1)S(1)}, bf16[24,1024]{1,0:T(8,128)(2,1)S(1)}, u32[]{:S(2)}, u32[]{:S(2)}) collective-permute-start(bf16[24,1024]{1,0:T(8,128)(2,1)S(1)} %get-tuple-element.74), channel_id=1, source_target_pairs={{0,8},{2,10},{4,12},{6,14},{8,0},{10,2},{12,4},{14,6},{16,24},{18,... | collective-permute-start | bytes 147464 | tf_op jit(solution)/shard_map/return_out/ppermute | solution.py:44
  47.3 7.5 %collective-permute-start.22 = (bf16[24,1024]{1,0:T(8,128)(2,1)S(1)}, bf16[24,1024]{1,0:T(8,128)(2,1)S(1)}, u32[]{:S(2)}, u32[]{:S(2)}) collective-permute-start(bf16[24,1024]{1,0:T(8,128)(2,1)S(1)} %get-tuple-element.93), channel_id=1, source_target_pairs={{0,24},{2,26},{4,28},{6,30},{8,16},{10,18},{12,20},{14,22},{16,8},... | collective-permute-start | bytes 147464 | tf_op jit(solution)/shard_map/return_grad/ppermute | solution.py:44
  49.7 5.1 %collective-permute-start.23 = (bf16[24,1024]{1,0:T(8,128)(2,1)S(1)}, bf16[24,1024]{1,0:T(8,128)(2,1)S(1)}, u32[]{:S(2)}, u32[]{:S(2)}) collective-permute-start(bf16[24,1024]{1,0:T(8,128)(2,1)S(1)} %get-tuple-element.94), channel_id=1, source_target_pairs={{0,16},{2,18},{4,20},{6,22},{8,24},{10,26},{12,28},{14,30},{16,0},... | collective-permute-start | bytes 147464 | tf_op jit(solution)/shard_map/return_grad/ppermute | solution.py:44
  49.7 5.1 %collective-permute-start.24 = (bf16[24,1024]{1,0:T(8,128)(2,1)S(1)}, bf16[24,1024]{1,0:T(8,128)(2,1)S(1)}, u32[]{:S(2)}, u32[]{:S(2)}) collective-permute-start(bf16[24,1024]{1,0:T(8,128)(2,1)S(1)} %get-tuple-element.95), channel_id=1, source_target_pairs={{0,8},{2,10},{4,12},{6,14},{8,0},{10,2},{12,4},{14,6},{16,24},{18,... | collective-permute-start | bytes 147464 | tf_op jit(solution)/shard_map/return_grad/ppermute | solution.py:44

commit v7 on v6

v7 whole, which is shorter than its diff:
```python
import functools
import jax
import jax.numpy as jnp
from jax import lax
from jax.experimental import pallas as pl
from jax.experimental.pallas import tpu as pltpu
from jax.sharding import PartitionSpec as P

BF16 = jnp.bfloat16
F32 = jnp.float32
META = 128
COSTS = {"PREPARE": 20, "ROUTE0": 9, "ROUTE1": 9}
SUBLANES = 8
VMEM_LIMIT = 20 * 1024 * 1024


def group_sizes(experts):
    inner = 1
    while inner * inner * 4 <= experts and experts % (inner * 2) == 0:
        inner *= 2
    return experts // inner, inner


def partner(index, step, size):
    return index ^ step if size & (size - 1) == 0 else (index + step) % size


def origin(index, step, size):
    return index ^ step if size & (size - 1) == 0 else (index - step) % size


def traced_partner(index, step, size):
    return index ^ step if size & (size - 1) == 0 else lax.rem(index + step, size)


def traced_origin(index, step, size):
    return index ^ step if size & (size - 1) == 0 else lax.rem(index + size - step, size)


def send_outer(x, step, outer, inner, back=False):
    move = origin if back else partner
    pairs = [
        (a * inner + b, move(a, step, outer) * inner + b) for a in range(outer) for b in range(inner)
    ]
    return lax.ppermute(x, "expert", pairs)


def send_inner(x, step, outer, inner, back=False):
    move = origin if back else partner
    pairs = [
        (a * inner + b, a * inner + move(b, step, inner)) for a in range(outer) for b in range(inner)
    ]
    return lax.ppermute(x, "expert", pairs)


def send_core(x, step, cores, back=False):
    move = origin if back else partner
    return lax.ppermute(x, "etp", [(i, move(i, step, cores)) for i in range(cores)])


def flipped(parts):
    return [parts[0], *parts[:0:-1]]


def contract(left, right, left_dim, right_dim):
    return lax.dot_general(
        left, right, (((left_dim,), (right_dim,)), ((), ())), preferred_element_type=F32
    )


def whole_specs(count):
    return [pl.BlockSpec(memory_space=pltpu.VMEM)] * count


def any_specs(count):
    return [pl.BlockSpec(memory_space=pl.ANY)] * count


def cost(name):
    return pl.CostEstimate(flops=int(COSTS.get(name, 0) * 1e9) + 1, bytes_accessed=1, transcendentals=0)


def params():
    return pltpu.CompilerParams(vmem_limit_bytes=VMEM_LIMIT)


def in_hbm(x):
    return pltpu.with_memory_space_constraint(x, pltpu.HBM)


def hbm_specs(count):
    return [pl.BlockSpec(memory_space=pltpu.HBM)] * count


def prepare_kernel(dims, *refs):
    tokens, top, half = dims
    sources, out_ref, held, sems = refs[:4], refs[4], refs[5:9], refs[9]
    copies = [pltpu.make_async_copy(a, b, sems.at[n]) for n, (a, b) in enumerate(zip(sources, held))]
    for copy in copies:
        copy.start()
    for copy in copies:
        copy.wait()
    ids_ref, gates_ref, hidden_ref, grad_ref = held
    gates = gates_ref[...]
    gate_hi = gates.astype(BF16)
    rest = gates - gate_hi.astype(F32)
    gate_mid = rest.astype(BF16)
    gate_lo = rest - gate_mid.astype(F32)
    values = [ids_ref[...].astype(F32), gate_hi.astype(F32), gate_mid.astype(F32), gate_lo]
    values = jnp.concatenate(values, axis=0).astype(BF16)
    entry = lax.broadcasted_iota(jnp.int32, (4 * top, META), 0)
    lane = lax.broadcasted_iota(jnp.int32, (4 * top, META), 1)
    meta = contract(values, (lane == entry).astype(F32).astype(BF16), 0, 0)
    meta = jnp.concatenate([meta, meta], axis=0)
    tiles = 2 * tokens // SUBLANES
    for n, source in enumerate((hidden_ref, grad_ref)):
        value = source[...].astype(F32)
        value = jnp.concatenate([value[:, :half], value[:, half:]], axis=0)
        for i in range(tiles):
            start = (n * tiles + i) * half
            out_ref[:, start : start + half] = value[i * SUBLANES : (i + 1) * SUBLANES].astype(BF16)
    packed = meta[:SUBLANES]
    for i in range(1, tiles):
        packed = packed + pltpu.roll(meta[i * SUBLANES : (i + 1) * SUBLANES], i * 4 * top, 1)
    out_ref[:, 2 * tiles * half :] = packed.astype(BF16)


def block_rows(blocks, start, width, tiles, shift=0):
    parts = []
    for block in blocks:
        for i in range(tiles):
            if shift:
                part = block[:, start : start + width].astype(F32)
                parts.append(pltpu.roll(part, width - i * shift, 1) if i else part)
            else:
                parts.append(block[:, start + i * width : start + (i + 1) * width].astype(F32))
    return jnp.concatenate(parts, axis=0)


def stacked(refs):
    return jnp.concatenate([r[...].astype(F32) for r in refs], axis=0).astype(BF16)


def count_above(index, unit, total):
    value = jnp.zeros_like(index)
    for m in range(unit, total, unit):
        value = value + (index >= m).astype(jnp.int32)
    return value


def routing(blocks, fold, dims):
    inner, tokens, top, cap, half = dims
    tiles = 2 * tokens // SUBLANES
    rows = len(blocks) * 2 * tokens
    shape = (rows, inner * fold)
    me = lax.axis_index("expert")
    my_inner = lax.rem(me, inner)
    my_base = me - my_inner
    lane = lax.broadcasted_iota(jnp.int32, shape, 1)
    step = count_above(lane, fold, shape[1])
    dest = jnp.zeros(shape, F32)
    for q in range(inner):
        expert = (my_base + traced_partner(my_inner, q, inner)).astype(F32)
        dest = jnp.where(step == q, expert, dest)
    meta = block_rows(blocks, 2 * tiles * half, META, tiles, 4 * top)
    named = jnp.zeros(shape, F32)
    gate = jnp.zeros(shape, F32)
    for k in range(top):
        hit = meta[:, k : k + 1] == dest
        value = sum(meta[:, n * top + k : n * top + k + 1] for n in range(1, 4))
        named = jnp.where(hit, 1.0, named)
        gate = jnp.where(hit, value, gate)
    left = lax.broadcasted_iota(jnp.int32, (rows, rows), 1)
    down = lax.broadcasted_iota(jnp.int32, (rows, rows), 0)
    same = count_above(left, tokens, rows) == count_above(down, tokens, rows)
    before = (same & (left < down)).astype(F32).astype(BF16)
    rank = jnp.dot(before, named.astype(BF16), preferred_element_type=F32)
    row = lax.broadcasted_iota(jnp.int32, (rows, 1), 0)
    block = count_above(row, 2 * tokens, rows)
    row_side = count_above(row, tokens, rows) - 2 * block
    position = block * cap + rank.astype(jnp.int32)
    return lane - step * fold, named, gate, position, row_side


def gate_parts(gate):
    gate_hi = gate.astype(BF16)
    rest = gate - gate_hi.astype(F32)
    gate_mid = rest.astype(BF16)
    return gate_hi, gate_mid, (rest - gate_mid.astype(F32)).astype(BF16)


def route_kernel(dims, count, reach, *refs):
    inner, tokens, top, cap, half = dims
    blocks = refs[:count]
    sends = refs[-inner:]
    fold = 4 * reach
    tiles = 2 * tokens // SUBLANES
    lane, named, gate, position, row_side = routing(blocks, fold, dims)
    segment = count_above(lane, reach, fold)
    grads = segment >= 2
    side = segment - 2 * grads.astype(jnp.int32)
    pick = jnp.where((position == lane - segment * reach) & (row_side == side), named, 0.0)
    pick_in = jnp.where(grads, 0.0, pick).astype(BF16)
    pick_grad = jnp.where(grads, pick, 0.0).astype(BF16)
    ones = jnp.ones((pick.shape[0], META), BF16)
    column = sum(contract(part, ones, 0, 0) for part in gate_parts(pick * gate))
    table = block_rows(blocks, 0, half, tiles).astype(BF16)
    out = contract(pick_in, table, 0, 0)
    table = block_rows(blocks, tiles * half, half, tiles).astype(BF16)
    out = out + contract(pick_grad, table, 0, 0) * column[:, :1]
    for q, send in enumerate(sends):
        send[...] = out[q * fold : (q + 1) * fold].astype(BF16)


def tables_kernel(dims, count, reach, *refs):
    pick_ref, gate_hi_ref, gate_mid_ref, _ = refs[-4:]
    lane, named, gate, position, row_side = routing(refs[:count], 2 * reach, dims)
    side = (lane >= reach).astype(jnp.int32)
    pick = jnp.where((position == lane - side * reach) & (row_side == side), named, 0.0)
    pick_ref[...] = pick.astype(BF16)
    gate_hi_ref[...], gate_mid_ref[...], _ = gate_parts(pick * gate)


def stack_kernel(dims, *refs):
    inner, reach, held = dims
    fold, half = refs[0].shape
    values = stacked(flipped(refs[:inner]))
    rows = inner * held
    row = lax.broadcasted_iota(jnp.int32, (rows, 1), 0)
    step = count_above(row, held, rows)
    item = row - step * held
    column = lax.broadcasted_iota(jnp.int32, (rows, inner * fold), 1)
    wanted = jnp.where(item < reach, step * fold + item, -4 * reach)
    chosen = [(column == wanted + n * reach).astype(F32) for n in range(4)]
    out = jnp.dot(jnp.concatenate(chosen, axis=0).astype(BF16), values, preferred_element_type=F32)
    for segment in range(4):
        array, side = divmod(segment, 2)
        part = out[segment * rows : (segment + 1) * rows].astype(BF16)
        refs[-1][array * rows : (array + 1) * rows, side * half : (side + 1) * half] = part


def turn_kernel(count, *refs):
    for source, target in zip(refs[:count], refs[count + 1 : -1]):
        target[...] = source[0].T


def core_spans(cores, width, move):
    core = lax.axis_index("etp")
    return [pl.ds(pl.multiple_of(move(core, d, cores) * width, width), width) for d in range(cores)]


def array_rows(stacks, sizes, array):
    return jnp.concatenate([s[array * n : (array + 1) * n, :] for s, n in zip(stacks, sizes)], axis=0)


def forward_own_kernel(dims, sizes, *refs):
    gate_w, up_w, gate_ref, up_ref = refs[len(sizes) :]
    rows = array_rows(refs, sizes, 0)
    span = core_spans(*dims, traced_origin)[0]
    gate_ref[...] = jnp.dot(rows, gate_w[0, span, :], preferred_element_type=F32)
    up_ref[...] = jnp.dot(rows, up_w[0, span, :], preferred_element_type=F32)


def forward_kernel(dims, sizes, *refs):
    cores, width = dims
    groups = len(sizes)
    gate_own, up_own, gate_w, up_w, down_w, *stacks = refs[: 5 + groups * (cores - 1)]
    gate_ref, up_ref, act_ref, *parts = refs[-(3 + cores) :]
    spans = core_spans(cores, width, traced_origin)
    gate_pre = gate_own[...]
    up_pre = up_own[...]
    for n, span in enumerate(spans[1:]):
        rows = array_rows(stacks[n * groups : (n + 1) * groups], sizes, 0)
        gate_pre = gate_pre + jnp.dot(rows, gate_w[0, span, :], preferred_element_type=F32)
        up_pre = up_pre + jnp.dot(rows, up_w[0, span, :], preferred_element_type=F32)
    act = (gate_pre * jax.nn.sigmoid(gate_pre) * up_pre).astype(BF16)
    gate_ref[...] = gate_pre
    up_ref[...] = up_pre
    act_ref[...] = act
    spans = core_spans(cores, width, traced_partner)
    for d in reversed(range(cores)):
        parts[d][...] = jnp.dot(act, down_w[0, :, spans[d]], preferred_element_type=F32).astype(BF16)


def backward_own_kernel(dims, sizes, *refs):
    down_t, out_ref = refs[len(sizes)], refs[-1]
    rows = array_rows(refs, sizes, 1)
    span = core_spans(*dims, traced_origin)[0]
    out_ref[...] = jnp.dot(rows, down_t[span, :], preferred_element_type=F32)


def backward_kernel(dims, sizes, *refs):
    cores, width = dims
    groups = len(sizes)
    act_own, gate_t, up_t, down_t, gate_ref, up_ref, *stacks = refs[: 6 + groups * (cores - 1)]
    gate_out, up_out, *parts = refs[-(cores + 1) :]
    spans = core_spans(cores, width, traced_origin)
    act_grad = act_own[...]
    for n, span in enumerate(spans[1:]):
        rows = array_rows(stacks[n * groups : (n + 1) * groups], sizes, 1)
        act_grad = act_grad + jnp.dot(rows, down_t[span, :], preferred_element_type=F32)
    gate_pre = gate_ref[...]
    sigmoid = jax.nn.sigmoid(gate_pre)
    gate_grad = (act_grad * up_ref[...] * sigmoid * (1.0 + gate_pre * (1.0 - sigmoid))).astype(BF16)
    up_grad = (act_grad * (gate_pre * sigmoid)).astype(BF16)
    gate_out[...] = gate_grad
    up_out[...] = up_grad
    spans = core_spans(cores, width, traced_partner)
    for part, span in zip(parts, spans[1:]):
        value = jnp.dot(gate_grad, gate_t[:, span], preferred_element_type=F32)
        value = value + jnp.dot(up_grad, up_t[:, span], preferred_element_type=F32)
        part[...] = value.astype(BF16)


def input_own_kernel(dims, *refs):
    gate_grad, up_grad, gate_t, up_t = refs[:4]
    span = core_spans(*dims, traced_partner)[0]
    value = jnp.dot(gate_grad[...], gate_t[:, span], preferred_element_type=F32)
    value = value + jnp.dot(up_grad[...], up_t[:, span], preferred_element_type=F32)
    refs[-1][...] = value.astype(BF16)


def down_kernel(dims, sizes, chunks, *refs):
    cores, width = dims
    groups = len(sizes)
    act_ref = refs[cores * groups]
    out_hbm, result, out_sems = refs[-3:]
    core = lax.axis_index("etp")
    act = act_ref[...].T
    chunk = width // chunks
    copies = []
    for d in range(cores):
        rows = array_rows(refs[d * groups : (d + 1) * groups], sizes, 1)
        base = traced_origin(core, d, cores) * width
        for n in range(chunks):
            slot = d * chunks + n
            value = jnp.dot(act, rows[:, n * chunk : (n + 1) * chunk], preferred_element_type=F32)
            result[slot] = value.astype(BF16)
            span = pl.ds(pl.multiple_of(base + n * chunk, chunk), chunk)
            copy = pltpu.make_async_copy(result.at[slot], out_hbm.at[0, :, span], out_sems.at[slot])
            copy.start()
            copies.append(copy)
    for copy in copies:
        copy.wait()


def split_kernel(dims, groups, *refs):
    cores, inner, reach = dims
    total = refs[0][...].astype(F32)
    for part in refs[1:cores]:
        total = total + part[...].astype(F32)
    total = total.astype(BF16)
    half = total.shape[1] // 2
    fold = 2 * reach
    row = lax.broadcasted_iota(jnp.int32, (inner * fold, 1), 0)
    step = count_above(row, fold, inner * fold)
    place = row - step * fold
    row_side = (place >= reach).astype(jnp.int32)
    slot = place - row_side * reach
    wanted = jnp.zeros_like(row)
    first = 0
    base = 0
    for size, held in groups:
        wanted = jnp.where(slot >= first, base + step * held + slot - first, wanted)
        first += size
        base += inner * held
    column = lax.broadcasted_iota(jnp.int32, (inner * fold, total.shape[0]), 1)
    out = None
    for side in range(2):
        chosen = ((column == wanted) & (row_side == side)).astype(F32).astype(BF16)
        term = jnp.dot(chosen, total[:, side * half : (side + 1) * half], preferred_element_type=F32)
        out = term if out is None else out + term
    for q in range(inner):
        refs[q - inner][...] = out[q * fold : (q + 1) * fold].astype(BF16)


def combine_kernel(dims, weighted, *refs):
    outer, inner, unit = dims
    tables = refs[inner : inner + weighted]
    outs = refs[-outer:]
    rows = stacked(flipped(refs[:inner]))
    total = None
    for table in tables:
        term = jnp.dot(table[...], rows, preferred_element_type=F32)
        total = term if total is None else total + term
    for b in range(outer):
        outs[b][...] = total[b * unit : (b + 1) * unit].astype(BF16)


def final_kernel(dims, *refs):
    outer, tokens, half = dims
    out_ref = refs[-2]
    total = refs[0][...].astype(F32)
    for part in refs[1:outer]:
        total = total + part[...].astype(F32)
    out_ref[:, :half] = total[:tokens].astype(BF16)
    out_ref[:, half:] = total[tokens:].astype(BF16)


def shape(rows, columns, kind=BF16):
    return jax.ShapeDtypeStruct((rows, columns), kind)


def on_device(hidden_in, expert_ids, gate_weights, out_grad, gate_weight, up_weight, down_weight):
    tokens, top = expert_ids.shape
    experts = lax.axis_size("expert")
    cores = lax.axis_size("etp")
    outer, inner = group_sizes(experts)
    cap = min(tokens, tokens * top // experts + 1)
    width = hidden_in.shape[1]
    half = width // 2
    hidden = gate_weight.shape[2]
    reach = outer * cap
    unit = 2 * tokens
    near = min(2, outer)
    groups = [g for g in (range(near), range(near, outer)) if len(g)]
    sizes = [(len(g) * cap, -(-len(g) * cap // 16) * 16) for g in groups]
    route_dims = (inner, tokens, top, cap, half)

    with jax.named_scope("prepare"):
        packed = pl.pallas_call(
            functools.partial(prepare_kernel, (tokens, top, half)),
            out_shape=shape(SUBLANES, 2 * unit // SUBLANES * half + META),
            in_specs=hbm_specs(4),
            out_specs=pl.BlockSpec(memory_space=pltpu.VMEM),
            scratch_shapes=[
                pltpu.VMEM((top, tokens), jnp.int32),
                pltpu.VMEM((top, tokens), F32),
                pltpu.VMEM((tokens, width), BF16),
                pltpu.VMEM((tokens, width), BF16),
                pltpu.SemaphoreType.DMA((4,)),
            ],
            compiler_params=params(),
            cost_estimate=cost("PREPARE"),
            name="prepare",
        )(in_hbm(expert_ids.T), in_hbm(gate_weights.T), in_hbm(hidden_in), in_hbm(out_grad))

    with jax.named_scope("gather_blocks"):
        blocks = [packed] + [send_outer(packed, s, outer, inner) for s in range(1, outer)]

    piece_shapes = [shape(2 * reach, half)] * inner
    table_shape = shape(outer * unit, inner * 2 * reach)
    token_shape = shape(8, META, F32)
    weights = [pltpu.with_memory_space_constraint(w, pltpu.VMEM) for w in (gate_weight, up_weight, down_weight)]
    dims = (cores, width)

    def route(g, after=()):
        members = [blocks[i] for i in groups[g]]
        size = sizes[g][0]
        return pl.pallas_call(
            functools.partial(route_kernel, route_dims, len(members), size),
            out_shape=[shape(4 * size, half)] * inner,
            in_specs=whole_specs(len(members) + len(after)),
            out_specs=whole_specs(inner),
            compiler_params=params(),
            cost_estimate=cost(f"ROUTE{g}"),
            name=f"route{g}",
        )(*members, *after)

    def spread(sends):
        return [sends[0]] + [send_inner(sends[q], q, outer, inner) for q in range(1, inner)]

    def gather_cores(g, pieces, after=()):
        size, held = sizes[g]
        stack = pl.pallas_call(
            functools.partial(stack_kernel, (inner, size, held)),
            out_shape=shape(2 * inner * held, width),
            in_specs=whole_specs(inner) + any_specs(len(after)),
            out_specs=pl.BlockSpec(memory_space=pltpu.VMEM),
            compiler_params=params(),
            cost_estimate=cost(f"STACK{g}"),
            name=f"stack{g}",
        )(*flipped(pieces), *after)
        return [stack] + [send_core(stack, d, cores) for d in range(1, cores)]

    with jax.named_scope("near_blocks"):
        sends = route(0)
        near_pieces = spread(sends)
    def turn(picked, after, name):
        return pl.pallas_call(
            functools.partial(turn_kernel, len(picked)),
            out_shape=[pltpu.VMEM((w.shape[2], w.shape[1]), BF16) for w in picked] + [token_shape],
            in_specs=whole_specs(len(picked)) + any_specs(1),
            out_specs=whole_specs(len(picked) + 1),
            compiler_params=params(),
            cost_estimate=cost(name.upper()),
            name=name,
        )(*picked, after)

    with jax.named_scope("turn_weights"):
        down_t, ready = turn(weights[2:], sends[0], "turn_down")
    with jax.named_scope("far_blocks"):
        far_pieces = [spread(route(g, (ready,))) for g in range(1, len(groups))]
    with jax.named_scope("turn_weights"):
        gate_t, up_t, turned = turn(weights[:2], (far_pieces or [near_pieces])[0][0], "turn_rest")
    with jax.named_scope("tables"):
        pick, gate_hi, gate_lo, listed = pl.pallas_call(
            functools.partial(tables_kernel, route_dims, outer, reach),
            out_shape=[table_shape] * 3 + [token_shape],
            in_specs=whole_specs(outer) + any_specs(1),
            out_specs=whole_specs(4),
            compiler_params=params(),
            cost_estimate=cost("TABLES"),
            name="tables",
        )(*blocks, sends[0])
    counts = [inner * held for _, held in sizes]
    rows = sum(counts)
    with jax.named_scope("gather_cores"):
        stacks = [gather_cores(0, near_pieces, [pieces[0] for pieces in far_pieces])]
        for g, pieces in enumerate(far_pieces, 1):
            stacks.append(gather_cores(g, pieces, (listed, turned)))
        own_stacks = [stack[0] for stack in stacks]
        other_stacks = [stack[d] for d in range(1, cores) for stack in stacks]

    with jax.named_scope("forward"):
        own = pl.pallas_call(
            functools.partial(forward_own_kernel, dims, counts),
            out_shape=[shape(rows, hidden, F32)] * 2,
            in_specs=whole_specs(len(counts) + 2),
            out_specs=whole_specs(2),
            compiler_params=params(),
            cost_estimate=cost("FORWARD_OWN"),
            name="forward_own",
        )(*own_stacks, *weights[:2])
        gate_pre, up_pre, act, *out_parts = pl.pallas_call(
            functools.partial(forward_kernel, dims, counts),
            out_shape=[shape(rows, hidden, F32)] * 2 + [shape(rows, hidden)] + [shape(rows, width)] * cores,
            in_specs=whole_specs(5 + len(other_stacks)),
            out_specs=whole_specs(3 + cores),
            compiler_params=params(),
            cost_estimate=cost("FORWARD"),
            name="forward",
        )(*own, *weights, *other_stacks)

    def give_back(parts, after=()):
        got = [parts[0]] + [send_core(parts[d], d, cores) for d in range(1, cores)]
        sends = pl.pallas_call(
            functools.partial(split_kernel, (cores, inner, reach), sizes),
            out_shape=piece_shapes,
            in_specs=whole_specs(cores) + any_specs(len(after)),
            out_specs=whole_specs(inner),
            compiler_params=params(),
            name="split",
        )(*got, *after)
        return [sends[0]] + [send_inner(sends[q], q, outer, inner, back=True) for q in range(1, inner)]

    def combine(pieces, tables):
        blocks = pl.pallas_call(
            functools.partial(combine_kernel, (outer, inner, unit), len(tables)),
            out_shape=[shape(unit, half)] * outer,
            in_specs=whole_specs(inner + len(tables)),
            out_specs=whole_specs(outer),
            compiler_params=params(),
            name="combine",
        )(*flipped(pieces), *tables)
        return [blocks[0]] + [send_outer(blocks[s], s, outer, inner, back=True) for s in range(1, outer)]

    def finish(blocks, after=()):
        return pl.pallas_call(
            functools.partial(final_kernel, (outer, tokens, half)),
            out_shape=[shape(tokens, width), shape(8, META, F32)],
            in_specs=whole_specs(outer + len(after)),
            out_specs=whole_specs(2),
            compiler_params=params(),
            name="final",
        )(*flipped(blocks), *after)

    with jax.named_scope("return_out"):
        out_back = give_back(out_parts)
        out_blocks = combine(out_back, (gate_hi, gate_lo))

    with jax.named_scope("backward"):
        act_own = pl.pallas_call(
            functools.partial(backward_own_kernel, dims, counts),
            out_shape=shape(rows, hidden, F32),
            in_specs=whole_specs(len(counts) + 1),
            out_specs=pl.BlockSpec(memory_space=pltpu.VMEM),
            compiler_params=params(),
            cost_estimate=cost("BACKWARD_OWN"),
            name="backward_own",
        )(*own_stacks, down_t)
        gate_grad, up_grad, *grad_parts = pl.pallas_call(
            functools.partial(backward_kernel, dims, counts),
            out_shape=[shape(rows, hidden)] * 2 + [shape(rows, width)] * (cores - 1),
            in_specs=whole_specs(6 + len(other_stacks)),
            out_specs=whole_specs(cores + 1),
            compiler_params=params(),
            cost_estimate=cost("BACKWARD"),
            name="backward",
        )(act_own, gate_t, up_t, down_t, gate_pre, up_pre, *other_stacks)
        own_part = pl.pallas_call(
            functools.partial(input_own_kernel, dims),
            out_shape=shape(rows, width),
            in_specs=whole_specs(4) + any_specs(1),
            out_specs=pl.BlockSpec(memory_space=pltpu.VMEM),
            compiler_params=params(),
            cost_estimate=cost("INPUT_OWN"),
            name="input_own",
        )(gate_grad, up_grad, gate_t, up_t, out_back[0])
        grad_parts = [own_part, *grad_parts]

    with jax.named_scope("return_grad"):
        back_blocks = combine(give_back(grad_parts, out_back[:1]), (pick,))

    with jax.named_scope("down_grad"):
        chunks = max(1, width // 512)
        down_grad = pl.pallas_call(
            functools.partial(down_kernel, dims, counts, chunks),
            out_shape=pltpu.HBM(down_weight.shape, BF16),
            in_specs=whole_specs(cores * len(groups) + 1) + any_specs(1),
            out_specs=pl.BlockSpec(memory_space=pltpu.HBM),
            scratch_shapes=[
                pltpu.VMEM((cores * chunks, hidden, width // chunks), BF16),
                pltpu.SemaphoreType.DMA((cores * chunks,)),
            ],
            compiler_params=params(),
            name="down_grad",
        )(*own_stacks, *other_stacks, act, back_blocks[0])

    mixed_out, done = finish(out_blocks)
    input_grad, done = finish(back_blocks, (done,))
    return (mixed_out, input_grad, down_grad)


def solution(mesh):
    return jax.shard_map(
        on_device,
        mesh=mesh,
        in_specs=(
            P("expert", "etp"),
            P("expert", None),
            P("expert", None),
            P("expert", "etp"),
            P("expert", None, "etp"),
            P("expert", None, "etp"),
            P("expert", "etp", None),
        ),
        out_specs=(P("expert", "etp"), P("expert", "etp"), P("expert", "etp", None)),
        check_vma=False,
    )
```

time: 55.7 us -> 53.9 us (0.968)
  starting transfers between devices: 30.6 us -> 29.6 us
  waiting for transfers between devices: 6.86 us -> 6.14 us
    ppermute x12, waiting for transfers between devices: 4.48 us -> 2.19 us  [send_inner(): return lax.ppermute(x, 'expert', pairs)]
    ppermute x4, waiting for transfers between devices: 0.01 us -> 1.14 us  [send_core(): lax.ppermute(x, 'etp', [(i, move(i, step, cores)) for i in range(cores)])]
    ppermute x12, starting transfers between devices: 15.2 us -> 14.2 us  [send_inner(): return lax.ppermute(x, 'expert', pairs)]
    pallas_call x12 -> x14, Pallas kernels: 13.5 us -> 13.4 us  [the longest x2 3.56 us: turn(): pl.pallas_call(functools.partial(turn_kernel, len(picked)), out_shape=[pl...]
  transfers between devices with their start and end apart: 25 -> 25, of which waited for: 6 -> 7; matrix products, arithmetic and copies ran while one was open for 0% -> 0% of each run, Pallas kernels for 26% -> 26%
where the time goes in v7:
time: 53.9 us; the launch traced here: 53.8 us
  starting transfers between devices  29.6 us (55%)
  Pallas kernels  17.2 us (32%)
  waiting for transfers between devices  6.14 us (11%)
  between operations  0.86 us (2%)
    ppermute x9, starting transfers between devices, send_outer(): return lax.ppermute(x, 'expert', pairs)  14.6 us
    ppermute x12, starting transfers between devices, send_inner(): return lax.ppermute(x, 'expert', pairs)  14.2 us
    pallas_call x2, Pallas kernels, turn(): pl.pallas_call(functools.partial(turn_kernel, len(picked)), out_shape=[pl...  3.56 us
    ppermute x9, waiting for transfers between devices, send_outer(): return lax.ppermute(x, 'expert', pairs)  2.8 us
    pallas_call x1, Pallas kernels, on_device(): pl.pallas_call(functools.partial(down_kernel, dims, counts, chunks), out_...  2.38 us
    ppermute x12, waiting for transfers between devices, send_inner(): return lax.ppermute(x, 'expert', pairs)  2.19 us
    pallas_call x2, Pallas kernels, route(): pl.pallas_call(functools.partial(route_kernel, route_dims, len(members),...  1.72 us
    pallas_call x1, Pallas kernels, on_device(): pl.pallas_call(functools.partial(forward_kernel, dims, counts), out_shape...  1.43 us
  transfers between devices with their start and end apart: 25, of which 7 were waited for; matrix products, arithmetic and copies ran while one was open for 0% of the time, Pallas kernels for 26%

profile of v7, /device:TPU:0, one launch (start us, length us, event | category | flops | bytes accessed | tf_op | source)
XLA Modules:
  0.0 53.8 jit_solution(15826352494276584179)
XLA Ops:
  0.6 1.2 %prepare.1.refs_0_ = bf16[8,6272]{1,0:T(8,128)(2,1)S(1)} custom-call(s32[8,12]{1,0:T(8,128)} %bitcast.2, f32[8,12]{1,0:T(8,128)} %bitcast.3, bf16[12,2048]{1,0:T(8,128)(2,1)} %refs_2_.3, bf16[12,2048]{1,0:T(8,128)(2,1)} %refs_3_.3), custom_call_target="tpu_custom_call" | custom-call | flops 20000000000 | bytes 1 | tf_op jit(solution)/shard_map/prepare/prepare/pallas_call | solution.py:421
  1.8 3.1 %collective-permute-start = (bf16[8,6272]{1,0:T(8,128)(2,1)S(1)}, bf16[8,6272]{1,0:T(8,128)(2,1)S(1)}, u32[]{:S(2)}, u32[]{:S(2)}) collective-permute-start(bf16[8,6272]{1,0:T(8,128)(2,1)S(1)} %prepare.1.refs_0_), channel_id=1, source_target_pairs={{0,8},{2,10},{4,12},{6,14},{8,0},{10,2},{12,4},{14,6},{16,24},{18,... | collective-permute-start | bytes 301064 | tf_op jit(solution)/shard_map/gather_blocks/ppermute | solution.py:45
  4.9 2.6 %collective-permute-start.4 = (bf16[8,6272]{1,0:T(8,128)(2,1)S(1)}, bf16[8,6272]{1,0:T(8,128)(2,1)S(1)}, u32[]{:S(2)}, u32[]{:S(2)}) collective-permute-start(bf16[8,6272]{1,0:T(8,128)(2,1)S(1)} %prepare.1.refs_0_), channel_id=1, source_target_pairs={{0,16},{2,18},{4,20},{6,22},{8,24},{10,26},{12,28},{14,30},{16,0},... | collective-permute-start | bytes 301064 | tf_op jit(solution)/shard_map/gather_blocks/ppermute | solution.py:45
  7.8 0.9 %route0.1 = (bf16[56,1024]{1,0:T(8,128)(2,1)S(1)}, bf16[56,1024]{1,0:T(8,128)(2,1)S(1)}, bf16[56,1024]{1,0:T(8,128)(2,1)S(1)}, bf16[56,1024]{1,0:T(8,128)(2,1)S(1)}) custom-call(bf16[8,6272]{1,0:T(8,128)(2,1)S(1)} %prepare.1.refs_0_, bf16[8,6272]{1,0:T(8,128)(2,1)S(1)} %collective-permute-done.refs_1_), custom_call_target="tpu_custom_call" | custom-call | flops 9000000512 | bytes 1 | tf_op jit(solution)/shard_map/near_blocks/route0/pallas_call | solution.py:450
  8.6 2.8 %collective-permute-start.1 = (bf16[56,1024]{1,0:T(8,128)(2,1)S(1)}, bf16[56,1024]{1,0:T(8,128)(2,1)S(1)}, u32[]{:S(2)}, u32[]{:S(2)}) collective-permute-start(bf16[56,1024]{1,0:T(8,128)(2,1)S(1)} %get-tuple-element.50), channel_id=1, source_target_pairs={{0,6},{2,4},{4,2},{6,0},{8,14},{10,12},{12,10},{14,8},{16,22},{18,... | collective-permute-start | bytes 344072 | tf_op jit(solution)/shard_map/near_blocks/ppermute | solution.py:53
  12.2 1.2 %turn_down.1 = (bf16[4096,512]{1,0:T(8,128)(2,1)S(1)}, f32[8,128]{1,0:T(8,128)S(1)}) custom-call(bf16[1,512,4096]{2,1,0:T(8,128)(2,1)S(1)} %copy-done.2, bf16[56,1024]{1,0:T(8,128)(2,1)S(1)} %get-tuple-element.49.refs_1_.refs_0_.refs_4_), custom_call_target="tpu_custom_call" | custom-call | flops 1 | bytes 1 | tf_op jit(solution)/shard_map/turn_weights/turn_down/pallas_call | solution.py:480
  13.3 2.2 %collective-permute-done.4.refs_0_.refs_2_ = bf16[8,6272]{1,0:T(8,128)(2,1)S(1)} collective-permute-done((bf16[8,6272]{1,0:T(8,128)(2,1)S(1)}, bf16[8,6272]{1,0:T(8,128)(2,1)S(1)}, u32[]{:S(2)}, u32[]{:S(2)}) %collective-permute-start.4) | collective-permute-done | bytes 100384 | tf_op jit(solution)/shard_map/gather_blocks/ppermute | solution.py:45
  15.5 0.9 %route1.1 = (bf16[56,1024]{1,0:T(8,128)(2,1)S(1)}, bf16[56,1024]{1,0:T(8,128)(2,1)S(1)}, bf16[56,1024]{1,0:T(8,128)(2,1)S(1)}, bf16[56,1024]{1,0:T(8,128)(2,1)S(1)}) custom-call(bf16[8,6272]{1,0:T(8,128)(2,1)S(1)} %collective-permute-done.4.refs_0_.refs_2_, bf16[8,6272]{1,0:T(8,128)(2,1)S(1)} %collective-permute-done.5.refs_1_.refs_3_, ...), custom_call_target="tpu_custom_call" | custom-call | flops 9000000512 | bytes 1 | tf_op jit(solution)/shard_map/far_blocks/route1/pallas_call | solution.py:450
  16.4 2.5 %collective-permute-start.6 = (bf16[56,1024]{1,0:T(8,128)(2,1)S(1)}, bf16[56,1024]{1,0:T(8,128)(2,1)S(1)}, u32[]{:S(2)}, u32[]{:S(2)}) collective-permute-start(bf16[56,1024]{1,0:T(8,128)(2,1)S(1)} %get-tuple-element.55), channel_id=1, source_target_pairs={{0,6},{2,4},{4,2},{6,0},{8,14},{10,12},{12,10},{14,8},{16,22},{18,... | collective-permute-start | bytes 344072 | tf_op jit(solution)/shard_map/far_blocks/ppermute | solution.py:53
  18.9 0.5 collective-permute-start.7
  19.4 0.5 %collective-permute-start.8 = (bf16[56,1024]{1,0:T(8,128)(2,1)S(1)}, bf16[56,1024]{1,0:T(8,128)(2,1)S(1)}, u32[]{:S(2)}, u32[]{:S(2)}) collective-permute-start(bf16[56,1024]{1,0:T(8,128)(2,1)S(1)} %get-tuple-element.57), channel_id=1, source_target_pairs={{0,2},{2,0},{4,6},{6,4},{8,10},{10,8},{12,14},{14,12},{16,18},{18,... | collective-permute-start | bytes 344072 | tf_op jit(solution)/shard_map/far_blocks/ppermute | solution.py:53
  19.9 2.4 %turn_rest.1 = (bf16[512,4096]{1,0:T(8,128)(2,1)S(1)}, bf16[512,4096]{1,0:T(8,128)(2,1)S(1)}, f32[8,128]{1,0:T(8,128)S(1)}) custom-call(bf16[1,4096,512]{2,1,0:T(8,128)(2,1)S(1)} %copy-done, bf16[1,4096,512]{2,1,0:T(8,128)(2,1)S(1)} %copy-done.1, bf16[56,1024]{1,0:T(8,128)(2,1)S(1)} %get-tuple-element.54.refs_4_.refs_2_.refs_0_), custom_call_target="tpu_custom_call" | custom-call | flops 1 | bytes 1 | tf_op jit(solution)/shard_map/turn_weights/turn_rest/pallas_call | solution.py:480
  23.3 0.8 %collective-permute-done.7.refs_2_ = bf16[56,1024]{1,0:T(8,128)(2,1)S(1)} collective-permute-done((bf16[56,1024]{1,0:T(8,128)(2,1)S(1)}, bf16[56,1024]{1,0:T(8,128)(2,1)S(1)}, u32[]{:S(2)}, u32[]{:S(2)}) %collective-permute-start.7) | collective-permute-done | bytes 114720 | tf_op jit(solution)/shard_map/far_blocks/ppermute | solution.py:53
  24.6 0.7 %forward_own.1 = (f32[128,512]{1,0:T(8,128)S(1)}, f32[128,512]{1,0:T(8,128)S(1)}) custom-call(bf16[128,2048]{1,0:T(8,128)(2,1)S(1)} %stack0.1.refs_0_, bf16[128,2048]{1,0:T(8,128)(2,1)S(1)} %stack1.1.refs_1_, bf16[1,4096,512]{2,1,0:T(8,128)(2,1)S(1)} %copy-done, bf16[1,4096,512]{2,1,0:T(8,128)(2,1)S(1)} %copy-done.1), custom_call_target="tpu_custom_call" | custom-call | flops 1 | bytes 1 | tf_op jit(solution)/shard_map/forward/forward_own/pallas_call | solution.py:516
  25.3 1.1 %collective-permute-done.10.refs_6_.refs_7_.refs_3_ = bf16[128,2048]{1,0:T(8,128)(2,1)S(1)} collective-permute-done((bf16[128,2048]{1,0:T(8,128)(2,1)S(1)}, bf16[128,2048]{1,0:T(8,128)(2,1)S(1)}, u32[]{:S(2)}, u32[]{:S(2)}) %collective-permute-start.10) | collective-permute-done | bytes 524320 | tf_op jit(solution)/shard_map/gather_cores/ppermute | solution.py:58
  26.5 1.4 %forward.1 = (f32[128,512]{1,0:T(8,128)S(1)}, f32[128,512]{1,0:T(8,128)S(1)}, bf16[128,512]{1,0:T(8,128)(2,1)S(1)}, bf16[128,2048]{1,0:T(8,128)(2,1)S(1)}, bf16[128,2048]{1,0:T(8,128)(2,1)S(1)}) custom-call(f32[128,512]{1,0:T(8,128)S(1)} %get-tuple-element.60.refs_0_, f32[128,512]{1,0:T(8,128)S(1)} %get-tuple-element.61.refs_1_, ...), custom_call_target="tpu_custom_call" | custom-call | flops 1 | bytes 1 | tf_op jit(solution)/shard_map/forward/forward/pallas_call | solution.py:525
  28.6 1.2 %backward.1 = (bf16[128,512]{1,0:T(8,128)(2,1)S(1)}, bf16[128,512]{1,0:T(8,128)(2,1)S(1)}, bf16[128,2048]{1,0:T(8,128)(2,1)S(1)}) custom-call(f32[128,512]{1,0:T(8,128)S(1)} %backward_own.1.refs_0_, bf16[512,4096]{1,0:T(8,128)(2,1)S(1)} %get-tuple-element.76.refs_1_.refs_2_, bf16[512,4096]{1,0:T(8,128)(2,1)S(1)} %get-tuple-element.77.refs_2_.refs_3_, ...), custom_call_target="tpu_custom_call" | custom-call | flops 1 | bytes 1 | tf_op jit(solution)/shard_map/backward/backward/pallas_call | solution.py:582
  30.6 1.9 %collective-permute-start.12 = (bf16[56,1024]{1,0:T(8,128)(2,1)S(1)}, bf16[56,1024]{1,0:T(8,128)(2,1)S(1)}, u32[]{:S(2)}, u32[]{:S(2)}) collective-permute-start(bf16[56,1024]{1,0:T(8,128)(2,1)S(1)} %get-tuple-element.65), channel_id=1, source_target_pairs={{0,6},{2,4},{4,2},{6,0},{8,14},{10,12},{12,10},{14,8},{16,22},{18,... | collective-permute-start | bytes 344072 | tf_op jit(solution)/shard_map/return_out/ppermute | solution.py:53
  32.6 0.5 collective-permute-start.13
  33.1 1.1 %collective-permute-start.14 = (bf16[56,1024]{1,0:T(8,128)(2,1)S(1)}, bf16[56,1024]{1,0:T(8,128)(2,1)S(1)}, u32[]{:S(2)}, u32[]{:S(2)}) collective-permute-start(bf16[56,1024]{1,0:T(8,128)(2,1)S(1)} %get-tuple-element.67), channel_id=1, source_target_pairs={{0,2},{2,0},{4,6},{6,4},{8,10},{10,8},{12,14},{14,12},{16,18},{18,... | collective-permute-start | bytes 344072 | tf_op jit(solution)/shard_map/return_out/ppermute | solution.py:53
  34.2 0.8 %input_own.1.refs_0_ = bf16[128,2048]{1,0:T(8,128)(2,1)S(1)} custom-call(bf16[128,512]{1,0:T(8,128)(2,1)S(1)} %get-tuple-element.80.refs_0_, bf16[128,512]{1,0:T(8,128)(2,1)S(1)} %get-tuple-element.81.refs_1_, bf16[512,4096]{1,0:T(8,128)(2,1)S(1)} %get-tuple-element.76.refs_1_.refs_2_, bf16[512,4096]{1,0:T(8,128)(2,1)S(1)} %get-tuple-element.77.refs_2_.refs_3_, ...), custom_call_target="tpu_custom_call" | custom-call | flops 1 | bytes 1 | tf_op jit(solution)/shard_map/backward/input_own/pallas_call | solution.py:591
  35.4 1.9 %collective-permute-start.19 = (bf16[56,1024]{1,0:T(8,128)(2,1)S(1)}, bf16[56,1024]{1,0:T(8,128)(2,1)S(1)}, u32[]{:S(2)}, u32[]{:S(2)}) collective-permute-start(bf16[56,1024]{1,0:T(8,128)(2,1)S(1)} %get-tuple-element.84), channel_id=1, source_target_pairs={{0,6},{2,4},{4,2},{6,0},{8,14},{10,12},{12,10},{14,8},{16,22},{18,... | collective-permute-start | bytes 344072 | tf_op jit(solution)/shard_map/return_grad/ppermute | solution.py:53
  37.3 0.5 collective-permute-start.20
  37.8 1.1 %collective-permute-start.21 = (bf16[56,1024]{1,0:T(8,128)(2,1)S(1)}, bf16[56,1024]{1,0:T(8,128)(2,1)S(1)}, u32[]{:S(2)}, u32[]{:S(2)}) collective-permute-start(bf16[56,1024]{1,0:T(8,128)(2,1)S(1)} %get-tuple-element.86), channel_id=1, source_target_pairs={{0,2},{2,0},{4,6},{6,4},{8,10},{10,8},{12,14},{14,12},{16,18},{18,... | collective-permute-start | bytes 344072 | tf_op jit(solution)/shard_map/return_grad/ppermute | solution.py:53
  39.0 1.2 %collective-permute-done.13.refs_2_ = bf16[56,1024]{1,0:T(8,128)(2,1)S(1)} collective-permute-done((bf16[56,1024]{1,0:T(8,128)(2,1)S(1)}, bf16[56,1024]{1,0:T(8,128)(2,1)S(1)}, u32[]{:S(2)}, u32[]{:S(2)}) %collective-permute-start.13) | collective-permute-done | bytes 114720 | tf_op jit(solution)/shard_map/return_out/ppermute | solution.py:53
  40.5 2.8 %collective-permute-start.15 = (bf16[24,1024]{1,0:T(8,128)(2,1)S(1)}, bf16[24,1024]{1,0:T(8,128)(2,1)S(1)}, u32[]{:S(2)}, u32[]{:S(2)}) collective-permute-start(bf16[24,1024]{1,0:T(8,128)(2,1)S(1)} %get-tuple-element.71), channel_id=1, source_target_pairs={{0,24},{2,26},{4,28},{6,30},{8,16},{10,18},{12,20},{14,22},{16,8},... | collective-permute-start | bytes 147464 | tf_op jit(solution)/shard_map/return_out/ppermute | solution.py:45
  43.7 1.3 %collective-permute-start.17 = (bf16[24,1024]{1,0:T(8,128)(2,1)S(1)}, bf16[24,1024]{1,0:T(8,128)(2,1)S(1)}, u32[]{:S(2)}, u32[]{:S(2)}) collective-permute-start(bf16[24,1024]{1,0:T(8,128)(2,1)S(1)} %get-tuple-element.73), channel_id=1, source_target_pairs={{0,8},{2,10},{4,12},{6,14},{8,0},{10,2},{12,4},{14,6},{16,24},{18,... | collective-permute-start | bytes 147464 | tf_op jit(solution)/shard_map/return_out/ppermute | solution.py:45
  45.2 2.8 %collective-permute-start.22 = (bf16[24,1024]{1,0:T(8,128)(2,1)S(1)}, bf16[24,1024]{1,0:T(8,128)(2,1)S(1)}, u32[]{:S(2)}, u32[]{:S(2)}) collective-permute-start(bf16[24,1024]{1,0:T(8,128)(2,1)S(1)} %get-tuple-element.89), channel_id=1, source_target_pairs={{0,24},{2,26},{4,28},{6,30},{8,16},{10,18},{12,20},{14,22},{16,8},... | collective-permute-start | bytes 147464 | tf_op jit(solution)/shard_map/return_grad/ppermute | solution.py:45
  48.0 1.7 %collective-permute-start.24 = (bf16[24,1024]{1,0:T(8,128)(2,1)S(1)}, bf16[24,1024]{1,0:T(8,128)(2,1)S(1)}, u32[]{:S(2)}, u32[]{:S(2)}) collective-permute-start(bf16[24,1024]{1,0:T(8,128)(2,1)S(1)} %get-tuple-element.91), channel_id=1, source_target_pairs={{0,8},{2,10},{4,12},{6,14},{8,0},{10,2},{12,4},{14,6},{16,24},{18,... | collective-permute-start | bytes 147464 | tf_op jit(solution)/shard_map/return_grad/ppermute | solution.py:45
  49.6 2.4 %down_grad.1 = bf16[1,512,4096]{2,1,0:T(8,128)(2,1)} custom-call(bf16[128,2048]{1,0:T(8,128)(2,1)S(1)} %stack0.1.refs_0_, bf16[128,2048]{1,0:T(8,128)(2,1)S(1)} %stack1.1.refs_1_, bf16[128,2048]{1,0:T(8,128)(2,1)S(1)} %collective-permute-done.9.refs_5_.refs_6_.refs_2_, bf16[128,2048]{1,0:T(8,128)(2,1)S(1)} %collective-permute-done.10.refs_6_.refs_7_.refs_3_, ...), custom_call_target="tpu_custom_call" | custom-call | tf_op jit(solution)/shard_map/down_grad/down_grad/pallas_call | solution.py:607
  52.0 0.7 %final.2 = (bf16[12,2048]{1,0:T(8,128)(2,1)}, f32[8,128]{1,0:T(8,128)S(1)}) custom-call(bf16[24,1024]{1,0:T(8,128)(2,1)S(1)} %get-tuple-element.70.refs_0_, bf16[24,1024]{1,0:T(8,128)(2,1)S(1)} %collective-permute-done.15.refs_1_, bf16[24,1024]{1,0:T(8,128)(2,1)S(1)} %collective-permute-done.16.refs_2_, bf16[24,1024]{1,0:T(8,128)(2,1)S(1)} %collective-permute-done.17.refs_3_), custom_call_target="tpu_custom_call" | custom-call | tf_op jit(solution)/shard_map/final/pallas_call | solution.py:559
  53.1 0.7 %final.3 = (bf16[12,2048]{1,0:T(8,128)(2,1)}, f32[8,128]{1,0:T(8,128)}) custom-call(bf16[24,1024]{1,0:T(8,128)(2,1)S(1)} %get-tuple-element.88.refs_0_.refs_5_, bf16[24,1024]{1,0:T(8,128)(2,1)S(1)} %collective-permute-done.22.refs_1_, bf16[24,1024]{1,0:T(8,128)(2,1)S(1)} %collective-permute-done.23.refs_2_, ...), custom_call_target="tpu_custom_call" | custom-call | tf_op jit(solution)/shard_map/final/pallas_call | solution.py:559
  (44 shorter events, 5.6 us)
Async XLA Ops:
  1.8 10.4 %copy-start.2 = (bf16[1,512,4096]{2,1,0:T(8,128)(2,1)S(1)}, bf16[1,512,4096]{2,1,0:T(8,128)(2,1)}, u32[]{:S(2)}) copy-start(bf16[1,512,4096]{2,1,0:T(8,128)(2,1)} %refs_4_.1) | copy-start | bytes 12582916
  1.8 5.9 %collective-permute-start = (bf16[8,6272]{1,0:T(8,128)(2,1)S(1)}, bf16[8,6272]{1,0:T(8,128)(2,1)S(1)}, u32[]{:S(2)}, u32[]{:S(2)}) collective-permute-start(bf16[8,6272]{1,0:T(8,128)(2,1)S(1)} %prepare.1.refs_0_), channel_id=1, source_target_pairs={{0,8},{2,10},{4,12},{6,14},{8,0},{10,2},{12,4},{14,6},{16,24},{18,... | collective-permute-start | bytes 301064 | tf_op jit(solution)/shard_map/gather_blocks/ppermute | solution.py:45
  4.9 10.6 %collective-permute-start.4 = (bf16[8,6272]{1,0:T(8,128)(2,1)S(1)}, bf16[8,6272]{1,0:T(8,128)(2,1)S(1)}, u32[]{:S(2)}, u32[]{:S(2)}) collective-permute-start(bf16[8,6272]{1,0:T(8,128)(2,1)S(1)} %prepare.1.refs_0_), channel_id=1, source_target_pairs={{0,16},{2,18},{4,20},{6,22},{8,24},{10,26},{12,28},{14,30},{16,0},... | collective-permute-start | bytes 301064 | tf_op jit(solution)/shard_map/gather_blocks/ppermute | solution.py:45
  7.5 8.0 %collective-permute-start.5 = (bf16[8,6272]{1,0:T(8,128)(2,1)S(1)}, bf16[8,6272]{1,0:T(8,128)(2,1)S(1)}, u32[]{:S(2)}, u32[]{:S(2)}) collective-permute-start(bf16[8,6272]{1,0:T(8,128)(2,1)S(1)} %prepare.1.refs_0_), channel_id=1, source_target_pairs={{0,24},{2,26},{4,28},{6,30},{8,16},{10,18},{12,20},{14,22},{16,8},... | collective-permute-start | bytes 301064 | tf_op jit(solution)/shard_map/gather_blocks/ppermute | solution.py:45
  8.6 10.8 %collective-permute-start.1 = (bf16[56,1024]{1,0:T(8,128)(2,1)S(1)}, bf16[56,1024]{1,0:T(8,128)(2,1)S(1)}, u32[]{:S(2)}, u32[]{:S(2)}) collective-permute-start(bf16[56,1024]{1,0:T(8,128)(2,1)S(1)} %get-tuple-element.50), channel_id=1, source_target_pairs={{0,6},{2,4},{4,2},{6,0},{8,14},{10,12},{12,10},{14,8},{16,22},{18,... | collective-permute-start | bytes 344072 | tf_op jit(solution)/shard_map/near_blocks/ppermute | solution.py:53
  11.4 11.5 %collective-permute-start.2 = (bf16[56,1024]{1,0:T(8,128)(2,1)S(1)}, bf16[56,1024]{1,0:T(8,128)(2,1)S(1)}, u32[]{:S(2)}, u32[]{:S(2)}) collective-permute-start(bf16[56,1024]{1,0:T(8,128)(2,1)S(1)} %get-tuple-element.51), channel_id=1, source_target_pairs={{0,4},{2,6},{4,0},{6,2},{8,12},{10,14},{12,8},{14,10},{16,20},{18,... | collective-permute-start | bytes 344072 | tf_op jit(solution)/shard_map/near_blocks/ppermute | solution.py:53
  11.9 11.0 %collective-permute-start.3 = (bf16[56,1024]{1,0:T(8,128)(2,1)S(1)}, bf16[56,1024]{1,0:T(8,128)(2,1)S(1)}, u32[]{:S(2)}, u32[]{:S(2)}) collective-permute-start(bf16[56,1024]{1,0:T(8,128)(2,1)S(1)} %get-tuple-element.52), channel_id=1, source_target_pairs={{0,2},{2,0},{4,6},{6,4},{8,10},{10,8},{12,14},{14,12},{16,18},{18,... | collective-permute-start | bytes 344072 | tf_op jit(solution)/shard_map/near_blocks/ppermute | solution.py:53
  15.5 4.4 %copy-start = (bf16[1,4096,512]{2,1,0:T(8,128)(2,1)S(1)}, bf16[1,4096,512]{2,1,0:T(8,128)(2,1)}, u32[]{:S(2)}) copy-start(bf16[1,4096,512]{2,1,0:T(8,128)(2,1)} %refs_2_.5) | copy-start | bytes 12582916
  15.5 4.4 %copy-start.1 = (bf16[1,4096,512]{2,1,0:T(8,128)(2,1)S(1)}, bf16[1,4096,512]{2,1,0:T(8,128)(2,1)}, u32[]{:S(2)}) copy-start(bf16[1,4096,512]{2,1,0:T(8,128)(2,1)} %refs_3_.5) | copy-start | bytes 12582916
  16.4 6.9 %collective-permute-start.6 = (bf16[56,1024]{1,0:T(8,128)(2,1)S(1)}, bf16[56,1024]{1,0:T(8,128)(2,1)S(1)}, u32[]{:S(2)}, u32[]{:S(2)}) collective-permute-start(bf16[56,1024]{1,0:T(8,128)(2,1)S(1)} %get-tuple-element.55), channel_id=1, source_target_pairs={{0,6},{2,4},{4,2},{6,0},{8,14},{10,12},{12,10},{14,8},{16,22},{18,... | collective-permute-start | bytes 344072 | tf_op jit(solution)/shard_map/far_blocks/ppermute | solution.py:53
  18.9 5.2 %collective-permute-start.7 = (bf16[56,1024]{1,0:T(8,128)(2,1)S(1)}, bf16[56,1024]{1,0:T(8,128)(2,1)S(1)}, u32[]{:S(2)}, u32[]{:S(2)}) collective-permute-start(bf16[56,1024]{1,0:T(8,128)(2,1)S(1)} %get-tuple-element.56), channel_id=1, source_target_pairs={{0,4},{2,6},{4,0},{6,2},{8,12},{10,14},{12,8},{14,10},{16,20},{18,... | collective-permute-start | bytes 344072 | tf_op jit(solution)/shard_map/far_blocks/ppermute | solution.py:53
  19.4 4.8 %collective-permute-start.8 = (bf16[56,1024]{1,0:T(8,128)(2,1)S(1)}, bf16[56,1024]{1,0:T(8,128)(2,1)S(1)}, u32[]{:S(2)}, u32[]{:S(2)}) collective-permute-start(bf16[56,1024]{1,0:T(8,128)(2,1)S(1)} %get-tuple-element.57), channel_id=1, source_target_pairs={{0,2},{2,0},{4,6},{6,4},{8,10},{10,8},{12,14},{14,12},{16,18},{18,... | collective-permute-start | bytes 344072 | tf_op jit(solution)/shard_map/far_blocks/ppermute | solution.py:53
  23.2 2.1 %collective-permute-start.9 = (bf16[128,2048]{1,0:T(8,128)(2,1)S(1)}, bf16[128,2048]{1,0:T(8,128)(2,1)S(1)}, u32[]{:S(2)}, u32[]{:S(2)}) collective-permute-start(bf16[128,2048]{1,0:T(8,128)(2,1)S(1)} %stack0.1.refs_0_), channel_id=1, source_target_pairs={{0,1},{1,0},{2,3},{3,2},{4,5},{5,4},{6,7},{7,6},{8,9},{9,8},{10,11... | collective-permute-start | bytes 1572872 | tf_op jit(solution)/shard_map/gather_cores/ppermute | solution.py:58
  24.5 2.0 %collective-permute-start.10 = (bf16[128,2048]{1,0:T(8,128)(2,1)S(1)}, bf16[128,2048]{1,0:T(8,128)(2,1)S(1)}, u32[]{:S(2)}, u32[]{:S(2)}) collective-permute-start(bf16[128,2048]{1,0:T(8,128)(2,1)S(1)} %stack1.1.refs_1_), channel_id=1, source_target_pairs={{0,1},{1,0},{2,3},{3,2},{4,5},{5,4},{6,7},{7,6},{8,9},{9,8},{10,11... | collective-permute-start | bytes 1572872 | tf_op jit(solution)/shard_map/gather_cores/ppermute | solution.py:58
  27.9 2.3 %collective-permute-start.11 = (bf16[128,2048]{1,0:T(8,128)(2,1)S(1)}, bf16[128,2048]{1,0:T(8,128)(2,1)S(1)}, u32[]{:S(2)}, u32[]{:S(2)}) collective-permute-start(bf16[128,2048]{1,0:T(8,128)(2,1)S(1)} %get-tuple-element.63), channel_id=1, source_target_pairs={{0,1},{1,0},{2,3},{3,2},{4,5},{5,4},{6,7},{7,6},{8,9},{9,8},{10,11... | collective-permute-start | bytes 1572872 | tf_op jit(solution)/shard_map/return_out/ppermute | solution.py:58
  29.8 5.2 %collective-permute-start.18 = (bf16[128,2048]{1,0:T(8,128)(2,1)S(1)}, bf16[128,2048]{1,0:T(8,128)(2,1)S(1)}, u32[]{:S(2)}, u32[]{:S(2)}) collective-permute-start(bf16[128,2048]{1,0:T(8,128)(2,1)S(1)} %get-tuple-element.82), channel_id=1, source_target_pairs={{0,1},{1,0},{2,3},{3,2},{4,5},{5,4},{6,7},{7,6},{8,9},{9,8},{10,11... | collective-permute-start | bytes 1572872 | tf_op jit(solution)/shard_map/return_grad/ppermute | solution.py:58
  30.6 7.2 %collective-permute-start.12 = (bf16[56,1024]{1,0:T(8,128)(2,1)S(1)}, bf16[56,1024]{1,0:T(8,128)(2,1)S(1)}, u32[]{:S(2)}, u32[]{:S(2)}) collective-permute-start(bf16[56,1024]{1,0:T(8,128)(2,1)S(1)} %get-tuple-element.65), channel_id=1, source_target_pairs={{0,6},{2,4},{4,2},{6,0},{8,14},{10,12},{12,10},{14,8},{16,22},{18,... | collective-permute-start | bytes 344072 | tf_op jit(solution)/shard_map/return_out/ppermute | solution.py:53
  32.6 7.6 %collective-permute-start.13 = (bf16[56,1024]{1,0:T(8,128)(2,1)S(1)}, bf16[56,1024]{1,0:T(8,128)(2,1)S(1)}, u32[]{:S(2)}, u32[]{:S(2)}) collective-permute-start(bf16[56,1024]{1,0:T(8,128)(2,1)S(1)} %get-tuple-element.66), channel_id=1, source_target_pairs={{0,4},{2,6},{4,0},{6,2},{8,12},{10,14},{12,8},{14,10},{16,20},{18,... | collective-permute-start | bytes 344072 | tf_op jit(solution)/shard_map/return_out/ppermute | solution.py:53
  33.1 7.1 %collective-permute-start.14 = (bf16[56,1024]{1,0:T(8,128)(2,1)S(1)}, bf16[56,1024]{1,0:T(8,128)(2,1)S(1)}, u32[]{:S(2)}, u32[]{:S(2)}) collective-permute-start(bf16[56,1024]{1,0:T(8,128)(2,1)S(1)} %get-tuple-element.67), channel_id=1, source_target_pairs={{0,2},{2,0},{4,6},{6,4},{8,10},{10,8},{12,14},{14,12},{16,18},{18,... | collective-permute-start | bytes 344072 | tf_op jit(solution)/shard_map/return_out/ppermute | solution.py:53
  35.4 8.3 %collective-permute-start.19 = (bf16[56,1024]{1,0:T(8,128)(2,1)S(1)}, bf16[56,1024]{1,0:T(8,128)(2,1)S(1)}, u32[]{:S(2)}, u32[]{:S(2)}) collective-permute-start(bf16[56,1024]{1,0:T(8,128)(2,1)S(1)} %get-tuple-element.84), channel_id=1, source_target_pairs={{0,6},{2,4},{4,2},{6,0},{8,14},{10,12},{12,10},{14,8},{16,22},{18,... | collective-permute-start | bytes 344072 | tf_op jit(solution)/shard_map/return_grad/ppermute | solution.py:53
  37.3 7.6 %collective-permute-start.20 = (bf16[56,1024]{1,0:T(8,128)(2,1)S(1)}, bf16[56,1024]{1,0:T(8,128)(2,1)S(1)}, u32[]{:S(2)}, u32[]{:S(2)}) collective-permute-start(bf16[56,1024]{1,0:T(8,128)(2,1)S(1)} %get-tuple-element.85), channel_id=1, source_target_pairs={{0,4},{2,6},{4,0},{6,2},{8,12},{10,14},{12,8},{14,10},{16,20},{18,... | collective-permute-start | bytes 344072 | tf_op jit(solution)/shard_map/return_grad/ppermute | solution.py:53
  37.8 7.1 %collective-permute-start.21 = (bf16[56,1024]{1,0:T(8,128)(2,1)S(1)}, bf16[56,1024]{1,0:T(8,128)(2,1)S(1)}, u32[]{:S(2)}, u32[]{:S(2)}) collective-permute-start(bf16[56,1024]{1,0:T(8,128)(2,1)S(1)} %get-tuple-element.86), channel_id=1, source_target_pairs={{0,2},{2,0},{4,6},{6,4},{8,10},{10,8},{12,14},{14,12},{16,18},{18,... | collective-permute-start | bytes 344072 | tf_op jit(solution)/shard_map/return_grad/ppermute | solution.py:53
  40.5 7.5 %collective-permute-start.15 = (bf16[24,1024]{1,0:T(8,128)(2,1)S(1)}, bf16[24,1024]{1,0:T(8,128)(2,1)S(1)}, u32[]{:S(2)}, u32[]{:S(2)}) collective-permute-start(bf16[24,1024]{1,0:T(8,128)(2,1)S(1)} %get-tuple-element.71), channel_id=1, source_target_pairs={{0,24},{2,26},{4,28},{6,30},{8,16},{10,18},{12,20},{14,22},{16,8},... | collective-permute-start | bytes 147464 | tf_op jit(solution)/shard_map/return_out/ppermute | solution.py:45
  43.3 8.7 %collective-permute-start.16 = (bf16[24,1024]{1,0:T(8,128)(2,1)S(1)}, bf16[24,1024]{1,0:T(8,128)(2,1)S(1)}, u32[]{:S(2)}, u32[]{:S(2)}) collective-permute-start(bf16[24,1024]{1,0:T(8,128)(2,1)S(1)} %get-tuple-element.72), channel_id=1, source_target_pairs={{0,16},{2,18},{4,20},{6,22},{8,24},{10,26},{12,28},{14,30},{16,0},... | collective-permute-start | bytes 147464 | tf_op jit(solution)/shard_map/return_out/ppermute | solution.py:45
  43.7 8.4 %collective-permute-start.17 = (bf16[24,1024]{1,0:T(8,128)(2,1)S(1)}, bf16[24,1024]{1,0:T(8,128)(2,1)S(1)}, u32[]{:S(2)}, u32[]{:S(2)}) collective-permute-start(bf16[24,1024]{1,0:T(8,128)(2,1)S(1)} %get-tuple-element.73), channel_id=1, source_target_pairs={{0,8},{2,10},{4,12},{6,14},{8,0},{10,2},{12,4},{14,6},{16,24},{18,... | collective-permute-start | bytes 147464 | tf_op jit(solution)/shard_map/return_out/ppermute | solution.py:45
  45.2 7.5 %collective-permute-start.22 = (bf16[24,1024]{1,0:T(8,128)(2,1)S(1)}, bf16[24,1024]{1,0:T(8,128)(2,1)S(1)}, u32[]{:S(2)}, u32[]{:S(2)}) collective-permute-start(bf16[24,1024]{1,0:T(8,128)(2,1)S(1)} %get-tuple-element.89), channel_id=1, source_target_pairs={{0,24},{2,26},{4,28},{6,30},{8,16},{10,18},{12,20},{14,22},{16,8},... | collective-permute-start | bytes 147464 | tf_op jit(solution)/shard_map/return_grad/ppermute | solution.py:45
  48.0 5.1 %collective-permute-start.23 = (bf16[24,1024]{1,0:T(8,128)(2,1)S(1)}, bf16[24,1024]{1,0:T(8,128)(2,1)S(1)}, u32[]{:S(2)}, u32[]{:S(2)}) collective-permute-start(bf16[24,1024]{1,0:T(8,128)(2,1)S(1)} %get-tuple-element.90), channel_id=1, source_target_pairs={{0,16},{2,18},{4,20},{6,22},{8,24},{10,26},{12,28},{14,30},{16,0},... | collective-permute-start | bytes 147464 | tf_op jit(solution)/shard_map/return_grad/ppermute | solution.py:45
  48.0 5.1 %collective-permute-start.24 = (bf16[24,1024]{1,0:T(8,128)(2,1)S(1)}, bf16[24,1024]{1,0:T(8,128)(2,1)S(1)}, u32[]{:S(2)}, u32[]{:S(2)}) collective-permute-start(bf16[24,1024]{1,0:T(8,128)(2,1)S(1)} %get-tuple-element.91), channel_id=1, source_target_pairs={{0,8},{2,10},{4,12},{6,14},{8,0},{10,2},{12,4},{14,6},{16,24},{18,... | collective-permute-start | bytes 147464 | tf_op jit(solution)/shard_map/return_grad/ppermute | solution.py:45

commit v8 on v7

--- a/solution.py
+++ b/solution.py
@@ -221,22 +221,36 @@
     gate_hi_ref[...], gate_mid_ref[...], _ = gate_parts(pick * gate)
 
 
+def shifted(rows, shift):
+    return pltpu.roll(rows, shift % rows.shape[0], 0) if shift else rows
+
+
+def padded(rows, before, after):
+    parts = [rows]
+    if before:
+        parts.insert(0, jnp.zeros((before, rows.shape[1]), F32))
+    if after:
+        parts.append(jnp.zeros((after, rows.shape[1]), F32))
+    return jnp.concatenate(parts, axis=0) if len(parts) > 1 else rows
+
+
 def stack_kernel(dims, *refs):
     inner, reach, held = dims
-    fold, half = refs[0].shape
-    values = stacked(flipped(refs[:inner]))
+    half = refs[0].shape[1]
     rows = inner * held
-    row = lax.broadcasted_iota(jnp.int32, (rows, 1), 0)
-    step = count_above(row, held, rows)
-    item = row - step * held
-    column = lax.broadcasted_iota(jnp.int32, (rows, inner * fold), 1)
-    wanted = jnp.where(item < reach, step * fold + item, -4 * reach)
-    chosen = [(column == wanted + n * reach).astype(F32) for n in range(4)]
-    out = jnp.dot(jnp.concatenate(chosen, axis=0).astype(BF16), values, preferred_element_type=F32)
-    for segment in range(4):
-        array, side = divmod(segment, 2)
-        part = out[segment * rows : (segment + 1) * rows].astype(BF16)
-        refs[-1][array * rows : (array + 1) * rows, side * half : (side + 1) * half] = part
+    live = lax.broadcasted_iota(jnp.int32, (held, half), 0) < reach
+    for q, piece in enumerate(flipped(refs[:inner])):
+        values = piece[...].astype(F32)
+        for segment in range(4):
+            array, side = divmod(segment, 2)
+            start = segment * reach // SUBLANES * SUBLANES
+            shift = segment * reach - start
+            frame = -(-(shift + reach) // SUBLANES) * SUBLANES
+            part = shifted(values[start : start + frame], -shift)
+            part = part[:held] if frame > held else padded(part, 0, held - frame)
+            first = array * rows + q * held
+            target = refs[-1].at[first : first + held, side * half : (side + 1) * half]
+            target[...] = jnp.where(live, part, 0.0).astype(BF16)
 
 
 def turn_kernel(count, *refs):
@@ -349,36 +363,33 @@
     total = refs[0][...].astype(F32)
     for part in refs[1:cores]:
         total = total + part[...].astype(F32)
-    total = total.astype(BF16)
     half = total.shape[1] // 2
     fold = 2 * reach
-    row = lax.broadcasted_iota(jnp.int32, (inner * fold, 1), 0)
-    step = count_above(row, fold, inner * fold)
-    place = row - step * fold
-    row_side = (place >= reach).astype(jnp.int32)
-    slot = place - row_side * reach
-    wanted = jnp.zeros_like(row)
-    first = 0
-    base = 0
-    for size, held in groups:
-        wanted = jnp.where(slot >= first, base + step * held + slot - first, wanted)
-        first += size
-        base += inner * held
-    column = lax.broadcasted_iota(jnp.int32, (inner * fold, total.shape[0]), 1)
-    out = None
-    for side in range(2):
-        chosen = ((column == wanted) & (row_side == side)).astype(F32).astype(BF16)
-        term = jnp.dot(chosen, total[:, side * half : (side + 1) * half], preferred_element_type=F32)
-        out = term if out is None else out + term
     for q in range(inner):
-        refs[q - inner][...] = out[q * fold : (q + 1) * fold].astype(BF16)
+        out = None
+        first = 0
+        base = 0
+        for size, held in groups:
+            rows = total[base + q * held : base + (q + 1) * held]
+            for side in range(2):
+                place = side * reach + first
+                start = place // SUBLANES * SUBLANES
+                frame = -(-(place - start + size) // SUBLANES) * SUBLANES
+                part = rows[:, side * half : (side + 1) * half]
+                part = part[:frame] if frame < held else padded(part, 0, frame - held)
+                part = shifted(part, place - start)
+                part = padded(part, start, fold - start - frame)
+                out = part if out is None else out + part
+            first += size
+            base += inner * held
+        refs[q - inner][...] = out.astype(BF16)
 
 
 def combine_kernel(dims, weighted, *refs):
     outer, inner, unit = dims
     tables = refs[inner : inner + weighted]
     outs = refs[-outer:]
-    rows = stacked(flipped(refs[:inner]))
+    rows = stacked(refs[:inner])
     total = None
     for table in tables:
         term = jnp.dot(table[...], rows, preferred_element_type=F32)
@@ -522,15 +533,24 @@
             cost_estimate=cost("FORWARD_OWN"),
             name="forward_own",
         )(*own_stacks, *weights[:2])
+        act_own = pl.pallas_call(
+            functools.partial(backward_own_kernel, dims, counts),
+            out_shape=shape(rows, hidden, F32),
+            in_specs=whole_specs(len(counts) + 1),
+            out_specs=pl.BlockSpec(memory_space=pltpu.VMEM),
+            compiler_params=params(),
+            cost_estimate=cost("BACKWARD_OWN"),
+            name="backward_own",
+        )(*own_stacks, down_t)
         gate_pre, up_pre, act, *out_parts = pl.pallas_call(
             functools.partial(forward_kernel, dims, counts),
             out_shape=[shape(rows, hidden, F32)] * 2 + [shape(rows, hidden)] + [shape(rows, width)] * cores,
-            in_specs=whole_specs(5 + len(other_stacks)),
+            in_specs=whole_specs(5 + len(other_stacks)) + any_specs(1),
             out_specs=whole_specs(3 + cores),
             compiler_params=params(),
             cost_estimate=cost("FORWARD"),
             name="forward",
-        )(*own, *weights, *other_stacks)
+        )(*own, *weights, *other_stacks, act_own)
 
     def give_back(parts, after=()):
         got = [parts[0]] + [send_core(parts[d], d, cores) for d in range(1, cores)]
@@ -552,7 +572,7 @@
             out_specs=whole_specs(outer),
             compiler_params=params(),
             name="combine",
-        )(*flipped(pieces), *tables)
+        )(*pieces, *tables)
         return [blocks[0]] + [send_outer(blocks[s], s, outer, inner, back=True) for s in range(1, outer)]
 
     def finish(blocks, after=()):
@@ -570,15 +590,6 @@
         out_blocks = combine(out_back, (gate_hi, gate_lo))
 
     with jax.named_scope("backward"):
-        act_own = pl.pallas_call(
-            functools.partial(backward_own_kernel, dims, counts),
-            out_shape=shape(rows, hidden, F32),
-            in_specs=whole_specs(len(counts) + 1),
-            out_specs=pl.BlockSpec(memory_space=pltpu.VMEM),
-            compiler_params=params(),
-            cost_estimate=cost("BACKWARD_OWN"),
-            name="backward_own",
-        )(*own_stacks, down_t)
         gate_grad, up_grad, *grad_parts = pl.pallas_call(
             functools.partial(backward_kernel, dims, counts),
             out_shape=[shape(rows, hidden)] * 2 + [shape(rows, width)] * (cores - 1),

time: 53.9 us -> 53 us (0.983)
  Pallas kernels: 17.2 us -> 16.4 us
  transfers between devices with their start and end apart: 25 -> 25, of which waited for: 7 -> 8; matrix products, arithmetic and copies ran while one was open for 0% -> 0% of each run, Pallas kernels for 26% -> 25%
where the time goes in v8:
time: 53 us; the launch traced here: 52.8 us
  starting transfers between devices  29.6 us (56%)
  Pallas kernels  16.4 us (31%)
  waiting for transfers between devices  5.98 us (11%)
  between operations  0.86 us (2%)
    ppermute x9, starting transfers between devices, send_outer(): return lax.ppermute(x, 'expert', pairs)  14.6 us
    ppermute x12, starting transfers between devices, send_inner(): return lax.ppermute(x, 'expert', pairs)  14.2 us
    pallas_call x2, Pallas kernels, turn(): pl.pallas_call(functools.partial(turn_kernel, len(picked)), out_shape=[pl...  3.56 us
    ppermute x9, waiting for transfers between devices, send_outer(): return lax.ppermute(x, 'expert', pairs)  2.66 us
    ppermute x12, waiting for transfers between devices, send_inner(): return lax.ppermute(x, 'expert', pairs)  2.5 us
    pallas_call x1, Pallas kernels, on_device(): pl.pallas_call(functools.partial(down_kernel, dims, counts, chunks), out_...  2.38 us
    pallas_call x2, Pallas kernels, route(): pl.pallas_call(functools.partial(route_kernel, route_dims, len(members),...  1.72 us
    pallas_call x1, Pallas kernels, on_device(): pl.pallas_call(functools.partial(forward_kernel, dims, counts), out_shape...  1.43 us
  transfers between devices with their start and end apart: 25, of which 8 were waited for; matrix products, arithmetic and copies ran while one was open for 0% of the time, Pallas kernels for 25%

profile of v8, /device:TPU:0, one launch (start us, length us, event | category | flops | bytes accessed | tf_op | source)
XLA Modules:
  0.0 52.8 jit_solution(14615296071724809017)
XLA Ops:
  0.6 1.2 %prepare.1.refs_0_ = bf16[8,6272]{1,0:T(8,128)(2,1)S(1)} custom-call(s32[8,12]{1,0:T(8,128)} %bitcast.2, f32[8,12]{1,0:T(8,128)} %bitcast.3, bf16[12,2048]{1,0:T(8,128)(2,1)} %refs_2_.3, bf16[12,2048]{1,0:T(8,128)(2,1)} %refs_3_.3), custom_call_target="tpu_custom_call" | custom-call | flops 20000000000 | bytes 1 | tf_op jit(solution)/shard_map/prepare/prepare/pallas_call | solution.py:432
  1.8 3.1 %collective-permute-start = (bf16[8,6272]{1,0:T(8,128)(2,1)S(1)}, bf16[8,6272]{1,0:T(8,128)(2,1)S(1)}, u32[]{:S(2)}, u32[]{:S(2)}) collective-permute-start(bf16[8,6272]{1,0:T(8,128)(2,1)S(1)} %prepare.1.refs_0_), channel_id=1, source_target_pairs={{0,8},{2,10},{4,12},{6,14},{8,0},{10,2},{12,4},{14,6},{16,24},{18,... | collective-permute-start | bytes 301064 | tf_op jit(solution)/shard_map/gather_blocks/ppermute | solution.py:45
  4.9 2.6 %collective-permute-start.4 = (bf16[8,6272]{1,0:T(8,128)(2,1)S(1)}, bf16[8,6272]{1,0:T(8,128)(2,1)S(1)}, u32[]{:S(2)}, u32[]{:S(2)}) collective-permute-start(bf16[8,6272]{1,0:T(8,128)(2,1)S(1)} %prepare.1.refs_0_), channel_id=1, source_target_pairs={{0,16},{2,18},{4,20},{6,22},{8,24},{10,26},{12,28},{14,30},{16,0},... | collective-permute-start | bytes 301064 | tf_op jit(solution)/shard_map/gather_blocks/ppermute | solution.py:45
  7.8 0.9 %route0.1 = (bf16[56,1024]{1,0:T(8,128)(2,1)S(1)}, bf16[56,1024]{1,0:T(8,128)(2,1)S(1)}, bf16[56,1024]{1,0:T(8,128)(2,1)S(1)}, bf16[56,1024]{1,0:T(8,128)(2,1)S(1)}) custom-call(bf16[8,6272]{1,0:T(8,128)(2,1)S(1)} %prepare.1.refs_0_, bf16[8,6272]{1,0:T(8,128)(2,1)S(1)} %collective-permute-done.refs_1_), custom_call_target="tpu_custom_call" | custom-call | flops 9000000512 | bytes 1 | tf_op jit(solution)/shard_map/near_blocks/route0/pallas_call | solution.py:461
  8.6 2.8 %collective-permute-start.1 = (bf16[56,1024]{1,0:T(8,128)(2,1)S(1)}, bf16[56,1024]{1,0:T(8,128)(2,1)S(1)}, u32[]{:S(2)}, u32[]{:S(2)}) collective-permute-start(bf16[56,1024]{1,0:T(8,128)(2,1)S(1)} %get-tuple-element.50), channel_id=1, source_target_pairs={{0,6},{2,4},{4,2},{6,0},{8,14},{10,12},{12,10},{14,8},{16,22},{18,... | collective-permute-start | bytes 344072 | tf_op jit(solution)/shard_map/near_blocks/ppermute | solution.py:53
  12.2 1.2 %turn_down.1 = (bf16[4096,512]{1,0:T(8,128)(2,1)S(1)}, f32[8,128]{1,0:T(8,128)S(1)}) custom-call(bf16[1,512,4096]{2,1,0:T(8,128)(2,1)S(1)} %copy-done.2, bf16[56,1024]{1,0:T(8,128)(2,1)S(1)} %get-tuple-element.49.refs_1_.refs_0_.refs_4_), custom_call_target="tpu_custom_call" | custom-call | flops 1 | bytes 1 | tf_op jit(solution)/shard_map/turn_weights/turn_down/pallas_call | solution.py:491
  13.3 2.2 %collective-permute-done.4.refs_0_.refs_2_ = bf16[8,6272]{1,0:T(8,128)(2,1)S(1)} collective-permute-done((bf16[8,6272]{1,0:T(8,128)(2,1)S(1)}, bf16[8,6272]{1,0:T(8,128)(2,1)S(1)}, u32[]{:S(2)}, u32[]{:S(2)}) %collective-permute-start.4) | collective-permute-done | bytes 100384 | tf_op jit(solution)/shard_map/gather_blocks/ppermute | solution.py:45
  15.5 0.9 %route1.1 = (bf16[56,1024]{1,0:T(8,128)(2,1)S(1)}, bf16[56,1024]{1,0:T(8,128)(2,1)S(1)}, bf16[56,1024]{1,0:T(8,128)(2,1)S(1)}, bf16[56,1024]{1,0:T(8,128)(2,1)S(1)}) custom-call(bf16[8,6272]{1,0:T(8,128)(2,1)S(1)} %collective-permute-done.4.refs_0_.refs_2_, bf16[8,6272]{1,0:T(8,128)(2,1)S(1)} %collective-permute-done.5.refs_1_.refs_3_, ...), custom_call_target="tpu_custom_call" | custom-call | flops 9000000512 | bytes 1 | tf_op jit(solution)/shard_map/far_blocks/route1/pallas_call | solution.py:461
  16.4 2.5 %collective-permute-start.6 = (bf16[56,1024]{1,0:T(8,128)(2,1)S(1)}, bf16[56,1024]{1,0:T(8,128)(2,1)S(1)}, u32[]{:S(2)}, u32[]{:S(2)}) collective-permute-start(bf16[56,1024]{1,0:T(8,128)(2,1)S(1)} %get-tuple-element.55), channel_id=1, source_target_pairs={{0,6},{2,4},{4,2},{6,0},{8,14},{10,12},{12,10},{14,8},{16,22},{18,... | collective-permute-start | bytes 344072 | tf_op jit(solution)/shard_map/far_blocks/ppermute | solution.py:53
  18.9 0.5 collective-permute-start.7
  19.4 0.5 %collective-permute-start.8 = (bf16[56,1024]{1,0:T(8,128)(2,1)S(1)}, bf16[56,1024]{1,0:T(8,128)(2,1)S(1)}, u32[]{:S(2)}, u32[]{:S(2)}) collective-permute-start(bf16[56,1024]{1,0:T(8,128)(2,1)S(1)} %get-tuple-element.57), channel_id=1, source_target_pairs={{0,2},{2,0},{4,6},{6,4},{8,10},{10,8},{12,14},{14,12},{16,18},{18,... | collective-permute-start | bytes 344072 | tf_op jit(solution)/shard_map/far_blocks/ppermute | solution.py:53
  19.9 2.4 %turn_rest.1 = (bf16[512,4096]{1,0:T(8,128)(2,1)S(1)}, bf16[512,4096]{1,0:T(8,128)(2,1)S(1)}, f32[8,128]{1,0:T(8,128)S(1)}) custom-call(bf16[1,4096,512]{2,1,0:T(8,128)(2,1)S(1)} %copy-done, bf16[1,4096,512]{2,1,0:T(8,128)(2,1)S(1)} %copy-done.1, bf16[56,1024]{1,0:T(8,128)(2,1)S(1)} %get-tuple-element.54.refs_4_.refs_2_.refs_0_), custom_call_target="tpu_custom_call" | custom-call | flops 1 | bytes 1 | tf_op jit(solution)/shard_map/turn_weights/turn_rest/pallas_call | solution.py:491
  23.1 1.0 %collective-permute-done.7.refs_2_ = bf16[56,1024]{1,0:T(8,128)(2,1)S(1)} collective-permute-done((bf16[56,1024]{1,0:T(8,128)(2,1)S(1)}, bf16[56,1024]{1,0:T(8,128)(2,1)S(1)}, u32[]{:S(2)}, u32[]{:S(2)}) %collective-permute-start.7) | collective-permute-done | bytes 114720 | tf_op jit(solution)/shard_map/far_blocks/ppermute | solution.py:53
  24.4 0.7 %forward_own.1 = (f32[128,512]{1,0:T(8,128)S(1)}, f32[128,512]{1,0:T(8,128)S(1)}) custom-call(bf16[128,2048]{1,0:T(8,128)(2,1)S(1)} %stack0.1.refs_0_, bf16[128,2048]{1,0:T(8,128)(2,1)S(1)} %stack1.1.refs_1_, bf16[1,4096,512]{2,1,0:T(8,128)(2,1)S(1)} %copy-done, bf16[1,4096,512]{2,1,0:T(8,128)(2,1)S(1)} %copy-done.1), custom_call_target="tpu_custom_call" | custom-call | flops 1 | bytes 1 | tf_op jit(solution)/shard_map/forward/forward_own/pallas_call | solution.py:527
  25.6 0.7 %collective-permute-done.10.refs_6_.refs_7_.refs_3_ = bf16[128,2048]{1,0:T(8,128)(2,1)S(1)} collective-permute-done((bf16[128,2048]{1,0:T(8,128)(2,1)S(1)}, bf16[128,2048]{1,0:T(8,128)(2,1)S(1)}, u32[]{:S(2)}, u32[]{:S(2)}) %collective-permute-start.10) | collective-permute-done | bytes 524320 | tf_op jit(solution)/shard_map/gather_cores/ppermute | solution.py:58
  26.3 1.4 %forward.1 = (f32[128,512]{1,0:T(8,128)S(1)}, f32[128,512]{1,0:T(8,128)S(1)}, bf16[128,512]{1,0:T(8,128)(2,1)S(1)}, bf16[128,2048]{1,0:T(8,128)(2,1)S(1)}, bf16[128,2048]{1,0:T(8,128)(2,1)S(1)}) custom-call(f32[128,512]{1,0:T(8,128)S(1)} %get-tuple-element.60.refs_0_, f32[128,512]{1,0:T(8,128)S(1)} %get-tuple-element.61.refs_1_, ...), custom_call_target="tpu_custom_call" | custom-call | flops 1 | bytes 1 | tf_op jit(solution)/shard_map/forward/forward/pallas_call | solution.py:545
  27.9 1.2 %backward.1 = (bf16[128,512]{1,0:T(8,128)(2,1)S(1)}, bf16[128,512]{1,0:T(8,128)(2,1)S(1)}, bf16[128,2048]{1,0:T(8,128)(2,1)S(1)}) custom-call(f32[128,512]{1,0:T(8,128)S(1)} %backward_own.1.refs_7_.refs_0_, bf16[512,4096]{1,0:T(8,128)(2,1)S(1)} %get-tuple-element.76.refs_1_.refs_2_, bf16[512,4096]{1,0:T(8,128)(2,1)S(1)} %get-tuple-element.77.refs_2_.refs_3_, ...), custom_call_target="tpu_custom_call" | custom-call | flops 1 | bytes 1 | tf_op jit(solution)/shard_map/backward/backward/pallas_call | solution.py:593
  29.9 1.0 %collective-permute-start.12 = (bf16[56,1024]{1,0:T(8,128)(2,1)S(1)}, bf16[56,1024]{1,0:T(8,128)(2,1)S(1)}, u32[]{:S(2)}, u32[]{:S(2)}) collective-permute-start(bf16[56,1024]{1,0:T(8,128)(2,1)S(1)} %get-tuple-element.66), channel_id=1, source_target_pairs={{0,2},{2,0},{4,6},{6,4},{8,10},{10,8},{12,14},{14,12},{16,18},{18,... | collective-permute-start | bytes 344072 | tf_op jit(solution)/shard_map/return_out/ppermute | solution.py:53
  30.9 1.5 %collective-permute-start.13 = (bf16[56,1024]{1,0:T(8,128)(2,1)S(1)}, bf16[56,1024]{1,0:T(8,128)(2,1)S(1)}, u32[]{:S(2)}, u32[]{:S(2)}) collective-permute-start(bf16[56,1024]{1,0:T(8,128)(2,1)S(1)} %get-tuple-element.67), channel_id=1, source_target_pairs={{0,4},{2,6},{4,0},{6,2},{8,12},{10,14},{12,8},{14,10},{16,20},{18,... | collective-permute-start | bytes 344072 | tf_op jit(solution)/shard_map/return_out/ppermute | solution.py:53
  32.4 1.0 %collective-permute-start.14 = (bf16[56,1024]{1,0:T(8,128)(2,1)S(1)}, bf16[56,1024]{1,0:T(8,128)(2,1)S(1)}, u32[]{:S(2)}, u32[]{:S(2)}) collective-permute-start(bf16[56,1024]{1,0:T(8,128)(2,1)S(1)} %get-tuple-element.68), channel_id=1, source_target_pairs={{0,6},{2,4},{4,2},{6,0},{8,14},{10,12},{12,10},{14,8},{16,22},{18,... | collective-permute-start | bytes 344072 | tf_op jit(solution)/shard_map/return_out/ppermute | solution.py:53
  33.5 0.8 %input_own.1.refs_0_ = bf16[128,2048]{1,0:T(8,128)(2,1)S(1)} custom-call(bf16[128,512]{1,0:T(8,128)(2,1)S(1)} %get-tuple-element.80.refs_0_, bf16[128,512]{1,0:T(8,128)(2,1)S(1)} %get-tuple-element.81.refs_1_, bf16[512,4096]{1,0:T(8,128)(2,1)S(1)} %get-tuple-element.76.refs_1_.refs_2_, bf16[512,4096]{1,0:T(8,128)(2,1)S(1)} %get-tuple-element.77.refs_2_.refs_3_, ...), custom_call_target="tpu_custom_call" | custom-call | flops 1 | bytes 1 | tf_op jit(solution)/shard_map/backward/input_own/pallas_call | solution.py:602
  34.4 1.0 %collective-permute-start.19 = (bf16[56,1024]{1,0:T(8,128)(2,1)S(1)}, bf16[56,1024]{1,0:T(8,128)(2,1)S(1)}, u32[]{:S(2)}, u32[]{:S(2)}) collective-permute-start(bf16[56,1024]{1,0:T(8,128)(2,1)S(1)} %get-tuple-element.84), channel_id=1, source_target_pairs={{0,2},{2,0},{4,6},{6,4},{8,10},{10,8},{12,14},{14,12},{16,18},{18,... | collective-permute-start | bytes 344072 | tf_op jit(solution)/shard_map/return_grad/ppermute | solution.py:53
  35.4 1.5 %collective-permute-start.20 = (bf16[56,1024]{1,0:T(8,128)(2,1)S(1)}, bf16[56,1024]{1,0:T(8,128)(2,1)S(1)}, u32[]{:S(2)}, u32[]{:S(2)}) collective-permute-start(bf16[56,1024]{1,0:T(8,128)(2,1)S(1)} %get-tuple-element.85), channel_id=1, source_target_pairs={{0,4},{2,6},{4,0},{6,2},{8,12},{10,14},{12,8},{14,10},{16,20},{18,... | collective-permute-start | bytes 344072 | tf_op jit(solution)/shard_map/return_grad/ppermute | solution.py:53
  37.0 1.0 %collective-permute-start.21 = (bf16[56,1024]{1,0:T(8,128)(2,1)S(1)}, bf16[56,1024]{1,0:T(8,128)(2,1)S(1)}, u32[]{:S(2)}, u32[]{:S(2)}) collective-permute-start(bf16[56,1024]{1,0:T(8,128)(2,1)S(1)} %get-tuple-element.86), channel_id=1, source_target_pairs={{0,6},{2,4},{4,2},{6,0},{8,14},{10,12},{12,10},{14,8},{16,22},{18,... | collective-permute-start | bytes 344072 | tf_op jit(solution)/shard_map/return_grad/ppermute | solution.py:53
  38.0 1.4 %collective-permute-done.14.refs_3_ = bf16[56,1024]{1,0:T(8,128)(2,1)S(1)} collective-permute-done((bf16[56,1024]{1,0:T(8,128)(2,1)S(1)}, bf16[56,1024]{1,0:T(8,128)(2,1)S(1)}, u32[]{:S(2)}, u32[]{:S(2)}) %collective-permute-start.14) | collective-permute-done | bytes 114720 | tf_op jit(solution)/shard_map/return_out/ppermute | solution.py:53
  39.7 2.8 %collective-permute-start.15 = (bf16[24,1024]{1,0:T(8,128)(2,1)S(1)}, bf16[24,1024]{1,0:T(8,128)(2,1)S(1)}, u32[]{:S(2)}, u32[]{:S(2)}) collective-permute-start(bf16[24,1024]{1,0:T(8,128)(2,1)S(1)} %get-tuple-element.72), channel_id=1, source_target_pairs={{0,24},{2,26},{4,28},{6,30},{8,16},{10,18},{12,20},{14,22},{16,8},... | collective-permute-start | bytes 147464 | tf_op jit(solution)/shard_map/return_out/ppermute | solution.py:45
  42.8 1.3 %collective-permute-start.17 = (bf16[24,1024]{1,0:T(8,128)(2,1)S(1)}, bf16[24,1024]{1,0:T(8,128)(2,1)S(1)}, u32[]{:S(2)}, u32[]{:S(2)}) collective-permute-start(bf16[24,1024]{1,0:T(8,128)(2,1)S(1)} %get-tuple-element.74), channel_id=1, source_target_pairs={{0,8},{2,10},{4,12},{6,14},{8,0},{10,2},{12,4},{14,6},{16,24},{18,... | collective-permute-start | bytes 147464 | tf_op jit(solution)/shard_map/return_out/ppermute | solution.py:45
  44.4 2.8 %collective-permute-start.22 = (bf16[24,1024]{1,0:T(8,128)(2,1)S(1)}, bf16[24,1024]{1,0:T(8,128)(2,1)S(1)}, u32[]{:S(2)}, u32[]{:S(2)}) collective-permute-start(bf16[24,1024]{1,0:T(8,128)(2,1)S(1)} %get-tuple-element.89), channel_id=1, source_target_pairs={{0,24},{2,26},{4,28},{6,30},{8,16},{10,18},{12,20},{14,22},{16,8},... | collective-permute-start | bytes 147464 | tf_op jit(solution)/shard_map/return_grad/ppermute | solution.py:45
  47.2 1.7 %collective-permute-start.24 = (bf16[24,1024]{1,0:T(8,128)(2,1)S(1)}, bf16[24,1024]{1,0:T(8,128)(2,1)S(1)}, u32[]{:S(2)}, u32[]{:S(2)}) collective-permute-start(bf16[24,1024]{1,0:T(8,128)(2,1)S(1)} %get-tuple-element.91), channel_id=1, source_target_pairs={{0,8},{2,10},{4,12},{6,14},{8,0},{10,2},{12,4},{14,6},{16,24},{18,... | collective-permute-start | bytes 147464 | tf_op jit(solution)/shard_map/return_grad/ppermute | solution.py:45
  48.8 2.4 %down_grad.1 = bf16[1,512,4096]{2,1,0:T(8,128)(2,1)} custom-call(bf16[128,2048]{1,0:T(8,128)(2,1)S(1)} %stack0.1.refs_0_, bf16[128,2048]{1,0:T(8,128)(2,1)S(1)} %stack1.1.refs_1_, bf16[128,2048]{1,0:T(8,128)(2,1)S(1)} %collective-permute-done.9.refs_5_.refs_6_.refs_2_, bf16[128,2048]{1,0:T(8,128)(2,1)S(1)} %collective-permute-done.10.refs_6_.refs_7_.refs_3_, ...), custom_call_target="tpu_custom_call" | custom-call | tf_op jit(solution)/shard_map/down_grad/down_grad/pallas_call | solution.py:618
  51.2 0.7 %final.2 = (bf16[12,2048]{1,0:T(8,128)(2,1)}, f32[8,128]{1,0:T(8,128)S(1)}) custom-call(bf16[24,1024]{1,0:T(8,128)(2,1)S(1)} %get-tuple-element.71.refs_0_, bf16[24,1024]{1,0:T(8,128)(2,1)S(1)} %collective-permute-done.15.refs_1_, bf16[24,1024]{1,0:T(8,128)(2,1)S(1)} %collective-permute-done.16.refs_2_, bf16[24,1024]{1,0:T(8,128)(2,1)S(1)} %collective-permute-done.17.refs_3_), custom_call_target="tpu_custom_call" | custom-call | tf_op jit(solution)/shard_map/final/pallas_call | solution.py:579
  52.1 0.7 %final.3 = (bf16[12,2048]{1,0:T(8,128)(2,1)}, f32[8,128]{1,0:T(8,128)}) custom-call(bf16[24,1024]{1,0:T(8,128)(2,1)S(1)} %get-tuple-element.88.refs_0_.refs_5_, bf16[24,1024]{1,0:T(8,128)(2,1)S(1)} %collective-permute-done.22.refs_1_, bf16[24,1024]{1,0:T(8,128)(2,1)S(1)} %collective-permute-done.23.refs_2_, ...), custom_call_target="tpu_custom_call" | custom-call | tf_op jit(solution)/shard_map/final/pallas_call | solution.py:579
  (44 shorter events, 4.8 us)
Async XLA Ops:
  1.8 10.4 %copy-start.2 = (bf16[1,512,4096]{2,1,0:T(8,128)(2,1)S(1)}, bf16[1,512,4096]{2,1,0:T(8,128)(2,1)}, u32[]{:S(2)}) copy-start(bf16[1,512,4096]{2,1,0:T(8,128)(2,1)} %refs_4_.1) | copy-start | bytes 12582916
  1.8 5.9 %collective-permute-start = (bf16[8,6272]{1,0:T(8,128)(2,1)S(1)}, bf16[8,6272]{1,0:T(8,128)(2,1)S(1)}, u32[]{:S(2)}, u32[]{:S(2)}) collective-permute-start(bf16[8,6272]{1,0:T(8,128)(2,1)S(1)} %prepare.1.refs_0_), channel_id=1, source_target_pairs={{0,8},{2,10},{4,12},{6,14},{8,0},{10,2},{12,4},{14,6},{16,24},{18,... | collective-permute-start | bytes 301064 | tf_op jit(solution)/shard_map/gather_blocks/ppermute | solution.py:45
  4.9 10.6 %collective-permute-start.4 = (bf16[8,6272]{1,0:T(8,128)(2,1)S(1)}, bf16[8,6272]{1,0:T(8,128)(2,1)S(1)}, u32[]{:S(2)}, u32[]{:S(2)}) collective-permute-start(bf16[8,6272]{1,0:T(8,128)(2,1)S(1)} %prepare.1.refs_0_), channel_id=1, source_target_pairs={{0,16},{2,18},{4,20},{6,22},{8,24},{10,26},{12,28},{14,30},{16,0},... | collective-permute-start | bytes 301064 | tf_op jit(solution)/shard_map/gather_blocks/ppermute | solution.py:45
  7.5 8.0 %collective-permute-start.5 = (bf16[8,6272]{1,0:T(8,128)(2,1)S(1)}, bf16[8,6272]{1,0:T(8,128)(2,1)S(1)}, u32[]{:S(2)}, u32[]{:S(2)}) collective-permute-start(bf16[8,6272]{1,0:T(8,128)(2,1)S(1)} %prepare.1.refs_0_), channel_id=1, source_target_pairs={{0,24},{2,26},{4,28},{6,30},{8,16},{10,18},{12,20},{14,22},{16,8},... | collective-permute-start | bytes 301064 | tf_op jit(solution)/shard_map/gather_blocks/ppermute | solution.py:45
  8.6 10.8 %collective-permute-start.1 = (bf16[56,1024]{1,0:T(8,128)(2,1)S(1)}, bf16[56,1024]{1,0:T(8,128)(2,1)S(1)}, u32[]{:S(2)}, u32[]{:S(2)}) collective-permute-start(bf16[56,1024]{1,0:T(8,128)(2,1)S(1)} %get-tuple-element.50), channel_id=1, source_target_pairs={{0,6},{2,4},{4,2},{6,0},{8,14},{10,12},{12,10},{14,8},{16,22},{18,... | collective-permute-start | bytes 344072 | tf_op jit(solution)/shard_map/near_blocks/ppermute | solution.py:53
  11.4 11.5 %collective-permute-start.2 = (bf16[56,1024]{1,0:T(8,128)(2,1)S(1)}, bf16[56,1024]{1,0:T(8,128)(2,1)S(1)}, u32[]{:S(2)}, u32[]{:S(2)}) collective-permute-start(bf16[56,1024]{1,0:T(8,128)(2,1)S(1)} %get-tuple-element.51), channel_id=1, source_target_pairs={{0,4},{2,6},{4,0},{6,2},{8,12},{10,14},{12,8},{14,10},{16,20},{18,... | collective-permute-start | bytes 344072 | tf_op jit(solution)/shard_map/near_blocks/ppermute | solution.py:53
  11.9 11.0 %collective-permute-start.3 = (bf16[56,1024]{1,0:T(8,128)(2,1)S(1)}, bf16[56,1024]{1,0:T(8,128)(2,1)S(1)}, u32[]{:S(2)}, u32[]{:S(2)}) collective-permute-start(bf16[56,1024]{1,0:T(8,128)(2,1)S(1)} %get-tuple-element.52), channel_id=1, source_target_pairs={{0,2},{2,0},{4,6},{6,4},{8,10},{10,8},{12,14},{14,12},{16,18},{18,... | collective-permute-start | bytes 344072 | tf_op jit(solution)/shard_map/near_blocks/ppermute | solution.py:53
  15.5 4.4 %copy-start = (bf16[1,4096,512]{2,1,0:T(8,128)(2,1)S(1)}, bf16[1,4096,512]{2,1,0:T(8,128)(2,1)}, u32[]{:S(2)}) copy-start(bf16[1,4096,512]{2,1,0:T(8,128)(2,1)} %refs_2_.5) | copy-start | bytes 12582916
  15.5 4.4 %copy-start.1 = (bf16[1,4096,512]{2,1,0:T(8,128)(2,1)S(1)}, bf16[1,4096,512]{2,1,0:T(8,128)(2,1)}, u32[]{:S(2)}) copy-start(bf16[1,4096,512]{2,1,0:T(8,128)(2,1)} %refs_3_.5) | copy-start | bytes 12582916
  16.4 6.7 %collective-permute-start.6 = (bf16[56,1024]{1,0:T(8,128)(2,1)S(1)}, bf16[56,1024]{1,0:T(8,128)(2,1)S(1)}, u32[]{:S(2)}, u32[]{:S(2)}) collective-permute-start(bf16[56,1024]{1,0:T(8,128)(2,1)S(1)} %get-tuple-element.55), channel_id=1, source_target_pairs={{0,6},{2,4},{4,2},{6,0},{8,14},{10,12},{12,10},{14,8},{16,22},{18,... | collective-permute-start | bytes 344072 | tf_op jit(solution)/shard_map/far_blocks/ppermute | solution.py:53
  18.9 5.2 %collective-permute-start.7 = (bf16[56,1024]{1,0:T(8,128)(2,1)S(1)}, bf16[56,1024]{1,0:T(8,128)(2,1)S(1)}, u32[]{:S(2)}, u32[]{:S(2)}) collective-permute-start(bf16[56,1024]{1,0:T(8,128)(2,1)S(1)} %get-tuple-element.56), channel_id=1, source_target_pairs={{0,4},{2,6},{4,0},{6,2},{8,12},{10,14},{12,8},{14,10},{16,20},{18,... | collective-permute-start | bytes 344072 | tf_op jit(solution)/shard_map/far_blocks/ppermute | solution.py:53
  19.4 4.8 %collective-permute-start.8 = (bf16[56,1024]{1,0:T(8,128)(2,1)S(1)}, bf16[56,1024]{1,0:T(8,128)(2,1)S(1)}, u32[]{:S(2)}, u32[]{:S(2)}) collective-permute-start(bf16[56,1024]{1,0:T(8,128)(2,1)S(1)} %get-tuple-element.57), channel_id=1, source_target_pairs={{0,2},{2,0},{4,6},{6,4},{8,10},{10,8},{12,14},{14,12},{16,18},{18,... | collective-permute-start | bytes 344072 | tf_op jit(solution)/shard_map/far_blocks/ppermute | solution.py:53
  23.0 2.6 %collective-permute-start.9 = (bf16[128,2048]{1,0:T(8,128)(2,1)S(1)}, bf16[128,2048]{1,0:T(8,128)(2,1)S(1)}, u32[]{:S(2)}, u32[]{:S(2)}) collective-permute-start(bf16[128,2048]{1,0:T(8,128)(2,1)S(1)} %stack0.1.refs_0_), channel_id=1, source_target_pairs={{0,1},{1,0},{2,3},{3,2},{4,5},{5,4},{6,7},{7,6},{8,9},{9,8},{10,11... | collective-permute-start | bytes 1572872 | tf_op jit(solution)/shard_map/gather_cores/ppermute | solution.py:58
  24.3 2.0 %collective-permute-start.10 = (bf16[128,2048]{1,0:T(8,128)(2,1)S(1)}, bf16[128,2048]{1,0:T(8,128)(2,1)S(1)}, u32[]{:S(2)}, u32[]{:S(2)}) collective-permute-start(bf16[128,2048]{1,0:T(8,128)(2,1)S(1)} %stack1.1.refs_1_), channel_id=1, source_target_pairs={{0,1},{1,0},{2,3},{3,2},{4,5},{5,4},{6,7},{7,6},{8,9},{9,8},{10,11... | collective-permute-start | bytes 1572872 | tf_op jit(solution)/shard_map/gather_cores/ppermute | solution.py:58
  27.7 2.0 %collective-permute-start.11 = (bf16[128,2048]{1,0:T(8,128)(2,1)S(1)}, bf16[128,2048]{1,0:T(8,128)(2,1)S(1)}, u32[]{:S(2)}, u32[]{:S(2)}) collective-permute-start(bf16[128,2048]{1,0:T(8,128)(2,1)S(1)} %get-tuple-element.64), channel_id=1, source_target_pairs={{0,1},{1,0},{2,3},{3,2},{4,5},{5,4},{6,7},{7,6},{8,9},{9,8},{10,11... | collective-permute-start | bytes 1572872 | tf_op jit(solution)/shard_map/return_out/ppermute | solution.py:58
  29.1 5.1 %collective-permute-start.18 = (bf16[128,2048]{1,0:T(8,128)(2,1)S(1)}, bf16[128,2048]{1,0:T(8,128)(2,1)S(1)}, u32[]{:S(2)}, u32[]{:S(2)}) collective-permute-start(bf16[128,2048]{1,0:T(8,128)(2,1)S(1)} %get-tuple-element.82), channel_id=1, source_target_pairs={{0,1},{1,0},{2,3},{3,2},{4,5},{5,4},{6,7},{7,6},{8,9},{9,8},{10,11... | collective-permute-start | bytes 1572872 | tf_op jit(solution)/shard_map/return_grad/ppermute | solution.py:58
  29.9 7.1 %collective-permute-start.12 = (bf16[56,1024]{1,0:T(8,128)(2,1)S(1)}, bf16[56,1024]{1,0:T(8,128)(2,1)S(1)}, u32[]{:S(2)}, u32[]{:S(2)}) collective-permute-start(bf16[56,1024]{1,0:T(8,128)(2,1)S(1)} %get-tuple-element.66), channel_id=1, source_target_pairs={{0,2},{2,0},{4,6},{6,4},{8,10},{10,8},{12,14},{14,12},{16,18},{18,... | collective-permute-start | bytes 344072 | tf_op jit(solution)/shard_map/return_out/ppermute | solution.py:53
  30.9 7.1 %collective-permute-start.13 = (bf16[56,1024]{1,0:T(8,128)(2,1)S(1)}, bf16[56,1024]{1,0:T(8,128)(2,1)S(1)}, u32[]{:S(2)}, u32[]{:S(2)}) collective-permute-start(bf16[56,1024]{1,0:T(8,128)(2,1)S(1)} %get-tuple-element.67), channel_id=1, source_target_pairs={{0,4},{2,6},{4,0},{6,2},{8,12},{10,14},{12,8},{14,10},{16,20},{18,... | collective-permute-start | bytes 344072 | tf_op jit(solution)/shard_map/return_out/ppermute | solution.py:53
  32.4 7.0 %collective-permute-start.14 = (bf16[56,1024]{1,0:T(8,128)(2,1)S(1)}, bf16[56,1024]{1,0:T(8,128)(2,1)S(1)}, u32[]{:S(2)}, u32[]{:S(2)}) collective-permute-start(bf16[56,1024]{1,0:T(8,128)(2,1)S(1)} %get-tuple-element.68), channel_id=1, source_target_pairs={{0,6},{2,4},{4,2},{6,0},{8,14},{10,12},{12,10},{14,8},{16,22},{18,... | collective-permute-start | bytes 344072 | tf_op jit(solution)/shard_map/return_out/ppermute | solution.py:53
  34.4 8.4 %collective-permute-start.19 = (bf16[56,1024]{1,0:T(8,128)(2,1)S(1)}, bf16[56,1024]{1,0:T(8,128)(2,1)S(1)}, u32[]{:S(2)}, u32[]{:S(2)}) collective-permute-start(bf16[56,1024]{1,0:T(8,128)(2,1)S(1)} %get-tuple-element.84), channel_id=1, source_target_pairs={{0,2},{2,0},{4,6},{6,4},{8,10},{10,8},{12,14},{14,12},{16,18},{18,... | collective-permute-start | bytes 344072 | tf_op jit(solution)/shard_map/return_grad/ppermute | solution.py:53
  35.4 8.7 %collective-permute-start.20 = (bf16[56,1024]{1,0:T(8,128)(2,1)S(1)}, bf16[56,1024]{1,0:T(8,128)(2,1)S(1)}, u32[]{:S(2)}, u32[]{:S(2)}) collective-permute-start(bf16[56,1024]{1,0:T(8,128)(2,1)S(1)} %get-tuple-element.85), channel_id=1, source_target_pairs={{0,4},{2,6},{4,0},{6,2},{8,12},{10,14},{12,8},{14,10},{16,20},{18,... | collective-permute-start | bytes 344072 | tf_op jit(solution)/shard_map/return_grad/ppermute | solution.py:53
  37.0 7.2 %collective-permute-start.21 = (bf16[56,1024]{1,0:T(8,128)(2,1)S(1)}, bf16[56,1024]{1,0:T(8,128)(2,1)S(1)}, u32[]{:S(2)}, u32[]{:S(2)}) collective-permute-start(bf16[56,1024]{1,0:T(8,128)(2,1)S(1)} %get-tuple-element.86), channel_id=1, source_target_pairs={{0,6},{2,4},{4,2},{6,0},{8,14},{10,12},{12,10},{14,8},{16,22},{18,... | collective-permute-start | bytes 344072 | tf_op jit(solution)/shard_map/return_grad/ppermute | solution.py:53
  39.7 7.5 %collective-permute-start.15 = (bf16[24,1024]{1,0:T(8,128)(2,1)S(1)}, bf16[24,1024]{1,0:T(8,128)(2,1)S(1)}, u32[]{:S(2)}, u32[]{:S(2)}) collective-permute-start(bf16[24,1024]{1,0:T(8,128)(2,1)S(1)} %get-tuple-element.72), channel_id=1, source_target_pairs={{0,24},{2,26},{4,28},{6,30},{8,16},{10,18},{12,20},{14,22},{16,8},... | collective-permute-start | bytes 147464 | tf_op jit(solution)/shard_map/return_out/ppermute | solution.py:45
  42.5 8.7 %collective-permute-start.16 = (bf16[24,1024]{1,0:T(8,128)(2,1)S(1)}, bf16[24,1024]{1,0:T(8,128)(2,1)S(1)}, u32[]{:S(2)}, u32[]{:S(2)}) collective-permute-start(bf16[24,1024]{1,0:T(8,128)(2,1)S(1)} %get-tuple-element.73), channel_id=1, source_target_pairs={{0,16},{2,18},{4,20},{6,22},{8,24},{10,26},{12,28},{14,30},{16,0},... | collective-permute-start | bytes 147464 | tf_op jit(solution)/shard_map/return_out/ppermute | solution.py:45
  42.8 8.4 %collective-permute-start.17 = (bf16[24,1024]{1,0:T(8,128)(2,1)S(1)}, bf16[24,1024]{1,0:T(8,128)(2,1)S(1)}, u32[]{:S(2)}, u32[]{:S(2)}) collective-permute-start(bf16[24,1024]{1,0:T(8,128)(2,1)S(1)} %get-tuple-element.74), channel_id=1, source_target_pairs={{0,8},{2,10},{4,12},{6,14},{8,0},{10,2},{12,4},{14,6},{16,24},{18,... | collective-permute-start | bytes 147464 | tf_op jit(solution)/shard_map/return_out/ppermute | solution.py:45
  44.4 7.5 %collective-permute-start.22 = (bf16[24,1024]{1,0:T(8,128)(2,1)S(1)}, bf16[24,1024]{1,0:T(8,128)(2,1)S(1)}, u32[]{:S(2)}, u32[]{:S(2)}) collective-permute-start(bf16[24,1024]{1,0:T(8,128)(2,1)S(1)} %get-tuple-element.89), channel_id=1, source_target_pairs={{0,24},{2,26},{4,28},{6,30},{8,16},{10,18},{12,20},{14,22},{16,8},... | collective-permute-start | bytes 147464 | tf_op jit(solution)/shard_map/return_grad/ppermute | solution.py:45
  47.1 5.0 %collective-permute-start.23 = (bf16[24,1024]{1,0:T(8,128)(2,1)S(1)}, bf16[24,1024]{1,0:T(8,128)(2,1)S(1)}, u32[]{:S(2)}, u32[]{:S(2)}) collective-permute-start(bf16[24,1024]{1,0:T(8,128)(2,1)S(1)} %get-tuple-element.90), channel_id=1, source_target_pairs={{0,16},{2,18},{4,20},{6,22},{8,24},{10,26},{12,28},{14,30},{16,0},... | collective-permute-start | bytes 147464 | tf_op jit(solution)/shard_map/return_grad/ppermute | solution.py:45
  47.2 5.0 %collective-permute-start.24 = (bf16[24,1024]{1,0:T(8,128)(2,1)S(1)}, bf16[24,1024]{1,0:T(8,128)(2,1)S(1)}, u32[]{:S(2)}, u32[]{:S(2)}) collective-permute-start(bf16[24,1024]{1,0:T(8,128)(2,1)S(1)} %get-tuple-element.91), channel_id=1, source_target_pairs={{0,8},{2,10},{4,12},{6,14},{8,0},{10,2},{12,4},{14,6},{16,24},{18,... | collective-permute-start | bytes 147464 | tf_op jit(solution)/shard_map/return_grad/ppermute | solution.py:45

commit v9 on v8

--- a/solution.py
+++ b/solution.py
@@ -156,18 +156,19 @@
     me = lax.axis_index("expert")
     my_inner = lax.rem(me, inner)
     my_base = me - my_inner
-    lane = lax.broadcasted_iota(jnp.int32, shape, 1)
+    lane = lax.broadcasted_iota(jnp.int32, (1, shape[1]), 1)
     step = count_above(lane, fold, shape[1])
-    dest = jnp.zeros(shape, F32)
+    dest = jnp.zeros(lane.shape, F32)
     for q in range(inner):
         expert = (my_base + traced_partner(my_inner, q, inner)).astype(F32)
         dest = jnp.where(step == q, expert, dest)
     meta = block_rows(blocks, 2 * tiles * half, META, tiles, 4 * top)
+    weights = meta + pltpu.roll(meta, META - top, 1) + pltpu.roll(meta, META - 2 * top, 1)
     named = jnp.zeros(shape, F32)
     gate = jnp.zeros(shape, F32)
     for k in range(top):
         hit = meta[:, k : k + 1] == dest
-        value = sum(meta[:, n * top + k : n * top + k + 1] for n in range(1, 4))
+        value = weights[:, top + k : top + k + 1]
         named = jnp.where(hit, 1.0, named)
         gate = jnp.where(hit, value, gate)
     left = lax.broadcasted_iota(jnp.int32, (rows, rows), 1)
@@ -200,14 +201,11 @@
     grads = segment >= 2
     side = segment - 2 * grads.astype(jnp.int32)
     pick = jnp.where((position == lane - segment * reach) & (row_side == side), named, 0.0)
-    pick_in = jnp.where(grads, 0.0, pick).astype(BF16)
-    pick_grad = jnp.where(grads, pick, 0.0).astype(BF16)
     ones = jnp.ones((pick.shape[0], META), BF16)
-    column = sum(contract(part, ones, 0, 0) for part in gate_parts(pick * gate))
-    table = block_rows(blocks, 0, half, tiles).astype(BF16)
-    out = contract(pick_in, table, 0, 0)
-    table = block_rows(blocks, tiles * half, half, tiles).astype(BF16)
-    out = out + contract(pick_grad, table, 0, 0) * column[:, :1]
+    column = sum(contract(part, ones, 0, 0) for part in gate_parts(pick * jnp.where(grads, gate, 1.0)))
+    chosen = jnp.concatenate([jnp.where(grads, 0.0, pick), jnp.where(grads, pick, 0.0)], axis=0).astype(BF16)
+    table = [block_rows(blocks, n * tiles * half, half, tiles) for n in range(2)]
+    out = contract(chosen, jnp.concatenate(table, axis=0).astype(BF16), 0, 0) * column[:, :1]
     for q, send in enumerate(sends):
         send[...] = out[q * fold : (q + 1) * fold].astype(BF16)
 

time: 53 us -> 52.7 us (level)
  transfers between devices with their start and end apart: 25 -> 25, of which waited for: 8 -> 8; matrix products, arithmetic and copies ran while one was open for 0% -> 0% of each run, Pallas kernels for 25% -> 24%
where the time goes in v9:
time: 52.7 us; the launch traced here: 52.6 us
  starting transfers between devices  29.6 us (56%)
  Pallas kernels  16.1 us (31%)
  waiting for transfers between devices  5.95 us (11%)
  between operations  0.86 us (2%)
    ppermute x9, starting transfers between devices, send_outer(): return lax.ppermute(x, 'expert', pairs)  14.6 us
    ppermute x12, starting transfers between devices, send_inner(): return lax.ppermute(x, 'expert', pairs)  14.2 us
    pallas_call x2, Pallas kernels, turn(): pl.pallas_call(functools.partial(turn_kernel, len(picked)), out_shape=[pl...  3.56 us
    ppermute x9, waiting for transfers between devices, send_outer(): return lax.ppermute(x, 'expert', pairs)  2.66 us
    ppermute x12, waiting for transfers between devices, send_inner(): return lax.ppermute(x, 'expert', pairs)  2.48 us
    pallas_call x1, Pallas kernels, on_device(): pl.pallas_call(functools.partial(down_kernel, dims, counts, chunks), out_...  2.38 us
    pallas_call x2, Pallas kernels, route(): pl.pallas_call(functools.partial(route_kernel, route_dims, len(members),...  1.46 us
    pallas_call x1, Pallas kernels, on_device(): pl.pallas_call(functools.partial(forward_kernel, dims, counts), out_shape...  1.43 us
  transfers between devices with their start and end apart: 25, of which 8 were waited for; matrix products, arithmetic and copies ran while one was open for 0% of the time, Pallas kernels for 24%

profile of v9, /device:TPU:0, one launch (start us, length us, event | category | flops | bytes accessed | tf_op | source)
XLA Modules:
  0.0 52.6 jit_solution(4220283767125478342)
XLA Ops:
  0.6 1.2 %prepare.1.refs_0_ = bf16[8,6272]{1,0:T(8,128)(2,1)S(1)} custom-call(s32[8,12]{1,0:T(8,128)} %bitcast.2, f32[8,12]{1,0:T(8,128)} %bitcast.3, bf16[12,2048]{1,0:T(8,128)(2,1)} %refs_2_.3, bf16[12,2048]{1,0:T(8,128)(2,1)} %refs_3_.3), custom_call_target="tpu_custom_call" | custom-call | flops 20000000000 | bytes 1 | tf_op jit(solution)/shard_map/prepare/prepare/pallas_call | solution.py:430
  1.8 3.1 %collective-permute-start = (bf16[8,6272]{1,0:T(8,128)(2,1)S(1)}, bf16[8,6272]{1,0:T(8,128)(2,1)S(1)}, u32[]{:S(2)}, u32[]{:S(2)}) collective-permute-start(bf16[8,6272]{1,0:T(8,128)(2,1)S(1)} %prepare.1.refs_0_), channel_id=1, source_target_pairs={{0,8},{2,10},{4,12},{6,14},{8,0},{10,2},{12,4},{14,6},{16,24},{18,... | collective-permute-start | bytes 301064 | tf_op jit(solution)/shard_map/gather_blocks/ppermute | solution.py:45
  4.9 2.6 %collective-permute-start.4 = (bf16[8,6272]{1,0:T(8,128)(2,1)S(1)}, bf16[8,6272]{1,0:T(8,128)(2,1)S(1)}, u32[]{:S(2)}, u32[]{:S(2)}) collective-permute-start(bf16[8,6272]{1,0:T(8,128)(2,1)S(1)} %prepare.1.refs_0_), channel_id=1, source_target_pairs={{0,16},{2,18},{4,20},{6,22},{8,24},{10,26},{12,28},{14,30},{16,0},... | collective-permute-start | bytes 301064 | tf_op jit(solution)/shard_map/gather_blocks/ppermute | solution.py:45
  7.8 0.7 %route0.1 = (bf16[56,1024]{1,0:T(8,128)(2,1)S(1)}, bf16[56,1024]{1,0:T(8,128)(2,1)S(1)}, bf16[56,1024]{1,0:T(8,128)(2,1)S(1)}, bf16[56,1024]{1,0:T(8,128)(2,1)S(1)}) custom-call(bf16[8,6272]{1,0:T(8,128)(2,1)S(1)} %prepare.1.refs_0_, bf16[8,6272]{1,0:T(8,128)(2,1)S(1)} %collective-permute-done.refs_1_), custom_call_target="tpu_custom_call" | custom-call | flops 9000000512 | bytes 1 | tf_op jit(solution)/shard_map/near_blocks/route0/pallas_call | solution.py:459
  8.5 2.7 %collective-permute-start.1 = (bf16[56,1024]{1,0:T(8,128)(2,1)S(1)}, bf16[56,1024]{1,0:T(8,128)(2,1)S(1)}, u32[]{:S(2)}, u32[]{:S(2)}) collective-permute-start(bf16[56,1024]{1,0:T(8,128)(2,1)S(1)} %get-tuple-element.50), channel_id=1, source_target_pairs={{0,6},{2,4},{4,2},{6,0},{8,14},{10,12},{12,10},{14,8},{16,22},{18,... | collective-permute-start | bytes 344072 | tf_op jit(solution)/shard_map/near_blocks/ppermute | solution.py:53
  11.2 0.5 collective-permute-start.2
  12.1 1.2 %turn_down.1 = (bf16[4096,512]{1,0:T(8,128)(2,1)S(1)}, f32[8,128]{1,0:T(8,128)S(1)}) custom-call(bf16[1,512,4096]{2,1,0:T(8,128)(2,1)S(1)} %copy-done.2, bf16[56,1024]{1,0:T(8,128)(2,1)S(1)} %get-tuple-element.49.refs_1_.refs_0_.refs_4_), custom_call_target="tpu_custom_call" | custom-call | flops 1 | bytes 1 | tf_op jit(solution)/shard_map/turn_weights/turn_down/pallas_call | solution.py:489
  13.2 2.3 %collective-permute-done.4.refs_0_.refs_2_ = bf16[8,6272]{1,0:T(8,128)(2,1)S(1)} collective-permute-done((bf16[8,6272]{1,0:T(8,128)(2,1)S(1)}, bf16[8,6272]{1,0:T(8,128)(2,1)S(1)}, u32[]{:S(2)}, u32[]{:S(2)}) %collective-permute-start.4) | collective-permute-done | bytes 100384 | tf_op jit(solution)/shard_map/gather_blocks/ppermute | solution.py:45
  15.5 0.7 %route1.1 = (bf16[56,1024]{1,0:T(8,128)(2,1)S(1)}, bf16[56,1024]{1,0:T(8,128)(2,1)S(1)}, bf16[56,1024]{1,0:T(8,128)(2,1)S(1)}, bf16[56,1024]{1,0:T(8,128)(2,1)S(1)}) custom-call(bf16[8,6272]{1,0:T(8,128)(2,1)S(1)} %collective-permute-done.4.refs_0_.refs_2_, bf16[8,6272]{1,0:T(8,128)(2,1)S(1)} %collective-permute-done.5.refs_1_.refs_3_, ...), custom_call_target="tpu_custom_call" | custom-call | flops 9000000512 | bytes 1 | tf_op jit(solution)/shard_map/far_blocks/route1/pallas_call | solution.py:459
  16.2 2.5 %collective-permute-start.6 = (bf16[56,1024]{1,0:T(8,128)(2,1)S(1)}, bf16[56,1024]{1,0:T(8,128)(2,1)S(1)}, u32[]{:S(2)}, u32[]{:S(2)}) collective-permute-start(bf16[56,1024]{1,0:T(8,128)(2,1)S(1)} %get-tuple-element.55), channel_id=1, source_target_pairs={{0,6},{2,4},{4,2},{6,0},{8,14},{10,12},{12,10},{14,8},{16,22},{18,... | collective-permute-start | bytes 344072 | tf_op jit(solution)/shard_map/far_blocks/ppermute | solution.py:53
  19.3 0.5 %collective-permute-start.8 = (bf16[56,1024]{1,0:T(8,128)(2,1)S(1)}, bf16[56,1024]{1,0:T(8,128)(2,1)S(1)}, u32[]{:S(2)}, u32[]{:S(2)}) collective-permute-start(bf16[56,1024]{1,0:T(8,128)(2,1)S(1)} %get-tuple-element.57), channel_id=1, source_target_pairs={{0,2},{2,0},{4,6},{6,4},{8,10},{10,8},{12,14},{14,12},{16,18},{18,... | collective-permute-start | bytes 344072 | tf_op jit(solution)/shard_map/far_blocks/ppermute | solution.py:53
  19.8 2.4 %turn_rest.1 = (bf16[512,4096]{1,0:T(8,128)(2,1)S(1)}, bf16[512,4096]{1,0:T(8,128)(2,1)S(1)}, f32[8,128]{1,0:T(8,128)S(1)}) custom-call(bf16[1,4096,512]{2,1,0:T(8,128)(2,1)S(1)} %copy-done, bf16[1,4096,512]{2,1,0:T(8,128)(2,1)S(1)} %copy-done.1, bf16[56,1024]{1,0:T(8,128)(2,1)S(1)} %get-tuple-element.54.refs_4_.refs_2_.refs_0_), custom_call_target="tpu_custom_call" | custom-call | flops 1 | bytes 1 | tf_op jit(solution)/shard_map/turn_weights/turn_rest/pallas_call | solution.py:489
  23.0 1.0 %collective-permute-done.7.refs_2_ = bf16[56,1024]{1,0:T(8,128)(2,1)S(1)} collective-permute-done((bf16[56,1024]{1,0:T(8,128)(2,1)S(1)}, bf16[56,1024]{1,0:T(8,128)(2,1)S(1)}, u32[]{:S(2)}, u32[]{:S(2)}) %collective-permute-start.7) | collective-permute-done | bytes 114720 | tf_op jit(solution)/shard_map/far_blocks/ppermute | solution.py:53
  24.3 0.7 %forward_own.1 = (f32[128,512]{1,0:T(8,128)S(1)}, f32[128,512]{1,0:T(8,128)S(1)}) custom-call(bf16[128,2048]{1,0:T(8,128)(2,1)S(1)} %stack0.1.refs_0_, bf16[128,2048]{1,0:T(8,128)(2,1)S(1)} %stack1.1.refs_1_, bf16[1,4096,512]{2,1,0:T(8,128)(2,1)S(1)} %copy-done, bf16[1,4096,512]{2,1,0:T(8,128)(2,1)S(1)} %copy-done.1), custom_call_target="tpu_custom_call" | custom-call | flops 1 | bytes 1 | tf_op jit(solution)/shard_map/forward/forward_own/pallas_call | solution.py:525
  25.5 0.7 %collective-permute-done.10.refs_6_.refs_7_.refs_3_ = bf16[128,2048]{1,0:T(8,128)(2,1)S(1)} collective-permute-done((bf16[128,2048]{1,0:T(8,128)(2,1)S(1)}, bf16[128,2048]{1,0:T(8,128)(2,1)S(1)}, u32[]{:S(2)}, u32[]{:S(2)}) %collective-permute-start.10) | collective-permute-done | bytes 524320 | tf_op jit(solution)/shard_map/gather_cores/ppermute | solution.py:58
  26.2 1.4 %forward.1 = (f32[128,512]{1,0:T(8,128)S(1)}, f32[128,512]{1,0:T(8,128)S(1)}, bf16[128,512]{1,0:T(8,128)(2,1)S(1)}, bf16[128,2048]{1,0:T(8,128)(2,1)S(1)}, bf16[128,2048]{1,0:T(8,128)(2,1)S(1)}) custom-call(f32[128,512]{1,0:T(8,128)S(1)} %get-tuple-element.60.refs_0_, f32[128,512]{1,0:T(8,128)S(1)} %get-tuple-element.61.refs_1_, ...), custom_call_target="tpu_custom_call" | custom-call | flops 1 | bytes 1 | tf_op jit(solution)/shard_map/forward/forward/pallas_call | solution.py:543
  27.8 1.2 %backward.1 = (bf16[128,512]{1,0:T(8,128)(2,1)S(1)}, bf16[128,512]{1,0:T(8,128)(2,1)S(1)}, bf16[128,2048]{1,0:T(8,128)(2,1)S(1)}) custom-call(f32[128,512]{1,0:T(8,128)S(1)} %backward_own.1.refs_7_.refs_0_, bf16[512,4096]{1,0:T(8,128)(2,1)S(1)} %get-tuple-element.76.refs_1_.refs_2_, bf16[512,4096]{1,0:T(8,128)(2,1)S(1)} %get-tuple-element.77.refs_2_.refs_3_, ...), custom_call_target="tpu_custom_call" | custom-call | flops 1 | bytes 1 | tf_op jit(solution)/shard_map/backward/backward/pallas_call | solution.py:591
  29.8 1.0 %collective-permute-start.12 = (bf16[56,1024]{1,0:T(8,128)(2,1)S(1)}, bf16[56,1024]{1,0:T(8,128)(2,1)S(1)}, u32[]{:S(2)}, u32[]{:S(2)}) collective-permute-start(bf16[56,1024]{1,0:T(8,128)(2,1)S(1)} %get-tuple-element.66), channel_id=1, source_target_pairs={{0,2},{2,0},{4,6},{6,4},{8,10},{10,8},{12,14},{14,12},{16,18},{18,... | collective-permute-start | bytes 344072 | tf_op jit(solution)/shard_map/return_out/ppermute | solution.py:53
  30.8 1.5 %collective-permute-start.13 = (bf16[56,1024]{1,0:T(8,128)(2,1)S(1)}, bf16[56,1024]{1,0:T(8,128)(2,1)S(1)}, u32[]{:S(2)}, u32[]{:S(2)}) collective-permute-start(bf16[56,1024]{1,0:T(8,128)(2,1)S(1)} %get-tuple-element.67), channel_id=1, source_target_pairs={{0,4},{2,6},{4,0},{6,2},{8,12},{10,14},{12,8},{14,10},{16,20},{18,... | collective-permute-start | bytes 344072 | tf_op jit(solution)/shard_map/return_out/ppermute | solution.py:53
  32.3 1.0 %collective-permute-start.14 = (bf16[56,1024]{1,0:T(8,128)(2,1)S(1)}, bf16[56,1024]{1,0:T(8,128)(2,1)S(1)}, u32[]{:S(2)}, u32[]{:S(2)}) collective-permute-start(bf16[56,1024]{1,0:T(8,128)(2,1)S(1)} %get-tuple-element.68), channel_id=1, source_target_pairs={{0,6},{2,4},{4,2},{6,0},{8,14},{10,12},{12,10},{14,8},{16,22},{18,... | collective-permute-start | bytes 344072 | tf_op jit(solution)/shard_map/return_out/ppermute | solution.py:53
  33.3 0.8 %input_own.1.refs_0_ = bf16[128,2048]{1,0:T(8,128)(2,1)S(1)} custom-call(bf16[128,512]{1,0:T(8,128)(2,1)S(1)} %get-tuple-element.80.refs_0_, bf16[128,512]{1,0:T(8,128)(2,1)S(1)} %get-tuple-element.81.refs_1_, bf16[512,4096]{1,0:T(8,128)(2,1)S(1)} %get-tuple-element.76.refs_1_.refs_2_, bf16[512,4096]{1,0:T(8,128)(2,1)S(1)} %get-tuple-element.77.refs_2_.refs_3_, ...), custom_call_target="tpu_custom_call" | custom-call | flops 1 | bytes 1 | tf_op jit(solution)/shard_map/backward/input_own/pallas_call | solution.py:600
  34.4 1.0 %collective-permute-start.19 = (bf16[56,1024]{1,0:T(8,128)(2,1)S(1)}, bf16[56,1024]{1,0:T(8,128)(2,1)S(1)}, u32[]{:S(2)}, u32[]{:S(2)}) collective-permute-start(bf16[56,1024]{1,0:T(8,128)(2,1)S(1)} %get-tuple-element.84), channel_id=1, source_target_pairs={{0,2},{2,0},{4,6},{6,4},{8,10},{10,8},{12,14},{14,12},{16,18},{18,... | collective-permute-start | bytes 344072 | tf_op jit(solution)/shard_map/return_grad/ppermute | solution.py:53
  35.3 1.5 %collective-permute-start.20 = (bf16[56,1024]{1,0:T(8,128)(2,1)S(1)}, bf16[56,1024]{1,0:T(8,128)(2,1)S(1)}, u32[]{:S(2)}, u32[]{:S(2)}) collective-permute-start(bf16[56,1024]{1,0:T(8,128)(2,1)S(1)} %get-tuple-element.85), channel_id=1, source_target_pairs={{0,4},{2,6},{4,0},{6,2},{8,12},{10,14},{12,8},{14,10},{16,20},{18,... | collective-permute-start | bytes 344072 | tf_op jit(solution)/shard_map/return_grad/ppermute | solution.py:53
  36.8 1.1 %collective-permute-start.21 = (bf16[56,1024]{1,0:T(8,128)(2,1)S(1)}, bf16[56,1024]{1,0:T(8,128)(2,1)S(1)}, u32[]{:S(2)}, u32[]{:S(2)}) collective-permute-start(bf16[56,1024]{1,0:T(8,128)(2,1)S(1)} %get-tuple-element.86), channel_id=1, source_target_pairs={{0,6},{2,4},{4,2},{6,0},{8,14},{10,12},{12,10},{14,8},{16,22},{18,... | collective-permute-start | bytes 344072 | tf_op jit(solution)/shard_map/return_grad/ppermute | solution.py:53
  37.9 1.3 %collective-permute-done.14.refs_3_ = bf16[56,1024]{1,0:T(8,128)(2,1)S(1)} collective-permute-done((bf16[56,1024]{1,0:T(8,128)(2,1)S(1)}, bf16[56,1024]{1,0:T(8,128)(2,1)S(1)}, u32[]{:S(2)}, u32[]{:S(2)}) %collective-permute-start.14) | collective-permute-done | bytes 114720 | tf_op jit(solution)/shard_map/return_out/ppermute | solution.py:53
  39.5 2.7 %collective-permute-start.15 = (bf16[24,1024]{1,0:T(8,128)(2,1)S(1)}, bf16[24,1024]{1,0:T(8,128)(2,1)S(1)}, u32[]{:S(2)}, u32[]{:S(2)}) collective-permute-start(bf16[24,1024]{1,0:T(8,128)(2,1)S(1)} %get-tuple-element.72), channel_id=1, source_target_pairs={{0,24},{2,26},{4,28},{6,30},{8,16},{10,18},{12,20},{14,22},{16,8},... | collective-permute-start | bytes 147464 | tf_op jit(solution)/shard_map/return_out/ppermute | solution.py:45
  42.7 1.3 %collective-permute-start.17 = (bf16[24,1024]{1,0:T(8,128)(2,1)S(1)}, bf16[24,1024]{1,0:T(8,128)(2,1)S(1)}, u32[]{:S(2)}, u32[]{:S(2)}) collective-permute-start(bf16[24,1024]{1,0:T(8,128)(2,1)S(1)} %get-tuple-element.74), channel_id=1, source_target_pairs={{0,8},{2,10},{4,12},{6,14},{8,0},{10,2},{12,4},{14,6},{16,24},{18,... | collective-permute-start | bytes 147464 | tf_op jit(solution)/shard_map/return_out/ppermute | solution.py:45
  44.2 2.7 %collective-permute-start.22 = (bf16[24,1024]{1,0:T(8,128)(2,1)S(1)}, bf16[24,1024]{1,0:T(8,128)(2,1)S(1)}, u32[]{:S(2)}, u32[]{:S(2)}) collective-permute-start(bf16[24,1024]{1,0:T(8,128)(2,1)S(1)} %get-tuple-element.89), channel_id=1, source_target_pairs={{0,24},{2,26},{4,28},{6,30},{8,16},{10,18},{12,20},{14,22},{16,8},... | collective-permute-start | bytes 147464 | tf_op jit(solution)/shard_map/return_grad/ppermute | solution.py:45
  46.9 1.8 %collective-permute-start.24 = (bf16[24,1024]{1,0:T(8,128)(2,1)S(1)}, bf16[24,1024]{1,0:T(8,128)(2,1)S(1)}, u32[]{:S(2)}, u32[]{:S(2)}) collective-permute-start(bf16[24,1024]{1,0:T(8,128)(2,1)S(1)} %get-tuple-element.91), channel_id=1, source_target_pairs={{0,8},{2,10},{4,12},{6,14},{8,0},{10,2},{12,4},{14,6},{16,24},{18,... | collective-permute-start | bytes 147464 | tf_op jit(solution)/shard_map/return_grad/ppermute | solution.py:45
  48.7 2.4 %down_grad.1 = bf16[1,512,4096]{2,1,0:T(8,128)(2,1)} custom-call(bf16[128,2048]{1,0:T(8,128)(2,1)S(1)} %stack0.1.refs_0_, bf16[128,2048]{1,0:T(8,128)(2,1)S(1)} %stack1.1.refs_1_, bf16[128,2048]{1,0:T(8,128)(2,1)S(1)} %collective-permute-done.9.refs_5_.refs_6_.refs_2_, bf16[128,2048]{1,0:T(8,128)(2,1)S(1)} %collective-permute-done.10.refs_6_.refs_7_.refs_3_, ...), custom_call_target="tpu_custom_call" | custom-call | tf_op jit(solution)/shard_map/down_grad/down_grad/pallas_call | solution.py:616
  51.1 0.7 %final.2 = (bf16[12,2048]{1,0:T(8,128)(2,1)}, f32[8,128]{1,0:T(8,128)S(1)}) custom-call(bf16[24,1024]{1,0:T(8,128)(2,1)S(1)} %get-tuple-element.71.refs_0_, bf16[24,1024]{1,0:T(8,128)(2,1)S(1)} %collective-permute-done.15.refs_1_, bf16[24,1024]{1,0:T(8,128)(2,1)S(1)} %collective-permute-done.16.refs_2_, bf16[24,1024]{1,0:T(8,128)(2,1)S(1)} %collective-permute-done.17.refs_3_), custom_call_target="tpu_custom_call" | custom-call | tf_op jit(solution)/shard_map/final/pallas_call | solution.py:577
  51.9 0.7 %final.3 = (bf16[12,2048]{1,0:T(8,128)(2,1)}, f32[8,128]{1,0:T(8,128)}) custom-call(bf16[24,1024]{1,0:T(8,128)(2,1)S(1)} %get-tuple-element.88.refs_0_.refs_5_, bf16[24,1024]{1,0:T(8,128)(2,1)S(1)} %collective-permute-done.22.refs_1_, bf16[24,1024]{1,0:T(8,128)(2,1)S(1)} %collective-permute-done.23.refs_2_, ...), custom_call_target="tpu_custom_call" | custom-call | tf_op jit(solution)/shard_map/final/pallas_call | solution.py:577
  (44 shorter events, 4.8 us)
Async XLA Ops:
  1.8 10.2 %copy-start.2 = (bf16[1,512,4096]{2,1,0:T(8,128)(2,1)S(1)}, bf16[1,512,4096]{2,1,0:T(8,128)(2,1)}, u32[]{:S(2)}) copy-start(bf16[1,512,4096]{2,1,0:T(8,128)(2,1)} %refs_4_.1) | copy-start | bytes 12582916
  1.8 5.9 %collective-permute-start = (bf16[8,6272]{1,0:T(8,128)(2,1)S(1)}, bf16[8,6272]{1,0:T(8,128)(2,1)S(1)}, u32[]{:S(2)}, u32[]{:S(2)}) collective-permute-start(bf16[8,6272]{1,0:T(8,128)(2,1)S(1)} %prepare.1.refs_0_), channel_id=1, source_target_pairs={{0,8},{2,10},{4,12},{6,14},{8,0},{10,2},{12,4},{14,6},{16,24},{18,... | collective-permute-start | bytes 301064 | tf_op jit(solution)/shard_map/gather_blocks/ppermute | solution.py:45
  4.9 10.6 %collective-permute-start.4 = (bf16[8,6272]{1,0:T(8,128)(2,1)S(1)}, bf16[8,6272]{1,0:T(8,128)(2,1)S(1)}, u32[]{:S(2)}, u32[]{:S(2)}) collective-permute-start(bf16[8,6272]{1,0:T(8,128)(2,1)S(1)} %prepare.1.refs_0_), channel_id=1, source_target_pairs={{0,16},{2,18},{4,20},{6,22},{8,24},{10,26},{12,28},{14,30},{16,0},... | collective-permute-start | bytes 301064 | tf_op jit(solution)/shard_map/gather_blocks/ppermute | solution.py:45
  7.5 8.0 %collective-permute-start.5 = (bf16[8,6272]{1,0:T(8,128)(2,1)S(1)}, bf16[8,6272]{1,0:T(8,128)(2,1)S(1)}, u32[]{:S(2)}, u32[]{:S(2)}) collective-permute-start(bf16[8,6272]{1,0:T(8,128)(2,1)S(1)} %prepare.1.refs_0_), channel_id=1, source_target_pairs={{0,24},{2,26},{4,28},{6,30},{8,16},{10,18},{12,20},{14,22},{16,8},... | collective-permute-start | bytes 301064 | tf_op jit(solution)/shard_map/gather_blocks/ppermute | solution.py:45
  8.5 10.8 %collective-permute-start.1 = (bf16[56,1024]{1,0:T(8,128)(2,1)S(1)}, bf16[56,1024]{1,0:T(8,128)(2,1)S(1)}, u32[]{:S(2)}, u32[]{:S(2)}) collective-permute-start(bf16[56,1024]{1,0:T(8,128)(2,1)S(1)} %get-tuple-element.50), channel_id=1, source_target_pairs={{0,6},{2,4},{4,2},{6,0},{8,14},{10,12},{12,10},{14,8},{16,22},{18,... | collective-permute-start | bytes 344072 | tf_op jit(solution)/shard_map/near_blocks/ppermute | solution.py:53
  11.2 11.5 %collective-permute-start.2 = (bf16[56,1024]{1,0:T(8,128)(2,1)S(1)}, bf16[56,1024]{1,0:T(8,128)(2,1)S(1)}, u32[]{:S(2)}, u32[]{:S(2)}) collective-permute-start(bf16[56,1024]{1,0:T(8,128)(2,1)S(1)} %get-tuple-element.51), channel_id=1, source_target_pairs={{0,4},{2,6},{4,0},{6,2},{8,12},{10,14},{12,8},{14,10},{16,20},{18,... | collective-permute-start | bytes 344072 | tf_op jit(solution)/shard_map/near_blocks/ppermute | solution.py:53
  11.8 11.0 %collective-permute-start.3 = (bf16[56,1024]{1,0:T(8,128)(2,1)S(1)}, bf16[56,1024]{1,0:T(8,128)(2,1)S(1)}, u32[]{:S(2)}, u32[]{:S(2)}) collective-permute-start(bf16[56,1024]{1,0:T(8,128)(2,1)S(1)} %get-tuple-element.52), channel_id=1, source_target_pairs={{0,2},{2,0},{4,6},{6,4},{8,10},{10,8},{12,14},{14,12},{16,18},{18,... | collective-permute-start | bytes 344072 | tf_op jit(solution)/shard_map/near_blocks/ppermute | solution.py:53
  15.5 4.3 %copy-start = (bf16[1,4096,512]{2,1,0:T(8,128)(2,1)S(1)}, bf16[1,4096,512]{2,1,0:T(8,128)(2,1)}, u32[]{:S(2)}) copy-start(bf16[1,4096,512]{2,1,0:T(8,128)(2,1)} %refs_2_.5) | copy-start | bytes 12582916
  15.5 4.3 %copy-start.1 = (bf16[1,4096,512]{2,1,0:T(8,128)(2,1)S(1)}, bf16[1,4096,512]{2,1,0:T(8,128)(2,1)}, u32[]{:S(2)}) copy-start(bf16[1,4096,512]{2,1,0:T(8,128)(2,1)} %refs_3_.5) | copy-start | bytes 12582916
  16.2 6.7 %collective-permute-start.6 = (bf16[56,1024]{1,0:T(8,128)(2,1)S(1)}, bf16[56,1024]{1,0:T(8,128)(2,1)S(1)}, u32[]{:S(2)}, u32[]{:S(2)}) collective-permute-start(bf16[56,1024]{1,0:T(8,128)(2,1)S(1)} %get-tuple-element.55), channel_id=1, source_target_pairs={{0,6},{2,4},{4,2},{6,0},{8,14},{10,12},{12,10},{14,8},{16,22},{18,... | collective-permute-start | bytes 344072 | tf_op jit(solution)/shard_map/far_blocks/ppermute | solution.py:53
  18.8 5.2 %collective-permute-start.7 = (bf16[56,1024]{1,0:T(8,128)(2,1)S(1)}, bf16[56,1024]{1,0:T(8,128)(2,1)S(1)}, u32[]{:S(2)}, u32[]{:S(2)}) collective-permute-start(bf16[56,1024]{1,0:T(8,128)(2,1)S(1)} %get-tuple-element.56), channel_id=1, source_target_pairs={{0,4},{2,6},{4,0},{6,2},{8,12},{10,14},{12,8},{14,10},{16,20},{18,... | collective-permute-start | bytes 344072 | tf_op jit(solution)/shard_map/far_blocks/ppermute | solution.py:53
  19.3 4.8 %collective-permute-start.8 = (bf16[56,1024]{1,0:T(8,128)(2,1)S(1)}, bf16[56,1024]{1,0:T(8,128)(2,1)S(1)}, u32[]{:S(2)}, u32[]{:S(2)}) collective-permute-start(bf16[56,1024]{1,0:T(8,128)(2,1)S(1)} %get-tuple-element.57), channel_id=1, source_target_pairs={{0,2},{2,0},{4,6},{6,4},{8,10},{10,8},{12,14},{14,12},{16,18},{18,... | collective-permute-start | bytes 344072 | tf_op jit(solution)/shard_map/far_blocks/ppermute | solution.py:53
  22.9 2.6 %collective-permute-start.9 = (bf16[128,2048]{1,0:T(8,128)(2,1)S(1)}, bf16[128,2048]{1,0:T(8,128)(2,1)S(1)}, u32[]{:S(2)}, u32[]{:S(2)}) collective-permute-start(bf16[128,2048]{1,0:T(8,128)(2,1)S(1)} %stack0.1.refs_0_), channel_id=1, source_target_pairs={{0,1},{1,0},{2,3},{3,2},{4,5},{5,4},{6,7},{7,6},{8,9},{9,8},{10,11... | collective-permute-start | bytes 1572872 | tf_op jit(solution)/shard_map/gather_cores/ppermute | solution.py:58
  24.2 2.0 %collective-permute-start.10 = (bf16[128,2048]{1,0:T(8,128)(2,1)S(1)}, bf16[128,2048]{1,0:T(8,128)(2,1)S(1)}, u32[]{:S(2)}, u32[]{:S(2)}) collective-permute-start(bf16[128,2048]{1,0:T(8,128)(2,1)S(1)} %stack1.1.refs_1_), channel_id=1, source_target_pairs={{0,1},{1,0},{2,3},{3,2},{4,5},{5,4},{6,7},{7,6},{8,9},{9,8},{10,11... | collective-permute-start | bytes 1572872 | tf_op jit(solution)/shard_map/gather_cores/ppermute | solution.py:58
  27.6 2.0 %collective-permute-start.11 = (bf16[128,2048]{1,0:T(8,128)(2,1)S(1)}, bf16[128,2048]{1,0:T(8,128)(2,1)S(1)}, u32[]{:S(2)}, u32[]{:S(2)}) collective-permute-start(bf16[128,2048]{1,0:T(8,128)(2,1)S(1)} %get-tuple-element.64), channel_id=1, source_target_pairs={{0,1},{1,0},{2,3},{3,2},{4,5},{5,4},{6,7},{7,6},{8,9},{9,8},{10,11... | collective-permute-start | bytes 1572872 | tf_op jit(solution)/shard_map/return_out/ppermute | solution.py:58
  29.0 5.1 %collective-permute-start.18 = (bf16[128,2048]{1,0:T(8,128)(2,1)S(1)}, bf16[128,2048]{1,0:T(8,128)(2,1)S(1)}, u32[]{:S(2)}, u32[]{:S(2)}) collective-permute-start(bf16[128,2048]{1,0:T(8,128)(2,1)S(1)} %get-tuple-element.82), channel_id=1, source_target_pairs={{0,1},{1,0},{2,3},{3,2},{4,5},{5,4},{6,7},{7,6},{8,9},{9,8},{10,11... | collective-permute-start | bytes 1572872 | tf_op jit(solution)/shard_map/return_grad/ppermute | solution.py:58
  29.8 7.0 %collective-permute-start.12 = (bf16[56,1024]{1,0:T(8,128)(2,1)S(1)}, bf16[56,1024]{1,0:T(8,128)(2,1)S(1)}, u32[]{:S(2)}, u32[]{:S(2)}) collective-permute-start(bf16[56,1024]{1,0:T(8,128)(2,1)S(1)} %get-tuple-element.66), channel_id=1, source_target_pairs={{0,2},{2,0},{4,6},{6,4},{8,10},{10,8},{12,14},{14,12},{16,18},{18,... | collective-permute-start | bytes 344072 | tf_op jit(solution)/shard_map/return_out/ppermute | solution.py:53
  30.8 7.1 %collective-permute-start.13 = (bf16[56,1024]{1,0:T(8,128)(2,1)S(1)}, bf16[56,1024]{1,0:T(8,128)(2,1)S(1)}, u32[]{:S(2)}, u32[]{:S(2)}) collective-permute-start(bf16[56,1024]{1,0:T(8,128)(2,1)S(1)} %get-tuple-element.67), channel_id=1, source_target_pairs={{0,4},{2,6},{4,0},{6,2},{8,12},{10,14},{12,8},{14,10},{16,20},{18,... | collective-permute-start | bytes 344072 | tf_op jit(solution)/shard_map/return_out/ppermute | solution.py:53
  32.3 7.0 %collective-permute-start.14 = (bf16[56,1024]{1,0:T(8,128)(2,1)S(1)}, bf16[56,1024]{1,0:T(8,128)(2,1)S(1)}, u32[]{:S(2)}, u32[]{:S(2)}) collective-permute-start(bf16[56,1024]{1,0:T(8,128)(2,1)S(1)} %get-tuple-element.68), channel_id=1, source_target_pairs={{0,6},{2,4},{4,2},{6,0},{8,14},{10,12},{12,10},{14,8},{16,22},{18,... | collective-permute-start | bytes 344072 | tf_op jit(solution)/shard_map/return_out/ppermute | solution.py:53
  34.4 8.4 %collective-permute-start.19 = (bf16[56,1024]{1,0:T(8,128)(2,1)S(1)}, bf16[56,1024]{1,0:T(8,128)(2,1)S(1)}, u32[]{:S(2)}, u32[]{:S(2)}) collective-permute-start(bf16[56,1024]{1,0:T(8,128)(2,1)S(1)} %get-tuple-element.84), channel_id=1, source_target_pairs={{0,2},{2,0},{4,6},{6,4},{8,10},{10,8},{12,14},{14,12},{16,18},{18,... | collective-permute-start | bytes 344072 | tf_op jit(solution)/shard_map/return_grad/ppermute | solution.py:53
  35.3 8.7 %collective-permute-start.20 = (bf16[56,1024]{1,0:T(8,128)(2,1)S(1)}, bf16[56,1024]{1,0:T(8,128)(2,1)S(1)}, u32[]{:S(2)}, u32[]{:S(2)}) collective-permute-start(bf16[56,1024]{1,0:T(8,128)(2,1)S(1)} %get-tuple-element.85), channel_id=1, source_target_pairs={{0,4},{2,6},{4,0},{6,2},{8,12},{10,14},{12,8},{14,10},{16,20},{18,... | collective-permute-start | bytes 344072 | tf_op jit(solution)/shard_map/return_grad/ppermute | solution.py:53
  36.8 7.2 %collective-permute-start.21 = (bf16[56,1024]{1,0:T(8,128)(2,1)S(1)}, bf16[56,1024]{1,0:T(8,128)(2,1)S(1)}, u32[]{:S(2)}, u32[]{:S(2)}) collective-permute-start(bf16[56,1024]{1,0:T(8,128)(2,1)S(1)} %get-tuple-element.86), channel_id=1, source_target_pairs={{0,6},{2,4},{4,2},{6,0},{8,14},{10,12},{12,10},{14,8},{16,22},{18,... | collective-permute-start | bytes 344072 | tf_op jit(solution)/shard_map/return_grad/ppermute | solution.py:53
  39.5 7.4 %collective-permute-start.15 = (bf16[24,1024]{1,0:T(8,128)(2,1)S(1)}, bf16[24,1024]{1,0:T(8,128)(2,1)S(1)}, u32[]{:S(2)}, u32[]{:S(2)}) collective-permute-start(bf16[24,1024]{1,0:T(8,128)(2,1)S(1)} %get-tuple-element.72), channel_id=1, source_target_pairs={{0,24},{2,26},{4,28},{6,30},{8,16},{10,18},{12,20},{14,22},{16,8},... | collective-permute-start | bytes 147464 | tf_op jit(solution)/shard_map/return_out/ppermute | solution.py:45
  42.2 8.9 %collective-permute-start.16 = (bf16[24,1024]{1,0:T(8,128)(2,1)S(1)}, bf16[24,1024]{1,0:T(8,128)(2,1)S(1)}, u32[]{:S(2)}, u32[]{:S(2)}) collective-permute-start(bf16[24,1024]{1,0:T(8,128)(2,1)S(1)} %get-tuple-element.73), channel_id=1, source_target_pairs={{0,16},{2,18},{4,20},{6,22},{8,24},{10,26},{12,28},{14,30},{16,0},... | collective-permute-start | bytes 147464 | tf_op jit(solution)/shard_map/return_out/ppermute | solution.py:45
  42.7 8.4 %collective-permute-start.17 = (bf16[24,1024]{1,0:T(8,128)(2,1)S(1)}, bf16[24,1024]{1,0:T(8,128)(2,1)S(1)}, u32[]{:S(2)}, u32[]{:S(2)}) collective-permute-start(bf16[24,1024]{1,0:T(8,128)(2,1)S(1)} %get-tuple-element.74), channel_id=1, source_target_pairs={{0,8},{2,10},{4,12},{6,14},{8,0},{10,2},{12,4},{14,6},{16,24},{18,... | collective-permute-start | bytes 147464 | tf_op jit(solution)/shard_map/return_out/ppermute | solution.py:45
  44.2 7.5 %collective-permute-start.22 = (bf16[24,1024]{1,0:T(8,128)(2,1)S(1)}, bf16[24,1024]{1,0:T(8,128)(2,1)S(1)}, u32[]{:S(2)}, u32[]{:S(2)}) collective-permute-start(bf16[24,1024]{1,0:T(8,128)(2,1)S(1)} %get-tuple-element.89), channel_id=1, source_target_pairs={{0,24},{2,26},{4,28},{6,30},{8,16},{10,18},{12,20},{14,22},{16,8},... | collective-permute-start | bytes 147464 | tf_op jit(solution)/shard_map/return_grad/ppermute | solution.py:45
  46.9 5.0 %collective-permute-start.23 = (bf16[24,1024]{1,0:T(8,128)(2,1)S(1)}, bf16[24,1024]{1,0:T(8,128)(2,1)S(1)}, u32[]{:S(2)}, u32[]{:S(2)}) collective-permute-start(bf16[24,1024]{1,0:T(8,128)(2,1)S(1)} %get-tuple-element.90), channel_id=1, source_target_pairs={{0,16},{2,18},{4,20},{6,22},{8,24},{10,26},{12,28},{14,30},{16,0},... | collective-permute-start | bytes 147464 | tf_op jit(solution)/shard_map/return_grad/ppermute | solution.py:45
  46.9 5.0 %collective-permute-start.24 = (bf16[24,1024]{1,0:T(8,128)(2,1)S(1)}, bf16[24,1024]{1,0:T(8,128)(2,1)S(1)}, u32[]{:S(2)}, u32[]{:S(2)}) collective-permute-start(bf16[24,1024]{1,0:T(8,128)(2,1)S(1)} %get-tuple-element.91), channel_id=1, source_target_pairs={{0,8},{2,10},{4,12},{6,14},{8,0},{10,2},{12,4},{14,6},{16,24},{18,... | collective-permute-start | bytes 147464 | tf_op jit(solution)/shard_map/return_grad/ppermute | solution.py:45

commit v10 on v9

--- a/solution.py
+++ b/solution.py
@@ -9,7 +9,7 @@
 BF16 = jnp.bfloat16
 F32 = jnp.float32
 META = 128
-COSTS = {"PREPARE": 20, "ROUTE0": 9, "ROUTE1": 9}
+COSTS = {"PREPARE": 20, "ROUTE0": 9, "ROUTE1": 9, "TURN_REST": 3}
 SUBLANES = 8
 VMEM_LIMIT = 20 * 1024 * 1024
 
@@ -397,8 +397,8 @@
 
 
 def final_kernel(dims, *refs):
-    outer, tokens, half = dims
-    out_ref = refs[-2]
+    outer, tokens, half, place = dims
+    out_ref = refs[place]
     total = refs[0][...].astype(F32)
     for part in refs[1:outer]:
         total = total + part[...].astype(F32)
@@ -575,10 +575,10 @@
 
     def finish(blocks, after=()):
         return pl.pallas_call(
-            functools.partial(final_kernel, (outer, tokens, half)),
-            out_shape=[shape(tokens, width), shape(8, META, F32)],
+            functools.partial(final_kernel, (outer, tokens, half, -1 if after else -2)),
+            out_shape=[shape(tokens, width)] + ([] if after else [shape(8, META, F32)]),
             in_specs=whole_specs(outer + len(after)),
-            out_specs=whole_specs(2),
+            out_specs=whole_specs(1 if after else 2),
             compiler_params=params(),
             name="final",
         )(*flipped(blocks), *after)
@@ -627,7 +627,7 @@
         )(*own_stacks, *other_stacks, act, back_blocks[0])
 
     mixed_out, done = finish(out_blocks)
-    input_grad, done = finish(back_blocks, (done,))
+    (input_grad,) = finish(back_blocks, (done,))
     return (mixed_out, input_grad, down_grad)
 
 

time: 52.7 us -> 52.7 us (level)
  transfers between devices with their start and end apart: 25 -> 25, of which waited for: 8 -> 8; matrix products, arithmetic and copies ran while one was open for 0% -> 0% of each run, Pallas kernels for 24% -> 25%
where the time goes in v10:
time: 52.7 us; the launch traced here: 52.5 us
  starting transfers between devices  29.6 us (56%)
  Pallas kernels  16.1 us (31%)
  waiting for transfers between devices  5.95 us (11%)
  between operations  0.86 us (2%)
    ppermute x9, starting transfers between devices, send_outer(): return lax.ppermute(x, 'expert', pairs)  14.6 us
    ppermute x12, starting transfers between devices, send_inner(): return lax.ppermute(x, 'expert', pairs)  14.2 us
    pallas_call x2, Pallas kernels, turn(): pl.pallas_call(functools.partial(turn_kernel, len(picked)), out_shape=[pl...  3.56 us
    ppermute x9, waiting for transfers between devices, send_outer(): return lax.ppermute(x, 'expert', pairs)  2.66 us
    ppermute x12, waiting for transfers between devices, send_inner(): return lax.ppermute(x, 'expert', pairs)  2.48 us
    pallas_call x1, Pallas kernels, on_device(): pl.pallas_call(functools.partial(down_kernel, dims, counts, chunks), out_...  2.38 us
    pallas_call x2, Pallas kernels, route(): pl.pallas_call(functools.partial(route_kernel, route_dims, len(members),...  1.46 us
    pallas_call x1, Pallas kernels, on_device(): pl.pallas_call(functools.partial(forward_kernel, dims, counts), out_shape...  1.43 us
  transfers between devices with their start and end apart: 25, of which 8 were waited for; matrix products, arithmetic and copies ran while one was open for 0% of the time, Pallas kernels for 25%

profile of v10, /device:TPU:0, one launch (start us, length us, event | category | flops | bytes accessed | tf_op | source)
XLA Modules:
  0.0 52.5 jit_solution(11854003165058536316)
XLA Ops:
  0.6 1.2 %prepare.1.refs_0_ = bf16[8,6272]{1,0:T(8,128)(2,1)S(1)} custom-call(s32[8,12]{1,0:T(8,128)} %bitcast.2, f32[8,12]{1,0:T(8,128)} %bitcast.3, bf16[12,2048]{1,0:T(8,128)(2,1)} %refs_2_.3, bf16[12,2048]{1,0:T(8,128)(2,1)} %refs_3_.3), custom_call_target="tpu_custom_call" | custom-call | flops 20000000000 | bytes 1 | tf_op jit(solution)/shard_map/prepare/prepare/pallas_call | solution.py:430
  1.8 3.1 %collective-permute-start = (bf16[8,6272]{1,0:T(8,128)(2,1)S(1)}, bf16[8,6272]{1,0:T(8,128)(2,1)S(1)}, u32[]{:S(2)}, u32[]{:S(2)}) collective-permute-start(bf16[8,6272]{1,0:T(8,128)(2,1)S(1)} %prepare.1.refs_0_), channel_id=1, source_target_pairs={{0,8},{2,10},{4,12},{6,14},{8,0},{10,2},{12,4},{14,6},{16,24},{18,... | collective-permute-start | bytes 301064 | tf_op jit(solution)/shard_map/gather_blocks/ppermute | solution.py:45
  4.9 2.6 %collective-permute-start.4 = (bf16[8,6272]{1,0:T(8,128)(2,1)S(1)}, bf16[8,6272]{1,0:T(8,128)(2,1)S(1)}, u32[]{:S(2)}, u32[]{:S(2)}) collective-permute-start(bf16[8,6272]{1,0:T(8,128)(2,1)S(1)} %prepare.1.refs_0_), channel_id=1, source_target_pairs={{0,16},{2,18},{4,20},{6,22},{8,24},{10,26},{12,28},{14,30},{16,0},... | collective-permute-start | bytes 301064 | tf_op jit(solution)/shard_map/gather_blocks/ppermute | solution.py:45
  7.8 0.7 %route0.1 = (bf16[56,1024]{1,0:T(8,128)(2,1)S(1)}, bf16[56,1024]{1,0:T(8,128)(2,1)S(1)}, bf16[56,1024]{1,0:T(8,128)(2,1)S(1)}, bf16[56,1024]{1,0:T(8,128)(2,1)S(1)}) custom-call(bf16[8,6272]{1,0:T(8,128)(2,1)S(1)} %prepare.1.refs_0_, bf16[8,6272]{1,0:T(8,128)(2,1)S(1)} %collective-permute-done.refs_1_), custom_call_target="tpu_custom_call" | custom-call | flops 9000000512 | bytes 1 | tf_op jit(solution)/shard_map/near_blocks/route0/pallas_call | solution.py:459
  8.5 2.7 %collective-permute-start.1 = (bf16[56,1024]{1,0:T(8,128)(2,1)S(1)}, bf16[56,1024]{1,0:T(8,128)(2,1)S(1)}, u32[]{:S(2)}, u32[]{:S(2)}) collective-permute-start(bf16[56,1024]{1,0:T(8,128)(2,1)S(1)} %get-tuple-element.49), channel_id=1, source_target_pairs={{0,6},{2,4},{4,2},{6,0},{8,14},{10,12},{12,10},{14,8},{16,22},{18,... | collective-permute-start | bytes 344072 | tf_op jit(solution)/shard_map/near_blocks/ppermute | solution.py:53
  11.2 0.5 collective-permute-start.2
  12.1 1.2 %turn_down.1 = (bf16[4096,512]{1,0:T(8,128)(2,1)S(1)}, f32[8,128]{1,0:T(8,128)S(1)}) custom-call(bf16[1,512,4096]{2,1,0:T(8,128)(2,1)S(1)} %copy-done, bf16[56,1024]{1,0:T(8,128)(2,1)S(1)} %get-tuple-element.48.refs_1_.refs_0_.refs_4_), custom_call_target="tpu_custom_call" | custom-call | flops 1 | bytes 1 | tf_op jit(solution)/shard_map/turn_weights/turn_down/pallas_call | solution.py:489
  13.2 2.3 %collective-permute-done.4.refs_0_.refs_2_ = bf16[8,6272]{1,0:T(8,128)(2,1)S(1)} collective-permute-done((bf16[8,6272]{1,0:T(8,128)(2,1)S(1)}, bf16[8,6272]{1,0:T(8,128)(2,1)S(1)}, u32[]{:S(2)}, u32[]{:S(2)}) %collective-permute-start.4) | collective-permute-done | bytes 100384 | tf_op jit(solution)/shard_map/gather_blocks/ppermute | solution.py:45
  15.5 0.7 %route1.1 = (bf16[56,1024]{1,0:T(8,128)(2,1)S(1)}, bf16[56,1024]{1,0:T(8,128)(2,1)S(1)}, bf16[56,1024]{1,0:T(8,128)(2,1)S(1)}, bf16[56,1024]{1,0:T(8,128)(2,1)S(1)}) custom-call(bf16[8,6272]{1,0:T(8,128)(2,1)S(1)} %collective-permute-done.4.refs_0_.refs_2_, bf16[8,6272]{1,0:T(8,128)(2,1)S(1)} %collective-permute-done.5.refs_1_.refs_3_, ...), custom_call_target="tpu_custom_call" | custom-call | flops 9000000512 | bytes 1 | tf_op jit(solution)/shard_map/far_blocks/route1/pallas_call | solution.py:459
  16.2 2.5 %collective-permute-start.6 = (bf16[56,1024]{1,0:T(8,128)(2,1)S(1)}, bf16[56,1024]{1,0:T(8,128)(2,1)S(1)}, u32[]{:S(2)}, u32[]{:S(2)}) collective-permute-start(bf16[56,1024]{1,0:T(8,128)(2,1)S(1)} %get-tuple-element.54), channel_id=1, source_target_pairs={{0,6},{2,4},{4,2},{6,0},{8,14},{10,12},{12,10},{14,8},{16,22},{18,... | collective-permute-start | bytes 344072 | tf_op jit(solution)/shard_map/far_blocks/ppermute | solution.py:53
  19.3 0.5 %collective-permute-start.8 = (bf16[56,1024]{1,0:T(8,128)(2,1)S(1)}, bf16[56,1024]{1,0:T(8,128)(2,1)S(1)}, u32[]{:S(2)}, u32[]{:S(2)}) collective-permute-start(bf16[56,1024]{1,0:T(8,128)(2,1)S(1)} %get-tuple-element.56), channel_id=1, source_target_pairs={{0,2},{2,0},{4,6},{6,4},{8,10},{10,8},{12,14},{14,12},{16,18},{18,... | collective-permute-start | bytes 344072 | tf_op jit(solution)/shard_map/far_blocks/ppermute | solution.py:53
  19.8 2.4 %turn_rest.1 = (bf16[512,4096]{1,0:T(8,128)(2,1)S(1)}, bf16[512,4096]{1,0:T(8,128)(2,1)S(1)}, f32[8,128]{1,0:T(8,128)S(1)}) custom-call(bf16[1,4096,512]{2,1,0:T(8,128)(2,1)S(1)} %copy-done.1, bf16[1,4096,512]{2,1,0:T(8,128)(2,1)S(1)} %copy-done.2, bf16[56,1024]{1,0:T(8,128)(2,1)S(1)} %get-tuple-element.53.refs_4_.refs_2_.refs_0_), custom_call_target="tpu_custom_call" | custom-call | flops 3000000000 | bytes 1 | tf_op jit(solution)/shard_map/turn_weights/turn_rest/pallas_call | solution.py:489
  23.0 1.0 %collective-permute-done.7.refs_2_ = bf16[56,1024]{1,0:T(8,128)(2,1)S(1)} collective-permute-done((bf16[56,1024]{1,0:T(8,128)(2,1)S(1)}, bf16[56,1024]{1,0:T(8,128)(2,1)S(1)}, u32[]{:S(2)}, u32[]{:S(2)}) %collective-permute-start.7) | collective-permute-done | bytes 114720 | tf_op jit(solution)/shard_map/far_blocks/ppermute | solution.py:53
  24.3 0.7 %forward_own.1 = (f32[128,512]{1,0:T(8,128)S(1)}, f32[128,512]{1,0:T(8,128)S(1)}) custom-call(bf16[128,2048]{1,0:T(8,128)(2,1)S(1)} %stack0.1.refs_0_, bf16[128,2048]{1,0:T(8,128)(2,1)S(1)} %stack1.1.refs_1_, bf16[1,4096,512]{2,1,0:T(8,128)(2,1)S(1)} %copy-done.1, bf16[1,4096,512]{2,1,0:T(8,128)(2,1)S(1)} %copy-done.2), custom_call_target="tpu_custom_call" | custom-call | flops 1 | bytes 1 | tf_op jit(solution)/shard_map/forward/forward_own/pallas_call | solution.py:525
  25.5 0.7 %collective-permute-done.10.refs_6_.refs_7_.refs_3_ = bf16[128,2048]{1,0:T(8,128)(2,1)S(1)} collective-permute-done((bf16[128,2048]{1,0:T(8,128)(2,1)S(1)}, bf16[128,2048]{1,0:T(8,128)(2,1)S(1)}, u32[]{:S(2)}, u32[]{:S(2)}) %collective-permute-start.10) | collective-permute-done | bytes 524320 | tf_op jit(solution)/shard_map/gather_cores/ppermute | solution.py:58
  26.2 1.4 %forward.1 = (f32[128,512]{1,0:T(8,128)S(1)}, f32[128,512]{1,0:T(8,128)S(1)}, bf16[128,512]{1,0:T(8,128)(2,1)S(1)}, bf16[128,2048]{1,0:T(8,128)(2,1)S(1)}, bf16[128,2048]{1,0:T(8,128)(2,1)S(1)}) custom-call(f32[128,512]{1,0:T(8,128)S(1)} %get-tuple-element.59.refs_0_, f32[128,512]{1,0:T(8,128)S(1)} %get-tuple-element.60.refs_1_, ...), custom_call_target="tpu_custom_call" | custom-call | flops 1 | bytes 1 | tf_op jit(solution)/shard_map/forward/forward/pallas_call | solution.py:543
  27.8 1.2 %backward.1 = (bf16[128,512]{1,0:T(8,128)(2,1)S(1)}, bf16[128,512]{1,0:T(8,128)(2,1)S(1)}, bf16[128,2048]{1,0:T(8,128)(2,1)S(1)}) custom-call(f32[128,512]{1,0:T(8,128)S(1)} %backward_own.1.refs_7_.refs_0_, bf16[512,4096]{1,0:T(8,128)(2,1)S(1)} %get-tuple-element.75.refs_1_.refs_2_, bf16[512,4096]{1,0:T(8,128)(2,1)S(1)} %get-tuple-element.76.refs_2_.refs_3_, ...), custom_call_target="tpu_custom_call" | custom-call | flops 1 | bytes 1 | tf_op jit(solution)/shard_map/backward/backward/pallas_call | solution.py:591
  29.8 1.0 %collective-permute-start.12 = (bf16[56,1024]{1,0:T(8,128)(2,1)S(1)}, bf16[56,1024]{1,0:T(8,128)(2,1)S(1)}, u32[]{:S(2)}, u32[]{:S(2)}) collective-permute-start(bf16[56,1024]{1,0:T(8,128)(2,1)S(1)} %get-tuple-element.65), channel_id=1, source_target_pairs={{0,2},{2,0},{4,6},{6,4},{8,10},{10,8},{12,14},{14,12},{16,18},{18,... | collective-permute-start | bytes 344072 | tf_op jit(solution)/shard_map/return_out/ppermute | solution.py:53
  30.8 1.5 %collective-permute-start.13 = (bf16[56,1024]{1,0:T(8,128)(2,1)S(1)}, bf16[56,1024]{1,0:T(8,128)(2,1)S(1)}, u32[]{:S(2)}, u32[]{:S(2)}) collective-permute-start(bf16[56,1024]{1,0:T(8,128)(2,1)S(1)} %get-tuple-element.66), channel_id=1, source_target_pairs={{0,4},{2,6},{4,0},{6,2},{8,12},{10,14},{12,8},{14,10},{16,20},{18,... | collective-permute-start | bytes 344072 | tf_op jit(solution)/shard_map/return_out/ppermute | solution.py:53
  32.3 1.0 %collective-permute-start.14 = (bf16[56,1024]{1,0:T(8,128)(2,1)S(1)}, bf16[56,1024]{1,0:T(8,128)(2,1)S(1)}, u32[]{:S(2)}, u32[]{:S(2)}) collective-permute-start(bf16[56,1024]{1,0:T(8,128)(2,1)S(1)} %get-tuple-element.67), channel_id=1, source_target_pairs={{0,6},{2,4},{4,2},{6,0},{8,14},{10,12},{12,10},{14,8},{16,22},{18,... | collective-permute-start | bytes 344072 | tf_op jit(solution)/shard_map/return_out/ppermute | solution.py:53
  33.3 0.8 %input_own.1.refs_0_ = bf16[128,2048]{1,0:T(8,128)(2,1)S(1)} custom-call(bf16[128,512]{1,0:T(8,128)(2,1)S(1)} %get-tuple-element.79.refs_0_, bf16[128,512]{1,0:T(8,128)(2,1)S(1)} %get-tuple-element.80.refs_1_, bf16[512,4096]{1,0:T(8,128)(2,1)S(1)} %get-tuple-element.75.refs_1_.refs_2_, bf16[512,4096]{1,0:T(8,128)(2,1)S(1)} %get-tuple-element.76.refs_2_.refs_3_, ...), custom_call_target="tpu_custom_call" | custom-call | flops 1 | bytes 1 | tf_op jit(solution)/shard_map/backward/input_own/pallas_call | solution.py:600
  34.4 1.0 %collective-permute-start.19 = (bf16[56,1024]{1,0:T(8,128)(2,1)S(1)}, bf16[56,1024]{1,0:T(8,128)(2,1)S(1)}, u32[]{:S(2)}, u32[]{:S(2)}) collective-permute-start(bf16[56,1024]{1,0:T(8,128)(2,1)S(1)} %get-tuple-element.83), channel_id=1, source_target_pairs={{0,2},{2,0},{4,6},{6,4},{8,10},{10,8},{12,14},{14,12},{16,18},{18,... | collective-permute-start | bytes 344072 | tf_op jit(solution)/shard_map/return_grad/ppermute | solution.py:53
  35.3 1.5 %collective-permute-start.20 = (bf16[56,1024]{1,0:T(8,128)(2,1)S(1)}, bf16[56,1024]{1,0:T(8,128)(2,1)S(1)}, u32[]{:S(2)}, u32[]{:S(2)}) collective-permute-start(bf16[56,1024]{1,0:T(8,128)(2,1)S(1)} %get-tuple-element.84), channel_id=1, source_target_pairs={{0,4},{2,6},{4,0},{6,2},{8,12},{10,14},{12,8},{14,10},{16,20},{18,... | collective-permute-start | bytes 344072 | tf_op jit(solution)/shard_map/return_grad/ppermute | solution.py:53
  36.8 1.1 %collective-permute-start.21 = (bf16[56,1024]{1,0:T(8,128)(2,1)S(1)}, bf16[56,1024]{1,0:T(8,128)(2,1)S(1)}, u32[]{:S(2)}, u32[]{:S(2)}) collective-permute-start(bf16[56,1024]{1,0:T(8,128)(2,1)S(1)} %get-tuple-element.85), channel_id=1, source_target_pairs={{0,6},{2,4},{4,2},{6,0},{8,14},{10,12},{12,10},{14,8},{16,22},{18,... | collective-permute-start | bytes 344072 | tf_op jit(solution)/shard_map/return_grad/ppermute | solution.py:53
  37.9 1.3 %collective-permute-done.14.refs_3_ = bf16[56,1024]{1,0:T(8,128)(2,1)S(1)} collective-permute-done((bf16[56,1024]{1,0:T(8,128)(2,1)S(1)}, bf16[56,1024]{1,0:T(8,128)(2,1)S(1)}, u32[]{:S(2)}, u32[]{:S(2)}) %collective-permute-start.14) | collective-permute-done | bytes 114720 | tf_op jit(solution)/shard_map/return_out/ppermute | solution.py:53
  39.5 2.7 %collective-permute-start.15 = (bf16[24,1024]{1,0:T(8,128)(2,1)S(1)}, bf16[24,1024]{1,0:T(8,128)(2,1)S(1)}, u32[]{:S(2)}, u32[]{:S(2)}) collective-permute-start(bf16[24,1024]{1,0:T(8,128)(2,1)S(1)} %get-tuple-element.71), channel_id=1, source_target_pairs={{0,24},{2,26},{4,28},{6,30},{8,16},{10,18},{12,20},{14,22},{16,8},... | collective-permute-start | bytes 147464 | tf_op jit(solution)/shard_map/return_out/ppermute | solution.py:45
  42.7 1.3 %collective-permute-start.17 = (bf16[24,1024]{1,0:T(8,128)(2,1)S(1)}, bf16[24,1024]{1,0:T(8,128)(2,1)S(1)}, u32[]{:S(2)}, u32[]{:S(2)}) collective-permute-start(bf16[24,1024]{1,0:T(8,128)(2,1)S(1)} %get-tuple-element.73), channel_id=1, source_target_pairs={{0,8},{2,10},{4,12},{6,14},{8,0},{10,2},{12,4},{14,6},{16,24},{18,... | collective-permute-start | bytes 147464 | tf_op jit(solution)/shard_map/return_out/ppermute | solution.py:45
  44.2 2.7 %collective-permute-start.22 = (bf16[24,1024]{1,0:T(8,128)(2,1)S(1)}, bf16[24,1024]{1,0:T(8,128)(2,1)S(1)}, u32[]{:S(2)}, u32[]{:S(2)}) collective-permute-start(bf16[24,1024]{1,0:T(8,128)(2,1)S(1)} %get-tuple-element.88), channel_id=1, source_target_pairs={{0,24},{2,26},{4,28},{6,30},{8,16},{10,18},{12,20},{14,22},{16,8},... | collective-permute-start | bytes 147464 | tf_op jit(solution)/shard_map/return_grad/ppermute | solution.py:45
  46.9 1.8 %collective-permute-start.24 = (bf16[24,1024]{1,0:T(8,128)(2,1)S(1)}, bf16[24,1024]{1,0:T(8,128)(2,1)S(1)}, u32[]{:S(2)}, u32[]{:S(2)}) collective-permute-start(bf16[24,1024]{1,0:T(8,128)(2,1)S(1)} %get-tuple-element.90), channel_id=1, source_target_pairs={{0,8},{2,10},{4,12},{6,14},{8,0},{10,2},{12,4},{14,6},{16,24},{18,... | collective-permute-start | bytes 147464 | tf_op jit(solution)/shard_map/return_grad/ppermute | solution.py:45
  48.7 2.4 %down_grad.1 = bf16[1,512,4096]{2,1,0:T(8,128)(2,1)} custom-call(bf16[128,2048]{1,0:T(8,128)(2,1)S(1)} %stack0.1.refs_0_, bf16[128,2048]{1,0:T(8,128)(2,1)S(1)} %stack1.1.refs_1_, bf16[128,2048]{1,0:T(8,128)(2,1)S(1)} %collective-permute-done.9.refs_5_.refs_6_.refs_2_, bf16[128,2048]{1,0:T(8,128)(2,1)S(1)} %collective-permute-done.10.refs_6_.refs_7_.refs_3_, ...), custom_call_target="tpu_custom_call" | custom-call | tf_op jit(solution)/shard_map/down_grad/down_grad/pallas_call | solution.py:616
  51.1 0.7 %final.2 = (bf16[12,2048]{1,0:T(8,128)(2,1)}, f32[8,128]{1,0:T(8,128)S(1)}) custom-call(bf16[24,1024]{1,0:T(8,128)(2,1)S(1)} %get-tuple-element.70.refs_0_, bf16[24,1024]{1,0:T(8,128)(2,1)S(1)} %collective-permute-done.15.refs_1_, bf16[24,1024]{1,0:T(8,128)(2,1)S(1)} %collective-permute-done.16.refs_2_, bf16[24,1024]{1,0:T(8,128)(2,1)S(1)} %collective-permute-done.17.refs_3_), custom_call_target="tpu_custom_call" | custom-call | tf_op jit(solution)/shard_map/final/pallas_call | solution.py:577
  51.9 0.7 %final.3 = bf16[12,2048]{1,0:T(8,128)(2,1)} custom-call(bf16[24,1024]{1,0:T(8,128)(2,1)S(1)} %get-tuple-element.87.refs_0_.refs_5_, bf16[24,1024]{1,0:T(8,128)(2,1)S(1)} %collective-permute-done.22.refs_1_, bf16[24,1024]{1,0:T(8,128)(2,1)S(1)} %collective-permute-done.23.refs_2_, bf16[24,1024]{1,0:T(8,128)(2,1)S(1)} %collective-permute-done.24.refs_3_, ...), custom_call_target="tpu_custom_call" | custom-call | tf_op jit(solution)/shard_map/final/pallas_call | solution.py:577
  (44 shorter events, 4.8 us)
Async XLA Ops:
  1.8 10.2 %copy-start = (bf16[1,512,4096]{2,1,0:T(8,128)(2,1)S(1)}, bf16[1,512,4096]{2,1,0:T(8,128)(2,1)}, u32[]{:S(2)}) copy-start(bf16[1,512,4096]{2,1,0:T(8,128)(2,1)} %refs_4_.1) | copy-start | bytes 12582916
  1.8 5.9 %collective-permute-start = (bf16[8,6272]{1,0:T(8,128)(2,1)S(1)}, bf16[8,6272]{1,0:T(8,128)(2,1)S(1)}, u32[]{:S(2)}, u32[]{:S(2)}) collective-permute-start(bf16[8,6272]{1,0:T(8,128)(2,1)S(1)} %prepare.1.refs_0_), channel_id=1, source_target_pairs={{0,8},{2,10},{4,12},{6,14},{8,0},{10,2},{12,4},{14,6},{16,24},{18,... | collective-permute-start | bytes 301064 | tf_op jit(solution)/shard_map/gather_blocks/ppermute | solution.py:45
  4.9 10.6 %collective-permute-start.4 = (bf16[8,6272]{1,0:T(8,128)(2,1)S(1)}, bf16[8,6272]{1,0:T(8,128)(2,1)S(1)}, u32[]{:S(2)}, u32[]{:S(2)}) collective-permute-start(bf16[8,6272]{1,0:T(8,128)(2,1)S(1)} %prepare.1.refs_0_), channel_id=1, source_target_pairs={{0,16},{2,18},{4,20},{6,22},{8,24},{10,26},{12,28},{14,30},{16,0},... | collective-permute-start | bytes 301064 | tf_op jit(solution)/shard_map/gather_blocks/ppermute | solution.py:45
  7.5 8.0 %collective-permute-start.5 = (bf16[8,6272]{1,0:T(8,128)(2,1)S(1)}, bf16[8,6272]{1,0:T(8,128)(2,1)S(1)}, u32[]{:S(2)}, u32[]{:S(2)}) collective-permute-start(bf16[8,6272]{1,0:T(8,128)(2,1)S(1)} %prepare.1.refs_0_), channel_id=1, source_target_pairs={{0,24},{2,26},{4,28},{6,30},{8,16},{10,18},{12,20},{14,22},{16,8},... | collective-permute-start | bytes 301064 | tf_op jit(solution)/shard_map/gather_blocks/ppermute | solution.py:45
  8.5 10.8 %collective-permute-start.1 = (bf16[56,1024]{1,0:T(8,128)(2,1)S(1)}, bf16[56,1024]{1,0:T(8,128)(2,1)S(1)}, u32[]{:S(2)}, u32[]{:S(2)}) collective-permute-start(bf16[56,1024]{1,0:T(8,128)(2,1)S(1)} %get-tuple-element.49), channel_id=1, source_target_pairs={{0,6},{2,4},{4,2},{6,0},{8,14},{10,12},{12,10},{14,8},{16,22},{18,... | collective-permute-start | bytes 344072 | tf_op jit(solution)/shard_map/near_blocks/ppermute | solution.py:53
  11.2 11.5 %collective-permute-start.2 = (bf16[56,1024]{1,0:T(8,128)(2,1)S(1)}, bf16[56,1024]{1,0:T(8,128)(2,1)S(1)}, u32[]{:S(2)}, u32[]{:S(2)}) collective-permute-start(bf16[56,1024]{1,0:T(8,128)(2,1)S(1)} %get-tuple-element.50), channel_id=1, source_target_pairs={{0,4},{2,6},{4,0},{6,2},{8,12},{10,14},{12,8},{14,10},{16,20},{18,... | collective-permute-start | bytes 344072 | tf_op jit(solution)/shard_map/near_blocks/ppermute | solution.py:53
  11.8 11.0 %collective-permute-start.3 = (bf16[56,1024]{1,0:T(8,128)(2,1)S(1)}, bf16[56,1024]{1,0:T(8,128)(2,1)S(1)}, u32[]{:S(2)}, u32[]{:S(2)}) collective-permute-start(bf16[56,1024]{1,0:T(8,128)(2,1)S(1)} %get-tuple-element.51), channel_id=1, source_target_pairs={{0,2},{2,0},{4,6},{6,4},{8,10},{10,8},{12,14},{14,12},{16,18},{18,... | collective-permute-start | bytes 344072 | tf_op jit(solution)/shard_map/near_blocks/ppermute | solution.py:53
  15.5 4.3 %copy-start.1 = (bf16[1,4096,512]{2,1,0:T(8,128)(2,1)S(1)}, bf16[1,4096,512]{2,1,0:T(8,128)(2,1)}, u32[]{:S(2)}) copy-start(bf16[1,4096,512]{2,1,0:T(8,128)(2,1)} %refs_2_.5) | copy-start | bytes 12582916
  15.5 4.3 %copy-start.2 = (bf16[1,4096,512]{2,1,0:T(8,128)(2,1)S(1)}, bf16[1,4096,512]{2,1,0:T(8,128)(2,1)}, u32[]{:S(2)}) copy-start(bf16[1,4096,512]{2,1,0:T(8,128)(2,1)} %refs_3_.5) | copy-start | bytes 12582916
  16.2 6.7 %collective-permute-start.6 = (bf16[56,1024]{1,0:T(8,128)(2,1)S(1)}, bf16[56,1024]{1,0:T(8,128)(2,1)S(1)}, u32[]{:S(2)}, u32[]{:S(2)}) collective-permute-start(bf16[56,1024]{1,0:T(8,128)(2,1)S(1)} %get-tuple-element.54), channel_id=1, source_target_pairs={{0,6},{2,4},{4,2},{6,0},{8,14},{10,12},{12,10},{14,8},{16,22},{18,... | collective-permute-start | bytes 344072 | tf_op jit(solution)/shard_map/far_blocks/ppermute | solution.py:53
  18.8 5.2 %collective-permute-start.7 = (bf16[56,1024]{1,0:T(8,128)(2,1)S(1)}, bf16[56,1024]{1,0:T(8,128)(2,1)S(1)}, u32[]{:S(2)}, u32[]{:S(2)}) collective-permute-start(bf16[56,1024]{1,0:T(8,128)(2,1)S(1)} %get-tuple-element.55), channel_id=1, source_target_pairs={{0,4},{2,6},{4,0},{6,2},{8,12},{10,14},{12,8},{14,10},{16,20},{18,... | collective-permute-start | bytes 344072 | tf_op jit(solution)/shard_map/far_blocks/ppermute | solution.py:53
  19.3 4.8 %collective-permute-start.8 = (bf16[56,1024]{1,0:T(8,128)(2,1)S(1)}, bf16[56,1024]{1,0:T(8,128)(2,1)S(1)}, u32[]{:S(2)}, u32[]{:S(2)}) collective-permute-start(bf16[56,1024]{1,0:T(8,128)(2,1)S(1)} %get-tuple-element.56), channel_id=1, source_target_pairs={{0,2},{2,0},{4,6},{6,4},{8,10},{10,8},{12,14},{14,12},{16,18},{18,... | collective-permute-start | bytes 344072 | tf_op jit(solution)/shard_map/far_blocks/ppermute | solution.py:53
  22.9 2.6 %collective-permute-start.9 = (bf16[128,2048]{1,0:T(8,128)(2,1)S(1)}, bf16[128,2048]{1,0:T(8,128)(2,1)S(1)}, u32[]{:S(2)}, u32[]{:S(2)}) collective-permute-start(bf16[128,2048]{1,0:T(8,128)(2,1)S(1)} %stack0.1.refs_0_), channel_id=1, source_target_pairs={{0,1},{1,0},{2,3},{3,2},{4,5},{5,4},{6,7},{7,6},{8,9},{9,8},{10,11... | collective-permute-start | bytes 1572872 | tf_op jit(solution)/shard_map/gather_cores/ppermute | solution.py:58
  24.2 2.0 %collective-permute-start.10 = (bf16[128,2048]{1,0:T(8,128)(2,1)S(1)}, bf16[128,2048]{1,0:T(8,128)(2,1)S(1)}, u32[]{:S(2)}, u32[]{:S(2)}) collective-permute-start(bf16[128,2048]{1,0:T(8,128)(2,1)S(1)} %stack1.1.refs_1_), channel_id=1, source_target_pairs={{0,1},{1,0},{2,3},{3,2},{4,5},{5,4},{6,7},{7,6},{8,9},{9,8},{10,11... | collective-permute-start | bytes 1572872 | tf_op jit(solution)/shard_map/gather_cores/ppermute | solution.py:58
  27.6 2.0 %collective-permute-start.11 = (bf16[128,2048]{1,0:T(8,128)(2,1)S(1)}, bf16[128,2048]{1,0:T(8,128)(2,1)S(1)}, u32[]{:S(2)}, u32[]{:S(2)}) collective-permute-start(bf16[128,2048]{1,0:T(8,128)(2,1)S(1)} %get-tuple-element.63), channel_id=1, source_target_pairs={{0,1},{1,0},{2,3},{3,2},{4,5},{5,4},{6,7},{7,6},{8,9},{9,8},{10,11... | collective-permute-start | bytes 1572872 | tf_op jit(solution)/shard_map/return_out/ppermute | solution.py:58
  29.0 5.1 %collective-permute-start.18 = (bf16[128,2048]{1,0:T(8,128)(2,1)S(1)}, bf16[128,2048]{1,0:T(8,128)(2,1)S(1)}, u32[]{:S(2)}, u32[]{:S(2)}) collective-permute-start(bf16[128,2048]{1,0:T(8,128)(2,1)S(1)} %get-tuple-element.81), channel_id=1, source_target_pairs={{0,1},{1,0},{2,3},{3,2},{4,5},{5,4},{6,7},{7,6},{8,9},{9,8},{10,11... | collective-permute-start | bytes 1572872 | tf_op jit(solution)/shard_map/return_grad/ppermute | solution.py:58
  29.8 7.0 %collective-permute-start.12 = (bf16[56,1024]{1,0:T(8,128)(2,1)S(1)}, bf16[56,1024]{1,0:T(8,128)(2,1)S(1)}, u32[]{:S(2)}, u32[]{:S(2)}) collective-permute-start(bf16[56,1024]{1,0:T(8,128)(2,1)S(1)} %get-tuple-element.65), channel_id=1, source_target_pairs={{0,2},{2,0},{4,6},{6,4},{8,10},{10,8},{12,14},{14,12},{16,18},{18,... | collective-permute-start | bytes 344072 | tf_op jit(solution)/shard_map/return_out/ppermute | solution.py:53
  30.8 7.1 %collective-permute-start.13 = (bf16[56,1024]{1,0:T(8,128)(2,1)S(1)}, bf16[56,1024]{1,0:T(8,128)(2,1)S(1)}, u32[]{:S(2)}, u32[]{:S(2)}) collective-permute-start(bf16[56,1024]{1,0:T(8,128)(2,1)S(1)} %get-tuple-element.66), channel_id=1, source_target_pairs={{0,4},{2,6},{4,0},{6,2},{8,12},{10,14},{12,8},{14,10},{16,20},{18,... | collective-permute-start | bytes 344072 | tf_op jit(solution)/shard_map/return_out/ppermute | solution.py:53
  32.3 7.0 %collective-permute-start.14 = (bf16[56,1024]{1,0:T(8,128)(2,1)S(1)}, bf16[56,1024]{1,0:T(8,128)(2,1)S(1)}, u32[]{:S(2)}, u32[]{:S(2)}) collective-permute-start(bf16[56,1024]{1,0:T(8,128)(2,1)S(1)} %get-tuple-element.67), channel_id=1, source_target_pairs={{0,6},{2,4},{4,2},{6,0},{8,14},{10,12},{12,10},{14,8},{16,22},{18,... | collective-permute-start | bytes 344072 | tf_op jit(solution)/shard_map/return_out/ppermute | solution.py:53
  34.4 8.4 %collective-permute-start.19 = (bf16[56,1024]{1,0:T(8,128)(2,1)S(1)}, bf16[56,1024]{1,0:T(8,128)(2,1)S(1)}, u32[]{:S(2)}, u32[]{:S(2)}) collective-permute-start(bf16[56,1024]{1,0:T(8,128)(2,1)S(1)} %get-tuple-element.83), channel_id=1, source_target_pairs={{0,2},{2,0},{4,6},{6,4},{8,10},{10,8},{12,14},{14,12},{16,18},{18,... | collective-permute-start | bytes 344072 | tf_op jit(solution)/shard_map/return_grad/ppermute | solution.py:53
  35.3 8.7 %collective-permute-start.20 = (bf16[56,1024]{1,0:T(8,128)(2,1)S(1)}, bf16[56,1024]{1,0:T(8,128)(2,1)S(1)}, u32[]{:S(2)}, u32[]{:S(2)}) collective-permute-start(bf16[56,1024]{1,0:T(8,128)(2,1)S(1)} %get-tuple-element.84), channel_id=1, source_target_pairs={{0,4},{2,6},{4,0},{6,2},{8,12},{10,14},{12,8},{14,10},{16,20},{18,... | collective-permute-start | bytes 344072 | tf_op jit(solution)/shard_map/return_grad/ppermute | solution.py:53
  36.8 7.2 %collective-permute-start.21 = (bf16[56,1024]{1,0:T(8,128)(2,1)S(1)}, bf16[56,1024]{1,0:T(8,128)(2,1)S(1)}, u32[]{:S(2)}, u32[]{:S(2)}) collective-permute-start(bf16[56,1024]{1,0:T(8,128)(2,1)S(1)} %get-tuple-element.85), channel_id=1, source_target_pairs={{0,6},{2,4},{4,2},{6,0},{8,14},{10,12},{12,10},{14,8},{16,22},{18,... | collective-permute-start | bytes 344072 | tf_op jit(solution)/shard_map/return_grad/ppermute | solution.py:53
  39.5 7.4 %collective-permute-start.15 = (bf16[24,1024]{1,0:T(8,128)(2,1)S(1)}, bf16[24,1024]{1,0:T(8,128)(2,1)S(1)}, u32[]{:S(2)}, u32[]{:S(2)}) collective-permute-start(bf16[24,1024]{1,0:T(8,128)(2,1)S(1)} %get-tuple-element.71), channel_id=1, source_target_pairs={{0,24},{2,26},{4,28},{6,30},{8,16},{10,18},{12,20},{14,22},{16,8},... | collective-permute-start | bytes 147464 | tf_op jit(solution)/shard_map/return_out/ppermute | solution.py:45
  42.2 8.9 %collective-permute-start.16 = (bf16[24,1024]{1,0:T(8,128)(2,1)S(1)}, bf16[24,1024]{1,0:T(8,128)(2,1)S(1)}, u32[]{:S(2)}, u32[]{:S(2)}) collective-permute-start(bf16[24,1024]{1,0:T(8,128)(2,1)S(1)} %get-tuple-element.72), channel_id=1, source_target_pairs={{0,16},{2,18},{4,20},{6,22},{8,24},{10,26},{12,28},{14,30},{16,0},... | collective-permute-start | bytes 147464 | tf_op jit(solution)/shard_map/return_out/ppermute | solution.py:45
  42.7 8.4 %collective-permute-start.17 = (bf16[24,1024]{1,0:T(8,128)(2,1)S(1)}, bf16[24,1024]{1,0:T(8,128)(2,1)S(1)}, u32[]{:S(2)}, u32[]{:S(2)}) collective-permute-start(bf16[24,1024]{1,0:T(8,128)(2,1)S(1)} %get-tuple-element.73), channel_id=1, source_target_pairs={{0,8},{2,10},{4,12},{6,14},{8,0},{10,2},{12,4},{14,6},{16,24},{18,... | collective-permute-start | bytes 147464 | tf_op jit(solution)/shard_map/return_out/ppermute | solution.py:45
  44.2 7.5 %collective-permute-start.22 = (bf16[24,1024]{1,0:T(8,128)(2,1)S(1)}, bf16[24,1024]{1,0:T(8,128)(2,1)S(1)}, u32[]{:S(2)}, u32[]{:S(2)}) collective-permute-start(bf16[24,1024]{1,0:T(8,128)(2,1)S(1)} %get-tuple-element.88), channel_id=1, source_target_pairs={{0,24},{2,26},{4,28},{6,30},{8,16},{10,18},{12,20},{14,22},{16,8},... | collective-permute-start | bytes 147464 | tf_op jit(solution)/shard_map/return_grad/ppermute | solution.py:45
  46.9 5.0 %collective-permute-start.23 = (bf16[24,1024]{1,0:T(8,128)(2,1)S(1)}, bf16[24,1024]{1,0:T(8,128)(2,1)S(1)}, u32[]{:S(2)}, u32[]{:S(2)}) collective-permute-start(bf16[24,1024]{1,0:T(8,128)(2,1)S(1)} %get-tuple-element.89), channel_id=1, source_target_pairs={{0,16},{2,18},{4,20},{6,22},{8,24},{10,26},{12,28},{14,30},{16,0},... | collective-permute-start | bytes 147464 | tf_op jit(solution)/shard_map/return_grad/ppermute | solution.py:45
  46.9 5.0 %collective-permute-start.24 = (bf16[24,1024]{1,0:T(8,128)(2,1)S(1)}, bf16[24,1024]{1,0:T(8,128)(2,1)S(1)}, u32[]{:S(2)}, u32[]{:S(2)}) collective-permute-start(bf16[24,1024]{1,0:T(8,128)(2,1)S(1)} %get-tuple-element.90), channel_id=1, source_target_pairs={{0,8},{2,10},{4,12},{6,14},{8,0},{10,2},{12,4},{14,6},{16,24},{18,... | collective-permute-start | bytes 147464 | tf_op jit(solution)/shard_map/return_grad/ppermute | solution.py:45
